TPU v7x, 32 devices: a whole 2x2x4 slice. The times are simulated.
32 devices in a mesh: section: 4 (over y, x), seq: 8 (over z, core).
Axes of the slice: x: 2, y: 2, z: 4, core: 2. Of those that a mesh axis runs over, the one named last changes fastest.
Arguments:
- grad_out: bfloat16 [4, 1024, 8192], P('section', 'seq'), may hold values from -7.5 to 7.5
- queries: bfloat16 [4, 1024, 8192], P('section', 'seq'), may hold values from -2.5 to 2.5
- mem_out: bfloat16 [4, 1024, 8192], P('section', 'seq'), may hold values from -6 to 6
- row_total: bfloat16 [4, 1024, 64], P('section', 'seq'), may hold values from 8192 to 32768
- gate_logit: float32 [4, 64], P('section'), may hold values from -2 to 2
- mem_keys: bfloat16 [4, 8192, 1024], P('section', 'seq'), may hold values from -3.5 to 3.5
- mem_values: bfloat16 [4, 8192, 1024], P('section', 'seq'), may hold values from -7.5 to 7.5
- retrieved: int32 [4, 8, 8, 32], P('section'), may hold values from 0 to 63, all different within a row
Outputs:
- onward: bfloat16 [4, 1024, 8192], P('section', 'seq')
Inputs may be any that keep to these rules, and one draw needn't show every extreme that they name: `retrieved`: 32 different memory blocks for each section, key head and query block; every memory block is named somewhere, some far more often than others.
All inputs are finite; a program needn't handle non-finite values.
Results may differ from a plain program's by a relative error of at most 0.0054.
Values may be sent and summed in bfloat16 or wider, within the bound.
No kernel may reach another device: no remote copies, remote signals or barrier semaphores. Data moves between devices by JAX's collectives and lax.ppermute only.
A program may use at most 128 MiB of HBM per device.

v0:
```python
import jax
import jax.numpy as jnp
from jax import lax
from jax.sharding import PartitionSpec as P

BLOCK = 128


def passed_along(value, axis, steps):
    count = lax.axis_size(axis)
    pairs = [(source, (source + steps) % count) for source in range(count)]
    return lax.ppermute(value, axis, pairs)


def shards(grad_out, queries, mem_out, row_total, gate_logit, mem_keys, mem_values, retrieved):
    seq_count = lax.axis_size("seq")
    position = lax.axis_index("seq")
    tok_dev = grad_out.shape[1]
    full_width = grad_out.shape[2]
    head_count = gate_logit.shape[1]
    head_dim = full_width // head_count
    kv_heads = mem_keys.shape[2] // head_dim
    copies = seq_count // kv_heads
    local_heads = head_count // seq_count
    group_size = head_count // kv_heads
    mem_dev = mem_keys.shape[1]
    score_scale = head_dim ** (-0.5)
    gate_values = jax.nn.sigmoid(gate_logit[0])
    grad_three = (
        gate_values[None, :, None]
        * grad_out[0].reshape(tok_dev, head_count, head_dim).astype(jnp.float32)
    ).astype(jnp.bfloat16)
    token_delta = jnp.sum(
        grad_three.astype(jnp.float32)
        * mem_out[0].reshape(tok_dev, head_count, head_dim).astype(jnp.float32),
        axis=-1,
    )
    grad_mem = grad_three.reshape(tok_dev, full_width)
    head_grad, head_query = (
        lax.all_to_all(grad_mem, "seq", split_axis=1, concat_axis=0, tiled=True),
        lax.all_to_all(queries[0], "seq", split_axis=1, concat_axis=0, tiled=True),
    )
    row_delta, head_sum = (
        lax.all_to_all(token_delta, "seq", split_axis=1, concat_axis=0, tiled=True),
        lax.all_to_all(
            row_total[0].astype(jnp.float32), "seq", split_axis=1, concat_axis=0, tiled=True
        ),
    )
    tokens = head_grad.shape[0]
    kv_index = position * local_heads // group_size
    chosen = lax.dynamic_index_in_dim(retrieved[0], kv_index, 0, keepdims=False)
    keys_three = mem_keys[0].reshape(mem_dev, kv_heads, head_dim)
    values_three = mem_values[0].reshape(mem_dev, kv_heads, head_dim)
    keys_repeat = jnp.repeat(keys_three, copies, axis=1)
    values_repeat = jnp.repeat(values_three, copies, axis=1)
    head_keys, head_values = (
        lax.all_to_all(keys_repeat, "seq", split_axis=1, concat_axis=0, tiled=True),
        lax.all_to_all(values_repeat, "seq", split_axis=1, concat_axis=0, tiled=True),
    )
    key_blocks = head_keys.reshape(-1, BLOCK, head_dim)
    value_blocks = head_values.reshape(-1, BLOCK, head_dim)

    def one_block(pieces):
        query_tile, grad_tile, delta_tile, sum_tile, picks = pieces
        tile_keys = key_blocks[picks].reshape(-1, head_dim)
        tile_values = value_blocks[picks].reshape(-1, head_dim)
        scores = (
            jnp.einsum("qhd,kd->qhk", query_tile, tile_keys, preferred_element_type=jnp.float32)
            * score_scale
        )
        probs = jnp.exp(scores - jnp.log(sum_tile)[:, :, None])
        grad_probs = jnp.einsum(
            "qhd,kd->qhk", grad_tile, tile_values, preferred_element_type=jnp.float32
        )
        grad_scores = (probs * (grad_probs - delta_tile[:, :, None]) * score_scale).astype(
            jnp.bfloat16
        )
        result = jnp.einsum(
            "qhk,kd->qhd", grad_scores, tile_keys, preferred_element_type=jnp.float32
        )
        return result.astype(jnp.bfloat16)

    query_blocks = tokens // BLOCK
    blocks_in = (
        head_query.reshape(query_blocks, BLOCK, local_heads, head_dim),
        head_grad.reshape(query_blocks, BLOCK, local_heads, head_dim),
        row_delta.reshape(query_blocks, BLOCK, local_heads),
        head_sum.reshape(query_blocks, BLOCK, local_heads),
        chosen,
    )
    grads = lax.map(one_block, blocks_in).reshape(tokens, local_heads * head_dim)
    returned = lax.all_to_all(grads, "seq", split_axis=0, concat_axis=1, tiled=True)
    delivered = passed_along(returned, "section", -1)
    return delivered[None]


def solution(mesh):
    return jax.shard_map(
        shards,
        mesh=mesh,
        in_specs=(
            P("section", "seq", None),
            P("section", "seq", None),
            P("section", "seq", None),
            P("section", "seq", None),
            P("section", None),
            P("section", "seq", None),
            P("section", "seq", None),
            P("section", None, None, None),
        ),
        out_specs=P("section", "seq", None),
        check_vma=False,
    )
```

profile of v0, /device:TPU:0, one launch (start us, length us, event | category | flops | bytes accessed | tf_op | source)
XLA Modules:
  0.0 555.5 jit_solution(6763569713863175612)
XLA Ops:
  14.4 6.3 %all-to-all-start.5 = ((f32[128,8,8]{0,2,1:T(8,128)}), f32[128,8,8]{0,2,1:T(8,128)S(1)}, u32[]{:S(2)}, u32[]{:S(2)}) async-start(f32[128,8,8]{0,2,1:T(8,128)} %bitcast.28), calls=%async_computation.5 | async-start | bytes 65536 | tf_op jit(solution)/shard_map/all_to_all | solution.py:44
  42.1 46.8 %all-to-all-done.3 = bf16[128,8,1024]{0,2,1:T(8,128)(2,1)} async-done(((bf16[128,8,1024]{0,2,1:T(8,128)(2,1)}), bf16[128,8,1024]{0,2,1:T(8,128)(2,1)}, u32[]{:S(2)}, u32[]{:S(2)}) %all-to-all-start.3) | async-done | bytes 2097184 | tf_op jit(solution)/shard_map/all_to_all | solution.py:40
  95.5 46.8 %all-to-all-done.1 = bf16[1024,8,128]{2,0,1:T(8,128)(2,1)} async-done(((bf16[1024,8,128]{2,0,1:T(8,128)(2,1)}), bf16[1024,8,128]{2,0,1:T(8,128)(2,1)}, u32[]{:S(2)}, u32[]{:S(2)}) %all-to-all-start.1) | async-done | bytes 2097184 | tf_op jit(solution)/shard_map/all_to_all | solution.py:57
  149.2 46.6 %all-to-all-done.4 = bf16[1024,8,128]{2,0,1:T(8,128)(2,1)} async-done(((bf16[1024,8,128]{2,0,1:T(8,128)(2,1)}), bf16[1024,8,128]{2,0,1:T(8,128)(2,1)}, u32[]{:S(2)}, u32[]{:S(2)}) %all-to-all-start.4) | async-done | bytes 2097184 | tf_op jit(solution)/shard_map/all_to_all | solution.py:58
  200.4 48.8 %all-to-all-done = bf16[128,8,1024]{0,2,1:T(8,128)(2,1)} async-done(((bf16[128,8,1024]{0,2,1:T(8,128)(2,1)}), bf16[128,8,1024]{0,2,1:T(8,128)(2,1)}, u32[]{:S(2)}, u32[]{:S(2)}) %all-to-all-start) | async-done | bytes 2097184 | tf_op jit(solution)/shard_map/all_to_all | solution.py:41
  249.2 202.2 %while.10 = (s32[]{:T(128)}, bf16[8,128,8,128]{1,3,2,0:T(8,128)(2,1)}, bf16[8,128,8,128]{1,3,2,0:T(8,128)(2,1)}, s32[8,32]{1,0:T(8,128)S(1)}, bf16[64,128,128]{2...) while((s32[]{:T(128)}, ...), condition=%wide.region_2.3_spmd, body=%wide.region_1.2_spmd.sunk | while | flops 3246523392 | bytes 42760428 | solution.py:91
  251.6 9.1 %fusion.35 = f32[128,8,4096]{2,0,1:T(8,128)} fusion(bf16[4096,128,1]{1,0,2:T(8,128)(2,1)S(1)} %bitcast.105, bf16[8,128,8,128]{1,3,2,0:T(8,128)(2,1)} %get-tuple-element.165, s32[]{:T(128)} %get-tuple-element.153), kind=kOutput, calls=%fused_computation.7.clone.1 | convolution fusion | flops 1073741824 | bytes 18088448 | tf_op jit(solution)/shard_map/while/body/eval_jaxpr/qhd,kd->qhk/dot_general | solution.py:68
  263.0 10.6 %fusion.36 = bf16[1,128,8,128]{3,1,2,0:T(8,128)(2,1)S(1)} fusion(bf16[4096,128,1]{1,0,2:T(8,128)(2,1)S(1)} %bitcast.106, f32[128,8,4096]{2,0,1:T(8,128)} %fusion.35, bf16[4096,128,1]{1,0,2:T(8,128)(2,1)S(1)} %bitcast.107, f32[128,8]{0,1:T(8,128)S(1)} %get-tuple-element.141, f32[128,8]{0,1:T(8,128)S(1)} %get-tuple-element.142, ...), kind=kOutput, calls=%fused_computation.5.clone.1 | convolution fusion | flops 2172780544 | bytes 19407360 | tf_op jit(solution)/shard_map/while/body/eval_jaxpr/qhk,kd->qhd/dot_general | solution.py:78
  276.8 9.1 %fusion.35 = f32[128,8,4096]{2,0,1:T(8,128)} fusion(bf16[4096,128,1]{1,0,2:T(8,128)(2,1)S(1)} %bitcast.105, bf16[8,128,8,128]{1,3,2,0:T(8,128)(2,1)} %get-tuple-element.165, s32[]{:T(128)} %get-tuple-element.153), kind=kOutput, calls=%fused_computation.7.clone.1 | convolution fusion | flops 1073741824 | bytes 18088448 | tf_op jit(solution)/shard_map/while/body/eval_jaxpr/qhd,kd->qhk/dot_general | solution.py:68
  288.3 10.6 %fusion.36 = bf16[1,128,8,128]{3,1,2,0:T(8,128)(2,1)S(1)} fusion(bf16[4096,128,1]{1,0,2:T(8,128)(2,1)S(1)} %bitcast.106, f32[128,8,4096]{2,0,1:T(8,128)} %fusion.35, bf16[4096,128,1]{1,0,2:T(8,128)(2,1)S(1)} %bitcast.107, f32[128,8]{0,1:T(8,128)S(1)} %get-tuple-element.141, f32[128,8]{0,1:T(8,128)S(1)} %get-tuple-element.142, ...), kind=kOutput, calls=%fused_computation.5.clone.1 | convolution fusion | flops 2172780544 | bytes 19407360 | tf_op jit(solution)/shard_map/while/body/eval_jaxpr/qhk,kd->qhd/dot_general | solution.py:78
  302.1 9.1 %fusion.35 = f32[128,8,4096]{2,0,1:T(8,128)} fusion(bf16[4096,128,1]{1,0,2:T(8,128)(2,1)S(1)} %bitcast.105, bf16[8,128,8,128]{1,3,2,0:T(8,128)(2,1)} %get-tuple-element.165, s32[]{:T(128)} %get-tuple-element.153), kind=kOutput, calls=%fused_computation.7.clone.1 | convolution fusion | flops 1073741824 | bytes 18088448 | tf_op jit(solution)/shard_map/while/body/eval_jaxpr/qhd,kd->qhk/dot_general | solution.py:68
  313.5 10.6 %fusion.36 = bf16[1,128,8,128]{3,1,2,0:T(8,128)(2,1)S(1)} fusion(bf16[4096,128,1]{1,0,2:T(8,128)(2,1)S(1)} %bitcast.106, f32[128,8,4096]{2,0,1:T(8,128)} %fusion.35, bf16[4096,128,1]{1,0,2:T(8,128)(2,1)S(1)} %bitcast.107, f32[128,8]{0,1:T(8,128)S(1)} %get-tuple-element.141, f32[128,8]{0,1:T(8,128)S(1)} %get-tuple-element.142, ...), kind=kOutput, calls=%fused_computation.5.clone.1 | convolution fusion | flops 2172780544 | bytes 19407360 | tf_op jit(solution)/shard_map/while/body/eval_jaxpr/qhk,kd->qhd/dot_general | solution.py:78
  327.4 9.1 %fusion.35 = f32[128,8,4096]{2,0,1:T(8,128)} fusion(bf16[4096,128,1]{1,0,2:T(8,128)(2,1)S(1)} %bitcast.105, bf16[8,128,8,128]{1,3,2,0:T(8,128)(2,1)} %get-tuple-element.165, s32[]{:T(128)} %get-tuple-element.153), kind=kOutput, calls=%fused_computation.7.clone.1 | convolution fusion | flops 1073741824 | bytes 18088448 | tf_op jit(solution)/shard_map/while/body/eval_jaxpr/qhd,kd->qhk/dot_general | solution.py:68
  338.8 10.6 %fusion.36 = bf16[1,128,8,128]{3,1,2,0:T(8,128)(2,1)S(1)} fusion(bf16[4096,128,1]{1,0,2:T(8,128)(2,1)S(1)} %bitcast.106, f32[128,8,4096]{2,0,1:T(8,128)} %fusion.35, bf16[4096,128,1]{1,0,2:T(8,128)(2,1)S(1)} %bitcast.107, f32[128,8]{0,1:T(8,128)S(1)} %get-tuple-element.141, f32[128,8]{0,1:T(8,128)S(1)} %get-tuple-element.142, ...), kind=kOutput, calls=%fused_computation.5.clone.1 | convolution fusion | flops 2172780544 | bytes 19407360 | tf_op jit(solution)/shard_map/while/body/eval_jaxpr/qhk,kd->qhd/dot_general | solution.py:78
  352.7 9.1 %fusion.35 = f32[128,8,4096]{2,0,1:T(8,128)} fusion(bf16[4096,128,1]{1,0,2:T(8,128)(2,1)S(1)} %bitcast.105, bf16[8,128,8,128]{1,3,2,0:T(8,128)(2,1)} %get-tuple-element.165, s32[]{:T(128)} %get-tuple-element.153), kind=kOutput, calls=%fused_computation.7.clone.1 | convolution fusion | flops 1073741824 | bytes 18088448 | tf_op jit(solution)/shard_map/while/body/eval_jaxpr/qhd,kd->qhk/dot_general | solution.py:68
  364.1 10.6 %fusion.36 = bf16[1,128,8,128]{3,1,2,0:T(8,128)(2,1)S(1)} fusion(bf16[4096,128,1]{1,0,2:T(8,128)(2,1)S(1)} %bitcast.106, f32[128,8,4096]{2,0,1:T(8,128)} %fusion.35, bf16[4096,128,1]{1,0,2:T(8,128)(2,1)S(1)} %bitcast.107, f32[128,8]{0,1:T(8,128)S(1)} %get-tuple-element.141, f32[128,8]{0,1:T(8,128)S(1)} %get-tuple-element.142, ...), kind=kOutput, calls=%fused_computation.5.clone.1 | convolution fusion | flops 2172780544 | bytes 19407360 | tf_op jit(solution)/shard_map/while/body/eval_jaxpr/qhk,kd->qhd/dot_general | solution.py:78
  378.0 9.1 %fusion.35 = f32[128,8,4096]{2,0,1:T(8,128)} fusion(bf16[4096,128,1]{1,0,2:T(8,128)(2,1)S(1)} %bitcast.105, bf16[8,128,8,128]{1,3,2,0:T(8,128)(2,1)} %get-tuple-element.165, s32[]{:T(128)} %get-tuple-element.153), kind=kOutput, calls=%fused_computation.7.clone.1 | convolution fusion | flops 1073741824 | bytes 18088448 | tf_op jit(solution)/shard_map/while/body/eval_jaxpr/qhd,kd->qhk/dot_general | solution.py:68
  389.4 10.6 %fusion.36 = bf16[1,128,8,128]{3,1,2,0:T(8,128)(2,1)S(1)} fusion(bf16[4096,128,1]{1,0,2:T(8,128)(2,1)S(1)} %bitcast.106, f32[128,8,4096]{2,0,1:T(8,128)} %fusion.35, bf16[4096,128,1]{1,0,2:T(8,128)(2,1)S(1)} %bitcast.107, f32[128,8]{0,1:T(8,128)S(1)} %get-tuple-element.141, f32[128,8]{0,1:T(8,128)S(1)} %get-tuple-element.142, ...), kind=kOutput, calls=%fused_computation.5.clone.1 | convolution fusion | flops 2172780544 | bytes 19407360 | tf_op jit(solution)/shard_map/while/body/eval_jaxpr/qhk,kd->qhd/dot_general | solution.py:78
  403.2 9.1 %fusion.35 = f32[128,8,4096]{2,0,1:T(8,128)} fusion(bf16[4096,128,1]{1,0,2:T(8,128)(2,1)S(1)} %bitcast.105, bf16[8,128,8,128]{1,3,2,0:T(8,128)(2,1)} %get-tuple-element.165, s32[]{:T(128)} %get-tuple-element.153), kind=kOutput, calls=%fused_computation.7.clone.1 | convolution fusion | flops 1073741824 | bytes 18088448 | tf_op jit(solution)/shard_map/while/body/eval_jaxpr/qhd,kd->qhk/dot_general | solution.py:68
  414.7 10.6 %fusion.36 = bf16[1,128,8,128]{3,1,2,0:T(8,128)(2,1)S(1)} fusion(bf16[4096,128,1]{1,0,2:T(8,128)(2,1)S(1)} %bitcast.106, f32[128,8,4096]{2,0,1:T(8,128)} %fusion.35, bf16[4096,128,1]{1,0,2:T(8,128)(2,1)S(1)} %bitcast.107, f32[128,8]{0,1:T(8,128)S(1)} %get-tuple-element.141, f32[128,8]{0,1:T(8,128)S(1)} %get-tuple-element.142, ...), kind=kOutput, calls=%fused_computation.5.clone.1 | convolution fusion | flops 2172780544 | bytes 19407360 | tf_op jit(solution)/shard_map/while/body/eval_jaxpr/qhk,kd->qhd/dot_general | solution.py:78
  428.5 9.1 %fusion.35 = f32[128,8,4096]{2,0,1:T(8,128)} fusion(bf16[4096,128,1]{1,0,2:T(8,128)(2,1)S(1)} %bitcast.105, bf16[8,128,8,128]{1,3,2,0:T(8,128)(2,1)} %get-tuple-element.165, s32[]{:T(128)} %get-tuple-element.153), kind=kOutput, calls=%fused_computation.7.clone.1 | convolution fusion | flops 1073741824 | bytes 18088448 | tf_op jit(solution)/shard_map/while/body/eval_jaxpr/qhd,kd->qhk/dot_general | solution.py:68
  439.9 10.6 %fusion.36 = bf16[1,128,8,128]{3,1,2,0:T(8,128)(2,1)S(1)} fusion(bf16[4096,128,1]{1,0,2:T(8,128)(2,1)S(1)} %bitcast.106, f32[128,8,4096]{2,0,1:T(8,128)} %fusion.35, bf16[4096,128,1]{1,0,2:T(8,128)(2,1)S(1)} %bitcast.107, f32[128,8]{0,1:T(8,128)S(1)} %get-tuple-element.141, f32[128,8]{0,1:T(8,128)S(1)} %get-tuple-element.142, ...), kind=kOutput, calls=%fused_computation.5.clone.1 | convolution fusion | flops 2172780544 | bytes 19407360 | tf_op jit(solution)/shard_map/while/body/eval_jaxpr/qhk,kd->qhd/dot_general | solution.py:78
  451.4 52.6 %all_to_all.107 = bf16[8,128,1024]{1,2,0:T(8,128)(2,1)S(1)} all-to-all(bf16[8,128,1024]{1,2,0:T(8,128)(2,1)} %bitcast.115), channel_id=1, replica_groups=mesh['section'=4,'seq'=8] {'seq'}, dimensions={0} | all-to-all | bytes 4194304 | tf_op jit(solution)/shard_map/all_to_all | solution.py:92
  509.3 44.8 %collective-permute-done = bf16[128,8192]{1,0:T(8,128)(2,1)S(1)} collective-permute-done((bf16[128,8192]{1,0:T(8,128)(2,1)}, bf16[128,8192]{1,0:T(8,128)(2,1)S(1)}, u32[]{:S(2)}, u32[]{:S(2)}) %collective-permute-start) | collective-permute-done | bytes 2097184 | tf_op jit(solution)/shard_map/ppermute | solution.py:12
  (108 shorter events, 105.3 us)
Async XLA Ops:
  0.0 200.3 %copy-start = (s32[1,8,8,32]{3,2,1,0:T(8,128)S(1)}, s32[1,8,8,32]{3,2,1,0:T(8,128)}, u32[]{:S(2)}) copy-start(s32[1,8,8,32]{3,2,1,0:T(8,128)} %param.17) | copy-start | bytes 24580
  2.0 2.7 copy-start.4
  5.2 3.2 copy-start.9
  9.1 3.5 copy-start.2
  12.5 8.3 %copy-start.8 = (bf16[1,128,64]{1,2,0:T(8,128)(2,1)S(1)}, bf16[1,128,64]{1,2,0:T(8,128)(2,1)}, u32[]{:S(2)}) copy-start(bf16[1,128,64]{1,2,0:T(8,128)(2,1)} %param.13) | copy-start | bytes 49156
  12.5 9.0 %copy-start.3 = (bf16[1,128,8192]{2,1,0:T(8,128)(2,1)S(1)}, bf16[1,128,8192]{2,1,0:T(8,128)(2,1)}, u32[]{:S(2)}) copy-start(bf16[1,128,8192]{2,1,0:T(8,128)(2,1)} %param.10) | copy-start | bytes 6291460
  14.4 12.1 %all-to-all-start.5 = ((f32[128,8,8]{0,2,1:T(8,128)}), f32[128,8,8]{0,2,1:T(8,128)S(1)}, u32[]{:S(2)}, u32[]{:S(2)}) async-start(f32[128,8,8]{0,2,1:T(8,128)} %bitcast.28), calls=%async_computation.5 | async-start | bytes 65536 | tf_op jit(solution)/shard_map/all_to_all | solution.py:44
  26.5 9.0 %all-to-all-start.2 = ((f32[128,8,8]{0,2,1:T(8,128)}), f32[128,8,8]{0,2,1:T(8,128)S(1)}, u32[]{:S(2)}, u32[]{:S(2)}) async-start(f32[128,8,8]{0,2,1:T(8,128)} %bitcast_convert_fusion), calls=%async_computation.2 | async-start | bytes 65536 | tf_op jit(solution)/shard_map/all_to_all | solution.py:45
  33.6 6.2 %copy-start.5 = (bf16[1,1024,1024]{2,1,0:T(8,128)(2,1)S(1)}, bf16[1,1024,1024]{2,1,0:T(8,128)(2,1)}, u32[]{:S(2)}) copy-start(bf16[1,1024,1024]{2,1,0:T(8,128)(2,1)} %param.15) | copy-start | bytes 6291460
  35.5 53.4 %all-to-all-start.3 = ((bf16[128,8,1024]{0,2,1:T(8,128)(2,1)}), bf16[128,8,1024]{0,2,1:T(8,128)(2,1)}, u32[]{:S(2)}, u32[]{:S(2)}) async-start(bf16[128,8,1024]{0,2,1:T(8,128)(2,1)} %multiply_convert_fusion.1), calls=%async_computation.3 | async-start | bytes 4194304 | tf_op jit(solution)/shard_map/all_to_all | solution.py:40
  42.1 51.1 %copy-start.6 = (bf16[1,1024,1024]{2,1,0:T(8,128)(2,1)S(1)}, bf16[1,1024,1024]{2,1,0:T(8,128)(2,1)}, u32[]{:S(2)}) copy-start(bf16[1,1024,1024]{2,1,0:T(8,128)(2,1)} %param.16) | copy-start | bytes 6291460
  88.9 53.4 %all-to-all-start.1 = ((bf16[1024,8,128]{2,0,1:T(8,128)(2,1)}), bf16[1024,8,128]{2,0,1:T(8,128)(2,1)}, u32[]{:S(2)}, u32[]{:S(2)}) async-start(bf16[1024,8,128]{2,0,1:T(8,128)(2,1)} %copy.28), calls=%async_computation.1 | async-start | bytes 4194304 | tf_op jit(solution)/shard_map/all_to_all | solution.py:57
  95.5 51.1 %copy-start.7 = (bf16[1,128,8192]{2,1,0:T(8,128)(2,1)S(1)}, bf16[1,128,8192]{2,1,0:T(8,128)(2,1)}, u32[]{:S(2)}) copy-start(bf16[1,128,8192]{2,1,0:T(8,128)(2,1)} %param.11) | copy-start | bytes 6291460
  142.3 53.4 %all-to-all-start.4 = ((bf16[1024,8,128]{2,0,1:T(8,128)(2,1)}), bf16[1024,8,128]{2,0,1:T(8,128)(2,1)}, u32[]{:S(2)}, u32[]{:S(2)}) async-start(bf16[1024,8,128]{2,0,1:T(8,128)(2,1)} %copy.31), calls=%async_computation.4 | async-start | bytes 4194304 | tf_op jit(solution)/shard_map/all_to_all | solution.py:58
  195.7 53.4 %all-to-all-start = ((bf16[128,8,1024]{0,2,1:T(8,128)(2,1)}), bf16[128,8,1024]{0,2,1:T(8,128)(2,1)}, u32[]{:S(2)}, u32[]{:S(2)}) async-start(bf16[128,8,1024]{0,2,1:T(8,128)(2,1)} %bitcast.11), calls=%async_computation | async-start | bytes 4194304 | tf_op jit(solution)/shard_map/all_to_all | solution.py:41
  506.9 47.3 %collective-permute-start = (bf16[128,8192]{1,0:T(8,128)(2,1)}, bf16[128,8192]{1,0:T(8,128)(2,1)S(1)}, u32[]{:S(2)}, u32[]{:S(2)}) collective-permute-start(bf16[128,8192]{1,0:T(8,128)(2,1)} %copy.36), channel_id=1, source_target_pairs={{0,24},{8,0},{16,8},{24,16},{1,25},{9,1},{17,9},{25,17},{2,26},{10... | collective-permute-start | bytes 6291464 | tf_op jit(solution)/shard_map/ppermute | solution.py:12
  554.2 1.3 copy-start.1
where the time goes:
time: 557 us; the launch traced here: 555 us
  waiting for transfers between devices  238 us (43%)
  matrix products  157 us (28%)
  local copies, waits for them, and re-layouts  66.3 us (12%)
  blocking collectives  52.6 us (9%)
  starting transfers between devices  29.7 us (5%)
  other arithmetic  11.8 us (2%)
    dot_general x8, matrix products, one_block(): jnp.einsum('qhk,kd->qhd', grad_scores, tile_keys, preferred_element_type=...  84.5 us
    dot_general x8, matrix products, one_block(): jnp.einsum('qhd,kd->qhk', query_tile, tile_keys, preferred_element_type=j...  72.6 us
    all_to_all x1, blocking collectives, shards(): lax.all_to_all(grads, 'seq', split_axis=0, concat_axis=1, tiled=True)  52.6 us
    all_to_all x1, waiting for transfers between devices, shards(): lax.all_to_all(queries[0], 'seq', split_axis=1, concat_axis=0, tiled=True)  48.8 us
    all_to_all x1, waiting for transfers between devices, shards(): lax.all_to_all(keys_repeat, 'seq', split_axis=1, concat_axis=0, tiled=True)  46.8 us
    all_to_all x1, waiting for transfers between devices, shards(): lax.all_to_all(grad_mem, 'seq', split_axis=1, concat_axis=0, tiled=True)  46.8 us
    all_to_all x1, waiting for transfers between devices, shards(): lax.all_to_all(values_repeat, 'seq', split_axis=1, concat_axis=0, tiled=T...  46.6 us
    ppermute x1, waiting for transfers between devices, passed_along(): return lax.ppermute(value, axis, pairs)  44.8 us
  transfers between devices with their start and end apart: 7, of which 7 were waited for; matrix products, arithmetic and copies ran while one was open for 3% of the time, Pallas kernels for 0%

commit v1 on v0

v1 whole, which is shorter than its diff:
```python
import functools
import math

import jax
import jax.numpy as jnp
from jax import lax
from jax.experimental import pallas as pl
from jax.experimental.pallas import tpu as pltpu
from jax.sharding import PartitionSpec as P

BLOCK = 128
PARTS = 3
VMEM_LIMIT = 48 * 1024 * 1024

NT = (((1,), (1,)), ((), ()))
NN = (((1,), (0,)), ((), ()))


def split_parts(value):
    terms = []
    for _ in range(PARTS):
        term = value.astype(jnp.bfloat16)
        terms.append(term)
        value = value - term.astype(jnp.float32)
    return terms


def prepare_kernel(heads, dim, gate_ref, grad_ref, query_ref, out_ref, log_ref, packed_ref):
    rows = grad_ref.shape[0]
    first = pl.program_id(0) * heads
    deltas = []
    for h in range(heads):
        columns = slice(h * dim, (h + 1) * dim)
        gated = (gate_ref[first + h] * grad_ref[:, columns].astype(jnp.float32)).astype(jnp.bfloat16)
        packed_ref[0, h * rows:(h + 1) * rows, :] = query_ref[:, columns]
        packed_ref[0, (heads + h) * rows:(heads + h + 1) * rows, :] = gated
        product = gated.astype(jnp.float32) * out_ref[:, columns].astype(jnp.float32)
        deltas.append(jnp.sum(product.T, axis=0, keepdims=True))
    stats = jnp.concatenate(deltas + [log_ref[...]], axis=0)
    base = 2 * heads * rows
    for part, term in enumerate(split_parts(stats)):
        packed_ref[0, base + part * 2 * heads:base + (part + 1) * 2 * heads, :] = term


def prepare(grad_out, queries, mem_out, logs, gates, kv_heads, dim):
    rows, width = grad_out.shape
    heads = width // dim // kv_heads
    span = 2 * heads * rows + PARTS * 2 * heads
    wide = pl.BlockSpec((rows, heads * dim), lambda k, _: (0, k))
    return pl.pallas_call(
        functools.partial(prepare_kernel, heads, dim),
        out_shape=jax.ShapeDtypeStruct((kv_heads, span, dim), jnp.bfloat16),
        grid_spec=pltpu.PrefetchScalarGridSpec(
            num_scalar_prefetch=1,
            grid=(kv_heads,),
            in_specs=[wide, wide, wide, pl.BlockSpec((heads, rows), lambda k, _: (k, 0))],
            out_specs=pl.BlockSpec((1, span, dim), lambda k, _: (k, 0, 0)),
        ),
        compiler_params=pltpu.CompilerParams(vmem_limit_bytes=VMEM_LIMIT),
        cost_estimate=pl.CostEstimate(flops=rows * width * 4, bytes_accessed=rows * width * 12, transcendentals=0),
    )(gates, grad_out, queries, mem_out, logs)


def attend_kernel(heads, rows, dim, scale, fresh, last, places, *refs):
    count = len(places)
    picks_ref, starts_ref = refs[:2]
    packed_ref = refs[2]
    memory_refs = refs[3:3 + count]
    rest = refs[3 + count:]
    acc_in = None if fresh else rest[0]
    out_ref = rest[0] if fresh else rest[1]
    turned, total = rest[-2:]
    tile = pl.program_id(0)
    blocks = memory_refs[0].shape[1] // BLOCK
    pair = 2 * rows

    @pl.when(tile == 0)
    def _():
        for at, memory in enumerate(memory_refs):
            for block in range(blocks):
                turned[at, block] = memory[0, block * BLOCK:(block + 1) * BLOCK, :].T

    if fresh:
        total[...] = jnp.zeros_like(total)
    else:
        total[...] = acc_in[0]

    base = 2 * heads * rows
    stats = sum(
        packed_ref[0, base + part * 2 * heads:base + (part + 1) * 2 * heads, :].astype(jnp.float32)
        for part in range(PARTS)
    )
    exponent = scale * math.log2(math.e)

    for at, (place, memory) in enumerate(zip(places, memory_refs)):
        low = starts_ref[tile, place]
        high = starts_ref[tile, place + 1]

        def step(turn, carry):
            here = low + 2 * turn
            second = here + 1 < high
            one = picks_ref[tile, here]
            two = picks_ref[tile, jnp.where(second, here + 1, here)]
            row_one = pl.ds(pl.multiple_of(one * BLOCK, BLOCK), BLOCK)
            row_two = pl.ds(pl.multiple_of(two * BLOCK, BLOCK), BLOCK)
            keys = jnp.concatenate([memory[0, row_one, :], memory[0, row_two, :]], axis=0)
            values = jnp.concatenate([memory[1, row_one, :], memory[1, row_two, :]], axis=0)
            later = turned[at, two]
            later = jnp.where(second, later, jnp.zeros_like(later))
            across = jnp.concatenate([turned[at, one], later], axis=1)
            for p in range(heads // 2):
                span = slice(p * pair, (p + 1) * pair)
                grads = slice(heads * rows + p * pair, heads * rows + (p + 1) * pair)
                scores = lax.dot_general(keys, packed_ref[0, span, :], NT, preferred_element_type=jnp.float32)
                grad_probs = lax.dot_general(values, packed_ref[0, grads, :], NT, preferred_element_type=jnp.float32)
                log_row = jnp.concatenate([stats[heads + 2 * p:heads + 2 * p + 1], stats[heads + 2 * p + 1:heads + 2 * p + 2]], axis=1)
                delta_row = jnp.concatenate([stats[2 * p:2 * p + 1], stats[2 * p + 1:2 * p + 2]], axis=1)
                probs = jnp.exp2(scores * exponent - log_row)
                grad_scores = (probs * (grad_probs - delta_row)).astype(jnp.bfloat16)
                total[:, span] += lax.dot_general(across, grad_scores, NN, preferred_element_type=jnp.float32)
            return carry

        lax.fori_loop(0, (high - low + 1) // 2, step, 0)

    if last:
        for h in range(heads):
            out_ref[0, :, h * dim:(h + 1) * dim] = total[:, h * rows:(h + 1) * rows].T.astype(jnp.bfloat16)
    else:
        out_ref[0] = total[...]


def attend(packed, memories, places, acc, picks, starts, heads, rows, dim, scale, last):
    tiles, span, _ = packed.shape
    fresh = acc is None
    count = len(places)
    blocks = memories[0].shape[1] // BLOCK
    width = heads * rows
    acc_spec = pl.BlockSpec((1, dim, width), lambda t, *_: (t, 0, 0))
    if last:
        out_shape = jax.ShapeDtypeStruct((tiles, rows, heads * dim), jnp.bfloat16)
        out_spec = pl.BlockSpec((1, rows, heads * dim), lambda t, *_: (t, 0, 0))
    else:
        out_shape = jax.ShapeDtypeStruct((tiles, dim, width), jnp.float32)
        out_spec = acc_spec
    flops = tiles * count * (blocks // 2) * BLOCK * width * dim * 6
    return pl.pallas_call(
        functools.partial(attend_kernel, heads, rows, dim, scale, fresh, last, places),
        out_shape=out_shape,
        grid_spec=pltpu.PrefetchScalarGridSpec(
            num_scalar_prefetch=2,
            grid=(tiles,),
            in_specs=[pl.BlockSpec((1, span, dim), lambda t, *_: (t, 0, 0))]
            + [pl.BlockSpec(m.shape, lambda t, *_: (0, 0, 0)) for m in memories]
            + ([] if fresh else [acc_spec]),
            out_specs=out_spec,
            scratch_shapes=[
                pltpu.VMEM((count, blocks, dim, BLOCK), jnp.bfloat16),
                pltpu.VMEM((dim, width), jnp.float32),
            ],
        ),
        compiler_params=pltpu.CompilerParams(vmem_limit_bytes=VMEM_LIMIT),
        cost_estimate=pl.CostEstimate(
            flops=flops * 2, bytes_accessed=tiles * span * dim * 2 + tiles * width * dim * 8, transcendentals=0
        ),
    )(picks, starts, packed, *memories, *([] if fresh else [acc]))


def shards(grad_out, queries, mem_out, row_total, gate_logit, mem_keys, mem_values, retrieved):
    seq = lax.axis_size("seq")
    sections = lax.axis_size("section")
    position = lax.axis_index("seq")
    rows, width = grad_out.shape[1:]
    head_count = gate_logit.shape[1]
    dim = width // head_count
    kv_heads = mem_keys.shape[2] // dim
    heads = head_count // kv_heads
    mem_dev = mem_keys.shape[1]
    blocks = mem_dev // BLOCK
    group = min(kv_heads, seq // 2)
    own = kv_heads // group
    at = position % group
    scale = dim ** (-0.5)

    def swapped(value, step):
        return lax.ppermute(value, "seq", [(p, p ^ step) for p in range(seq)])

    memory = jnp.stack([mem_keys[0], mem_values[0]]).reshape(2, mem_dev, kv_heads, dim).transpose(2, 0, 1, 3)

    logs = jnp.log2(row_total[0].T.astype(jnp.float32)) - math.log2(scale)
    gates = jax.nn.sigmoid(gate_logit[0])
    packed = prepare(grad_out[0], queries[0], mem_out[0], logs, gates, kv_heads, dim)
    packed = packed.reshape(group, own, *packed.shape[1:])

    tile_of = (position // group) * group + jnp.arange(group)
    mine = lax.dynamic_slice_in_dim(retrieved[0], at * own, own, 0)
    mine = lax.dynamic_slice_in_dim(mine, (position // group) * group, group, 1)
    distance = ((mine // blocks) ^ position) * blocks + mine % blocks
    rank = jnp.sum(distance[..., None, :] < distance[..., :, None], axis=-1)
    order = jnp.arange(distance.shape[-1])
    ordered = jnp.sum(jnp.where(rank[..., :, None] == order, distance[..., :, None], 0), axis=-2)
    picks = (ordered % blocks).astype(jnp.int32)
    starts = jnp.sum(distance[..., None, :] < (jnp.arange(seq + 1) * blocks)[:, None], axis=-1).astype(jnp.int32)

    stages = [tuple(range(group))]
    half = group + (seq - group) // 2
    stages.append(tuple(range(group, half)))
    stages.append(tuple(range(half, seq)))

    groups = [list(range(g * group, (g + 1) * group)) for g in range(seq // group)]
    out = jnp.zeros((rows, width), jnp.bfloat16)
    for i in range(own):
        sends = [
            lax.dynamic_index_in_dim(memory, (at ^ x) * own + i, 0, keepdims=False) for x in range(group)
        ]
        arrived = {0: sends[0]}
        for step in range(group, seq):
            arrived[step] = swapped(sends[step % group], step)
        mixed = lax.all_to_all(
            packed[:, i], "seq", split_axis=0, concat_axis=0, axis_index_groups=groups, tiled=True
        )
        for step in range(1, group):
            arrived[step] = swapped(sends[step], step)
        acc = None
        for number, places in enumerate(stages):
            acc = attend(
                mixed, [arrived[p] for p in places], places, acc, picks[i], starts[i],
                heads, rows, dim, scale, number == len(stages) - 1,
            )
        for x in range(group):
            piece = lax.dynamic_index_in_dim(acc, at ^ x, 0, keepdims=False)
            pairs = [
                (s * seq + p, ((s - 1) % sections) * seq + (p ^ x)) for s in range(sections) for p in range(seq)
            ]
            piece = lax.ppermute(piece, ("section", "seq"), pairs)
            out = lax.dynamic_update_slice_in_dim(out, piece, ((at ^ x) * own + i) * heads * dim, 1)
    return out[None]


def solution(mesh):
    return jax.shard_map(
        shards,
        mesh=mesh,
        in_specs=(
            P("section", "seq", None),
            P("section", "seq", None),
            P("section", "seq", None),
            P("section", "seq", None),
            P("section", None),
            P("section", "seq", None),
            P("section", "seq", None),
            P("section", None, None, None),
        ),
        out_specs=P("section", "seq", None),
        check_vma=False,
    )
```

time: 557 us -> 336 us (0.60)
  Pallas kernels: 0 us -> 180 us
  waiting for transfers between devices: 238 us -> 59.4 us
  matrix products: 157 us -> 0 us
  blocking collectives: 52.6 us -> 0 us
  local copies, waits for them, and re-layouts: 66.3 us -> 47.6 us
  starting transfers between devices: 29.7 us -> 43.7 us
  other arithmetic: 11.8 us -> 5.02 us
    all_to_all x6 -> x2, waiting for transfers between devices: 193 us -> 0.01 us  [shards(): lax.all_to_all(packed[:, i], 'seq', split_axis=0, concat_axis=0, axis_ind...]
    pallas_call x0 -> x7, Pallas kernels: none -> 180 us  [the longest x6 172 us: attend(): pl.pallas_call(functools.partial(attend_kernel, heads, rows, dim, scale,...]
    dot_general x16 -> x0, matrix products: 157 us -> none  [the longest x8 84.5 us: one_block(): jnp.einsum('qhk,kd->qhd', grad_scores, tile_keys, preferred_element_type=...]
    all_to_all x1 -> x0, blocking collectives: 52.6 us -> none  [shards(): lax.all_to_all(grads, 'seq', split_axis=0, concat_axis=1, tiled=True)]
    gather x16 -> x0, local copies, waits for them, and re-layouts: 37.4 us -> none  [the longest x8 18.7 us: one_block(): tile_keys = key_blocks[picks].reshape(-1, head_dim)]
    ppermute x1 -> x22, starting transfers between devices: 2.45 us -> 34.5 us  [the longest x14 19 us: swapped(): return lax.ppermute(value, 'seq', [(p, p ^ step) for p in range(seq)])]
    another operation x2 -> x1, local copies, waits for them, and re-layouts: 3.32 us -> 21.4 us  [the longest x1 1.66 us: shards(): keys_repeat = jnp.repeat(keys_three, copies, axis=1)]
    all_to_all x6 -> x2, starting transfers between devices: 27.3 us -> 9.25 us  [shards(): lax.all_to_all(packed[:, i], 'seq', split_axis=0, concat_axis=0, axis_ind...]
  transfers between devices with their start and end apart: 7 -> 24, of which waited for: 7 -> 8; matrix products, arithmetic and copies ran while one was open for 3% -> 12% of each run, Pallas kernels for 0% -> 51%
where the time goes in v1:
time: 336 us
  Pallas kernels  180 us (54%)
  waiting for transfers between devices  59.4 us (18%)
  local copies, waits for them, and re-layouts  47.6 us (14%)
  starting transfers between devices  43.7 us (13%)
  other arithmetic  5.02 us (1%)
    pallas_call x6, Pallas kernels, attend(): pl.pallas_call(functools.partial(attend_kernel, heads, rows, dim, scale,...  172 us
    ppermute x14, waiting for transfers between devices, swapped(): return lax.ppermute(value, 'seq', [(p, p ^ step) for p in range(seq)])  33.4 us
    ppermute x8, waiting for transfers between devices, shards(): piece = lax.ppermute(piece, ('section', 'seq'), pairs)  26 us
    another operation x1, local copies, waits for them, and re-layouts  21.4 us
    ppermute x14, starting transfers between devices, swapped(): return lax.ppermute(value, 'seq', [(p, p ^ step) for p in range(seq)])  19 us
    unnamed x25, local copies, waits for them, and re-layouts  18.4 us
    ppermute x8, starting transfers between devices, shards(): piece = lax.ppermute(piece, ('section', 'seq'), pairs)  15.5 us
    all_to_all x2, starting transfers between devices, shards(): lax.all_to_all(packed[:, i], 'seq', split_axis=0, concat_axis=0, axis_ind...  9.25 us
  transfers between devices with their start and end apart: 24, of which 8 were waited for; matrix products, arithmetic and copies ran while one was open for 12% of the time, Pallas kernels for 51%

profile of v1, /device:TPU:0, one launch (start us, length us, event | category | flops | bytes accessed | tf_op | source)
XLA Modules:
  0.0 335.7 jit_solution(14591289045215335014)
XLA Ops:
  4.6 7.4 %shard_map.82 = bf16[8,2096,128]{2,1,0:T(8,128)(2,1)} custom-call(f32[64]{0:T(128)S(1)} %divide_bitcast_fusion.gate_ref, bf16[128,8192]{1,0:T(8,128)(2,1)S(1)} %bitcast.88, bf16[128,8192]{1,0:T(8,128)(2,1)S(1)} %bitcast.89, bf16[128,8192]{1,0:T(8,128)(2,1)} %bitcast.103, f32[64,128]{1,0:T(8,128)S(1)} %add_bitcast_fusion.log_ref), custom_call_target="tpu_custom_call" | custom-call | flops 4194304 | bytes 12582912 | tf_op jit(solution)/shard_map/pallas_call | solution.py:50
  12.0 4.6 %slice_bitcast_fusion = (bf16[4,2096,128]{2,1,0:T(8,128)(2,1)}, bf16[4,2096,128]{2,1,0:T(8,128)(2,1)}) fusion(bf16[4,2,2096,128]{3,2,1,0:T(8,128)(2,1)} %bitcast.101), kind=kLoop, calls=%fused_computation.1 | loop fusion | bytes 8585216 | tf_op jit(solution)/shard_map/squeeze | solution.py:219
  16.6 4.6 %all-to-all-start = ((bf16[4,2096,128]{2,1,0:T(8,128)(2,1)}), bf16[4,2096,128]{2,1,0:T(8,128)(2,1)}, u32[]{:S(2)}, u32[]{:S(2)}) async-start(bf16[4,2096,128]{2,1,0:T(8,128)(2,1)} %get-tuple-element.6), calls=%async_computation | async-start | bytes 4292608 | tf_op jit(solution)/shard_map/all_to_all | solution.py:218
  23.3 3.1 copy.49
  26.3 21.4 %constant_dynamic-slice_fusion = (bf16[2,1024,1,128]{3,2,1,0:T(2,128)(2,1)S(1)}, bf16[2,1024,1,128]{3,2,1,0:T(2,128)(2,1)}, bf16[2,1024,1,128]{3,2,1,0:T(2,128)(...) fusion(bf16[2,1024,8,128]{3,2,1,0:T(8,128)(2,1)} %bitcast.100, ...), kind=kLoop, calls=%fused_computation.32 | loop fusion | bytes 8388640 | tf_op jit(solution)/shard_map/dynamic-slice.9
  49.0 3.7 %collective-permute-start.14 = (bf16[2,1024,128]{2,1,0:T(8,128)(2,1)}, bf16[2,1024,128]{2,1,0:T(8,128)(2,1)S(1)}, u32[]{:S(2)}, u32[]{:S(2)}) collective-permute-start(bf16[2,1024,128]{2,1,0:T(8,128)(2,1)} %bitcast.80), channel_id=1, source_target_pairs={{0,5},{1,4},{2,7},{3,6},{4,1},{5,0},{6,3},{7,2},{8,13},{9,12},{10,... | collective-permute-start | bytes 1572872 | tf_op jit(solution)/shard_map/ppermute | solution.py:185
  64.4 4.7 %all-to-all-start.1 = ((bf16[4,2096,128]{2,1,0:T(8,128)(2,1)}), bf16[4,2096,128]{2,1,0:T(8,128)(2,1)}, u32[]{:S(2)}, u32[]{:S(2)}) async-start(bf16[4,2096,128]{2,1,0:T(8,128)(2,1)} %get-tuple-element.5), calls=%async_computation.1 | async-start | bytes 4292608 | tf_op jit(solution)/shard_map/all_to_all | solution.py:218
  69.7 21.1 %collective-permute-done.5.refs_5_ = bf16[2,1024,128]{2,1,0:T(8,128)(2,1)S(1)} collective-permute-done((bf16[2,1024,128]{2,1,0:T(8,128)(2,1)}, bf16[2,1024,128]{2,1,0:T(8,128)(2,1)S(1)}, u32[]{:S(2)}, u32[]{:S(2)}) %collective-permute-start.5) | collective-permute-done | bytes 524320 | tf_op jit(solution)/shard_map/ppermute | solution.py:185
  90.8 2.7 collective-permute-start
  93.6 7.3 %collective-permute-done.6.refs_6_ = bf16[2,1024,128]{2,1,0:T(8,128)(2,1)} collective-permute-done((bf16[2,1024,128]{2,1,0:T(8,128)(2,1)}, bf16[2,1024,128]{2,1,0:T(8,128)(2,1)}, u32[]{:S(2)}, u32[]{:S(2)}) %collective-permute-start.6) | collective-permute-done | bytes 524320 | tf_op jit(solution)/shard_map/ppermute | solution.py:185
  103.0 43.2 %shard_map.83.refs_5_ = f32[4,128,1024]{2,1,0:T(8,128)S(1)} custom-call(s32[4,32]{1,0:T(4,128)S(1)} %get-tuple-element.26.refs_0_, s32[4,9]{1,0:T(4,128)S(1)} %bitcast.97, bf16[4,2096,128]{2,1,0:T(8,128)(2,1)} %all-to-all-done.refs_2_, bf16[2,1024,128]{2,1,0:T(8,128)(2,1)S(1)} %bitcast.93, bf16[2,1024,128]{2,1,0:T(8,128)(2,1)S(1)} %collective-permute-done.4.refs_4_, ...), custom_call_target="tpu_custom_call" | custom-call | flops 12884901888 | bytes 6340608 | tf_op jit(solution)/shard_map/pallas_call | solution.py:146
  146.2 3.8 %collective-permute-done.2.refs_3_ = bf16[2,1024,128]{2,1,0:T(8,128)(2,1)S(1)} collective-permute-done((bf16[2,1024,128]{2,1,0:T(8,128)(2,1)S(1)}, bf16[2,1024,128]{2,1,0:T(8,128)(2,1)S(1)}, u32[]{:S(2)}, u32[]{:S(2)}) %collective-permute-start.2) | collective-permute-done | bytes 524320 | tf_op jit(solution)/shard_map/ppermute | solution.py:185
  152.3 20.5 %shard_map.84.refs_5_ = f32[4,128,1024]{2,1,0:T(8,128)S(1)} custom-call(s32[4,32]{1,0:T(4,128)S(1)} %get-tuple-element.26.refs_0_, s32[4,9]{1,0:T(4,128)S(1)} %bitcast.98, bf16[4,2096,128]{2,1,0:T(8,128)(2,1)} %all-to-all-done.refs_2_, bf16[2,1024,128]{2,1,0:T(8,128)(2,1)S(1)} %collective-permute-done.2.refs_3_, ...), custom_call_target="tpu_custom_call" | custom-call | flops 6442450944 | bytes 6340608 | tf_op jit(solution)/shard_map/pallas_call | solution.py:146
  172.8 5.1 %collective-permute-start.17 = (bf16[2,1024,128]{2,1,0:T(8,128)(2,1)}, bf16[2,1024,128]{2,1,0:T(8,128)(2,1)S(1)}, u32[]{:S(2)}, u32[]{:S(2)}) collective-permute-start(bf16[2,1024,128]{2,1,0:T(8,128)(2,1)} %bitcast.82), channel_id=1, source_target_pairs={{0,3},{1,2},{2,1},{3,0},{4,7},{5,6},{6,5},{7,4},{8,11},{9,10},{10,... | collective-permute-start | bytes 1572872 | tf_op jit(solution)/shard_map/ppermute | solution.py:185
  177.9 24.1 %shard_map.85 = bf16[4,128,1024]{2,1,0:T(8,128)(2,1)S(1)} custom-call(s32[4,32]{1,0:T(4,128)S(1)} %get-tuple-element.26.refs_0_, s32[4,9]{1,0:T(4,128)S(1)} %bitcast.99, bf16[4,2096,128]{2,1,0:T(8,128)(2,1)} %all-to-all-done.refs_2_, bf16[2,1024,128]{2,1,0:T(8,128)(2,1)S(1)} %collective-permute-done.refs_3_, ...), custom_call_target="tpu_custom_call" | custom-call | flops 6442450944 | bytes 6340608 | tf_op jit(solution)/shard_map/pallas_call | solution.py:146
  204.2 2.7 collective-permute-start.7
  207.9 40.8 %shard_map.86.refs_5_ = f32[4,128,1024]{2,1,0:T(8,128)S(1)} custom-call(s32[4,32]{1,0:T(4,128)S(1)} %get-tuple-element.25.refs_0_, s32[4,9]{1,0:T(4,128)S(1)} %bitcast.94, bf16[4,2096,128]{2,1,0:T(8,128)(2,1)} %all-to-all-done.1.refs_2_, bf16[2,1024,128]{2,1,0:T(8,128)(2,1)S(1)} %bitcast.91, bf16[2,1024,128]{2,1,0:T(8,128)(2,1)S(1)} %collective-permute-done.15.refs_4_, ...), custom_call_target="tpu_custom_call" | custom-call | flops 12884901888 | bytes 6340608 | tf_op jit(solution)/shard_map/pallas_call | solution.py:146
  252.5 22.7 %shard_map.87.refs_5_ = f32[4,128,1024]{2,1,0:T(8,128)S(1)} custom-call(s32[4,32]{1,0:T(4,128)S(1)} %get-tuple-element.25.refs_0_, s32[4,9]{1,0:T(4,128)S(1)} %bitcast.95, bf16[4,2096,128]{2,1,0:T(8,128)(2,1)} %all-to-all-done.1.refs_2_, bf16[2,1024,128]{2,1,0:T(8,128)(2,1)} %collective-permute-done.13.refs_3_, ...), custom_call_target="tpu_custom_call" | custom-call | flops 6442450944 | bytes 6340608 | tf_op jit(solution)/shard_map/pallas_call | solution.py:146
  275.2 20.8 %shard_map.88 = bf16[4,128,1024]{2,1,0:T(8,128)(2,1)S(1)} custom-call(s32[4,32]{1,0:T(4,128)S(1)} %get-tuple-element.25.refs_0_, s32[4,9]{1,0:T(4,128)S(1)} %bitcast.96, bf16[4,2096,128]{2,1,0:T(8,128)(2,1)} %all-to-all-done.1.refs_2_, bf16[2,1024,128]{2,1,0:T(8,128)(2,1)S(1)} %collective-permute-done.11.refs_3_, ...), custom_call_target="tpu_custom_call" | custom-call | flops 6442450944 | bytes 6340608 | tf_op jit(solution)/shard_map/pallas_call | solution.py:146
  296.2 3.3 collective-permute-start.18
  304.1 3.4 %collective-permute-start.20 = (bf16[128,1024]{1,0:T(8,128)(2,1)S(1)}, bf16[128,1024]{1,0:T(8,128)(2,1)S(1)}, u32[]{:S(2)}, u32[]{:S(2)}) collective-permute-start(bf16[128,1024]{1,0:T(8,128)(2,1)S(1)} %get-tuple-element.16), channel_id=1, source_target_pairs={{0,26},{1,27},{2,24},{3,25},{4,30},{5,31},{6,28},{7,29},{8,2},{9,3... | collective-permute-start | bytes 786440 | tf_op jit(solution)/shard_map/ppermute | solution.py:234
  309.7 5.3 %collective-permute-done.10 = bf16[128,1024]{1,0:T(8,128)(2,1)S(1)} collective-permute-done((bf16[128,1024]{1,0:T(8,128)(2,1)S(1)}, bf16[128,1024]{1,0:T(8,128)(2,1)S(1)}, u32[]{:S(2)}, u32[]{:S(2)}) %collective-permute-start.10) | collective-permute-done | bytes 262176 | tf_op jit(solution)/shard_map/ppermute | solution.py:234
  315.0 13.6 %collective-permute-done.18 = bf16[128,1024]{1,0:T(8,128)(2,1)S(1)} collective-permute-done((bf16[128,1024]{1,0:T(8,128)(2,1)S(1)}, bf16[128,1024]{1,0:T(8,128)(2,1)S(1)}, u32[]{:S(2)}, u32[]{:S(2)}) %collective-permute-start.18) | collective-permute-done | bytes 262176 | tf_op jit(solution)/shard_map/ppermute | solution.py:234
  328.6 5.0 %collective-permute-done.19 = bf16[128,1024]{1,0:T(8,128)(2,1)S(1)} collective-permute-done((bf16[128,1024]{1,0:T(8,128)(2,1)S(1)}, bf16[128,1024]{1,0:T(8,128)(2,1)S(1)}, u32[]{:S(2)}, u32[]{:S(2)}) %collective-permute-start.19) | collective-permute-done | bytes 262176 | tf_op jit(solution)/shard_map/ppermute | solution.py:234
  (82 shorter events, 40.5 us)
Async XLA Ops:
  16.6 47.7 %all-to-all-start = ((bf16[4,2096,128]{2,1,0:T(8,128)(2,1)}), bf16[4,2096,128]{2,1,0:T(8,128)(2,1)}, u32[]{:S(2)}, u32[]{:S(2)}) async-start(bf16[4,2096,128]{2,1,0:T(8,128)(2,1)} %get-tuple-element.6), calls=%async_computation | async-start | bytes 4292608 | tf_op jit(solution)/shard_map/all_to_all | solution.py:218
  48.6 154.4 %collective-permute-start.15 = (bf16[2,1024,128]{2,1,0:T(8,128)(2,1)}, bf16[2,1024,128]{2,1,0:T(8,128)(2,1)S(1)}, u32[]{:S(2)}, u32[]{:S(2)}) collective-permute-start(bf16[2,1024,128]{2,1,0:T(8,128)(2,1)} %bitcast.80), channel_id=1, source_target_pairs={{0,1},{1,0},{2,3},{3,2},{4,5},{5,4},{6,7},{7,6},{8,9},{9,8},{10,11... | collective-permute-start | bytes 1572872 | tf_op jit(solution)/shard_map/ppermute | solution.py:185
  49.0 203.5 %collective-permute-start.14 = (bf16[2,1024,128]{2,1,0:T(8,128)(2,1)}, bf16[2,1024,128]{2,1,0:T(8,128)(2,1)S(1)}, u32[]{:S(2)}, u32[]{:S(2)}) collective-permute-start(bf16[2,1024,128]{2,1,0:T(8,128)(2,1)} %bitcast.80), channel_id=1, source_target_pairs={{0,5},{1,4},{2,7},{3,6},{4,1},{5,0},{6,3},{7,2},{8,13},{9,12},{10,... | collective-permute-start | bytes 1572872 | tf_op jit(solution)/shard_map/ppermute | solution.py:185
  53.6 15.9 %collective-permute-start.4 = (bf16[2,1024,128]{2,1,0:T(8,128)(2,1)}, bf16[2,1024,128]{2,1,0:T(8,128)(2,1)S(1)}, u32[]{:S(2)}, u32[]{:S(2)}) collective-permute-start(bf16[2,1024,128]{2,1,0:T(8,128)(2,1)} %bitcast.84), channel_id=1, source_target_pairs={{0,1},{1,0},{2,3},{3,2},{4,5},{5,4},{6,7},{7,6},{8,9},{9,8},{10,11... | collective-permute-start | bytes 1572872 | tf_op jit(solution)/shard_map/ppermute | solution.py:185
  54.9 36.0 %collective-permute-start.5 = (bf16[2,1024,128]{2,1,0:T(8,128)(2,1)}, bf16[2,1024,128]{2,1,0:T(8,128)(2,1)S(1)}, u32[]{:S(2)}, u32[]{:S(2)}) collective-permute-start(bf16[2,1024,128]{2,1,0:T(8,128)(2,1)} %bitcast.87), channel_id=1, source_target_pairs={{0,2},{1,3},{2,0},{3,1},{4,6},{5,7},{6,4},{7,5},{8,10},{9,11},{10,... | collective-permute-start | bytes 1572872 | tf_op jit(solution)/shard_map/ppermute | solution.py:185
  57.4 43.5 %collective-permute-start.6 = (bf16[2,1024,128]{2,1,0:T(8,128)(2,1)}, bf16[2,1024,128]{2,1,0:T(8,128)(2,1)}, u32[]{:S(2)}, u32[]{:S(2)}) collective-permute-start(bf16[2,1024,128]{2,1,0:T(8,128)(2,1)} %bitcast.86), channel_id=1, source_target_pairs={{0,3},{1,2},{2,1},{3,0},{4,7},{5,6},{6,5},{7,4},{8,11},{9,10},{10,... | collective-permute-start | bytes 1572872 | tf_op jit(solution)/shard_map/ppermute | solution.py:185
  64.4 142.5 %all-to-all-start.1 = ((bf16[4,2096,128]{2,1,0:T(8,128)(2,1)}), bf16[4,2096,128]{2,1,0:T(8,128)(2,1)}, u32[]{:S(2)}, u32[]{:S(2)}) async-start(bf16[4,2096,128]{2,1,0:T(8,128)(2,1)} %get-tuple-element.5), calls=%async_computation.1 | async-start | bytes 4292608 | tf_op jit(solution)/shard_map/all_to_all | solution.py:218
  69.5 82.7 %collective-permute-start.3 = (bf16[2,1024,128]{2,1,0:T(8,128)(2,1)}, bf16[2,1024,128]{2,1,0:T(8,128)(2,1)S(1)}, u32[]{:S(2)}, u32[]{:S(2)}) collective-permute-start(bf16[2,1024,128]{2,1,0:T(8,128)(2,1)} %bitcast.84), channel_id=1, source_target_pairs={{0,5},{1,4},{2,7},{3,6},{4,1},{5,0},{6,3},{7,2},{8,13},{9,12},{10,... | collective-permute-start | bytes 1572872 | tf_op jit(solution)/shard_map/ppermute | solution.py:185
  90.8 81.9 %collective-permute-start = (bf16[2,1024,128]{2,1,0:T(8,128)(2,1)}, bf16[2,1024,128]{2,1,0:T(8,128)(2,1)S(1)}, u32[]{:S(2)}, u32[]{:S(2)}) collective-permute-start(bf16[2,1024,128]{2,1,0:T(8,128)(2,1)} %bitcast.87), channel_id=1, source_target_pairs={{0,6},{1,7},{2,4},{3,5},{4,2},{5,3},{6,0},{7,1},{8,14},{9,15},{10,... | collective-permute-start | bytes 1572872 | tf_op jit(solution)/shard_map/ppermute | solution.py:185
  100.9 49.1 %collective-permute-start.2 = (bf16[2,1024,128]{2,1,0:T(8,128)(2,1)S(1)}, bf16[2,1024,128]{2,1,0:T(8,128)(2,1)S(1)}, u32[]{:S(2)}, u32[]{:S(2)}) collective-permute-start(bf16[2,1024,128]{2,1,0:T(8,128)(2,1)S(1)} %bitcast.92), channel_id=1, source_target_pairs={{0,4},{1,5},{2,6},{3,7},{4,0},{5,1},{6,2},{7,3},{8,12},{9,13},{10,... | collective-permute-start | bytes 1572872 | tf_op jit(solution)/shard_map/ppermute | solution.py:185
  150.1 22.8 %collective-permute-start.1 = (bf16[2,1024,128]{2,1,0:T(8,128)(2,1)}, bf16[2,1024,128]{2,1,0:T(8,128)(2,1)S(1)}, u32[]{:S(2)}, u32[]{:S(2)}) collective-permute-start(bf16[2,1024,128]{2,1,0:T(8,128)(2,1)} %bitcast.86), channel_id=1, source_target_pairs={{0,7},{1,6},{2,5},{3,4},{4,3},{5,2},{6,1},{7,0},{8,15},{9,14},{10,... | collective-permute-start | bytes 1572872 | tf_op jit(solution)/shard_map/ppermute | solution.py:185
  152.3 50.7 %collective-permute-start.16 = (bf16[2,1024,128]{2,1,0:T(8,128)(2,1)}, bf16[2,1024,128]{2,1,0:T(8,128)(2,1)S(1)}, u32[]{:S(2)}, u32[]{:S(2)}) collective-permute-start(bf16[2,1024,128]{2,1,0:T(8,128)(2,1)} %bitcast.83), channel_id=1, source_target_pairs={{0,2},{1,3},{2,0},{3,1},{4,6},{5,7},{6,4},{7,5},{8,10},{9,11},{10,... | collective-permute-start | bytes 1572872 | tf_op jit(solution)/shard_map/ppermute | solution.py:185
  172.7 102.5 %collective-permute-start.11 = (bf16[2,1024,128]{2,1,0:T(8,128)(2,1)}, bf16[2,1024,128]{2,1,0:T(8,128)(2,1)S(1)}, u32[]{:S(2)}, u32[]{:S(2)}) collective-permute-start(bf16[2,1024,128]{2,1,0:T(8,128)(2,1)} %bitcast.83), channel_id=1, source_target_pairs={{0,6},{1,7},{2,4},{3,5},{4,2},{5,3},{6,0},{7,1},{8,14},{9,15},{10,... | collective-permute-start | bytes 1572872 | tf_op jit(solution)/shard_map/ppermute | solution.py:185
  172.8 30.6 %collective-permute-start.17 = (bf16[2,1024,128]{2,1,0:T(8,128)(2,1)}, bf16[2,1024,128]{2,1,0:T(8,128)(2,1)S(1)}, u32[]{:S(2)}, u32[]{:S(2)}) collective-permute-start(bf16[2,1024,128]{2,1,0:T(8,128)(2,1)} %bitcast.82), channel_id=1, source_target_pairs={{0,3},{1,2},{2,1},{3,0},{4,7},{5,6},{6,5},{7,4},{8,11},{9,10},{10,... | collective-permute-start | bytes 1572872 | tf_op jit(solution)/shard_map/ppermute | solution.py:185
  203.0 72.2 %collective-permute-start.12 = (bf16[2,1024,128]{2,1,0:T(8,128)(2,1)}, bf16[2,1024,128]{2,1,0:T(8,128)(2,1)S(1)}, u32[]{:S(2)}, u32[]{:S(2)}) collective-permute-start(bf16[2,1024,128]{2,1,0:T(8,128)(2,1)} %bitcast.82), channel_id=1, source_target_pairs={{0,7},{1,6},{2,5},{3,4},{4,3},{5,2},{6,1},{7,0},{8,15},{9,14},{10,... | collective-permute-start | bytes 1572872 | tf_op jit(solution)/shard_map/ppermute | solution.py:185
  203.0 46.8 %collective-permute-start.13 = (bf16[2,1024,128]{2,1,0:T(8,128)(2,1)S(1)}, bf16[2,1024,128]{2,1,0:T(8,128)(2,1)}, u32[]{:S(2)}, u32[]{:S(2)}) collective-permute-start(bf16[2,1024,128]{2,1,0:T(8,128)(2,1)S(1)} %bitcast.90), channel_id=1, source_target_pairs={{0,4},{1,5},{2,6},{3,7},{4,0},{5,1},{6,2},{7,3},{8,12},{9,13},{10,... | collective-permute-start | bytes 1572872 | tf_op jit(solution)/shard_map/ppermute | solution.py:185
  204.2 97.6 %collective-permute-start.7 = (bf16[128,1024]{1,0:T(8,128)(2,1)}, bf16[128,1024]{1,0:T(8,128)(2,1)}, u32[]{:S(2)}, u32[]{:S(2)}) collective-permute-start(bf16[128,1024]{1,0:T(8,128)(2,1)} %get-tuple-element.22), channel_id=1, source_target_pairs={{0,24},{1,25},{2,26},{3,27},{4,28},{5,29},{6,30},{7,31},{8,0},{9,1... | collective-permute-start | bytes 786440 | tf_op jit(solution)/shard_map/ppermute | solution.py:234
  249.8 54.3 %collective-permute-start.8 = (bf16[128,1024]{1,0:T(8,128)(2,1)S(1)}, bf16[128,1024]{1,0:T(8,128)(2,1)S(1)}, u32[]{:S(2)}, u32[]{:S(2)}) collective-permute-start(bf16[128,1024]{1,0:T(8,128)(2,1)S(1)} %copy-done.7), channel_id=1, source_target_pairs={{0,25},{1,24},{2,27},{3,26},{4,29},{5,28},{6,31},{7,30},{8,1},{9,0... | collective-permute-start | bytes 786440 | tf_op jit(solution)/shard_map/ppermute | solution.py:234
  296.2 32.4 %collective-permute-start.18 = (bf16[128,1024]{1,0:T(8,128)(2,1)S(1)}, bf16[128,1024]{1,0:T(8,128)(2,1)S(1)}, u32[]{:S(2)}, u32[]{:S(2)}) collective-permute-start(bf16[128,1024]{1,0:T(8,128)(2,1)S(1)} %get-tuple-element.18), channel_id=1, source_target_pairs={{0,24},{1,25},{2,26},{3,27},{4,28},{5,29},{6,30},{7,31},{8,0},{9,1... | collective-permute-start | bytes 786440 | tf_op jit(solution)/shard_map/ppermute | solution.py:234
  299.5 10.2 %collective-permute-start.9 = (bf16[128,1024]{1,0:T(8,128)(2,1)S(1)}, bf16[128,1024]{1,0:T(8,128)(2,1)S(1)}, u32[]{:S(2)}, u32[]{:S(2)}) collective-permute-start(bf16[128,1024]{1,0:T(8,128)(2,1)S(1)} %copy-done.6), channel_id=1, source_target_pairs={{0,26},{1,27},{2,24},{3,25},{4,30},{5,31},{6,28},{7,29},{8,2},{9,3... | collective-permute-start | bytes 786440 | tf_op jit(solution)/shard_map/ppermute | solution.py:234
  301.5 13.5 %collective-permute-start.10 = (bf16[128,1024]{1,0:T(8,128)(2,1)S(1)}, bf16[128,1024]{1,0:T(8,128)(2,1)S(1)}, u32[]{:S(2)}, u32[]{:S(2)}) collective-permute-start(bf16[128,1024]{1,0:T(8,128)(2,1)S(1)} %get-tuple-element.19), channel_id=1, source_target_pairs={{0,27},{1,26},{2,25},{3,24},{4,31},{5,30},{6,29},{7,28},{8,3},{9,2... | collective-permute-start | bytes 786440 | tf_op jit(solution)/shard_map/ppermute | solution.py:234
  301.8 31.8 %collective-permute-start.19 = (bf16[128,1024]{1,0:T(8,128)(2,1)S(1)}, bf16[128,1024]{1,0:T(8,128)(2,1)S(1)}, u32[]{:S(2)}, u32[]{:S(2)}) collective-permute-start(bf16[128,1024]{1,0:T(8,128)(2,1)S(1)} %get-tuple-element.17), channel_id=1, source_target_pairs={{0,25},{1,24},{2,27},{3,26},{4,29},{5,28},{6,31},{7,30},{8,1},{9,0... | collective-permute-start | bytes 786440 | tf_op jit(solution)/shard_map/ppermute | solution.py:234
  304.1 29.5 %collective-permute-start.20 = (bf16[128,1024]{1,0:T(8,128)(2,1)S(1)}, bf16[128,1024]{1,0:T(8,128)(2,1)S(1)}, u32[]{:S(2)}, u32[]{:S(2)}) collective-permute-start(bf16[128,1024]{1,0:T(8,128)(2,1)S(1)} %get-tuple-element.16), channel_id=1, source_target_pairs={{0,26},{1,27},{2,24},{3,25},{4,30},{5,31},{6,28},{7,29},{8,2},{9,3... | collective-permute-start | bytes 786440 | tf_op jit(solution)/shard_map/ppermute | solution.py:234
  309.7 24.0 %collective-permute-start.21 = (bf16[128,1024]{1,0:T(8,128)(2,1)S(1)}, bf16[128,1024]{1,0:T(8,128)(2,1)S(1)}, u32[]{:S(2)}, u32[]{:S(2)}) collective-permute-start(bf16[128,1024]{1,0:T(8,128)(2,1)S(1)} %get-tuple-element.15), channel_id=1, source_target_pairs={{0,27},{1,26},{2,25},{3,24},{4,31},{5,30},{6,29},{7,28},{8,3},{9,2... | collective-permute-start | bytes 786440 | tf_op jit(solution)/shard_map/ppermute | solution.py:234
  (8 other events, 56.3 us)

commit v2 on v1

v2 whole, which is shorter than its diff:
```python
import functools
import math

import jax
import jax.numpy as jnp
from jax import lax
from jax.experimental import pallas as pl
from jax.experimental.pallas import tpu as pltpu
from jax.sharding import PartitionSpec as P

BLOCK = 128
PARTS = 3
STAT_ROWS = 16
VMEM_LIMIT = 48 * 1024 * 1024


def split_parts(value):
    terms = []
    for _ in range(PARTS):
        term = value.astype(jnp.bfloat16)
        terms.append(term)
        value = value - term.astype(jnp.float32)
    return terms


def pack_kernel(own, group, index, at_ref, keys_ref, values_ref, *refs):
    outs, sems = refs[:group], refs[group]
    dim = outs[0].shape[2]
    copies = []
    for x, out in enumerate(outs):
        column = pl.multiple_of(((at_ref[0] ^ x) * own + index) * dim, dim)
        for half, source in enumerate((keys_ref, values_ref)):
            copy = pltpu.make_async_copy(source.at[:, pl.ds(column, dim)], out.at[half], sems.at[2 * x + half])
            copy.start()
            copies.append(copy)
    for copy in copies:
        copy.wait()


def pack(mem_keys, mem_values, at, own, group, index, dim):
    mem_dev = mem_keys.shape[0]
    shape = jax.ShapeDtypeStruct((2, mem_dev, dim), mem_keys.dtype)
    anywhere = pl.BlockSpec(memory_space=pl.ANY)
    return pl.pallas_call(
        functools.partial(pack_kernel, own, group, index),
        out_shape=[shape] * group,
        grid_spec=pltpu.PrefetchScalarGridSpec(
            num_scalar_prefetch=1,
            in_specs=[anywhere, anywhere],
            out_specs=[anywhere] * group,
            scratch_shapes=[pltpu.SemaphoreType.DMA((2 * group,))],
        ),
        compiler_params=pltpu.CompilerParams(vmem_limit_bytes=VMEM_LIMIT),
        cost_estimate=pl.CostEstimate(flops=0, bytes_accessed=8 * group * mem_dev * dim, transcendentals=0),
    )(at[None], mem_keys, mem_values)


def prepare_kernel(heads, dim, own, index, gate_ref, grad_ref, query_ref, out_ref, log_ref, packed_ref):
    rows = grad_ref.shape[0]
    first = (pl.program_id(0) * own + index) * heads
    for h in range(heads):
        columns = slice(h * dim, (h + 1) * dim)
        place = slice(h * rows, (h + 1) * rows)
        packed_ref[0, :dim, place] = query_ref[:, columns].T
        gated = (gate_ref[first + h] * grad_ref[:, columns].T.astype(jnp.float32)).astype(jnp.bfloat16)
        packed_ref[0, dim:2 * dim, place] = gated
        product = gated.astype(jnp.float32) * out_ref[:, columns].T.astype(jnp.float32)
        delta = jnp.sum(product, axis=0, keepdims=True)
        terms = split_parts(delta) + split_parts(log_ref[h:h + 1, :])
        terms = [term.astype(jnp.float32) for term in terms]
        filler = jnp.zeros((STAT_ROWS - len(terms), rows), jnp.float32)
        packed_ref[0, 2 * dim:, place] = jnp.concatenate(terms + [filler], axis=0).astype(jnp.bfloat16)


def prepare(grad_out, queries, mem_out, logs, gates, kv_heads, dim, own, index):
    rows, width = grad_out.shape
    heads = width // dim // kv_heads
    group = kv_heads // own
    span = 2 * dim + STAT_ROWS
    wide = pl.BlockSpec((rows, heads * dim), lambda k, _: (0, k * own + index))
    return pl.pallas_call(
        functools.partial(prepare_kernel, heads, dim, own, index),
        out_shape=jax.ShapeDtypeStruct((group, span, heads * rows), jnp.bfloat16),
        grid_spec=pltpu.PrefetchScalarGridSpec(
            num_scalar_prefetch=1,
            grid=(group,),
            in_specs=[wide, wide, wide, pl.BlockSpec((heads, rows), lambda k, _: (k * own + index, 0))],
            out_specs=pl.BlockSpec((1, span, heads * rows), lambda k, _: (k, 0, 0)),
        ),
        compiler_params=pltpu.CompilerParams(vmem_limit_bytes=VMEM_LIMIT),
        cost_estimate=pl.CostEstimate(flops=rows * width * 4, bytes_accessed=rows * width * 12 // own, transcendentals=0),
    )(gates, grad_out, queries, mem_out, logs)


def attend_kernel(heads, rows, dim, scale, fresh, last, places, picks_ref, starts_ref, packed_ref, *refs):
    count = len(places)
    memory_refs = refs[:count]
    rest = refs[count:]
    acc_in = None if fresh else rest[0]
    out_ref = rest[0] if fresh else rest[1]
    keys_ref, values_ref, turned, total = rest[-4:]
    tile = pl.program_id(0)
    mem_dev = memory_refs[0].shape[1]
    blocks = mem_dev // BLOCK
    pair = 2 * rows

    @pl.when(tile == 0)
    def _():
        for at, memory in enumerate(memory_refs):
            here = slice(at * mem_dev, (at + 1) * mem_dev)
            keys_ref[here, :] = memory[0]
            values_ref[here, :] = memory[1]
            for block in range(blocks):
                turned[at * blocks + block] = memory[0, block * BLOCK:(block + 1) * BLOCK, :].T

    if fresh:
        total[...] = jnp.zeros_like(total)
    else:
        total[...] = acc_in[0]

    stats = packed_ref[0, 2 * dim:, :].astype(jnp.float32)
    delta_row = jnp.sum(stats[:PARTS], axis=0, keepdims=True)
    log_row = jnp.sum(stats[PARTS:2 * PARTS], axis=0, keepdims=True)

    low = starts_ref[tile, places[0]]
    high = starts_ref[tile, places[-1] + 1]
    offset = places[0] * blocks

    def add(here, number, checked):
        sides = []
        for two in range(0, number, 2):
            keys, values, across = [], [], []
            for j in (two, two + 1):
                valid = here + j < high
                block = picks_ref[tile, jnp.where(valid, here + j, here) if checked else here + j] - offset
                row = pl.ds(pl.multiple_of(block * BLOCK, BLOCK), BLOCK)
                keys.append(keys_ref[row, :])
                values.append(values_ref[row, :])
                side = turned[block]
                across.append(jnp.where(valid, side, jnp.zeros_like(side)) if checked and j else side)
            sides.append(
                (jnp.concatenate(keys, axis=0), jnp.concatenate(values, axis=0), jnp.concatenate(across, axis=1))
            )
        for p in range(heads // 2):
            span = slice(p * pair, (p + 1) * pair)
            query = packed_ref[0, :dim, span]
            grad = packed_ref[0, dim:2 * dim, span]
            gained = None
            for keys, values, across in sides:
                scores = jnp.dot(keys, query, preferred_element_type=jnp.float32)
                grad_probs = jnp.dot(values, grad, preferred_element_type=jnp.float32)
                probs = jnp.exp(scores * scale - log_row[:, span])
                grad_scores = (probs * (grad_probs - delta_row[:, span])).astype(jnp.bfloat16)
                part = jnp.dot(across, grad_scores, preferred_element_type=jnp.float32)
                gained = part if gained is None else gained + part
            total[:, span] += gained

    fours = (high - low) // 4

    def four(turn, carry):
        add(low + 4 * turn, 4, False)
        return carry

    def two(turn, carry):
        add(low + 4 * fours + 2 * turn, 2, True)
        return carry

    lax.fori_loop(0, fours, four, 0)
    lax.fori_loop(0, (high - low - 4 * fours + 1) // 2, two, 0)

    if last:
        for h in range(heads):
            out_ref[0, :, h * dim:(h + 1) * dim] = total[:, h * rows:(h + 1) * rows].T.astype(jnp.bfloat16)
    else:
        out_ref[0] = total[...]


def attend(packed, memories, places, acc, picks, starts, heads, rows, dim, scale, last):
    tiles, span, _ = packed.shape
    fresh = acc is None
    count = len(places)
    mem_dev = memories[0].shape[1]
    blocks = mem_dev // BLOCK
    width = heads * rows
    acc_spec = pl.BlockSpec((1, dim, width), lambda t, *_: (t, 0, 0))
    if last:
        out_shape = jax.ShapeDtypeStruct((tiles, rows, heads * dim), jnp.bfloat16)
        out_spec = pl.BlockSpec((1, rows, heads * dim), lambda t, *_: (t, 0, 0))
    else:
        out_shape = jax.ShapeDtypeStruct((tiles, dim, width), jnp.float32)
        out_spec = acc_spec
    flops = tiles * count * (blocks // 2) * BLOCK * width * dim * 6
    return pl.pallas_call(
        functools.partial(attend_kernel, heads, rows, dim, scale, fresh, last, places),
        out_shape=out_shape,
        grid_spec=pltpu.PrefetchScalarGridSpec(
            num_scalar_prefetch=2,
            grid=(tiles,),
            in_specs=[pl.BlockSpec((1, span, width), lambda t, *_: (t, 0, 0))]
            + [pl.BlockSpec(m.shape, lambda t, *_: (0, 0, 0)) for m in memories]
            + ([] if fresh else [acc_spec]),
            out_specs=out_spec,
            scratch_shapes=[
                pltpu.VMEM((count * mem_dev, dim), jnp.bfloat16),
                pltpu.VMEM((count * mem_dev, dim), jnp.bfloat16),
                pltpu.VMEM((count * blocks, dim, BLOCK), jnp.bfloat16),
                pltpu.VMEM((dim, width), jnp.float32),
            ],
        ),
        compiler_params=pltpu.CompilerParams(vmem_limit_bytes=VMEM_LIMIT),
        cost_estimate=pl.CostEstimate(
            flops=flops * 2, bytes_accessed=tiles * span * width * 2 + tiles * width * dim * 8, transcendentals=0
        ),
    )(picks, starts, packed, *memories, *([] if fresh else [acc]))


def shards(grad_out, queries, mem_out, row_total, gate_logit, mem_keys, mem_values, retrieved):
    seq = lax.axis_size("seq")
    sections = lax.axis_size("section")
    position = lax.axis_index("seq")
    rows, width = grad_out.shape[1:]
    head_count = gate_logit.shape[1]
    dim = width // head_count
    kv_heads = mem_keys.shape[2] // dim
    heads = head_count // kv_heads
    mem_dev = mem_keys.shape[1]
    blocks = mem_dev // BLOCK
    group = min(kv_heads, seq // 2)
    own = kv_heads // group
    at = position % group
    scale = dim ** (-0.5)

    def swapped(value, step):
        return lax.ppermute(value, "seq", [(p, p ^ step) for p in range(seq)])

    logs = jnp.log(row_total[0].T.astype(jnp.float32)) - math.log(scale)
    gates = jax.nn.sigmoid(gate_logit[0])

    mine = lax.dynamic_slice_in_dim(retrieved[0], at * own, own, 0)
    mine = lax.dynamic_slice_in_dim(mine, (position // group) * group, group, 1)
    distance = ((mine // blocks) ^ position) * blocks + mine % blocks
    rank = jnp.sum(distance[..., None, :] < distance[..., :, None], axis=-1)
    order = jnp.arange(distance.shape[-1])
    ordered = jnp.sum(jnp.where(rank[..., :, None] == order, distance[..., :, None], 0), axis=-2)
    picks = ordered.astype(jnp.int32)
    starts = jnp.sum(distance[..., None, :] < (jnp.arange(seq + 1) * blocks)[:, None], axis=-1).astype(jnp.int32)

    stages = [tuple(range(group))]
    half = group + (seq - group) // 2
    stages.append(tuple(range(group, half)))
    stages.append(tuple(range(half, seq)))

    groups = [list(range(g * group, (g + 1) * group)) for g in range(seq // group)]
    out = jnp.zeros((rows, width), jnp.bfloat16)
    for i in range(own):
        sends = pack(mem_keys[0], mem_values[0], at, own, group, i, dim)
        arrived = {0: sends[0]}
        for step in range(group, seq):
            arrived[step] = swapped(sends[step % group], step)
        packed = prepare(grad_out[0], queries[0], mem_out[0], logs, gates, kv_heads, dim, own, i)
        mixed = lax.all_to_all(
            packed, "seq", split_axis=0, concat_axis=0, axis_index_groups=groups, tiled=True
        )
        for step in range(1, group):
            arrived[step] = swapped(sends[step], step)
        acc = None
        for number, places in enumerate(stages):
            acc = attend(
                mixed, [arrived[p] for p in places], places, acc, picks[i], starts[i],
                heads, rows, dim, scale, number == len(stages) - 1,
            )
        for x in range(group):
            piece = lax.dynamic_index_in_dim(acc, at ^ x, 0, keepdims=False)
            pairs = [
                (s * seq + p, ((s - 1) % sections) * seq + (p ^ x)) for s in range(sections) for p in range(seq)
            ]
            piece = lax.ppermute(piece, ("section", "seq"), pairs)
            out = lax.dynamic_update_slice_in_dim(out, piece, ((at ^ x) * own + i) * heads * dim, 1)
    return out[None]


def solution(mesh):
    return jax.shard_map(
        shards,
        mesh=mesh,
        in_specs=(
            P("section", "seq", None),
            P("section", "seq", None),
            P("section", "seq", None),
            P("section", "seq", None),
            P("section", None),
            P("section", "seq", None),
            P("section", "seq", None),
            P("section", None, None, None),
        ),
        out_specs=P("section", "seq", None),
        check_vma=False,
    )
```

time: 336 us -> 306 us (0.911)
  local copies, waits for them, and re-layouts: 47.6 us -> 14.4 us
  waiting for transfers between devices: 59.4 us -> 75.1 us
  Pallas kernels: 180 us -> 167 us
    pallas_call x6, Pallas kernels: 172 us -> 124 us  [attend(): pl.pallas_call(functools.partial(attend_kernel, heads, rows, dim, scale,...]
    pallas_call x1 -> x4, Pallas kernels: 7.43 us -> 43.7 us  [the longest x2 34.3 us: pack(): pl.pallas_call(functools.partial(pack_kernel, own, group, index), out_sha...]
    another operation x1 -> x0, local copies, waits for them, and re-layouts: 21.4 us -> none
    ppermute x14, waiting for transfers between devices: 33.4 us -> 50.4 us  [swapped(): return lax.ppermute(value, 'seq', [(p, p ^ step) for p in range(seq)])]
    unnamed x25 -> x28, local copies, waits for them, and re-layouts: 18.4 us -> 11.1 us
    ppermute x8, starting transfers between devices: 15.5 us -> 10.2 us  [shards(): piece = lax.ppermute(piece, ('section', 'seq'), pairs)]
    squeeze x1 -> x0, local copies, waits for them, and re-layouts: 4.6 us -> none  [shards(): packed[:, i]]
    ppermute x14, starting transfers between devices: 19 us -> 23.3 us  [swapped(): return lax.ppermute(value, 'seq', [(p, p ^ step) for p in range(seq)])]
  transfers between devices with their start and end apart: 24 -> 24, of which waited for: 8 -> 8; matrix products, arithmetic and copies ran while one was open for 12% -> 1% of each run, Pallas kernels for 51% -> 54%
where the time goes in v2:
time: 306 us; the launch traced here: 303 us
  Pallas kernels  167 us (55%)
  waiting for transfers between devices  75.1 us (25%)
  starting transfers between devices  42.7 us (14%)
  local copies, waits for them, and re-layouts  14.4 us (5%)
    pallas_call x6, Pallas kernels, attend(): pl.pallas_call(functools.partial(attend_kernel, heads, rows, dim, scale,...  124 us
    ppermute x14, waiting for transfers between devices, swapped(): return lax.ppermute(value, 'seq', [(p, p ^ step) for p in range(seq)])  50.4 us
    pallas_call x2, Pallas kernels, pack(): pl.pallas_call(functools.partial(pack_kernel, own, group, index), out_sha...  34.3 us
    ppermute x8, waiting for transfers between devices, shards(): piece = lax.ppermute(piece, ('section', 'seq'), pairs)  24.7 us
    ppermute x14, starting transfers between devices, swapped(): return lax.ppermute(value, 'seq', [(p, p ^ step) for p in range(seq)])  23.3 us
    unnamed x28, local copies, waits for them, and re-layouts  11.1 us
    ppermute x8, starting transfers between devices, shards(): piece = lax.ppermute(piece, ('section', 'seq'), pairs)  10.2 us
    pallas_call x2, Pallas kernels, prepare(): pl.pallas_call(functools.partial(prepare_kernel, heads, dim, own, index),...  9.45 us
  transfers between devices with their start and end apart: 24, of which 8 were waited for; matrix products, arithmetic and copies ran while one was open for 1% of the time, Pallas kernels for 54%

profile of v2, /device:TPU:0, one launch (start us, length us, event | category | flops | bytes accessed | tf_op | source)
XLA Modules:
  0.0 303.1 jit_solution(15309506925335955811)
XLA Ops:
  4.6 4.7 %shard_map.82 = bf16[4,272,1024]{2,1,0:T(8,128)(2,1)} custom-call(f32[64]{0:T(128)S(1)} %divide_bitcast_fusion.gate_ref, bf16[128,8192]{1,0:T(8,128)(2,1)S(1)} %bitcast.56, bf16[128,8192]{1,0:T(8,128)(2,1)S(1)} %bitcast.58, bf16[128,8192]{1,0:T(8,128)(2,1)} %bitcast.68, f32[64,128]{1,0:T(8,128)S(1)} %add_bitcast_fusion.log_ref), custom_call_target="tpu_custom_call" | custom-call | flops 4194304 | bytes 6291456 | tf_op jit(solution)/shard_map/pallas_call | solution.py:81
  9.3 4.6 %all-to-all-start = ((bf16[4,272,1024]{2,1,0:T(8,128)(2,1)}), bf16[4,272,1024]{2,1,0:T(8,128)(2,1)}, u32[]{:S(2)}, u32[]{:S(2)}) async-start(bf16[4,272,1024]{2,1,0:T(8,128)(2,1)} %shard_map.82), calls=%async_computation | async-start | bytes 4456448 | tf_op jit(solution)/shard_map/all_to_all | solution.py:261
  14.0 9.2 %shard_map.88 = (bf16[2,1024,128]{2,1,0:T(8,128)(2,1)S(1)}, bf16[2,1024,128]{2,1,0:T(8,128)(2,1)}, bf16[2,1024,128]{2,1,0:T(8,128)(2,1)S(1)}, bf16[2,1024,128]{2,1,0:T(8,128)(2,1)S(1)}) custom-call(s32[1]{0:T(128)} %bitcast.9.at_ref, bf16[1024,1024]{1,0:T(8,128)(2,1)S(1)} %bitcast.54, bf16[1024,1024]{1,0:T(8,128)(2,1)} %bitcast.66), custom_call_target="tpu_custom_call" | custom-call | bytes 4194304 | tf_op jit(solution)/shard_map/pallas_call | solution.py:44
  23.7 3.7 %collective-permute-start.14 = (bf16[2,1024,128]{2,1,0:T(8,128)(2,1)}, bf16[2,1024,128]{2,1,0:T(8,128)(2,1)}, u32[]{:S(2)}, u32[]{:S(2)}) collective-permute-start(bf16[2,1024,128]{2,1,0:T(8,128)(2,1)} %get-tuple-element.20), channel_id=1, source_target_pairs={{0,5},{1,4},{2,7},{3,6},{4,1},{5,0},{6,3},{7,2},{8,13},{9,12},{10,... | collective-permute-start | bytes 1572872 | tf_op jit(solution)/shard_map/ppermute | solution.py:234
  27.4 25.1 %shard_map.83 = (bf16[2,1024,128]{2,1,0:T(8,128)(2,1)S(1)}, bf16[2,1024,128]{2,1,0:T(8,128)(2,1)}, bf16[2,1024,128]{2,1,0:T(8,128)(2,1)}, bf16[2,1024,128]{2,1,0:T(8,128)(2,1)}) custom-call(s32[1]{0:T(128)} %bitcast.9.at_ref, bf16[1024,1024]{1,0:T(8,128)(2,1)S(1)} %bitcast.55, bf16[1024,1024]{1,0:T(8,128)(2,1)} %bitcast.67), custom_call_target="tpu_custom_call" | custom-call | bytes 4194304 | tf_op jit(solution)/shard_map/pallas_call | solution.py:44
  58.6 4.7 %shard_map.87 = bf16[4,272,1024]{2,1,0:T(8,128)(2,1)} custom-call(f32[64]{0:T(128)S(1)} %divide_bitcast_fusion.gate_ref, bf16[128,8192]{1,0:T(8,128)(2,1)S(1)} %bitcast.57, bf16[128,8192]{1,0:T(8,128)(2,1)S(1)} %bitcast.59, bf16[128,8192]{1,0:T(8,128)(2,1)} %bitcast.69, f32[64,128]{1,0:T(8,128)S(1)} %add_bitcast_fusion.log_ref), custom_call_target="tpu_custom_call" | custom-call | flops 4194304 | bytes 6291456 | tf_op jit(solution)/shard_map/pallas_call | solution.py:81
  64.1 4.6 %all-to-all-start.1 = ((bf16[4,272,1024]{2,1,0:T(8,128)(2,1)}), bf16[4,272,1024]{2,1,0:T(8,128)(2,1)}, u32[]{:S(2)}, u32[]{:S(2)}) async-start(bf16[4,272,1024]{2,1,0:T(8,128)(2,1)} %shard_map.87), calls=%async_computation.1 | async-start | bytes 4456448 | tf_op jit(solution)/shard_map/all_to_all | solution.py:261
  70.2 3.8 %collective-permute-start = (bf16[2,1024,128]{2,1,0:T(8,128)(2,1)}, bf16[2,1024,128]{2,1,0:T(8,128)(2,1)S(1)}, u32[]{:S(2)}, u32[]{:S(2)}) collective-permute-start(bf16[2,1024,128]{2,1,0:T(8,128)(2,1)} %get-tuple-element.13), channel_id=1, source_target_pairs={{0,6},{1,7},{2,4},{3,5},{4,2},{5,3},{6,0},{7,1},{8,14},{9,15},{10,... | collective-permute-start | bytes 1572872 | tf_op jit(solution)/shard_map/ppermute | solution.py:234
  74.1 15.9 %collective-permute-done.6.refs_3_ = bf16[2,1024,128]{2,1,0:T(8,128)(2,1)} collective-permute-done((bf16[2,1024,128]{2,1,0:T(8,128)(2,1)}, bf16[2,1024,128]{2,1,0:T(8,128)(2,1)}, u32[]{:S(2)}, u32[]{:S(2)}) %collective-permute-start.6) | collective-permute-done | bytes 524320 | tf_op jit(solution)/shard_map/ppermute | solution.py:234
  90.7 29.6 %shard_map.84.refs_2_ = f32[4,128,1024]{2,1,0:T(8,128)S(1)} custom-call(s32[4,32]{1,0:T(4,128)S(1)} %get-tuple-element.32.picks_ref, s32[4,9]{1,0:T(4,128)S(1)} %bitcast.63, bf16[4,272,1024]{2,1,0:T(8,128)(2,1)} %all-to-all-done.packed_ref, bf16[2,1024,128]{2,1,0:T(8,128)(2,1)S(1)} %copy-done.8, bf16[2,1024,128]{2,1,0:T(8,128)(2,1)S(1)} %collective-permute-done.4.refs_1_, ...), custom_call_target="tpu_custom_call" | custom-call | flops 12884901888 | bytes 6422528 | tf_op jit(solution)/shard_map/pallas_call | solution.py:193
  120.3 21.3 %collective-permute-done.2.refs_0_ = bf16[2,1024,128]{2,1,0:T(8,128)(2,1)S(1)} collective-permute-done((bf16[2,1024,128]{2,1,0:T(8,128)(2,1)S(1)}, bf16[2,1024,128]{2,1,0:T(8,128)(2,1)S(1)}, u32[]{:S(2)}, u32[]{:S(2)}) %collective-permute-start.2) | collective-permute-done | bytes 524320 | tf_op jit(solution)/shard_map/ppermute | solution.py:234
  142.7 15.8 %shard_map.85.refs_2_ = f32[4,128,1024]{2,1,0:T(8,128)S(1)} custom-call(s32[4,32]{1,0:T(4,128)S(1)} %get-tuple-element.32.picks_ref, s32[4,9]{1,0:T(4,128)S(1)} %bitcast.64, bf16[4,272,1024]{2,1,0:T(8,128)(2,1)} %all-to-all-done.packed_ref, bf16[2,1024,128]{2,1,0:T(8,128)(2,1)S(1)} %collective-permute-done.2.refs_0_, ...), custom_call_target="tpu_custom_call" | custom-call | flops 6442450944 | bytes 6422528 | tf_op jit(solution)/shard_map/pallas_call | solution.py:193
  159.6 6.2 %collective-permute-start.17 = (bf16[2,1024,128]{2,1,0:T(8,128)(2,1)S(1)}, bf16[2,1024,128]{2,1,0:T(8,128)(2,1)S(1)}, u32[]{:S(2)}, u32[]{:S(2)}) collective-permute-start(bf16[2,1024,128]{2,1,0:T(8,128)(2,1)S(1)} %get-tuple-element.18), channel_id=1, source_target_pairs={{0,3},{1,2},{2,1},{3,0},{4,7},{5,6},{6,5},{7,4},{8,11},{9,10},{10,... | collective-permute-start | bytes 1572872 | tf_op jit(solution)/shard_map/ppermute | solution.py:234
  165.8 15.8 %shard_map.86 = bf16[4,128,1024]{2,1,0:T(8,128)(2,1)S(1)} custom-call(s32[4,32]{1,0:T(4,128)S(1)} %get-tuple-element.32.picks_ref, s32[4,9]{1,0:T(4,128)S(1)} %bitcast.65, bf16[4,272,1024]{2,1,0:T(8,128)(2,1)} %all-to-all-done.packed_ref, bf16[2,1024,128]{2,1,0:T(8,128)(2,1)S(1)} %collective-permute-done.refs_0_, ...), custom_call_target="tpu_custom_call" | custom-call | flops 6442450944 | bytes 6422528 | tf_op jit(solution)/shard_map/pallas_call | solution.py:193
  182.5 3.7 %collective-permute-start.12 = (bf16[2,1024,128]{2,1,0:T(8,128)(2,1)S(1)}, bf16[2,1024,128]{2,1,0:T(8,128)(2,1)S(1)}, u32[]{:S(2)}, u32[]{:S(2)}) collective-permute-start(bf16[2,1024,128]{2,1,0:T(8,128)(2,1)S(1)} %get-tuple-element.18), channel_id=1, source_target_pairs={{0,7},{1,6},{2,5},{3,4},{4,3},{5,2},{6,1},{7,0},{8,15},{9,14},{10,... | collective-permute-start | bytes 1572872 | tf_op jit(solution)/shard_map/ppermute | solution.py:234
  186.2 4.3 %collective-permute-done.17.refs_3_ = bf16[2,1024,128]{2,1,0:T(8,128)(2,1)S(1)} collective-permute-done((bf16[2,1024,128]{2,1,0:T(8,128)(2,1)S(1)}, bf16[2,1024,128]{2,1,0:T(8,128)(2,1)S(1)}, u32[]{:S(2)}, u32[]{:S(2)}) %collective-permute-start.17) | collective-permute-done | bytes 524320 | tf_op jit(solution)/shard_map/ppermute | solution.py:234
  191.4 2.6 collective-permute-start.7
  195.1 29.0 %shard_map.89.refs_2_ = f32[4,128,1024]{2,1,0:T(8,128)S(1)} custom-call(s32[4,32]{1,0:T(4,128)S(1)} %get-tuple-element.31.picks_ref, s32[4,9]{1,0:T(4,128)S(1)} %bitcast.60, bf16[4,272,1024]{2,1,0:T(8,128)(2,1)} %all-to-all-done.1.packed_ref, bf16[2,1024,128]{2,1,0:T(8,128)(2,1)S(1)} %copy-done.6, bf16[2,1024,128]{2,1,0:T(8,128)(2,1)} %collective-permute-done.15.refs_1_, ...), custom_call_target="tpu_custom_call" | custom-call | flops 12884901888 | bytes 6422528 | tf_op jit(solution)/shard_map/pallas_call | solution.py:193
  224.1 8.9 %collective-permute-done.13.refs_0_ = bf16[2,1024,128]{2,1,0:T(8,128)(2,1)} collective-permute-done((bf16[2,1024,128]{2,1,0:T(8,128)(2,1)S(1)}, bf16[2,1024,128]{2,1,0:T(8,128)(2,1)}, u32[]{:S(2)}, u32[]{:S(2)}) %collective-permute-start.13) | collective-permute-done | bytes 524320 | tf_op jit(solution)/shard_map/ppermute | solution.py:234
  235.2 16.7 %shard_map.90.refs_2_ = f32[4,128,1024]{2,1,0:T(8,128)S(1)} custom-call(s32[4,32]{1,0:T(4,128)S(1)} %get-tuple-element.31.picks_ref, s32[4,9]{1,0:T(4,128)S(1)} %bitcast.61, bf16[4,272,1024]{2,1,0:T(8,128)(2,1)} %all-to-all-done.1.packed_ref, bf16[2,1024,128]{2,1,0:T(8,128)(2,1)} %collective-permute-done.13.refs_0_, ...), custom_call_target="tpu_custom_call" | custom-call | flops 6442450944 | bytes 6422528 | tf_op jit(solution)/shard_map/pallas_call | solution.py:193
  252.0 16.8 %shard_map.91 = bf16[4,128,1024]{2,1,0:T(8,128)(2,1)S(1)} custom-call(s32[4,32]{1,0:T(4,128)S(1)} %get-tuple-element.31.picks_ref, s32[4,9]{1,0:T(4,128)S(1)} %bitcast.62, bf16[4,272,1024]{2,1,0:T(8,128)(2,1)} %all-to-all-done.1.packed_ref, bf16[2,1024,128]{2,1,0:T(8,128)(2,1)S(1)} %collective-permute-done.11.refs_0_, ...), custom_call_target="tpu_custom_call" | custom-call | flops 6442450944 | bytes 6422528 | tf_op jit(solution)/shard_map/pallas_call | solution.py:193
  269.8 2.4 collective-permute-start.10
  275.8 4.1 %collective-permute-done.9 = bf16[128,1024]{1,0:T(8,128)(2,1)S(1)} collective-permute-done((bf16[128,1024]{1,0:T(8,128)(2,1)S(1)}, bf16[128,1024]{1,0:T(8,128)(2,1)S(1)}, u32[]{:S(2)}, u32[]{:S(2)}) %collective-permute-start.9) | collective-permute-done | bytes 262176 | tf_op jit(solution)/shard_map/ppermute | solution.py:277
  282.1 17.6 %collective-permute-done.18 = bf16[128,1024]{1,0:T(8,128)(2,1)S(1)} collective-permute-done((bf16[128,1024]{1,0:T(8,128)(2,1)S(1)}, bf16[128,1024]{1,0:T(8,128)(2,1)S(1)}, u32[]{:S(2)}, u32[]{:S(2)}) %collective-permute-start.18) | collective-permute-done | bytes 262176 | tf_op jit(solution)/shard_map/ppermute | solution.py:277
  (84 shorter events, 31.2 us)
Async XLA Ops:
  9.3 54.8 %all-to-all-start = ((bf16[4,272,1024]{2,1,0:T(8,128)(2,1)}), bf16[4,272,1024]{2,1,0:T(8,128)(2,1)}, u32[]{:S(2)}, u32[]{:S(2)}) async-start(bf16[4,272,1024]{2,1,0:T(8,128)(2,1)} %shard_map.82), calls=%async_computation | async-start | bytes 4456448 | tf_op jit(solution)/shard_map/all_to_all | solution.py:261
  23.2 159.3 %collective-permute-start.15 = (bf16[2,1024,128]{2,1,0:T(8,128)(2,1)}, bf16[2,1024,128]{2,1,0:T(8,128)(2,1)}, u32[]{:S(2)}, u32[]{:S(2)}) collective-permute-start(bf16[2,1024,128]{2,1,0:T(8,128)(2,1)} %get-tuple-element.20), channel_id=1, source_target_pairs={{0,1},{1,0},{2,3},{3,2},{4,5},{5,4},{6,7},{7,6},{8,9},{9,8},{10,11... | collective-permute-start | bytes 1572872 | tf_op jit(solution)/shard_map/ppermute | solution.py:234
  23.7 211.5 %collective-permute-start.14 = (bf16[2,1024,128]{2,1,0:T(8,128)(2,1)}, bf16[2,1024,128]{2,1,0:T(8,128)(2,1)}, u32[]{:S(2)}, u32[]{:S(2)}) collective-permute-start(bf16[2,1024,128]{2,1,0:T(8,128)(2,1)} %get-tuple-element.20), channel_id=1, source_target_pairs={{0,5},{1,4},{2,7},{3,6},{4,1},{5,0},{6,3},{7,2},{8,13},{9,12},{10,... | collective-permute-start | bytes 1572872 | tf_op jit(solution)/shard_map/ppermute | solution.py:234
  53.3 16.6 %collective-permute-start.4 = (bf16[2,1024,128]{2,1,0:T(8,128)(2,1)}, bf16[2,1024,128]{2,1,0:T(8,128)(2,1)S(1)}, u32[]{:S(2)}, u32[]{:S(2)}) collective-permute-start(bf16[2,1024,128]{2,1,0:T(8,128)(2,1)} %get-tuple-element.16), channel_id=1, source_target_pairs={{0,1},{1,0},{2,3},{3,2},{4,5},{5,4},{6,7},{7,6},{8,9},{9,8},{10,11... | collective-permute-start | bytes 1572872 | tf_op jit(solution)/shard_map/ppermute | solution.py:234
  53.7 16.5 %collective-permute-start.5 = (bf16[2,1024,128]{2,1,0:T(8,128)(2,1)}, bf16[2,1024,128]{2,1,0:T(8,128)(2,1)S(1)}, u32[]{:S(2)}, u32[]{:S(2)}) collective-permute-start(bf16[2,1024,128]{2,1,0:T(8,128)(2,1)} %get-tuple-element.13), channel_id=1, source_target_pairs={{0,2},{1,3},{2,0},{3,1},{4,6},{5,7},{6,4},{7,5},{8,10},{9,11},{10,... | collective-permute-start | bytes 1572872 | tf_op jit(solution)/shard_map/ppermute | solution.py:234
  55.4 34.6 %collective-permute-start.6 = (bf16[2,1024,128]{2,1,0:T(8,128)(2,1)}, bf16[2,1024,128]{2,1,0:T(8,128)(2,1)}, u32[]{:S(2)}, u32[]{:S(2)}) collective-permute-start(bf16[2,1024,128]{2,1,0:T(8,128)(2,1)} %get-tuple-element.14), channel_id=1, source_target_pairs={{0,3},{1,2},{2,1},{3,0},{4,7},{5,6},{6,5},{7,4},{8,11},{9,10},{10,... | collective-permute-start | bytes 1572872 | tf_op jit(solution)/shard_map/ppermute | solution.py:234
  64.1 129.9 %all-to-all-start.1 = ((bf16[4,272,1024]{2,1,0:T(8,128)(2,1)}), bf16[4,272,1024]{2,1,0:T(8,128)(2,1)}, u32[]{:S(2)}, u32[]{:S(2)}) async-start(bf16[4,272,1024]{2,1,0:T(8,128)(2,1)} %shard_map.87), calls=%async_computation.1 | async-start | bytes 4456448 | tf_op jit(solution)/shard_map/all_to_all | solution.py:261
  69.9 72.8 %collective-permute-start.3 = (bf16[2,1024,128]{2,1,0:T(8,128)(2,1)}, bf16[2,1024,128]{2,1,0:T(8,128)(2,1)S(1)}, u32[]{:S(2)}, u32[]{:S(2)}) collective-permute-start(bf16[2,1024,128]{2,1,0:T(8,128)(2,1)} %get-tuple-element.16), channel_id=1, source_target_pairs={{0,5},{1,4},{2,7},{3,6},{4,1},{5,0},{6,3},{7,2},{8,13},{9,12},{10,... | collective-permute-start | bytes 1572872 | tf_op jit(solution)/shard_map/ppermute | solution.py:234
  70.2 88.3 %collective-permute-start = (bf16[2,1024,128]{2,1,0:T(8,128)(2,1)}, bf16[2,1024,128]{2,1,0:T(8,128)(2,1)S(1)}, u32[]{:S(2)}, u32[]{:S(2)}) collective-permute-start(bf16[2,1024,128]{2,1,0:T(8,128)(2,1)} %get-tuple-element.13), channel_id=1, source_target_pairs={{0,6},{1,7},{2,4},{3,5},{4,2},{5,3},{6,0},{7,1},{8,14},{9,15},{10,... | collective-permute-start | bytes 1572872 | tf_op jit(solution)/shard_map/ppermute | solution.py:234
  90.0 51.6 %collective-permute-start.2 = (bf16[2,1024,128]{2,1,0:T(8,128)(2,1)S(1)}, bf16[2,1024,128]{2,1,0:T(8,128)(2,1)S(1)}, u32[]{:S(2)}, u32[]{:S(2)}) collective-permute-start(bf16[2,1024,128]{2,1,0:T(8,128)(2,1)S(1)} %copy-done.8), channel_id=1, source_target_pairs={{0,4},{1,5},{2,6},{3,7},{4,0},{5,1},{6,2},{7,3},{8,12},{9,13},{10,... | collective-permute-start | bytes 1572872 | tf_op jit(solution)/shard_map/ppermute | solution.py:234
  141.6 18.0 %collective-permute-start.1 = (bf16[2,1024,128]{2,1,0:T(8,128)(2,1)}, bf16[2,1024,128]{2,1,0:T(8,128)(2,1)S(1)}, u32[]{:S(2)}, u32[]{:S(2)}) collective-permute-start(bf16[2,1024,128]{2,1,0:T(8,128)(2,1)} %get-tuple-element.14), channel_id=1, source_target_pairs={{0,7},{1,6},{2,5},{3,4},{4,3},{5,2},{6,1},{7,0},{8,15},{9,14},{10,... | collective-permute-start | bytes 1572872 | tf_op jit(solution)/shard_map/ppermute | solution.py:234
  142.7 43.5 %collective-permute-start.16 = (bf16[2,1024,128]{2,1,0:T(8,128)(2,1)S(1)}, bf16[2,1024,128]{2,1,0:T(8,128)(2,1)S(1)}, u32[]{:S(2)}, u32[]{:S(2)}) collective-permute-start(bf16[2,1024,128]{2,1,0:T(8,128)(2,1)S(1)} %get-tuple-element.17), channel_id=1, source_target_pairs={{0,2},{1,3},{2,0},{3,1},{4,6},{5,7},{6,4},{7,5},{8,10},{9,11},{10,... | collective-permute-start | bytes 1572872 | tf_op jit(solution)/shard_map/ppermute | solution.py:234
  158.5 93.5 %collective-permute-start.11 = (bf16[2,1024,128]{2,1,0:T(8,128)(2,1)S(1)}, bf16[2,1024,128]{2,1,0:T(8,128)(2,1)S(1)}, u32[]{:S(2)}, u32[]{:S(2)}) collective-permute-start(bf16[2,1024,128]{2,1,0:T(8,128)(2,1)S(1)} %get-tuple-element.17), channel_id=1, source_target_pairs={{0,6},{1,7},{2,4},{3,5},{4,2},{5,3},{6,0},{7,1},{8,14},{9,15},{10,... | collective-permute-start | bytes 1572872 | tf_op jit(solution)/shard_map/ppermute | solution.py:234
  159.6 31.0 %collective-permute-start.17 = (bf16[2,1024,128]{2,1,0:T(8,128)(2,1)S(1)}, bf16[2,1024,128]{2,1,0:T(8,128)(2,1)S(1)}, u32[]{:S(2)}, u32[]{:S(2)}) collective-permute-start(bf16[2,1024,128]{2,1,0:T(8,128)(2,1)S(1)} %get-tuple-element.18), channel_id=1, source_target_pairs={{0,3},{1,2},{2,1},{3,0},{4,7},{5,6},{6,5},{7,4},{8,11},{9,10},{10,... | collective-permute-start | bytes 1572872 | tf_op jit(solution)/shard_map/ppermute | solution.py:234
  182.5 69.4 %collective-permute-start.12 = (bf16[2,1024,128]{2,1,0:T(8,128)(2,1)S(1)}, bf16[2,1024,128]{2,1,0:T(8,128)(2,1)S(1)}, u32[]{:S(2)}, u32[]{:S(2)}) collective-permute-start(bf16[2,1024,128]{2,1,0:T(8,128)(2,1)S(1)} %get-tuple-element.18), channel_id=1, source_target_pairs={{0,7},{1,6},{2,5},{3,4},{4,3},{5,2},{6,1},{7,0},{8,15},{9,14},{10,... | collective-permute-start | bytes 1572872 | tf_op jit(solution)/shard_map/ppermute | solution.py:234
  186.2 46.7 %collective-permute-start.13 = (bf16[2,1024,128]{2,1,0:T(8,128)(2,1)S(1)}, bf16[2,1024,128]{2,1,0:T(8,128)(2,1)}, u32[]{:S(2)}, u32[]{:S(2)}) collective-permute-start(bf16[2,1024,128]{2,1,0:T(8,128)(2,1)S(1)} %copy-done.6), channel_id=1, source_target_pairs={{0,4},{1,5},{2,6},{3,7},{4,0},{5,1},{6,2},{7,3},{8,12},{9,13},{10,... | collective-permute-start | bytes 1572872 | tf_op jit(solution)/shard_map/ppermute | solution.py:234
  191.4 80.8 %collective-permute-start.7 = (bf16[128,1024]{1,0:T(8,128)(2,1)}, bf16[128,1024]{1,0:T(8,128)(2,1)}, u32[]{:S(2)}, u32[]{:S(2)}) collective-permute-start(bf16[128,1024]{1,0:T(8,128)(2,1)} %get-tuple-element.28), channel_id=1, source_target_pairs={{0,24},{1,25},{2,26},{3,27},{4,28},{5,29},{6,30},{7,31},{8,0},{9,1... | collective-permute-start | bytes 786440 | tf_op jit(solution)/shard_map/ppermute | solution.py:277
  233.0 42.7 %collective-permute-start.8 = (bf16[128,1024]{1,0:T(8,128)(2,1)S(1)}, bf16[128,1024]{1,0:T(8,128)(2,1)S(1)}, u32[]{:S(2)}, u32[]{:S(2)}) collective-permute-start(bf16[128,1024]{1,0:T(8,128)(2,1)S(1)} %copy-done.13), channel_id=1, source_target_pairs={{0,25},{1,24},{2,27},{3,26},{4,29},{5,28},{6,31},{7,30},{8,1},{9,0... | collective-permute-start | bytes 786440 | tf_op jit(solution)/shard_map/ppermute | solution.py:277
  268.9 30.9 %collective-permute-start.18 = (bf16[128,1024]{1,0:T(8,128)(2,1)S(1)}, bf16[128,1024]{1,0:T(8,128)(2,1)S(1)}, u32[]{:S(2)}, u32[]{:S(2)}) collective-permute-start(bf16[128,1024]{1,0:T(8,128)(2,1)S(1)} %get-tuple-element.24), channel_id=1, source_target_pairs={{0,24},{1,25},{2,26},{3,27},{4,28},{5,29},{6,30},{7,31},{8,0},{9,1... | collective-permute-start | bytes 786440 | tf_op jit(solution)/shard_map/ppermute | solution.py:277
  269.8 10.2 %collective-permute-start.9 = (bf16[128,1024]{1,0:T(8,128)(2,1)S(1)}, bf16[128,1024]{1,0:T(8,128)(2,1)S(1)}, u32[]{:S(2)}, u32[]{:S(2)}) collective-permute-start(bf16[128,1024]{1,0:T(8,128)(2,1)S(1)} %copy-done.12), channel_id=1, source_target_pairs={{0,26},{1,27},{2,24},{3,25},{4,30},{5,31},{6,28},{7,29},{8,2},{9,3... | collective-permute-start | bytes 786440 | tf_op jit(solution)/shard_map/ppermute | solution.py:277
  269.8 12.4 %collective-permute-start.10 = (bf16[128,1024]{1,0:T(8,128)(2,1)S(1)}, bf16[128,1024]{1,0:T(8,128)(2,1)S(1)}, u32[]{:S(2)}, u32[]{:S(2)}) collective-permute-start(bf16[128,1024]{1,0:T(8,128)(2,1)S(1)} %get-tuple-element.25), channel_id=1, source_target_pairs={{0,27},{1,26},{2,25},{3,24},{4,31},{5,30},{6,29},{7,28},{8,3},{9,2... | collective-permute-start | bytes 786440 | tf_op jit(solution)/shard_map/ppermute | solution.py:277
  272.2 28.7 %collective-permute-start.19 = (bf16[128,1024]{1,0:T(8,128)(2,1)S(1)}, bf16[128,1024]{1,0:T(8,128)(2,1)S(1)}, u32[]{:S(2)}, u32[]{:S(2)}) collective-permute-start(bf16[128,1024]{1,0:T(8,128)(2,1)S(1)} %get-tuple-element.23), channel_id=1, source_target_pairs={{0,25},{1,24},{2,27},{3,26},{4,29},{5,28},{6,31},{7,30},{8,1},{9,0... | collective-permute-start | bytes 786440 | tf_op jit(solution)/shard_map/ppermute | solution.py:277
  275.7 25.2 %collective-permute-start.20 = (bf16[128,1024]{1,0:T(8,128)(2,1)S(1)}, bf16[128,1024]{1,0:T(8,128)(2,1)S(1)}, u32[]{:S(2)}, u32[]{:S(2)}) collective-permute-start(bf16[128,1024]{1,0:T(8,128)(2,1)S(1)} %get-tuple-element.22), channel_id=1, source_target_pairs={{0,26},{1,27},{2,24},{3,25},{4,30},{5,31},{6,28},{7,29},{8,2},{9,3... | collective-permute-start | bytes 786440 | tf_op jit(solution)/shard_map/ppermute | solution.py:277
  280.0 21.1 %collective-permute-start.21 = (bf16[128,1024]{1,0:T(8,128)(2,1)S(1)}, bf16[128,1024]{1,0:T(8,128)(2,1)S(1)}, u32[]{:S(2)}, u32[]{:S(2)}) collective-permute-start(bf16[128,1024]{1,0:T(8,128)(2,1)S(1)} %get-tuple-element.21), channel_id=1, source_target_pairs={{0,27},{1,26},{2,25},{3,24},{4,31},{5,30},{6,29},{7,28},{8,3},{9,2... | collective-permute-start | bytes 786440 | tf_op jit(solution)/shard_map/ppermute | solution.py:277
  (14 other events, 113.7 us)

commit v3 on v2

v3 whole, which is shorter than its diff:
```python
import functools
import math

import jax
import jax.numpy as jnp
from jax import lax
from jax.experimental import pallas as pl
from jax.experimental.pallas import tpu as pltpu
from jax.sharding import PartitionSpec as P

BLOCK = 128
PARTS = 3
STAT_ROWS = 16
STEP = 4
VMEM_LIMIT = 48 * 1024 * 1024


def split_parts(value):
    terms = []
    for _ in range(PARTS):
        term = value.astype(jnp.bfloat16)
        terms.append(term.astype(jnp.float32))
        value = value - terms[-1]
    return terms


def pack_kernel(own, group, at_ref, keys_ref, values_ref, *outs):
    rows = keys_ref.shape[0]
    dim = outs[0].shape[2]
    for x in range(group):
        for index in range(own):
            column = pl.multiple_of(((at_ref[0] ^ x) * own + index) * dim, dim)
            out = outs[index * group + x]
            out[0, :rows, :] = keys_ref[:, pl.ds(column, dim)]
            out[0, rows:, :] = values_ref[:, pl.ds(column, dim)]


def pack(mem_keys, mem_values, at, own, group, dim):
    mem_dev, width = mem_keys.shape
    shape = jax.ShapeDtypeStruct((1, 2 * mem_dev, dim), mem_keys.dtype)
    whole = pl.BlockSpec((mem_dev, width), lambda i, _: (0, 0))
    return pl.pallas_call(
        functools.partial(pack_kernel, own, group),
        out_shape=[shape] * (own * group),
        grid_spec=pltpu.PrefetchScalarGridSpec(
            num_scalar_prefetch=1,
            grid=(1,),
            in_specs=[whole, whole],
            out_specs=[pl.BlockSpec((1, 2 * mem_dev, dim), lambda i, _: (0, 0, 0))] * (own * group),
        ),
        compiler_params=pltpu.CompilerParams(vmem_limit_bytes=VMEM_LIMIT),
        cost_estimate=pl.CostEstimate(flops=0, bytes_accessed=8 * mem_dev * width, transcendentals=0),
    )(at[None], mem_keys, mem_values)


def prepare_kernel(heads, dim, own, index, gate_ref, grad_ref, query_ref, out_ref, log_ref, keys_ref, values_ref, mixed_ref):
    rows = grad_ref.shape[0]
    mem_dev = keys_ref.shape[0]
    head = pl.program_id(0) * own + index
    column = pl.ds(pl.multiple_of(head * dim, dim), dim)
    mixed_ref[0, :mem_dev, :] = keys_ref[:, column]
    mixed_ref[0, mem_dev:2 * mem_dev, :] = values_ref[:, column]
    base = 2 * mem_dev
    for h in range(heads):
        columns = slice(h * dim, (h + 1) * dim)
        mixed_ref[0, base + h * dim:base + (h + 1) * dim, :] = query_ref[:, columns].T
        gated = (gate_ref[head * heads + h] * grad_ref[:, columns].T.astype(jnp.float32)).astype(jnp.bfloat16)
        mixed_ref[0, base + (heads + h) * dim:base + (heads + h + 1) * dim, :] = gated
        product = gated.astype(jnp.float32) * out_ref[:, columns].T.astype(jnp.float32)
        delta = jnp.sum(product, axis=0, keepdims=True)
        terms = split_parts(delta) + split_parts(log_ref[h:h + 1, :])
        filler = jnp.zeros((STAT_ROWS - len(terms), rows), jnp.float32)
        start = base + 2 * heads * dim + h * STAT_ROWS
        mixed_ref[0, start:start + STAT_ROWS, :] = jnp.concatenate(terms + [filler], axis=0).astype(jnp.bfloat16)


def prepare(grad_out, queries, mem_out, logs, gates, mem_keys, mem_values, kv_heads, dim, own, index):
    rows, width = grad_out.shape
    mem_dev, kv_width = mem_keys.shape
    heads = width // dim // kv_heads
    group = kv_heads // own
    span = 2 * mem_dev + heads * (2 * dim + STAT_ROWS)
    wide = pl.BlockSpec((rows, heads * dim), lambda k, _: (0, k * own + index))
    whole = pl.BlockSpec((mem_dev, kv_width), lambda k, _: (0, 0))
    return pl.pallas_call(
        functools.partial(prepare_kernel, heads, dim, own, index),
        out_shape=jax.ShapeDtypeStruct((group, span, rows), jnp.bfloat16),
        grid_spec=pltpu.PrefetchScalarGridSpec(
            num_scalar_prefetch=1,
            grid=(group,),
            in_specs=[
                wide, wide, wide, pl.BlockSpec((heads, rows), lambda k, _: (k * own + index, 0)), whole, whole,
            ],
            out_specs=pl.BlockSpec((1, span, rows), lambda k, _: (k, 0, 0)),
        ),
        compiler_params=pltpu.CompilerParams(vmem_limit_bytes=VMEM_LIMIT),
        cost_estimate=pl.CostEstimate(flops=rows * width * 4, bytes_accessed=rows * width * 12 // own, transcendentals=0),
    )(gates, grad_out, queries, mem_out, logs, mem_keys, mem_values)


def attend_kernel(heads, dim, rows, mem_dev, scale, fresh, last, places, only_ref, picks_ref, starts_ref, *refs):
    count = places[1] - places[0]
    query_ref, stat_ref = refs[:2]
    if fresh:
        memory_refs, acc_in = refs[2:-5], None
    else:
        memory_refs, acc_in = refs[2:-6], refs[-6]
    out_ref, keys_ref, values_ref, turned, total = refs[-5:]
    step = pl.program_id(0)
    tile = only_ref[0] + step
    blocks = mem_dev // BLOCK
    pair = 2 * rows

    @pl.when(step == 0)
    def _():
        at = 0
        for memory in memory_refs:
            for piece in range(memory.shape[0]):
                here = slice(at * mem_dev, (at + 1) * mem_dev)
                keys_ref[here, :] = memory[piece, :mem_dev, :]
                values_ref[here, :] = memory[piece, mem_dev:, :]
                for block in range(blocks):
                    turned[at * blocks + block] = memory[piece, block * BLOCK:(block + 1) * BLOCK, :].T
                at += 1

    if fresh:
        total[...] = jnp.zeros_like(total)
    else:
        total[...] = acc_in[0]

    deltas, logs = [], []
    for h in range(heads):
        stats = stat_ref[0, h * STAT_ROWS:(h + 1) * STAT_ROWS, :].astype(jnp.float32)
        deltas.append(jnp.sum(stats[:PARTS], axis=0, keepdims=True))
        logs.append(jnp.sum(stats[PARTS:2 * PARTS], axis=0, keepdims=True))

    def wide(ref, first):
        return jnp.concatenate([ref[0, first * dim:(first + 1) * dim, :], ref[0, (first + 1) * dim:(first + 2) * dim, :]], axis=1)

    low = starts_ref[tile, places[0]]
    high = starts_ref[tile, places[1]]
    offset = places[0] * blocks
    exponent = scale * math.log2(math.e)

    def add(here, number, checked):
        keys, values, across = [], [], []
        for j in range(number):
            valid = here + j < high
            block = picks_ref[tile, jnp.where(valid, here + j, here) if checked else here + j] - offset
            row = pl.ds(pl.multiple_of(block * BLOCK, BLOCK), BLOCK)
            keys.append(keys_ref[row, :])
            values.append(values_ref[row, :])
            side = turned[block]
            across.append(jnp.where(valid, side, jnp.zeros_like(side)) if checked and j else side)
        keys = jnp.concatenate(keys, axis=0)
        values = jnp.concatenate(values, axis=0)
        across = jnp.concatenate(across, axis=1)
        for p in range(heads // 2):
            span = slice(p * pair, (p + 1) * pair)
            log_row = jnp.concatenate(logs[2 * p:2 * p + 2], axis=1)
            delta_row = jnp.concatenate(deltas[2 * p:2 * p + 2], axis=1)
            scores = jnp.dot(keys, wide(query_ref, 2 * p), preferred_element_type=jnp.float32)
            grad_probs = jnp.dot(values, wide(query_ref, heads + 2 * p), preferred_element_type=jnp.float32)
            probs = jnp.exp2(scores * exponent - log_row)
            grad_scores = (probs * (grad_probs - delta_row)).astype(jnp.bfloat16)
            total[:, span] += jnp.dot(across, grad_scores, preferred_element_type=jnp.float32)

    full = (high - low) // STEP

    def many(turn, carry):
        add(low + STEP * turn, STEP, False)
        return carry

    def few(turn, carry):
        add(low + STEP * full + 2 * turn, 2, True)
        return carry

    lax.fori_loop(0, full, many, 0)
    lax.fori_loop(0, (high - low - STEP * full + 1) // 2, few, 0)

    if last:
        for h in range(heads):
            out_ref[0, :, h * dim:(h + 1) * dim] = total[:, h * rows:(h + 1) * rows].T.astype(jnp.bfloat16)
    else:
        out_ref[0] = total[...]


def attend(mixed, memories, places, acc, picks, starts, heads, dim, mem_dev, scale, last, only=None):
    tiles, span, rows = mixed.shape
    fresh = acc is None
    count = places[1] - places[0]
    blocks = mem_dev // BLOCK
    width = heads * rows
    big = 2 * heads * dim
    steps = tiles if only is None else 1
    acc_spec = pl.BlockSpec((1, dim, width), lambda t, o, *_: (o[0] + t, 0, 0))
    if last:
        out_shape = jax.ShapeDtypeStruct((steps, rows, heads * dim), jnp.bfloat16)
        out_spec = pl.BlockSpec((1, rows, heads * dim), lambda t, *_: (t, 0, 0))
    else:
        out_shape = jax.ShapeDtypeStruct((tiles, dim, width), jnp.float32)
        out_spec = acc_spec
    if memories is None:
        memories = [mixed]
        memory_specs = [pl.BlockSpec((tiles, 2 * mem_dev, dim), lambda t, *_: (0, 0, 0))]
    else:
        memory_specs = [pl.BlockSpec(m.shape, lambda t, *_: (0, 0, 0)) for m in memories]
    stat = heads * STAT_ROWS
    first = 2 * mem_dev // big
    last_block = (2 * mem_dev + big) // stat
    flops = steps * count * (blocks // 2) * BLOCK * width * dim * 6
    return pl.pallas_call(
        functools.partial(attend_kernel, heads, dim, rows, mem_dev, scale, fresh, last, places),
        out_shape=out_shape,
        grid_spec=pltpu.PrefetchScalarGridSpec(
            num_scalar_prefetch=3,
            grid=(steps,),
            in_specs=[
                pl.BlockSpec((1, big, rows), lambda t, o, *_: (o[0] + t, first, 0)),
                pl.BlockSpec((1, stat, rows), lambda t, o, *_: (o[0] + t, last_block, 0)),
            ]
            + memory_specs
            + ([] if fresh else [acc_spec]),
            out_specs=out_spec,
            scratch_shapes=[
                pltpu.VMEM((count * mem_dev, dim), jnp.bfloat16),
                pltpu.VMEM((count * mem_dev, dim), jnp.bfloat16),
                pltpu.VMEM((count * blocks, dim, BLOCK), jnp.bfloat16),
                pltpu.VMEM((dim, width), jnp.float32),
            ],
        ),
        compiler_params=pltpu.CompilerParams(vmem_limit_bytes=VMEM_LIMIT),
        cost_estimate=pl.CostEstimate(
            flops=flops * 4, bytes_accessed=0, transcendentals=0
        ),
    )(
        jnp.zeros((1,), jnp.int32) if only is None else only[None], picks, starts, mixed, mixed, *memories,
        *([] if fresh else [acc]),
    )


def after(value, *others):
    anywhere = pl.BlockSpec(memory_space=pl.ANY)
    return pl.pallas_call(
        lambda *refs: None,
        out_shape=jax.ShapeDtypeStruct(value.shape, value.dtype),
        in_specs=[anywhere] * (1 + len(others)),
        out_specs=anywhere,
        input_output_aliases={0: 0},
        cost_estimate=pl.CostEstimate(flops=0, bytes_accessed=0, transcendentals=0),
    )(value, *others)


def shards(grad_out, queries, mem_out, row_total, gate_logit, mem_keys, mem_values, retrieved):
    seq = lax.axis_size("seq")
    sections = lax.axis_size("section")
    position = lax.axis_index("seq")
    rows, width = grad_out.shape[1:]
    head_count = gate_logit.shape[1]
    dim = width // head_count
    kv_heads = mem_keys.shape[2] // dim
    heads = head_count // kv_heads
    mem_dev = mem_keys.shape[1]
    blocks = mem_dev // BLOCK
    group = min(kv_heads, seq // 2)
    own = kv_heads // group
    at = position % group
    home = position // group
    scale = dim ** (-0.5)

    def swapped(value, step):
        return lax.ppermute(value, "seq", [(p, p ^ step) for p in range(seq)])

    def delivered(value, step):
        pairs = [(s * seq + p, ((s - 1) % sections) * seq + (p ^ step)) for s in range(sections) for p in range(seq)]
        return lax.ppermute(value, ("section", "seq"), pairs)

    logs = jnp.log2(row_total[0].T.astype(jnp.float32)) - math.log2(scale)
    gates = jax.nn.sigmoid(gate_logit[0])

    mine = lax.dynamic_slice_in_dim(retrieved[0], at * own, own, 0)
    mine = lax.dynamic_slice_in_dim(mine, home * group, group, 1)
    holder = mine // blocks
    place = jnp.where(holder // group == home, holder % group, holder ^ position)
    block = place * blocks + mine % blocks
    rank = jnp.sum(block[..., None, :] < block[..., :, None], axis=-1)
    order = jnp.arange(block.shape[-1])
    picks = jnp.sum(jnp.where(rank[..., :, None] == order, block[..., :, None], 0), axis=-2).astype(jnp.int32)
    starts = jnp.sum(block[..., None, :] < (jnp.arange(seq + 1) * blocks)[:, None], axis=-1).astype(jnp.int32)

    half = group + (seq - group) // 2
    most = seq - 1

    def settle(acc, i, out):
        acc = lax.all_to_all(acc, "seq", split_axis=0, concat_axis=0, axis_index_groups=groups, tiled=True)
        acc = delivered(acc, 0)
        for t in range(group):
            out = lax.dynamic_update_slice_in_dim(out, acc[t], (t * own + i) * heads * dim, 1)
        return out

    groups = [list(range(g * group, (g + 1) * group)) for g in range(seq // group)]
    sends = list(pack(mem_keys[0], mem_values[0], at, own, group, dim))
    out = jnp.zeros((rows, width), jnp.bfloat16)
    def shared(i):
        mixed = prepare(
            grad_out[0], queries[0], mem_out[0], logs, gates, mem_keys[0], mem_values[0], kv_heads, dim, own, i
        )
        return lax.all_to_all(mixed, "seq", split_axis=0, concat_axis=0, axis_index_groups=groups, tiled=True)

    done = None
    coming = shared(0)
    for i in range(own):
        ending = i == own - 1
        mixed = coming
        arrived = {step: swapped(sends[i * group + step % group], step) for step in range(group, seq)}
        run = functools.partial(attend, mixed, heads=heads, dim=dim, mem_dev=mem_dev, scale=scale, picks=picks[i])
        where = starts[i]
        if not ending:
            coming = shared(i + 1)
            for step in range(group, half):
                later = (i + 1) * group + step % group
                sends[later] = after(sends[later], arrived[step])
            where = after(where, *[arrived[step] for step in range(group, half)])
        if i:
            where = after(where, done)
            out = settle(done, i - 1, out)
        acc = run(None, (0, group), None, starts=where, last=False)
        if not ending:
            for step in range(half, seq):
                later = (i + 1) * group + step % group
                sends[later] = after(sends[later], arrived[step], acc)
            where = after(where, coming)
            done = run([arrived[p] for p in range(group, seq)], (group, seq), acc, starts=where, last=True)
            continue
        acc = run([arrived[p] for p in range(group, half)], (group, half), acc, starts=where, last=False)
        if half < most:
            acc = run([arrived[p] for p in range(half, most)], (half, most), acc, starts=where, last=False)
        for x in range(group):
            only = (at ^ x).astype(jnp.int32)
            piece = run([arrived[most]], (most, seq), acc, starts=where, last=True, only=only)
            piece = delivered(piece[0], x)
            out = lax.dynamic_update_slice_in_dim(out, piece, ((at ^ x) * own + i) * heads * dim, 1)
    return out[None]


def solution(mesh):
    return jax.shard_map(
        shards,
        mesh=mesh,
        in_specs=(
            P("section", "seq", None),
            P("section", "seq", None),
            P("section", "seq", None),
            P("section", "seq", None),
            P("section", None),
            P("section", "seq", None),
            P("section", "seq", None),
            P("section", None, None, None),
        ),
        out_specs=P("section", "seq", None),
        check_vma=False,
    )
```

time: 306 us -> 358 us (1.17); the launches traced: 303 us -> 351 us
  starting transfers between devices: 42.7 us -> 80.7 us
  waiting for transfers between devices: 75.1 us -> 106 us
  Pallas kernels: 167 us -> 139 us
  local copies, waits for them, and re-layouts: 14.4 us -> 22.3 us
    all_to_all x2 -> x3, starting transfers between devices: 9.23 us -> 56 us  [the longest x1 46.1 us: settle(): lax.all_to_all(acc, 'seq', split_axis=0, concat_axis=0, axis_index_groups...]
    all_to_all x2 -> x3, waiting for transfers between devices: 0.01 us -> 42.1 us  [the longest x2 42.1 us: shared(): lax.all_to_all(mixed, 'seq', split_axis=0, concat_axis=0, axis_index_grou...]
    pallas_call x8 -> x17, Pallas kernels: 158 us -> 126 us  [the longest x9 122 us: attend(): pl.pallas_call(functools.partial(attend_kernel, heads, dim, rows, mem_dev...]
    ppermute x8 -> x5, waiting for transfers between devices: 24.7 us -> 15.2 us  [delivered(): return lax.ppermute(value, ('section', 'seq'), pairs)]
    unnamed x28 -> x48, local copies, waits for them, and re-layouts: 11.1 us -> 19.9 us
    ppermute x14 -> x8, starting transfers between devices: 23.3 us -> 17.5 us  [swapped(): return lax.ppermute(value, 'seq', [(p, p ^ step) for p in range(seq)])]
    pallas_call x2, Pallas kernels: 9.45 us -> 13.2 us  [prepare(): pl.pallas_call(functools.partial(prepare_kernel, heads, dim, own, index),...]
    ppermute x8 -> x5, starting transfers between devices: 10.2 us -> 7.29 us  [delivered(): return lax.ppermute(value, ('section', 'seq'), pairs)]
  transfers between devices with their start and end apart: 24 -> 16, of which waited for: 8 -> 4; matrix products, arithmetic and copies ran while one was open for 1% -> 1% of each run, Pallas kernels for 54% -> 38%
where the time goes in v3:
time: 358 us; the launch traced here: 351 us
  Pallas kernels  139 us (39%)
  waiting for transfers between devices  106 us (30%)
  starting transfers between devices  80.7 us (23%)
  local copies, waits for them, and re-layouts  22.3 us (6%)
    pallas_call x9, Pallas kernels, attend(): pl.pallas_call(functools.partial(attend_kernel, heads, dim, rows, mem_dev...  122 us
    ppermute x8, waiting for transfers between devices, swapped(): return lax.ppermute(value, 'seq', [(p, p ^ step) for p in range(seq)])  48.2 us
    all_to_all x1, starting transfers between devices, settle(): lax.all_to_all(acc, 'seq', split_axis=0, concat_axis=0, axis_index_groups...  46.1 us
    all_to_all x2, waiting for transfers between devices, shared(): lax.all_to_all(mixed, 'seq', split_axis=0, concat_axis=0, axis_index_grou...  42.1 us
    unnamed x48, local copies, waits for them, and re-layouts  19.9 us
    ppermute x8, starting transfers between devices, swapped(): return lax.ppermute(value, 'seq', [(p, p ^ step) for p in range(seq)])  17.5 us
    ppermute x5, waiting for transfers between devices, delivered(): return lax.ppermute(value, ('section', 'seq'), pairs)  15.2 us
    pallas_call x2, Pallas kernels, prepare(): pl.pallas_call(functools.partial(prepare_kernel, heads, dim, own, index),...  13.2 us
  transfers between devices with their start and end apart: 16, of which 4 were waited for; matrix products, arithmetic and copies ran while one was open for 1% of the time, Pallas kernels for 38%

profile of v3, /device:TPU:0, one launch (start us, length us, event | category | flops | bytes accessed | tf_op | source)
XLA Modules:
  0.0 351.1 jit_solution(2597568531529048789)
XLA Ops:
  4.6 6.6 %shard_map.86 = bf16[4,4224,128]{2,1,0:T(8,128)(2,1)} custom-call(f32[64]{0:T(128)S(1)} %divide_bitcast_fusion.gate_ref, bf16[128,8192]{1,0:T(8,128)(2,1)S(1)} %bitcast.55, bf16[128,8192]{1,0:T(8,128)(2,1)S(1)} %bitcast.57, bf16[128,8192]{1,0:T(8,128)(2,1)} %bitcast.71, f32[64,128]{1,0:T(8,128)S(1)} %add_bitcast_fusion.log_ref, bf16[1024,1024]{1,0:T(8,128)(2,1)} %bitcast.65, ...), custom_call_target="tpu_custom_call" | custom-call | flops 4194304 | bytes 6291456 | tf_op jit(solution)/shard_map/pallas_call | solution.py:85
  11.2 5.0 %all-to-all-start.1 = ((bf16[4,4224,128]{2,1,0:T(8,128)(2,1)}), bf16[4,4224,128]{2,1,0:T(8,128)(2,1)}, u32[]{:S(2)}, u32[]{:S(2)}) async-start(bf16[4,4224,128]{2,1,0:T(8,128)(2,1)} %shard_map.86), calls=%async_computation.1 | async-start | bytes 8650752 | tf_op jit(solution)/shard_map/all_to_all | solution.py:308
  17.8 6.6 %shard_map.84 = bf16[4,4224,128]{2,1,0:T(8,128)(2,1)} custom-call(f32[64]{0:T(128)S(1)} %divide_bitcast_fusion.gate_ref, bf16[128,8192]{1,0:T(8,128)(2,1)S(1)} %bitcast.56, bf16[128,8192]{1,0:T(8,128)(2,1)S(1)} %bitcast.58, bf16[128,8192]{1,0:T(8,128)(2,1)} %bitcast.72, f32[64,128]{1,0:T(8,128)S(1)} %add_bitcast_fusion.log_ref, bf16[1024,1024]{1,0:T(8,128)(2,1)} %bitcast.66, ...), custom_call_target="tpu_custom_call" | custom-call | flops 4194304 | bytes 6291456 | tf_op jit(solution)/shard_map/pallas_call | solution.py:85
  24.4 42.1 %all-to-all-done.1.refs_0_.refs_1_.refs_2_ = bf16[4,4224,128]{2,1,0:T(8,128)(2,1)} async-done(((bf16[4,4224,128]{2,1,0:T(8,128)(2,1)}), bf16[4,4224,128]{2,1,0:T(8,128)(2,1)}, u32[]{:S(2)}, u32[]{:S(2)}) %all-to-all-start.1) | async-done | bytes 4325408 | tf_op jit(solution)/shard_map/all_to_all | solution.py:308
  66.6 4.9 %all-to-all-start = ((bf16[4,4224,128]{2,1,0:T(8,128)(2,1)}), bf16[4,4224,128]{2,1,0:T(8,128)(2,1)}, u32[]{:S(2)}, u32[]{:S(2)}) async-start(bf16[4,4224,128]{2,1,0:T(8,128)(2,1)} %shard_map.84), calls=%async_computation | async-start | bytes 8650752 | tf_op jit(solution)/shard_map/all_to_all | solution.py:308
  71.5 4.3 %shard_map.82 = (bf16[1,2048,128]{2,1,0:T(8,128)(2,1)}, bf16[1,2048,128]{2,1,0:T(8,128)(2,1)}, bf16[1,2048,128]{2,1,0:T(8,128)(2,1)S(1)}, bf16[1,2048,128]{2,1,0...) custom-call(s32[1]{0:T(128)} %bitcast.3.at_ref.only_ref, ...), custom_call_target="tpu_custom_call" | custom-call | bytes 8388608 | tf_op jit(solution)/shard_map/pallas_call | solution.py:42
  78.9 3.3 collective-permute-start
  82.3 3.7 %collective-permute-start.2 = (bf16[1,2048,128]{2,1,0:T(8,128)(2,1)S(1)}, bf16[1,2048,128]{2,1,0:T(8,128)(2,1)S(1)}, u32[]{:S(2)}, u32[]{:S(2)}) collective-permute-start(bf16[1,2048,128]{2,1,0:T(8,128)(2,1)S(1)} %get-tuple-element.15), channel_id=1, source_target_pairs={{0,6},{1,7},{2,4},{3,5},{4,2},{5,3},{6,0},{7,1},{8,14},{9,15},{10,... | collective-permute-start | bytes 1572872 | tf_op jit(solution)/shard_map/ppermute | solution.py:272
  89.3 41.1 %collective-permute-done.refs_1_.refs_2_ = bf16[1,2048,128]{2,1,0:T(8,128)(2,1)S(1)} collective-permute-done((bf16[1,2048,128]{2,1,0:T(8,128)(2,1)}, bf16[1,2048,128]{2,1,0:T(8,128)(2,1)S(1)}, u32[]{:S(2)}, u32[]{:S(2)}) %collective-permute-start) | collective-permute-done | bytes 524320 | tf_op jit(solution)/shard_map/ppermute | solution.py:272
  131.3 3.3 collective-permute-start.7
  134.6 7.1 %collective-permute-done.1.refs_2_.refs_3_.refs_1_ = bf16[1,2048,128]{2,1,0:T(8,128)(2,1)S(1)} collective-permute-done((bf16[1,2048,128]{2,1,0:T(8,128)(2,1)}, bf16[1,2048,128]{2,1,0:T(8,128)(2,1)S(1)}, u32[]{:S(2)}, u32[]{:S(2)}) %collective-permute-start.1) | collective-permute-done | bytes 524320 | tf_op jit(solution)/shard_map/ppermute | solution.py:272
  145.9 28.6 %shard_map.87.refs_6_.refs_2_ = f32[4,128,1024]{2,1,0:T(8,128)S(1)} custom-call(s32[1]{0:T(128)} %constant.110.clone.1.only_ref, s32[4,32]{1,0:T(4,128)S(1)} %get-tuple-element.24.picks_ref, s32[4,9]{1,0:T(4,128)S(1)} %copy-done.21, bf16[4,4224,128]{2,1,0:T(8,128)(2,1)} %all-to-all-done.1.refs_0_.refs_1_.refs_2_, ...), custom_call_target="tpu_custom_call" | custom-call | flops 25769803776 | tf_op jit(solution)/shard_map/pallas_call | solution.py:212
  177.5 4.0 %collective-permute-start.6 = (bf16[1,2048,128]{2,1,0:T(8,128)(2,1)}, bf16[1,2048,128]{2,1,0:T(8,128)(2,1)}, u32[]{:S(2)}, u32[]{:S(2)}) collective-permute-start(bf16[1,2048,128]{2,1,0:T(8,128)(2,1)} %shard_map.91), channel_id=1, source_target_pairs={{0,6},{1,7},{2,4},{3,5},{4,2},{5,3},{6,0},{7,1},{8,14},{9,15},{10,... | collective-permute-start | bytes 1572872 | tf_op jit(solution)/shard_map/ppermute | solution.py:272
  185.3 23.6 %shard_map.88.refs_1_ = bf16[4,128,1024]{2,1,0:T(8,128)(2,1)S(1)} custom-call(s32[1]{0:T(128)} %constant.110.clone.1.only_ref, s32[4,32]{1,0:T(4,128)S(1)} %get-tuple-element.24.picks_ref, s32[4,9]{1,0:T(4,128)S(1)} %copy-done.22, bf16[4,4224,128]{2,1,0:T(8,128)(2,1)} %all-to-all-done.1.refs_0_.refs_1_.refs_2_, ...), custom_call_target="tpu_custom_call" | custom-call | flops 25769803776 | tf_op jit(solution)/shard_map/pallas_call | solution.py:212
  209.9 46.1 %all-to-all-start.2 = ((bf16[4,128,1024]{2,1,0:T(8,128)(2,1)}), bf16[4,128,1024]{2,1,0:T(8,128)(2,1)}, u32[]{:S(2)}, u32[]{:S(2)}) async-start(bf16[4,128,1024]{2,1,0:T(8,128)(2,1)} %copy-done.6), calls=%async_computation.2 | async-start | bytes 2097152 | tf_op jit(solution)/shard_map/all_to_all | solution.py:295
  256.6 29.7 %shard_map.94.refs_4_ = f32[4,128,1024]{2,1,0:T(8,128)S(1)} custom-call(s32[1]{0:T(128)} %constant.110.clone.1.only_ref, s32[4,32]{1,0:T(4,128)S(1)} %get-tuple-element.23.picks_ref, s32[4,9]{1,0:T(4,128)S(1)} %copy-done.19, bf16[4,4224,128]{2,1,0:T(8,128)(2,1)} %all-to-all-done.refs_1_.refs_0_.refs_2_, ...), custom_call_target="tpu_custom_call" | custom-call | flops 25769803776 | tf_op jit(solution)/shard_map/pallas_call | solution.py:212
  286.3 14.8 %shard_map.95.refs_3_ = f32[4,128,1024]{2,1,0:T(8,128)S(1)} custom-call(s32[1]{0:T(128)} %constant.110.clone.1.only_ref, s32[4,32]{1,0:T(4,128)S(1)} %get-tuple-element.23.picks_ref, s32[4,9]{1,0:T(4,128)S(1)} %copy-done.20, bf16[4,4224,128]{2,1,0:T(8,128)(2,1)} %all-to-all-done.refs_1_.refs_0_.refs_2_, ...), custom_call_target="tpu_custom_call" | custom-call | flops 12884901888 | tf_op jit(solution)/shard_map/pallas_call | solution.py:212
  303.1 8.2 %shard_map.96.refs_3_ = f32[4,128,1024]{2,1,0:T(8,128)S(1)} custom-call(s32[1]{0:T(128)} %constant.110.clone.1.only_ref, s32[4,32]{1,0:T(4,128)S(1)} %get-tuple-element.23.picks_ref, s32[4,9]{1,0:T(4,128)S(1)} %copy-done.20, bf16[4,4224,128]{2,1,0:T(8,128)(2,1)} %all-to-all-done.refs_1_.refs_0_.refs_2_, ...), custom_call_target="tpu_custom_call" | custom-call | flops 6442450944 | tf_op jit(solution)/shard_map/pallas_call | solution.py:212
  311.4 4.3 %shard_map.98 = bf16[1,128,1024]{2,1,0:T(8,128)(2,1)S(1)} custom-call(s32[1]{0:T(128)} %bitcast.19.only_ref, s32[4,32]{1,0:T(4,128)S(1)} %get-tuple-element.23.picks_ref, s32[4,9]{1,0:T(4,128)S(1)} %copy-done.20, bf16[4,4224,128]{2,1,0:T(8,128)(2,1)} %all-to-all-done.refs_1_.refs_0_.refs_2_, bf16[4,4224,128]{2,1,0:T(8,128)(2,1)} %all-to-all-done.refs_1_.refs_0_.refs_2_, ...), custom_call_target="tpu_custom_call" | custom-call | flops 1610612736 | tf_op jit(solution)/shard_map/pallas_call | solution.py:212
  315.8 4.0 %shard_map.97 = bf16[1,128,1024]{2,1,0:T(8,128)(2,1)S(1)} custom-call(s32[1]{0:T(128)} %bitcast.3.at_ref.only_ref, s32[4,32]{1,0:T(4,128)S(1)} %get-tuple-element.23.picks_ref, s32[4,9]{1,0:T(4,128)S(1)} %copy-done.20, bf16[4,4224,128]{2,1,0:T(8,128)(2,1)} %all-to-all-done.refs_1_.refs_0_.refs_2_, ...), custom_call_target="tpu_custom_call" | custom-call | flops 1610612736 | tf_op jit(solution)/shard_map/pallas_call | solution.py:212
  319.9 4.3 %shard_map.99 = bf16[1,128,1024]{2,1,0:T(8,128)(2,1)S(1)} custom-call(s32[1]{0:T(128)} %bitcast.22.only_ref, s32[4,32]{1,0:T(4,128)S(1)} %get-tuple-element.23.picks_ref, s32[4,9]{1,0:T(4,128)S(1)} %copy-done.20, bf16[4,4224,128]{2,1,0:T(8,128)(2,1)} %all-to-all-done.refs_1_.refs_0_.refs_2_, bf16[4,4224,128]{2,1,0:T(8,128)(2,1)} %all-to-all-done.refs_1_.refs_0_.refs_2_, ...), custom_call_target="tpu_custom_call" | custom-call | flops 1610612736 | tf_op jit(solution)/shard_map/pallas_call | solution.py:212
  324.2 4.8 %collective-permute-start.11 = (bf16[128,1024]{1,0:T(8,128)(2,1)S(1)}, bf16[128,1024]{1,0:T(8,128)(2,1)S(1)}, u32[]{:S(2)}, u32[]{:S(2)}) collective-permute-start(bf16[128,1024]{1,0:T(8,128)(2,1)S(1)} %bitcast.61), channel_id=1, source_target_pairs={{0,26},{1,27},{2,24},{3,25},{4,30},{5,31},{6,28},{7,29},{8,2},{9,3... | collective-permute-start | bytes 786440 | tf_op jit(solution)/shard_map/ppermute | solution.py:276
  328.9 4.0 %shard_map.100 = bf16[1,128,1024]{2,1,0:T(8,128)(2,1)S(1)} custom-call(s32[1]{0:T(128)} %bitcast.25.only_ref, s32[4,32]{1,0:T(4,128)S(1)} %get-tuple-element.23.picks_ref, s32[4,9]{1,0:T(4,128)S(1)} %copy-done.20, bf16[4,4224,128]{2,1,0:T(8,128)(2,1)} %all-to-all-done.refs_1_.refs_0_.refs_2_, bf16[4,4224,128]{2,1,0:T(8,128)(2,1)} %all-to-all-done.refs_1_.refs_0_.refs_2_, ...), custom_call_target="tpu_custom_call" | custom-call | flops 1610612736 | tf_op jit(solution)/shard_map/pallas_call | solution.py:212
  333.8 15.2 %collective-permute-done.9 = bf16[128,1024]{1,0:T(8,128)(2,1)S(1)} collective-permute-done((bf16[128,1024]{1,0:T(8,128)(2,1)S(1)}, bf16[128,1024]{1,0:T(8,128)(2,1)S(1)}, u32[]{:S(2)}, u32[]{:S(2)}) %collective-permute-start.9) | collective-permute-done | bytes 262176 | tf_op jit(solution)/shard_map/ppermute | solution.py:276
  (95 shorter events, 31.0 us)
Async XLA Ops:
  1.4 1.6 copy-start.2
  3.0 1.6 copy-start.4
  11.2 5.0 %copy-start.3 = (bf16[1,128,8192]{2,1,0:T(8,128)(2,1)S(1)}, bf16[1,128,8192]{2,1,0:T(8,128)(2,1)}, u32[]{:S(2)}) copy-start(bf16[1,128,8192]{2,1,0:T(8,128)(2,1)} %param.8) | copy-start | bytes 6291460
  11.2 55.4 %all-to-all-start.1 = ((bf16[4,4224,128]{2,1,0:T(8,128)(2,1)}), bf16[4,4224,128]{2,1,0:T(8,128)(2,1)}, u32[]{:S(2)}, u32[]{:S(2)}) async-start(bf16[4,4224,128]{2,1,0:T(8,128)(2,1)} %shard_map.86), calls=%async_computation.1 | async-start | bytes 8650752 | tf_op jit(solution)/shard_map/all_to_all | solution.py:308
  16.2 1.6 copy-start.5
  66.6 114.9 %all-to-all-start = ((bf16[4,4224,128]{2,1,0:T(8,128)(2,1)}), bf16[4,4224,128]{2,1,0:T(8,128)(2,1)}, u32[]{:S(2)}, u32[]{:S(2)}) async-start(bf16[4,4224,128]{2,1,0:T(8,128)(2,1)} %shard_map.84), calls=%async_computation | async-start | bytes 8650752 | tf_op jit(solution)/shard_map/all_to_all | solution.py:308
  78.9 51.5 %collective-permute-start = (bf16[1,2048,128]{2,1,0:T(8,128)(2,1)}, bf16[1,2048,128]{2,1,0:T(8,128)(2,1)S(1)}, u32[]{:S(2)}, u32[]{:S(2)}) collective-permute-start(bf16[1,2048,128]{2,1,0:T(8,128)(2,1)} %get-tuple-element.13), channel_id=1, source_target_pairs={{0,4},{1,5},{2,6},{3,7},{4,0},{5,1},{6,2},{7,3},{8,12},{9,13},{10,... | collective-permute-start | bytes 1572872 | tf_op jit(solution)/shard_map/ppermute | solution.py:272
  82.3 59.4 %collective-permute-start.1 = (bf16[1,2048,128]{2,1,0:T(8,128)(2,1)}, bf16[1,2048,128]{2,1,0:T(8,128)(2,1)S(1)}, u32[]{:S(2)}, u32[]{:S(2)}) collective-permute-start(bf16[1,2048,128]{2,1,0:T(8,128)(2,1)} %get-tuple-element.14), channel_id=1, source_target_pairs={{0,5},{1,4},{2,7},{3,6},{4,1},{5,0},{6,3},{7,2},{8,13},{9,12},{10,... | collective-permute-start | bytes 1572872 | tf_op jit(solution)/shard_map/ppermute | solution.py:272
  82.3 94.4 %collective-permute-start.2 = (bf16[1,2048,128]{2,1,0:T(8,128)(2,1)S(1)}, bf16[1,2048,128]{2,1,0:T(8,128)(2,1)S(1)}, u32[]{:S(2)}, u32[]{:S(2)}) collective-permute-start(bf16[1,2048,128]{2,1,0:T(8,128)(2,1)S(1)} %get-tuple-element.15), channel_id=1, source_target_pairs={{0,6},{1,7},{2,4},{3,5},{4,2},{5,3},{6,0},{7,1},{8,14},{9,15},{10,... | collective-permute-start | bytes 1572872 | tf_op jit(solution)/shard_map/ppermute | solution.py:272
  86.0 89.8 %collective-permute-start.3 = (bf16[1,2048,128]{2,1,0:T(8,128)(2,1)S(1)}, bf16[1,2048,128]{2,1,0:T(8,128)(2,1)S(1)}, u32[]{:S(2)}, u32[]{:S(2)}) collective-permute-start(bf16[1,2048,128]{2,1,0:T(8,128)(2,1)S(1)} %get-tuple-element.16), channel_id=1, source_target_pairs={{0,7},{1,6},{2,5},{3,4},{4,3},{5,2},{6,1},{7,0},{8,15},{9,14},{10,... | collective-permute-start | bytes 1572872 | tf_op jit(solution)/shard_map/ppermute | solution.py:272
  131.3 155.0 %collective-permute-start.7 = (bf16[1,2048,128]{2,1,0:T(8,128)(2,1)}, bf16[1,2048,128]{2,1,0:T(8,128)(2,1)}, u32[]{:S(2)}, u32[]{:S(2)}) collective-permute-start(bf16[1,2048,128]{2,1,0:T(8,128)(2,1)} %shard_map.92), channel_id=1, source_target_pairs={{0,4},{1,5},{2,6},{3,7},{4,0},{5,1},{6,2},{7,3},{8,12},{9,13},{10,... | collective-permute-start | bytes 1572872 | tf_op jit(solution)/shard_map/ppermute | solution.py:272
  142.5 143.8 %collective-permute-start.8 = (bf16[1,2048,128]{2,1,0:T(8,128)(2,1)}, bf16[1,2048,128]{2,1,0:T(8,128)(2,1)}, u32[]{:S(2)}, u32[]{:S(2)}) collective-permute-start(bf16[1,2048,128]{2,1,0:T(8,128)(2,1)} %shard_map.93), channel_id=1, source_target_pairs={{0,5},{1,4},{2,7},{3,6},{4,1},{5,0},{6,3},{7,2},{8,13},{9,12},{10,... | collective-permute-start | bytes 1572872 | tf_op jit(solution)/shard_map/ppermute | solution.py:272
  174.5 1.3 copy-start
  176.7 134.7 %collective-permute-start.5 = (bf16[1,2048,128]{2,1,0:T(8,128)(2,1)}, bf16[1,2048,128]{2,1,0:T(8,128)(2,1)S(1)}, u32[]{:S(2)}, u32[]{:S(2)}) collective-permute-start(bf16[1,2048,128]{2,1,0:T(8,128)(2,1)} %shard_map.90), channel_id=1, source_target_pairs={{0,7},{1,6},{2,5},{3,4},{4,3},{5,2},{6,1},{7,0},{8,15},{9,14},{10,... | collective-permute-start | bytes 1572872 | tf_op jit(solution)/shard_map/ppermute | solution.py:272
  177.5 4.0 %copy-start.1 = (f32[4,128,1024]{2,1,0:T(8,128)S(1)}, f32[4,128,1024]{2,1,0:T(8,128)}, u32[]{:S(2)}) copy-start(f32[4,128,1024]{2,1,0:T(8,128)} %copy-done) | copy-start | bytes 6291460
  177.5 4.0 %copy-start.8 = (bf16[1,2048,128]{2,1,0:T(8,128)(2,1)S(1)}, bf16[1,2048,128]{2,1,0:T(8,128)(2,1)}, u32[]{:S(2)}) copy-start(bf16[1,2048,128]{2,1,0:T(8,128)(2,1)} %copy-done.7) | copy-start | bytes 1572868
  177.5 125.6 %collective-permute-start.6 = (bf16[1,2048,128]{2,1,0:T(8,128)(2,1)}, bf16[1,2048,128]{2,1,0:T(8,128)(2,1)}, u32[]{:S(2)}, u32[]{:S(2)}) collective-permute-start(bf16[1,2048,128]{2,1,0:T(8,128)(2,1)} %shard_map.91), channel_id=1, source_target_pairs={{0,6},{1,7},{2,4},{3,5},{4,2},{5,3},{6,0},{7,1},{8,14},{9,15},{10,... | collective-permute-start | bytes 1572872 | tf_op jit(solution)/shard_map/ppermute | solution.py:272
  209.9 91.3 %all-to-all-start.2 = ((bf16[4,128,1024]{2,1,0:T(8,128)(2,1)}), bf16[4,128,1024]{2,1,0:T(8,128)(2,1)}, u32[]{:S(2)}, u32[]{:S(2)}) async-start(bf16[4,128,1024]{2,1,0:T(8,128)(2,1)} %copy-done.6), calls=%async_computation.2 | async-start | bytes 2097152 | tf_op jit(solution)/shard_map/all_to_all | solution.py:295
  256.6 29.7 %copy-start.20 = (s32[4,9]{1,0:T(4,128)S(1)}, s32[4,9]{1,0:T(4,128)}, u32[]{:S(2)}) copy-start(s32[4,9]{1,0:T(4,128)} %shard_map.89.starts_ref) | copy-start | bytes 436
  301.2 32.3 %collective-permute-start.4 = (bf16[4,128,1024]{2,1,0:T(8,128)(2,1)}, bf16[4,128,1024]{2,1,0:T(8,128)(2,1)S(1)}, u32[]{:S(2)}, u32[]{:S(2)}) collective-permute-start(bf16[4,128,1024]{2,1,0:T(8,128)(2,1)} %all-to-all-done.2), channel_id=1, source_target_pairs={{0,24},{1,25},{2,26},{3,27},{4,28},{5,29},{6,30},{7,31},{8,0},{9,1... | collective-permute-start | bytes 3145736 | tf_op jit(solution)/shard_map/ppermute | solution.py:276
  315.7 33.2 %collective-permute-start.10 = (bf16[128,1024]{1,0:T(8,128)(2,1)S(1)}, bf16[128,1024]{1,0:T(8,128)(2,1)S(1)}, u32[]{:S(2)}, u32[]{:S(2)}) collective-permute-start(bf16[128,1024]{1,0:T(8,128)(2,1)S(1)} %bitcast.59), channel_id=1, source_target_pairs={{0,25},{1,24},{2,27},{3,26},{4,29},{5,28},{6,31},{7,30},{8,1},{9,0... | collective-permute-start | bytes 786440 | tf_op jit(solution)/shard_map/ppermute | solution.py:276
  319.8 29.1 %collective-permute-start.9 = (bf16[128,1024]{1,0:T(8,128)(2,1)S(1)}, bf16[128,1024]{1,0:T(8,128)(2,1)S(1)}, u32[]{:S(2)}, u32[]{:S(2)}) collective-permute-start(bf16[128,1024]{1,0:T(8,128)(2,1)S(1)} %bitcast.62), channel_id=1, source_target_pairs={{0,24},{1,25},{2,26},{3,27},{4,28},{5,29},{6,30},{7,31},{8,0},{9,1... | collective-permute-start | bytes 786440 | tf_op jit(solution)/shard_map/ppermute | solution.py:276
  324.2 24.8 %collective-permute-start.11 = (bf16[128,1024]{1,0:T(8,128)(2,1)S(1)}, bf16[128,1024]{1,0:T(8,128)(2,1)S(1)}, u32[]{:S(2)}, u32[]{:S(2)}) collective-permute-start(bf16[128,1024]{1,0:T(8,128)(2,1)S(1)} %bitcast.61), channel_id=1, source_target_pairs={{0,26},{1,27},{2,24},{3,25},{4,30},{5,31},{6,28},{7,29},{8,2},{9,3... | collective-permute-start | bytes 786440 | tf_op jit(solution)/shard_map/ppermute | solution.py:276
  333.0 16.1 %collective-permute-start.12 = (bf16[128,1024]{1,0:T(8,128)(2,1)S(1)}, bf16[128,1024]{1,0:T(8,128)(2,1)S(1)}, u32[]{:S(2)}, u32[]{:S(2)}) collective-permute-start(bf16[128,1024]{1,0:T(8,128)(2,1)S(1)} %bitcast.60), channel_id=1, source_target_pairs={{0,27},{1,26},{2,25},{3,24},{4,31},{5,30},{6,29},{7,28},{8,3},{9,2... | collective-permute-start | bytes 786440 | tf_op jit(solution)/shard_map/ppermute | solution.py:276
  (16 other events, 13.8 us)

commit v4 on v3

v4 whole, which is shorter than its diff:
```python
import functools
import math

import jax
import jax.numpy as jnp
from jax import lax
from jax.experimental import pallas as pl
from jax.experimental.pallas import tpu as pltpu
from jax.sharding import PartitionSpec as P

BLOCK = 128
PARTS = 3
STEP = 4
HINT = 16
VMEM_LIMIT = 48 * 1024 * 1024

NT = (((1,), (1,)), ((), ()))


def split_parts(value):
    terms = []
    for _ in range(PARTS):
        term = value.astype(jnp.bfloat16)
        terms.append(term.astype(jnp.float32))
        value = value - terms[-1]
    return terms


def pack_kernel(own, group, by_distance, at_ref, keys_ref, values_ref, *outs):
    rows = keys_ref.shape[0]
    dim = outs[0].shape[2]
    for x in range(group):
        for index in range(own):
            device = at_ref[0] ^ x if by_distance else x
            column = pl.multiple_of((device * own + index) * dim, dim)
            out, slot = (outs[index * group + x], 0) if by_distance else (outs[index], x)
            out[slot, :rows, :] = keys_ref[:, pl.ds(column, dim)]
            out[slot, rows:, :] = values_ref[:, pl.ds(column, dim)]


def pack(mem_keys, mem_values, at, own, group, dim, by_distance):
    mem_dev, width = mem_keys.shape
    count, slots = (own * group, 1) if by_distance else (own, group)
    whole = pl.BlockSpec((mem_dev, width), lambda i, _: (0, 0))
    return pl.pallas_call(
        functools.partial(pack_kernel, own, group, by_distance),
        out_shape=[jax.ShapeDtypeStruct((slots, 2 * mem_dev, dim), mem_keys.dtype)] * count,
        grid_spec=pltpu.PrefetchScalarGridSpec(
            num_scalar_prefetch=1,
            grid=(1,),
            in_specs=[whole, whole],
            out_specs=[pl.BlockSpec((slots, 2 * mem_dev, dim), lambda i, _: (0, 0, 0))] * count,
        ),
        compiler_params=pltpu.CompilerParams(vmem_limit_bytes=VMEM_LIMIT),
        cost_estimate=pl.CostEstimate(flops=0, bytes_accessed=8 * mem_dev * width, transcendentals=0),
    )(at, mem_keys, mem_values)


def prepare_kernel(heads, dim, scale, own, index, gate_ref, grad_ref, query_ref, out_ref, total_ref, packed_ref):
    rows = grad_ref.shape[0]
    head = pl.program_id(0) * own + index
    count = total_ref.shape[1]
    logs = split_parts(jnp.log2(total_ref[...].astype(jnp.float32)) - math.log2(scale))
    source = lax.broadcasted_iota(jnp.int32, (count, dim), 0) - head * heads
    target = lax.broadcasted_iota(jnp.int32, (count, dim), 1)
    lane = lax.broadcasted_iota(jnp.int32, (rows, dim), 1)
    mine = (source >= 0) & (source < heads)
    stats = jnp.zeros((rows, dim), jnp.float32)
    for part, term in enumerate(logs):
        chosen = jnp.where(mine & (target == source + (2 * part + 1) * heads), 1.0, 0.0).astype(jnp.bfloat16)
        stats += jnp.dot(term.astype(jnp.bfloat16), chosen, preferred_element_type=jnp.float32)
    for h in range(heads):
        columns = slice(h * dim, (h + 1) * dim)
        gated = (gate_ref[head * heads + h] * grad_ref[:, columns].astype(jnp.float32)).astype(jnp.bfloat16)
        packed_ref[0, h * rows:(h + 1) * rows, :] = query_ref[:, columns]
        packed_ref[0, (heads + h) * rows:(heads + h + 1) * rows, :] = gated
        product = gated.astype(jnp.float32) * out_ref[:, columns].astype(jnp.float32)
        delta = jnp.sum(product, axis=1, keepdims=True)
        for part, term in enumerate(split_parts(delta)):
            stats = jnp.where(lane == 2 * part * heads + h, term, stats)
    packed_ref[0, 2 * heads * rows:, :] = stats.astype(jnp.bfloat16)


def prepare(grad_out, queries, mem_out, row_total, gates, kv_heads, dim, scale, own, index):
    rows, width = grad_out.shape
    heads = width // dim // kv_heads
    group = kv_heads // own
    span = 2 * heads * rows + rows
    wide = pl.BlockSpec((rows, heads * dim), lambda k, _: (0, k * own + index))
    return pl.pallas_call(
        functools.partial(prepare_kernel, heads, dim, scale, own, index),
        out_shape=jax.ShapeDtypeStruct((group, span, dim), jnp.bfloat16),
        grid_spec=pltpu.PrefetchScalarGridSpec(
            num_scalar_prefetch=1,
            grid=(group,),
            in_specs=[wide, wide, wide, pl.BlockSpec(row_total.shape, lambda k, _: (0, 0))],
            out_specs=pl.BlockSpec((1, span, dim), lambda k, _: (k, 0, 0)),
        ),
        compiler_params=pltpu.CompilerParams(vmem_limit_bytes=VMEM_LIMIT),
        cost_estimate=pl.CostEstimate(
            flops=rows * width * (4 if index == 0 else 1 << 17), bytes_accessed=rows * width * 12 // own, transcendentals=0
        ),
    )(gates, grad_out, queries, mem_out, row_total)


def attend_kernel(heads, dim, rows, mem_dev, scale, fresh, last, places, local, where_ref, picks_ref, starts_ref, *refs):
    query_ref, stat_ref = refs[:2]
    memory_refs, acc_in = (refs[2:-6], None) if fresh else (refs[2:-7], refs[-7])
    out_ref, keys_ref, values_ref, log_ref, delta_ref, total = refs[-6:]
    step = pl.program_id(0)
    tile = where_ref[0] + step
    blocks = mem_dev // BLOCK
    count = heads * rows

    @pl.when(step == 0)
    def _():
        at = 0
        for number, memory in enumerate(memory_refs):
            for piece in range(memory.shape[0]):
                here = slice(at * mem_dev, (at + 1) * mem_dev)

                def fill(memory=memory, piece=piece, here=here):
                    keys_ref[here, :] = memory[piece, :mem_dev, :]
                    values_ref[here, :] = memory[piece, mem_dev:, :]

                if number == local:
                    pl.when(where_ref[1] != piece)(fill)
                else:
                    fill()
                at += 1

    if fresh:
        total[...] = jnp.zeros_like(total)
    else:
        total[...] = acc_in[0]

    stats = stat_ref[0].astype(jnp.float32)
    for h in range(heads):
        for target, first in ((delta_ref, h), (log_ref, heads + h)):
            terms = [stats[:, first + 2 * part * heads:first + 2 * part * heads + 1] for part in range(PARTS)]
            target[h * rows:(h + 1) * rows, :] = jnp.broadcast_to(terms[0] + terms[1] + terms[2], (rows, dim))

    low = starts_ref[tile, places[0]]
    high = starts_ref[tile, places[1]]
    offset = places[0] * blocks
    exponent = scale * math.log2(math.e)

    def add(here, number, checked):
        sides = []
        for two in range(0, number, 2):
            keys, values = [], []
            for j in (two, two + 1):
                valid = here + j < high
                block = picks_ref[tile, jnp.where(valid, here + j, here) if checked else here + j] - offset
                row = pl.ds(pl.multiple_of(block * BLOCK, BLOCK), BLOCK)
                key = keys_ref[row, :]
                keys.append(jnp.where(valid, key, jnp.zeros_like(key)) if checked and j else key)
                values.append(values_ref[row, :])
            sides.append((jnp.concatenate(keys, axis=0), jnp.concatenate(values, axis=0)))

        def products(side):
            keys, values = side
            scores = lax.dot_general(query_ref[0, :count, :], keys, NT, preferred_element_type=jnp.float32)
            grad_probs = lax.dot_general(query_ref[0, count:, :], values, NT, preferred_element_type=jnp.float32)
            return scores, grad_probs

        ahead = products(sides[0])
        gained = None
        for at, (keys, _) in enumerate(sides):
            scores, grad_probs = ahead
            if at + 1 < len(sides):
                ahead = products(sides[at + 1])
            log_wide = jnp.concatenate([log_ref[...]] * 2, axis=1)
            delta_wide = jnp.concatenate([delta_ref[...]] * 2, axis=1)
            probs = jnp.exp2(scores * exponent - log_wide)
            grad_scores = (probs * (grad_probs - delta_wide)).astype(jnp.bfloat16)
            part = jnp.dot(grad_scores, keys, preferred_element_type=jnp.float32)
            gained = part if gained is None else gained + part
        total[...] += gained

    full = (high - low) // STEP

    def many(turn, carry):
        add(low + STEP * turn, STEP, False)
        return carry

    def few(turn, carry):
        add(low + STEP * full + 2 * turn, 2, True)
        return carry

    lax.fori_loop(0, full, many, 0)
    lax.fori_loop(0, (high - low - STEP * full + 1) // 2, few, 0)

    if last:
        for h in range(heads):
            out_ref[0, :, h * dim:(h + 1) * dim] = total[h * rows:(h + 1) * rows, :].astype(jnp.bfloat16)
    else:
        out_ref[0] = total[...]


def attend(packed, memories, places, acc, at, picks, starts, heads, dim, mem_dev, scale, last, local=None, only=None):
    tiles, span, _ = packed.shape
    rows = span // (2 * heads + 1)
    fresh = acc is None
    count = places[1] - places[0]
    width = heads * rows
    steps = tiles if only is None else 1
    acc_spec = pl.BlockSpec((1, width, dim), lambda t, o, *_: (o[0] + t, 0, 0))
    if last:
        out_shape = jax.ShapeDtypeStruct((steps, rows, heads * dim), jnp.bfloat16)
        out_spec = pl.BlockSpec((1, rows, heads * dim), lambda t, *_: (t, 0, 0))
    else:
        out_shape = jax.ShapeDtypeStruct((tiles, width, dim), jnp.float32)
        out_spec = acc_spec
    flops = steps * count * (mem_dev // 2) * width * dim * 6
    where = jnp.stack([jnp.zeros((), jnp.int32) if only is None else only, at]).astype(jnp.int32)
    return pl.pallas_call(
        functools.partial(attend_kernel, heads, dim, rows, mem_dev, scale, fresh, last, places, local),
        out_shape=out_shape,
        grid_spec=pltpu.PrefetchScalarGridSpec(
            num_scalar_prefetch=3,
            grid=(steps,),
            in_specs=[
                pl.BlockSpec((1, 2 * width, dim), lambda t, o, *_: (o[0] + t, 0, 0)),
                pl.BlockSpec((1, rows, dim), lambda t, o, *_: (o[0] + t, 2 * heads, 0)),
            ]
            + [pl.BlockSpec(m.shape, lambda t, *_: (0, 0, 0)) for m in memories]
            + ([] if fresh else [acc_spec]),
            out_specs=out_spec,
            scratch_shapes=[
                pltpu.VMEM((count * mem_dev, dim), jnp.bfloat16),
                pltpu.VMEM((count * mem_dev, dim), jnp.bfloat16),
                pltpu.VMEM((width, dim), jnp.float32),
                pltpu.VMEM((width, dim), jnp.float32),
                pltpu.VMEM((width, dim), jnp.float32),
            ],
        ),
        compiler_params=pltpu.CompilerParams(vmem_limit_bytes=VMEM_LIMIT),
        cost_estimate=pl.CostEstimate(flops=flops * 4, bytes_accessed=0, transcendentals=0),
    )(where, picks, starts, packed, packed, *memories, *([] if fresh else [acc]))


def after(value, *others):
    anywhere = pl.BlockSpec(memory_space=pl.ANY)
    hints = [other[:1, :HINT] for other in others]
    return pl.pallas_call(
        lambda *refs: None,
        out_shape=jax.ShapeDtypeStruct(value.shape, value.dtype),
        in_specs=[anywhere] * (1 + len(hints)),
        out_specs=anywhere,
        input_output_aliases={0: 0},
        cost_estimate=pl.CostEstimate(flops=0, bytes_accessed=0, transcendentals=0),
    )(value, *hints)


def shards(grad_out, queries, mem_out, row_total, gate_logit, mem_keys, mem_values, retrieved):
    seq = lax.axis_size("seq")
    sections = lax.axis_size("section")
    position = lax.axis_index("seq")
    rows, width = grad_out.shape[1:]
    head_count = gate_logit.shape[1]
    dim = width // head_count
    kv_heads = mem_keys.shape[2] // dim
    heads = head_count // kv_heads
    mem_dev = mem_keys.shape[1]
    blocks = mem_dev // BLOCK
    group = min(kv_heads, seq // 2)
    own = kv_heads // group
    at = position % group
    home = position // group
    scale = dim ** (-0.5)
    groups = [list(range(g * group, (g + 1) * group)) for g in range(seq // group)]

    def swapped(value, step):
        return lax.ppermute(value, "seq", [(p, p ^ step) for p in range(seq)])

    def delivered(value, step):
        pairs = [(s * seq + p, ((s - 1) % sections) * seq + (p ^ step)) for s in range(sections) for p in range(seq)]
        return lax.ppermute(value, ("section", "seq"), pairs)

    def shared(value):
        return lax.all_to_all(value, "seq", split_axis=0, concat_axis=0, axis_index_groups=groups, tiled=True)

    half = group + (seq - group) // 2
    near = 1 + half - group
    far = near + group
    end = far + seq - half
    mine = lax.dynamic_slice_in_dim(retrieved[0], at * own, own, 0)
    mine = lax.dynamic_slice_in_dim(mine, home * group, group, 1)
    holder = mine // blocks
    distance = holder ^ position
    place = jnp.where(
        holder == position, 0,
        jnp.where(
            holder // group == home, near + holder % group,
            jnp.where(distance < half, 1 + distance - group, far + distance - half),
        ),
    )
    block = place * blocks + mine % blocks
    rank = jnp.sum(block[..., None, :] < block[..., :, None], axis=-1)
    order = jnp.arange(block.shape[-1])
    picks = jnp.sum(jnp.where(rank[..., :, None] == order, block[..., :, None], 0), axis=-2).astype(jnp.int32)
    starts = jnp.sum(block[..., None, :] < (jnp.arange(end + 1) * blocks)[:, None], axis=-1).astype(jnp.int32)

    keys, values = mem_keys[0], mem_values[0]
    sends = list(pack(keys, values, at[None], own, group, dim, True))
    gates = jax.nn.sigmoid(gate_logit[0])

    def ready(i, *first):
        return prepare(
            grad_out[0], queries[0], mem_out[0], row_total[0], after(gates, *first), kv_heads, dim, scale, own, i
        )

    packed = shared(ready(0, sends[0]))
    locals_of = list(pack(keys, values, after(at[None], sends[0]), own, group, dim, False))
    nearby = shared(after(locals_of[0], packed))
    out = jnp.zeros((rows, width), jnp.bfloat16)
    arrived, finished, done = {}, [], None
    for i in range(own):
        ending = i == own - 1
        for step in range(group, seq):
            piece = sends[i * group + step % group]
            ahead = step - (half - group) if step >= half else step + (half - group)
            if ahead in arrived:
                piece = after(piece, arrived[ahead])
            arrived[step] = swapped(piece, step)
        first = [arrived[step] for step in range(group, half)]
        second = [arrived[step] for step in range(half, seq)]
        run = functools.partial(
            attend, packed, at=at, picks=picks[i], heads=heads, dim=dim, mem_dev=mem_dev, scale=scale
        )
        where = starts[i]
        if not ending:
            coming = ready(i + 1, *first)
            where = after(where, coming)
        if i:
            where = after(where, done)
        acc = run([sends[i * group]] + first, (0, near), None, starts=where, last=False)
        if not ending:
            done = run([nearby] + second, (near, end), acc, starts=where, last=True, local=0)
            finished.append(delivered(done, 0))
            packed = shared(after(coming, nearby))
            nearby = shared(after(locals_of[i + 1], packed))
            continue
        acc = run([nearby], (near, far), acc, starts=where, last=False, local=0)
        for j, result in enumerate(finished):
            result = shared(after(result, nearby))
            for t in range(group):
                out = lax.dynamic_update_slice_in_dim(out, result[t], (t * own + j) * heads * dim, 1)
        for x in range(group):
            piece = run(second, (far, end), acc, starts=where, last=True, only=at ^ x)
            piece = delivered(piece[0], x)
            out = lax.dynamic_update_slice_in_dim(out, piece, ((at ^ x) * own + i) * heads * dim, 1)
    return out[None]


def solution(mesh):
    return jax.shard_map(
        shards,
        mesh=mesh,
        in_specs=(
            P("section", "seq", None),
            P("section", "seq", None),
            P("section", "seq", None),
            P("section", "seq", None),
            P("section", None),
            P("section", "seq", None),
            P("section", "seq", None),
            P("section", None, None, None),
        ),
        out_specs=P("section", "seq", None),
        check_vma=False,
    )
```

time: 358 us -> 356 us (level)
  waiting for transfers between devices: 106 us -> 153 us
  starting transfers between devices: 80.7 us -> 37.1 us
  Pallas kernels: 139 us -> 116 us
  local copies, waits for them, and re-layouts: 22.3 us -> 43.7 us
    ppermute x8, waiting for transfers between devices: 48.2 us -> 128 us  [swapped(): return lax.ppermute(value, 'seq', [(p, p ^ step) for p in range(seq)])]
    all_to_all x3 -> x5, starting transfers between devices: 56 us -> 21.7 us  [shared(): lax.all_to_all(value, 'seq', split_axis=0, concat_axis=0, axis_index_grou...]
    all_to_all x3 -> x5, waiting for transfers between devices: 42.1 us -> 15.6 us  [shared(): lax.all_to_all(value, 'seq', split_axis=0, concat_axis=0, axis_index_grou...]
    pallas_call x9 -> x8, Pallas kernels: 122 us -> 98.2 us  [attend(): pl.pallas_call(functools.partial(attend_kernel, heads, dim, rows, mem_dev...]
    slice x0 -> x13, local copies, waits for them, and re-layouts: none -> 14 us  [after(): hints = [other[:1, :HINT] for other in others]]
    ppermute x8, starting transfers between devices: 17.5 us -> 10.1 us  [swapped(): return lax.ppermute(value, 'seq', [(p, p ^ step) for p in range(seq)])]
    unnamed x48 -> x58, local copies, waits for them, and re-layouts: 19.9 us -> 26.4 us
    ppermute x5, waiting for transfers between devices: 15.2 us -> 9.98 us  [delivered(): return lax.ppermute(value, ('section', 'seq'), pairs)]
  transfers between devices with their start and end apart: 16 -> 18, of which waited for: 4 -> 10; matrix products, arithmetic and copies ran while one was open for 1% -> 6% of each run, Pallas kernels for 38% -> 30%
where the time goes in v4:
time: 356 us; the launch traced here: 353 us
  waiting for transfers between devices  153 us (43%)
  Pallas kernels  116 us (33%)
  local copies, waits for them, and re-layouts  43.7 us (12%)
  starting transfers between devices  37.1 us (10%)
    ppermute x8, waiting for transfers between devices, swapped(): return lax.ppermute(value, 'seq', [(p, p ^ step) for p in range(seq)])  128 us
    pallas_call x8, Pallas kernels, attend(): pl.pallas_call(functools.partial(attend_kernel, heads, dim, rows, mem_dev...  98.2 us
    unnamed x58, local copies, waits for them, and re-layouts  26.4 us
    all_to_all x5, starting transfers between devices, shared(): lax.all_to_all(value, 'seq', split_axis=0, concat_axis=0, axis_index_grou...  21.7 us
    all_to_all x5, waiting for transfers between devices, shared(): lax.all_to_all(value, 'seq', split_axis=0, concat_axis=0, axis_index_grou...  15.6 us
    slice x13, local copies, waits for them, and re-layouts, after(): hints = [other[:1, :HINT] for other in others]  14 us
    ppermute x8, starting transfers between devices, swapped(): return lax.ppermute(value, 'seq', [(p, p ^ step) for p in range(seq)])  10.1 us
    ppermute x5, waiting for transfers between devices, delivered(): return lax.ppermute(value, ('section', 'seq'), pairs)  9.98 us
  transfers between devices with their start and end apart: 18, of which 10 were waited for; matrix products, arithmetic and copies ran while one was open for 6% of the time, Pallas kernels for 30%

profile of v4, /device:TPU:0, one launch (start us, length us, event | category | flops | bytes accessed | tf_op | source)
XLA Modules:
  0.0 352.7 jit_solution(937009227528477037)
XLA Ops:
  13.3 4.9 %shard_map.87 = bf16[4,2176,128]{2,1,0:T(8,128)(2,1)} custom-call(f32[64]{0:T(128)S(1)} %copy-done.20, bf16[128,8192]{1,0:T(8,128)(2,1)S(1)} %bitcast.52, bf16[128,8192]{1,0:T(8,128)(2,1)S(1)} %bitcast.54, bf16[128,8192]{1,0:T(8,128)(2,1)} %bitcast.68, bf16[128,64]{1,0:T(8,128)(2,1)S(1)} %bitcast.56), custom_call_target="tpu_custom_call" | custom-call | flops 4194304 | bytes 6291456 | tf_op jit(solution)/shard_map/pallas_call | solution.py:90
  18.1 4.3 %all-to-all-start = ((bf16[4,2176,128]{2,1,0:T(8,128)(2,1)}), bf16[4,2176,128]{2,1,0:T(8,128)(2,1)S(1)}, u32[]{:S(2)}, u32[]{:S(2)}) async-start(bf16[4,2176,128]{2,1,0:T(8,128)(2,1)} %shard_map.87), calls=%async_computation | async-start | bytes 4456448 | tf_op jit(solution)/shard_map/all_to_all | solution.py:282
  26.7 3.8 %shard_map.89 = (bf16[4,2048,128]{2,1,0:T(8,128)(2,1)S(1)}, bf16[4,2048,128]{2,1,0:T(8,128)(2,1)S(1)}) custom-call(s32[1]{0:T(128)} %shard_map.88.at_ref, bf16[1024,1024]{1,0:T(8,128)(2,1)} %bitcast.65, bf16[1024,1024]{1,0:T(8,128)(2,1)} %bitcast.67), custom_call_target="tpu_custom_call" | custom-call | bytes 8388608 | tf_op jit(solution)/shard_map/pallas_call | solution.py:45
  33.2 25.7 %collective-permute-done.refs_3_ = bf16[1,2048,128]{2,1,0:T(8,128)(2,1)} collective-permute-done((bf16[1,2048,128]{2,1,0:T(8,128)(2,1)S(1)}, bf16[1,2048,128]{2,1,0:T(8,128)(2,1)}, u32[]{:S(2)}, u32[]{:S(2)}) %collective-permute-start) | collective-permute-done | bytes 524320 | tf_op jit(solution)/shard_map/ppermute | solution.py:275
  60.1 9.9 %collective-permute-done.1.refs_4_ = bf16[1,2048,128]{2,1,0:T(8,128)(2,1)} collective-permute-done((bf16[1,2048,128]{2,1,0:T(8,128)(2,1)}, bf16[1,2048,128]{2,1,0:T(8,128)(2,1)}, u32[]{:S(2)}, u32[]{:S(2)}) %collective-permute-start.1) | collective-permute-done | bytes 524320 | tf_op jit(solution)/shard_map/ppermute | solution.py:275
  73.4 5.6 %all-to-all-start.1 = ((bf16[4,2048,128]{2,1,0:T(8,128)(2,1)}), bf16[4,2048,128]{2,1,0:T(8,128)(2,1)S(1)}, u32[]{:S(2)}, u32[]{:S(2)}) async-start(bf16[4,2048,128]{2,1,0:T(8,128)(2,1)} %shard_map.90), calls=%async_computation.1 | async-start | bytes 4194304 | tf_op jit(solution)/shard_map/all_to_all | solution.py:282
  82.2 4.9 %shard_map.84 = bf16[4,2176,128]{2,1,0:T(8,128)(2,1)} custom-call(f32[64]{0:T(128)S(1)} %copy-done.22, bf16[128,8192]{1,0:T(8,128)(2,1)S(1)} %bitcast.53, bf16[128,8192]{1,0:T(8,128)(2,1)S(1)} %bitcast.55, bf16[128,8192]{1,0:T(8,128)(2,1)} %bitcast.69, bf16[128,64]{1,0:T(8,128)(2,1)S(1)} %bitcast.57), custom_call_target="tpu_custom_call" | custom-call | flops 137438953472 | bytes 6291456 | tf_op jit(solution)/shard_map/pallas_call | solution.py:90
  90.3 14.9 %all-to-all-done.1.refs_2_ = bf16[4,2048,128]{2,1,0:T(8,128)(2,1)S(1)} async-done(((bf16[4,2048,128]{2,1,0:T(8,128)(2,1)}), bf16[4,2048,128]{2,1,0:T(8,128)(2,1)S(1)}, u32[]{:S(2)}, u32[]{:S(2)}) %all-to-all-start.1) | async-done | bytes 2097184 | tf_op jit(solution)/shard_map/all_to_all | solution.py:282
  115.8 33.7 %collective-permute-done.2.refs_3_ = bf16[1,2048,128]{2,1,0:T(8,128)(2,1)} collective-permute-done((bf16[1,2048,128]{2,1,0:T(8,128)(2,1)}, bf16[1,2048,128]{2,1,0:T(8,128)(2,1)}, u32[]{:S(2)}, u32[]{:S(2)}) %collective-permute-start.2) | collective-permute-done | bytes 524320 | tf_op jit(solution)/shard_map/ppermute | solution.py:275
  150.8 9.1 %collective-permute-done.3.refs_4_ = bf16[1,2048,128]{2,1,0:T(8,128)(2,1)} collective-permute-done((bf16[1,2048,128]{2,1,0:T(8,128)(2,1)}, bf16[1,2048,128]{2,1,0:T(8,128)(2,1)}, u32[]{:S(2)}, u32[]{:S(2)}) %collective-permute-start.3) | collective-permute-done | bytes 524320 | tf_op jit(solution)/shard_map/ppermute | solution.py:275
  164.3 29.8 %collective-permute-done.5.refs_3_ = bf16[1,2048,128]{2,1,0:T(8,128)(2,1)} collective-permute-done((bf16[1,2048,128]{2,1,0:T(8,128)(2,1)}, bf16[1,2048,128]{2,1,0:T(8,128)(2,1)}, u32[]{:S(2)}, u32[]{:S(2)}) %collective-permute-start.5) | collective-permute-done | bytes 524320 | tf_op jit(solution)/shard_map/ppermute | solution.py:275
  197.0 19.4 %collective-permute-done.7.refs_4_ = bf16[1,2048,128]{2,1,0:T(8,128)(2,1)} collective-permute-done((bf16[1,2048,128]{2,1,0:T(8,128)(2,1)}, bf16[1,2048,128]{2,1,0:T(8,128)(2,1)}, u32[]{:S(2)}, u32[]{:S(2)}) %collective-permute-start.7) | collective-permute-done | bytes 524320 | tf_op jit(solution)/shard_map/ppermute | solution.py:275
  220.6 17.0 %shard_map.93.refs_5_ = f32[4,1024,128]{2,1,0:T(8,128)S(1)} custom-call(s32[2]{0:T(128)S(1)} %pad_add_fusion.where_ref, s32[4,32]{1,0:T(4,128)S(1)} %get-tuple-element.28.picks_ref, s32[4,10]{1,0:T(4,128)S(1)} %copy-done.19, bf16[4,2176,128]{2,1,0:T(8,128)(2,1)S(1)} %copy-done.5, bf16[4,2176,128]{2,1,0:T(8,128)(2,1)S(1)} %copy-done.5, ...), custom_call_target="tpu_custom_call" | custom-call | flops 19327352832 | tf_op jit(solution)/shard_map/pallas_call | solution.py:217
  239.6 4.5 %all-to-all-start.3 = ((bf16[4,2048,128]{2,1,0:T(8,128)(2,1)}), bf16[4,2048,128]{2,1,0:T(8,128)(2,1)}, u32[]{:S(2)}, u32[]{:S(2)}) async-start(bf16[4,2048,128]{2,1,0:T(8,128)(2,1)} %shard_map.96), calls=%async_computation.3 | async-start | bytes 4194304 | tf_op jit(solution)/shard_map/all_to_all | solution.py:282
  245.7 27.5 %shard_map.94 = bf16[4,128,1024]{2,1,0:T(8,128)(2,1)} custom-call(s32[2]{0:T(128)S(1)} %pad_add_fusion.where_ref, s32[4,32]{1,0:T(4,128)S(1)} %get-tuple-element.28.picks_ref, s32[4,10]{1,0:T(4,128)S(1)} %copy-done.19, bf16[4,2176,128]{2,1,0:T(8,128)(2,1)} %copy-done.4, bf16[4,2176,128]{2,1,0:T(8,128)(2,1)} %copy-done.4, ...), custom_call_target="tpu_custom_call" | custom-call | flops 38654705664 | tf_op jit(solution)/shard_map/pallas_call | solution.py:217
  277.7 13.6 %shard_map.103.refs_3_ = f32[4,1024,128]{2,1,0:T(8,128)S(1)} custom-call(s32[2]{0:T(128)S(1)} %pad_add_fusion.where_ref, s32[4,32]{1,0:T(4,128)S(1)} %get-tuple-element.27.picks_ref, s32[4,10]{1,0:T(4,128)S(1)} %copy-done.17, bf16[4,2176,128]{2,1,0:T(8,128)(2,1)S(1)} %all-to-all-done.2.refs_0_.refs_1_, ...), custom_call_target="tpu_custom_call" | custom-call | flops 19327352832 | tf_op jit(solution)/shard_map/pallas_call | solution.py:217
  293.9 4.9 %collective-permute-done.4.refs_0_ = bf16[4,128,1024]{2,1,0:T(8,128)(2,1)} collective-permute-done((bf16[4,128,1024]{2,1,0:T(8,128)(2,1)}, bf16[4,128,1024]{2,1,0:T(8,128)(2,1)}, u32[]{:S(2)}, u32[]{:S(2)}) %collective-permute-start.4) | collective-permute-done | bytes 1048608 | tf_op jit(solution)/shard_map/ppermute | solution.py:279
  298.8 3.7 %all-to-all-start.4 = ((bf16[4,128,1024]{2,1,0:T(8,128)(2,1)}), bf16[4,128,1024]{2,1,0:T(8,128)(2,1)S(1)}, u32[]{:S(2)}, u32[]{:S(2)}) async-start(bf16[4,128,1024]{2,1,0:T(8,128)(2,1)} %shard_map.97), calls=%async_computation.4 | async-start | bytes 2097152 | tf_op jit(solution)/shard_map/all_to_all | solution.py:282
  302.5 18.5 %shard_map.104.refs_4_ = f32[4,1024,128]{2,1,0:T(8,128)S(1)} custom-call(s32[2]{0:T(128)S(1)} %pad_add_fusion.where_ref, s32[4,32]{1,0:T(4,128)S(1)} %get-tuple-element.27.picks_ref, s32[4,10]{1,0:T(4,128)S(1)} %copy-done.18, bf16[4,2176,128]{2,1,0:T(8,128)(2,1)} %copy-done.2, bf16[4,2176,128]{2,1,0:T(8,128)(2,1)} %copy-done.2, ...), custom_call_target="tpu_custom_call" | custom-call | flops 25769803776 | tf_op jit(solution)/shard_map/pallas_call | solution.py:217
  321.1 5.4 %shard_map.105 = bf16[1,128,1024]{2,1,0:T(8,128)(2,1)S(1)} custom-call(s32[2]{0:T(128)S(1)} %get-tuple-element.29.where_ref, s32[4,32]{1,0:T(4,128)S(1)} %get-tuple-element.27.picks_ref, s32[4,10]{1,0:T(4,128)S(1)} %copy-done.18, bf16[4,2176,128]{2,1,0:T(8,128)(2,1)S(1)} %copy-done.3, bf16[4,2176,128]{2,1,0:T(8,128)(2,1)S(1)} %copy-done.3, ...), custom_call_target="tpu_custom_call" | custom-call | flops 3221225472 | tf_op jit(solution)/shard_map/pallas_call | solution.py:217
  326.8 5.3 %shard_map.106 = bf16[1,128,1024]{2,1,0:T(8,128)(2,1)S(1)} custom-call(s32[2]{0:T(128)S(1)} %get-tuple-element.30.where_ref, s32[4,32]{1,0:T(4,128)S(1)} %get-tuple-element.27.picks_ref, s32[4,10]{1,0:T(4,128)S(1)} %copy-done.18, bf16[4,2176,128]{2,1,0:T(8,128)(2,1)S(1)} %copy-done.3, bf16[4,2176,128]{2,1,0:T(8,128)(2,1)S(1)} %copy-done.3, ...), custom_call_target="tpu_custom_call" | custom-call | flops 3221225472 | tf_op jit(solution)/shard_map/pallas_call | solution.py:217
  333.1 5.8 %shard_map.107 = bf16[1,128,1024]{2,1,0:T(8,128)(2,1)S(1)} custom-call(s32[2]{0:T(128)S(1)} %get-tuple-element.31.where_ref, s32[4,32]{1,0:T(4,128)S(1)} %get-tuple-element.27.picks_ref, s32[4,10]{1,0:T(4,128)S(1)} %copy-done.18, bf16[4,2176,128]{2,1,0:T(8,128)(2,1)S(1)} %copy-done.3, bf16[4,2176,128]{2,1,0:T(8,128)(2,1)S(1)} %copy-done.3, ...), custom_call_target="tpu_custom_call" | custom-call | flops 3221225472 | tf_op jit(solution)/shard_map/pallas_call | solution.py:217
  338.9 5.1 %shard_map.108 = bf16[1,128,1024]{2,1,0:T(8,128)(2,1)S(1)} custom-call(s32[2]{0:T(128)S(1)} %get-tuple-element.32.where_ref, s32[4,32]{1,0:T(4,128)S(1)} %get-tuple-element.27.picks_ref, s32[4,10]{1,0:T(4,128)S(1)} %copy-done.18, bf16[4,2176,128]{2,1,0:T(8,128)(2,1)S(1)} %copy-done.3, bf16[4,2176,128]{2,1,0:T(8,128)(2,1)S(1)} %copy-done.3, ...), custom_call_target="tpu_custom_call" | custom-call | flops 3221225472 | tf_op jit(solution)/shard_map/pallas_call | solution.py:217
  346.9 5.1 %collective-permute-done.12 = bf16[128,1024]{1,0:T(8,128)(2,1)S(1)} collective-permute-done((bf16[128,1024]{1,0:T(8,128)(2,1)S(1)}, bf16[128,1024]{1,0:T(8,128)(2,1)S(1)}, u32[]{:S(2)}, u32[]{:S(2)}) %collective-permute-start.12) | collective-permute-done | bytes 262176 | tf_op jit(solution)/shard_map/ppermute | solution.py:279
  (132 shorter events, 70.0 us)
Async XLA Ops:
  2.1 8.9 %copy-start.8 = (bf16[1,128,8192]{2,1,0:T(8,128)(2,1)S(1)}, bf16[1,128,8192]{2,1,0:T(8,128)(2,1)}, u32[]{:S(2)}) copy-start(bf16[1,128,8192]{2,1,0:T(8,128)(2,1)} %param.8) | copy-start | bytes 6291460
  18.1 53.9 %all-to-all-start = ((bf16[4,2176,128]{2,1,0:T(8,128)(2,1)}), bf16[4,2176,128]{2,1,0:T(8,128)(2,1)S(1)}, u32[]{:S(2)}, u32[]{:S(2)}) async-start(bf16[4,2176,128]{2,1,0:T(8,128)(2,1)} %shard_map.87), calls=%async_computation | async-start | bytes 4456448 | tf_op jit(solution)/shard_map/all_to_all | solution.py:282
  22.4 36.4 %collective-permute-start = (bf16[1,2048,128]{2,1,0:T(8,128)(2,1)S(1)}, bf16[1,2048,128]{2,1,0:T(8,128)(2,1)}, u32[]{:S(2)}, u32[]{:S(2)}) collective-permute-start(bf16[1,2048,128]{2,1,0:T(8,128)(2,1)S(1)} %get-tuple-element.15.refs_2_), channel_id=1, source_target_pairs={{0,4},{1,5},{2,6},{3,7},{4,0},{5,1},{6,2},{7,3},{8,12},{9,13},{10,... | collective-permute-start | bytes 1572872 | tf_op jit(solution)/shard_map/ppermute | solution.py:275
  25.9 44.2 %collective-permute-start.1 = (bf16[1,2048,128]{2,1,0:T(8,128)(2,1)}, bf16[1,2048,128]{2,1,0:T(8,128)(2,1)}, u32[]{:S(2)}, u32[]{:S(2)}) collective-permute-start(bf16[1,2048,128]{2,1,0:T(8,128)(2,1)} %copy-done.23), channel_id=1, source_target_pairs={{0,5},{1,4},{2,7},{3,6},{4,1},{5,0},{6,3},{7,2},{8,13},{9,12},{10,... | collective-permute-start | bytes 1572872 | tf_op jit(solution)/shard_map/ppermute | solution.py:275
  73.4 5.6 %copy-start.22 = (f32[64]{0:T(128)S(1)}, f32[64]{0:T(128)}, u32[]{:S(2)}) copy-start(f32[64]{0:T(128)} %shard_map.83.gate_ref) | copy-start | bytes 772
  73.4 31.8 %all-to-all-start.1 = ((bf16[4,2048,128]{2,1,0:T(8,128)(2,1)}), bf16[4,2048,128]{2,1,0:T(8,128)(2,1)S(1)}, u32[]{:S(2)}, u32[]{:S(2)}) async-start(bf16[4,2048,128]{2,1,0:T(8,128)(2,1)} %shard_map.90), calls=%async_computation.1 | async-start | bytes 4194304 | tf_op jit(solution)/shard_map/all_to_all | solution.py:282
  106.5 132.5 %all-to-all-start.2 = ((bf16[4,2176,128]{2,1,0:T(8,128)(2,1)}), bf16[4,2176,128]{2,1,0:T(8,128)(2,1)S(1)}, u32[]{:S(2)}, u32[]{:S(2)}) async-start(bf16[4,2176,128]{2,1,0:T(8,128)(2,1)} %shard_map.95), calls=%async_computation.2 | async-start | bytes 4456448 | tf_op jit(solution)/shard_map/all_to_all | solution.py:282
  110.1 39.4 %collective-permute-start.2 = (bf16[1,2048,128]{2,1,0:T(8,128)(2,1)}, bf16[1,2048,128]{2,1,0:T(8,128)(2,1)}, u32[]{:S(2)}, u32[]{:S(2)}) collective-permute-start(bf16[1,2048,128]{2,1,0:T(8,128)(2,1)} %shard_map.91), channel_id=1, source_target_pairs={{0,6},{1,7},{2,4},{3,5},{4,2},{5,3},{6,0},{7,1},{8,14},{9,15},{10,... | collective-permute-start | bytes 1572872 | tf_op jit(solution)/shard_map/ppermute | solution.py:275
  112.6 47.3 %collective-permute-start.3 = (bf16[1,2048,128]{2,1,0:T(8,128)(2,1)}, bf16[1,2048,128]{2,1,0:T(8,128)(2,1)}, u32[]{:S(2)}, u32[]{:S(2)}) collective-permute-start(bf16[1,2048,128]{2,1,0:T(8,128)(2,1)} %shard_map.92), channel_id=1, source_target_pairs={{0,7},{1,6},{2,5},{3,4},{4,3},{5,2},{6,1},{7,0},{8,15},{9,14},{10,... | collective-permute-start | bytes 1572872 | tf_op jit(solution)/shard_map/ppermute | solution.py:275
  150.8 43.3 %collective-permute-start.5 = (bf16[1,2048,128]{2,1,0:T(8,128)(2,1)}, bf16[1,2048,128]{2,1,0:T(8,128)(2,1)}, u32[]{:S(2)}, u32[]{:S(2)}) collective-permute-start(bf16[1,2048,128]{2,1,0:T(8,128)(2,1)} %shard_map.99), channel_id=1, source_target_pairs={{0,4},{1,5},{2,6},{3,7},{4,0},{5,1},{6,2},{7,3},{8,12},{9,13},{10,... | collective-permute-start | bytes 1572872 | tf_op jit(solution)/shard_map/ppermute | solution.py:275
  161.2 55.2 %collective-permute-start.7 = (bf16[1,2048,128]{2,1,0:T(8,128)(2,1)}, bf16[1,2048,128]{2,1,0:T(8,128)(2,1)}, u32[]{:S(2)}, u32[]{:S(2)}) collective-permute-start(bf16[1,2048,128]{2,1,0:T(8,128)(2,1)} %shard_map.101), channel_id=1, source_target_pairs={{0,5},{1,4},{2,7},{3,6},{4,1},{5,0},{6,3},{7,2},{8,13},{9,12},{10,... | collective-permute-start | bytes 1572872 | tf_op jit(solution)/shard_map/ppermute | solution.py:275
  164.3 54.7 %copy-start.19 = (s32[4,10]{1,0:T(4,128)S(1)}, s32[4,10]{1,0:T(4,128)}, u32[]{:S(2)}) copy-start(s32[4,10]{1,0:T(4,128)} %shard_map.85.starts_ref) | copy-start | bytes 484
  195.3 125.7 %collective-permute-start.6 = (bf16[1,2048,128]{2,1,0:T(8,128)(2,1)}, bf16[1,2048,128]{2,1,0:T(8,128)(2,1)}, u32[]{:S(2)}, u32[]{:S(2)}) collective-permute-start(bf16[1,2048,128]{2,1,0:T(8,128)(2,1)} %shard_map.100), channel_id=1, source_target_pairs={{0,6},{1,7},{2,4},{3,5},{4,2},{5,3},{6,0},{7,1},{8,14},{9,15},{10,... | collective-permute-start | bytes 1572872 | tf_op jit(solution)/shard_map/ppermute | solution.py:275
  217.6 103.4 %collective-permute-start.8 = (bf16[1,2048,128]{2,1,0:T(8,128)(2,1)}, bf16[1,2048,128]{2,1,0:T(8,128)(2,1)}, u32[]{:S(2)}, u32[]{:S(2)}) collective-permute-start(bf16[1,2048,128]{2,1,0:T(8,128)(2,1)} %shard_map.102), channel_id=1, source_target_pairs={{0,7},{1,6},{2,5},{3,4},{4,3},{5,2},{6,1},{7,0},{8,15},{9,14},{10,... | collective-permute-start | bytes 1572872 | tf_op jit(solution)/shard_map/ppermute | solution.py:275
  239.0 38.0 %copy-start.2 = (bf16[4,2176,128]{2,1,0:T(8,128)(2,1)}, bf16[4,2176,128]{2,1,0:T(8,128)(2,1)S(1)}, u32[]{:S(2)}) copy-start(bf16[4,2176,128]{2,1,0:T(8,128)(2,1)S(1)} %all-to-all-done.2.refs_0_.refs_1_) | copy-start | bytes 6684676
  239.6 53.1 %all-to-all-start.3 = ((bf16[4,2048,128]{2,1,0:T(8,128)(2,1)}), bf16[4,2048,128]{2,1,0:T(8,128)(2,1)}, u32[]{:S(2)}, u32[]{:S(2)}) async-start(bf16[4,2048,128]{2,1,0:T(8,128)(2,1)} %shard_map.96), calls=%async_computation.3 | async-start | bytes 4194304 | tf_op jit(solution)/shard_map/all_to_all | solution.py:282
  273.1 25.7 %collective-permute-start.4 = (bf16[4,128,1024]{2,1,0:T(8,128)(2,1)}, bf16[4,128,1024]{2,1,0:T(8,128)(2,1)}, u32[]{:S(2)}, u32[]{:S(2)}) collective-permute-start(bf16[4,128,1024]{2,1,0:T(8,128)(2,1)} %shard_map.94), channel_id=1, source_target_pairs={{0,24},{1,25},{2,26},{3,27},{4,28},{5,29},{6,30},{7,31},{8,0},{9,1... | collective-permute-start | bytes 3145736 | tf_op jit(solution)/shard_map/ppermute | solution.py:279
  293.9 8.6 %copy-start.18 = (s32[4,10]{1,0:T(4,128)S(1)}, s32[4,10]{1,0:T(4,128)}, u32[]{:S(2)}) copy-start(s32[4,10]{1,0:T(4,128)} %shard_map.98.starts_ref) | copy-start | bytes 484
  298.8 46.6 %all-to-all-start.4 = ((bf16[4,128,1024]{2,1,0:T(8,128)(2,1)}), bf16[4,128,1024]{2,1,0:T(8,128)(2,1)S(1)}, u32[]{:S(2)}, u32[]{:S(2)}) async-start(bf16[4,128,1024]{2,1,0:T(8,128)(2,1)} %shard_map.97), calls=%async_computation.4 | async-start | bytes 2097152 | tf_op jit(solution)/shard_map/all_to_all | solution.py:282
  302.5 18.5 %copy-start.3 = (bf16[4,2176,128]{2,1,0:T(8,128)(2,1)S(1)}, bf16[4,2176,128]{2,1,0:T(8,128)(2,1)}, u32[]{:S(2)}) copy-start(bf16[4,2176,128]{2,1,0:T(8,128)(2,1)} %copy-done.2) | copy-start | bytes 6684676
  326.4 19.4 %collective-permute-start.9 = (bf16[128,1024]{1,0:T(8,128)(2,1)S(1)}, bf16[128,1024]{1,0:T(8,128)(2,1)}, u32[]{:S(2)}, u32[]{:S(2)}) collective-permute-start(bf16[128,1024]{1,0:T(8,128)(2,1)S(1)} %bitcast.63), channel_id=1, source_target_pairs={{0,24},{1,25},{2,26},{3,27},{4,28},{5,29},{6,30},{7,31},{8,0},{9,1... | collective-permute-start | bytes 786440 | tf_op jit(solution)/shard_map/ppermute | solution.py:279
  332.2 14.6 %collective-permute-start.10 = (bf16[128,1024]{1,0:T(8,128)(2,1)S(1)}, bf16[128,1024]{1,0:T(8,128)(2,1)S(1)}, u32[]{:S(2)}, u32[]{:S(2)}) collective-permute-start(bf16[128,1024]{1,0:T(8,128)(2,1)S(1)} %bitcast.62), channel_id=1, source_target_pairs={{0,25},{1,24},{2,27},{3,26},{4,29},{5,28},{6,31},{7,30},{8,1},{9,0... | collective-permute-start | bytes 786440 | tf_op jit(solution)/shard_map/ppermute | solution.py:279
  338.8 8.0 %collective-permute-start.11 = (bf16[128,1024]{1,0:T(8,128)(2,1)S(1)}, bf16[128,1024]{1,0:T(8,128)(2,1)S(1)}, u32[]{:S(2)}, u32[]{:S(2)}) collective-permute-start(bf16[128,1024]{1,0:T(8,128)(2,1)S(1)} %bitcast.61), channel_id=1, source_target_pairs={{0,26},{1,27},{2,24},{3,25},{4,30},{5,31},{6,28},{7,29},{8,2},{9,3... | collective-permute-start | bytes 786440 | tf_op jit(solution)/shard_map/ppermute | solution.py:279
  344.0 7.9 %collective-permute-start.12 = (bf16[128,1024]{1,0:T(8,128)(2,1)S(1)}, bf16[128,1024]{1,0:T(8,128)(2,1)S(1)}, u32[]{:S(2)}, u32[]{:S(2)}) collective-permute-start(bf16[128,1024]{1,0:T(8,128)(2,1)S(1)} %bitcast.60), channel_id=1, source_target_pairs={{0,27},{1,26},{2,25},{3,24},{4,31},{5,30},{6,29},{7,28},{8,3},{9,2... | collective-permute-start | bytes 786440 | tf_op jit(solution)/shard_map/ppermute | solution.py:279
  (21 other events, 32.2 us)

commit v5 on v4

v5 whole, which is shorter than its diff:
```python
import functools
import math

import jax
import jax.numpy as jnp
from jax import lax
from jax.experimental import pallas as pl
from jax.experimental.pallas import tpu as pltpu
from jax.sharding import PartitionSpec as P

BLOCK = 128
PARTS = 3
STEP = 4
MOST = 1 << 10
HINT = 16
VMEM_LIMIT = 48 * 1024 * 1024

NT = (((1,), (1,)), ((), ()))


def split_parts(value):
    terms = []
    for _ in range(PARTS):
        term = value.astype(jnp.bfloat16)
        terms.append(term.astype(jnp.float32))
        value = value - terms[-1]
    return terms


def pack_kernel(own, group, cuts, keys_ref, values_ref, *outs):
    dim = outs[0].shape[2]
    at = 0
    for index, pieces in enumerate(cuts):
        for low, high in pieces:
            out = outs[at]
            at += 1
            rows = (high - low) * BLOCK
            for device in range(out.shape[0]):
                head = device % group * own + index
                for half, source in enumerate((keys_ref, values_ref)):
                    out[device, half * rows:(half + 1) * rows, :] = source[
                        low * BLOCK:high * BLOCK, head * dim:(head + 1) * dim
                    ]


def pack(mem_keys, mem_values, seq, own, group, dim, cuts):
    mem_dev, width = mem_keys.shape
    whole = pl.BlockSpec((mem_dev, width), lambda i: (0, 0))
    shapes = [(seq, 2 * (high - low) * BLOCK, dim) for pieces in cuts for low, high in pieces]
    return pl.pallas_call(
        functools.partial(pack_kernel, own, group, cuts),
        out_shape=[jax.ShapeDtypeStruct(shape, mem_keys.dtype) for shape in shapes],
        grid=(1,),
        in_specs=[whole, whole],
        out_specs=[pl.BlockSpec(shape, lambda i: (0, 0, 0)) for shape in shapes],
        compiler_params=pltpu.CompilerParams(vmem_limit_bytes=VMEM_LIMIT),
        cost_estimate=pl.CostEstimate(flops=0, bytes_accessed=8 * mem_dev * width, transcendentals=0),
    )(mem_keys, mem_values)


def prepare_kernel(heads, dim, scale, own, index, gate_ref, at_ref, grad_ref, query_ref, out_ref, total_ref, *packed_refs):
    rows = grad_ref.shape[0]
    count = total_ref.shape[1]
    logs = split_parts(jnp.log2(total_ref[...].astype(jnp.float32)) - math.log2(scale))
    target = lax.broadcasted_iota(jnp.int32, (count, dim), 1)
    lane = lax.broadcasted_iota(jnp.int32, (rows, dim), 1)
    for x, packed_ref in enumerate(packed_refs):
        head = (at_ref[0] ^ x) * own + index
        source = lax.broadcasted_iota(jnp.int32, (count, dim), 0) - head * heads
        mine = (source >= 0) & (source < heads)
        stats = jnp.zeros((rows, dim), jnp.float32)
        for part, term in enumerate(logs):
            chosen = jnp.where(mine & (target == source + (2 * part + 1) * heads), 1.0, 0.0).astype(jnp.bfloat16)
            stats += jnp.dot(term.astype(jnp.bfloat16), chosen, preferred_element_type=jnp.float32)
        for h in range(heads):
            columns = pl.ds(pl.multiple_of((head * heads + h) * dim, dim), dim)
            gated = (gate_ref[head * heads + h] * grad_ref[:, columns].astype(jnp.float32)).astype(jnp.bfloat16)
            packed_ref[h * rows:(h + 1) * rows, :] = query_ref[:, columns]
            packed_ref[(heads + h) * rows:(heads + h + 1) * rows, :] = gated
            product = gated.astype(jnp.float32) * out_ref[:, columns].astype(jnp.float32)
            delta = jnp.sum(product, axis=1, keepdims=True)
            for part, term in enumerate(split_parts(delta)):
                stats = jnp.where(lane == 2 * part * heads + h, term, stats)
        packed_ref[2 * heads * rows:, :] = stats.astype(jnp.bfloat16)


def prepare(grad_out, queries, mem_out, row_total, gates, at, kv_heads, dim, scale, own, index):
    rows, width = grad_out.shape
    heads = width // dim // kv_heads
    group = kv_heads // own
    span = 2 * heads * rows + rows
    wide = pl.BlockSpec((rows, width), lambda i, *_: (0, 0))
    return pl.pallas_call(
        functools.partial(prepare_kernel, heads, dim, scale, own, index),
        out_shape=[jax.ShapeDtypeStruct((span, dim), jnp.bfloat16)] * group,
        grid_spec=pltpu.PrefetchScalarGridSpec(
            num_scalar_prefetch=2,
            grid=(1,),
            in_specs=[wide, wide, wide, pl.BlockSpec(row_total.shape, lambda i, *_: (0, 0))],
            out_specs=[pl.BlockSpec((span, dim), lambda i, *_: (0, 0))] * group,
        ),
        compiler_params=pltpu.CompilerParams(vmem_limit_bytes=VMEM_LIMIT),
        cost_estimate=pl.CostEstimate(flops=rows * width * 4, bytes_accessed=rows * width * 12 // own, transcendentals=0),
    )(gates, at[None], grad_out, queries, mem_out, row_total)


def attend_kernel(heads, dim, rows, scale, fresh, last, first, picks_ref, starts_ref, query_ref, stat_ref, memory_ref, *refs):
    acc_in = None if fresh else refs[0]
    out_ref, log_ref, delta_ref, total = refs[-4:]
    tile = first + pl.program_id(0)
    blocks = memory_ref.shape[1] // 2
    count = heads * rows

    if fresh:
        total[...] = jnp.zeros_like(total)
    else:
        total[...] = acc_in[0]

    stats = stat_ref[0].astype(jnp.float32)
    for h in range(heads):
        for target, first in ((delta_ref, h), (log_ref, heads + h)):
            terms = [stats[:, first + 2 * part * heads:first + 2 * part * heads + 1] for part in range(PARTS)]
            target[h * rows:(h + 1) * rows, :] = jnp.broadcast_to(terms[0] + terms[1] + terms[2], (rows, dim))

    low = starts_ref[tile, 0]
    high = starts_ref[tile, 1]
    exponent = scale * math.log2(math.e)

    def add(here, number, checked):
        sides = []
        for two in range(0, number, 2):
            keys, values = [], []
            for j in (two, two + 1):
                valid = here + j < high
                pick = picks_ref[tile, jnp.where(valid, here + j, here) if checked else here + j]
                holder = pick // MOST
                block = pick % MOST
                key = memory_ref[holder, block]
                keys.append(jnp.where(valid, key, jnp.zeros_like(key)) if checked and j else key)
                values.append(memory_ref[holder, blocks + block])
            sides.append((jnp.concatenate(keys, axis=0), jnp.concatenate(values, axis=0)))

        def products(side):
            keys, values = side
            scores = lax.dot_general(query_ref[0, :count, :], keys, NT, preferred_element_type=jnp.float32)
            grad_probs = lax.dot_general(query_ref[0, count:, :], values, NT, preferred_element_type=jnp.float32)
            return scores, grad_probs

        ahead = products(sides[0])
        gained = None
        for at, (keys, _) in enumerate(sides):
            scores, grad_probs = ahead
            if at + 1 < len(sides):
                ahead = products(sides[at + 1])
            log_wide = jnp.concatenate([log_ref[...]] * 2, axis=1)
            delta_wide = jnp.concatenate([delta_ref[...]] * 2, axis=1)
            probs = jnp.exp2(scores * exponent - log_wide)
            grad_scores = (probs * (grad_probs - delta_wide)).astype(jnp.bfloat16)
            part = jnp.dot(grad_scores, keys, preferred_element_type=jnp.float32)
            gained = part if gained is None else gained + part
        total[...] += gained

    full = (high - low) // STEP

    def many(turn, carry):
        add(low + STEP * turn, STEP, False)
        return carry

    def few(turn, carry):
        add(low + STEP * full + 2 * turn, 2, True)
        return carry

    lax.fori_loop(0, full, many, 0)
    lax.fori_loop(0, (high - low - STEP * full + 1) // 2, few, 0)

    if last:
        for h in range(heads):
            out_ref[0, :, h * dim:(h + 1) * dim] = total[h * rows:(h + 1) * rows, :].astype(jnp.bfloat16)
    else:
        out_ref[0] = total[...]


def attend(packed, memory, acc, picks, starts, heads, dim, scale, last, only=None):
    tiles, span, _ = packed.shape
    rows = span // (2 * heads + 1)
    fresh = acc is None
    width = heads * rows
    holders = memory.shape[0]
    memory = memory.reshape(holders, -1, BLOCK, dim)
    steps, first = (tiles, 0) if only is None else (1, only)
    acc_spec = pl.BlockSpec((1, width, dim), lambda t, *_: (first + t, 0, 0))
    if last:
        out_shape = jax.ShapeDtypeStruct((steps, rows, heads * dim), jnp.bfloat16)
        out_spec = pl.BlockSpec((1, rows, heads * dim), lambda t, *_: (t, 0, 0))
    else:
        out_shape = jax.ShapeDtypeStruct((tiles, width, dim), jnp.float32)
        out_spec = acc_spec
    flops = steps * holders * (memory.shape[1] // 4) * BLOCK * width * dim * 6
    return pl.pallas_call(
        functools.partial(attend_kernel, heads, dim, rows, scale, fresh, last, first),
        out_shape=out_shape,
        grid_spec=pltpu.PrefetchScalarGridSpec(
            num_scalar_prefetch=2,
            grid=(steps,),
            in_specs=[
                pl.BlockSpec((1, 2 * width, dim), lambda t, *_: (first + t, 0, 0)),
                pl.BlockSpec((1, rows, dim), lambda t, *_: (first + t, 2 * heads, 0)),
                pl.BlockSpec(memory.shape, lambda t, *_: (0, 0, 0, 0)),
            ]
            + ([] if fresh else [acc_spec]),
            out_specs=out_spec,
            scratch_shapes=[pltpu.VMEM((width, dim), jnp.float32)] * 3,
        ),
        compiler_params=pltpu.CompilerParams(vmem_limit_bytes=VMEM_LIMIT),
        cost_estimate=pl.CostEstimate(flops=flops * 4, bytes_accessed=0, transcendentals=0),
    )(picks, starts, packed, packed, memory, *([] if fresh else [acc]))


def after(value, *others):
    anywhere = pl.BlockSpec(memory_space=pl.ANY)
    corners = [pl.BlockSpec((HINT, other.shape[1]), lambda i: (0, 0)) for other in others]
    return pl.pallas_call(
        lambda *refs: None,
        out_shape=jax.ShapeDtypeStruct(value.shape, value.dtype),
        grid=(1,),
        in_specs=[anywhere] + corners,
        out_specs=anywhere,
        input_output_aliases={0: 0},
        cost_estimate=pl.CostEstimate(flops=0, bytes_accessed=0, transcendentals=0),
    )(value, *others)


def shards(grad_out, queries, mem_out, row_total, gate_logit, mem_keys, mem_values, retrieved):
    seq = lax.axis_size("seq")
    sections = lax.axis_size("section")
    position = lax.axis_index("seq")
    rows, width = grad_out.shape[1:]
    head_count = gate_logit.shape[1]
    dim = width // head_count
    kv_heads = mem_keys.shape[2] // dim
    heads = head_count // kv_heads
    mem_dev = mem_keys.shape[1]
    blocks = mem_dev // BLOCK
    group = min(kv_heads, seq // 2)
    own = kv_heads // group
    at = position % group
    home = position // group
    scale = dim ** (-0.5)

    def swapped(value, step):
        return lax.ppermute(value, "seq", [(p, p ^ step) for p in range(seq)])

    def delivered(value, step):
        pairs = [(s * seq + p, ((s - 1) % sections) * seq + (p ^ step)) for s in range(sections) for p in range(seq)]
        return lax.ppermute(value, ("section", "seq"), pairs)

    cut = (5 * blocks + 7) // 8
    cuts = [[(0, blocks)]] * (own - 1) + [[(0, cut), (cut, blocks)]]

    def listed(i):
        mine = lax.dynamic_index_in_dim(retrieved[0], at * own + i, 0, keepdims=False)
        mine = jnp.stack(
            [lax.dynamic_index_in_dim(mine, home * group + (at ^ x), 0, keepdims=False) for x in range(group)]
        )
        holder, block = mine // blocks, mine % blocks
        piece = sum((block >= low).astype(jnp.int32) for low, _ in cuts[i][1:]) if len(cuts[i]) > 1 else 0 * block
        key = piece * seq * blocks + mine
        rank = jnp.sum(key[:, None, :] < key[:, :, None], axis=-1)
        order = jnp.arange(mine.shape[-1])
        low = sum((piece == j) * cuts[i][j][0] for j in range(len(cuts[i])))
        value = holder * MOST + block - low
        picks = jnp.sum(jnp.where(rank[:, :, None] == order, value[:, :, None], 0), axis=1).astype(jnp.int32)
        bounds = [jnp.sum(piece < j, axis=-1) for j in range(len(cuts[i]) + 1)]
        return picks, [
            jnp.stack([bounds[j], bounds[j + 1]], axis=1).astype(jnp.int32) for j in range(len(cuts[i]))
        ]

    gates = jax.nn.sigmoid(gate_logit[0])
    memories = list(pack(mem_keys[0], mem_values[0], seq, own, group, dim, cuts))
    out = jnp.zeros((rows, width), jnp.bfloat16)
    before = []
    for i in range(own):
        pieces = []
        for _ in cuts[i]:
            piece = memories.pop(0)
            pieces.append(lax.all_to_all(piece, "seq", split_axis=0, concat_axis=0, tiled=True))
        packed = prepare(grad_out[0], queries[0], mem_out[0], row_total[0], gates, at, kv_heads, dim, scale, own, i)
        packed = jnp.stack([packed[0]] + [swapped(packed[x], x) for x in range(1, group)])
        picks, starts = listed(i)
        run = functools.partial(attend, packed, picks=picks, heads=heads, dim=dim, scale=scale)
        acc = None
        for j in range(len(pieces) - 1):
            acc = run(pieces[j], acc, starts=starts[j], last=False)
        ending = i == own - 1
        if ending:
            bounds = after(starts[-1], *before) if before else starts[-1]
            results = [run(pieces[-1], acc, starts=bounds, last=True, only=x)[0] for x in range(group)]
        else:
            results = list(run(pieces[-1], acc, starts=starts[-1], last=True))
        for x in range(group):
            result = delivered(results[x], x)
            if not ending:
                before.append(result)
            out = lax.dynamic_update_slice_in_dim(out, result, ((at ^ x) * own + i) * heads * dim, 1)
    return out[None]


def solution(mesh):
    return jax.shard_map(
        shards,
        mesh=mesh,
        in_specs=(
            P("section", "seq", None),
            P("section", "seq", None),
            P("section", "seq", None),
            P("section", "seq", None),
            P("section", None),
            P("section", "seq", None),
            P("section", "seq", None),
            P("section", None, None, None),
        ),
        out_specs=P("section", "seq", None),
        check_vma=False,
    )
```

time: 356 us -> 334 us (0.938)
  blocking collectives: 0 us -> 66.7 us
  waiting for transfers between devices: 153 us -> 119 us
  local copies, waits for them, and re-layouts: 43.7 us -> 13.9 us
  Pallas kernels: 116 us -> 102 us
  starting transfers between devices: 37.1 us -> 24.8 us
  other arithmetic: 2.55 us -> 6.34 us
    all_to_all x0 -> x1, blocking collectives: none -> 66.7 us  [shards(): lax.all_to_all(piece, 'seq', split_axis=0, concat_axis=0, tiled=True)]
    ppermute x8 -> x6, waiting for transfers between devices: 128 us -> 98.3 us  [swapped(): return lax.ppermute(value, 'seq', [(p, p ^ step) for p in range(seq)])]
    all_to_all x5 -> x2, waiting for transfers between devices: 15.6 us -> 0.01 us  [shards(): lax.all_to_all(piece, 'seq', split_axis=0, concat_axis=0, tiled=True)]
    slice x16 -> x0, local copies, waits for them, and re-layouts: 15.3 us -> none  [the longest x13 14 us: after(): hints = [other[:1, :HINT] for other in others]]
    unnamed x58 -> x41, local copies, waits for them, and re-layouts: 26.4 us -> 11.6 us
    pallas_call x10 -> x7, Pallas kernels: 105 us -> 91 us  [the longest x6 86.4 us: attend(): pl.pallas_call(functools.partial(attend_kernel, heads, dim, rows, scale,...]
    all_to_all x5 -> x2, starting transfers between devices: 21.7 us -> 9 us  [shards(): lax.all_to_all(piece, 'seq', split_axis=0, concat_axis=0, tiled=True)]
    ppermute x5 -> x8, waiting for transfers between devices: 9.98 us -> 20.3 us  [delivered(): return lax.ppermute(value, ('section', 'seq'), pairs)]
  transfers between devices with their start and end apart: 18 -> 16, of which waited for: 10 -> 5; matrix products, arithmetic and copies ran while one was open for 6% -> 2% of each run, Pallas kernels for 30% -> 22%
where the time goes in v5:
time: 334 us; the launch traced here: 333 us
  waiting for transfers between devices  119 us (36%)
  Pallas kernels  102 us (31%)
  blocking collectives  66.7 us (20%)
  starting transfers between devices  24.8 us (7%)
  local copies, waits for them, and re-layouts  13.9 us (4%)
  other arithmetic  6.34 us (2%)
    ppermute x6, waiting for transfers between devices, swapped(): return lax.ppermute(value, 'seq', [(p, p ^ step) for p in range(seq)])  98.3 us
    pallas_call x6, Pallas kernels, attend(): pl.pallas_call(functools.partial(attend_kernel, heads, dim, rows, scale,...  86.4 us
    all_to_all x1, blocking collectives, shards(): lax.all_to_all(piece, 'seq', split_axis=0, concat_axis=0, tiled=True)  66.7 us
    ppermute x8, waiting for transfers between devices, delivered(): return lax.ppermute(value, ('section', 'seq'), pairs)  20.3 us
    unnamed x41, local copies, waits for them, and re-layouts  11.6 us
    ppermute x8, starting transfers between devices, delivered(): return lax.ppermute(value, ('section', 'seq'), pairs)  11.5 us
    pallas_call x2, Pallas kernels, prepare(): pl.pallas_call(functools.partial(prepare_kernel, heads, dim, scale, own,...  9.84 us
    all_to_all x2, starting transfers between devices, shards(): lax.all_to_all(piece, 'seq', split_axis=0, concat_axis=0, tiled=True)  9 us
  transfers between devices with their start and end apart: 16, of which 5 were waited for; matrix products, arithmetic and copies ran while one was open for 2% of the time, Pallas kernels for 22%

profile of v5, /device:TPU:0, one launch (start us, length us, event | category | flops | bytes accessed | tf_op | source)
XLA Modules:
  0.0 332.5 jit_solution(5254339176266341577)
XLA Ops:
  3.2 4.6 %shard_map.83 = (bf16[8,2048,128]{2,1,0:T(8,128)(2,1)}, bf16[8,1280,128]{2,1,0:T(8,128)(2,1)}, bf16[8,768,128]{2,1,0:T(8,128)(2,1)S(1)}) custom-call(bf16[1024,1024]{1,0:T(8,128)(2,1)S(1)} %bitcast.69, bf16[1024,1024]{1,0:T(8,128)(2,1)S(1)} %bitcast.70), custom_call_target="tpu_custom_call" | custom-call | bytes 8388608 | tf_op jit(solution)/shard_map/pallas_call | solution.py:50
  7.8 66.7 %all_to_all.15 = bf16[8,1280,128]{2,1,0:T(8,128)(2,1)} all-to-all(bf16[8,1280,128]{2,1,0:T(8,128)(2,1)} %get-tuple-element.26), channel_id=1, replica_groups=mesh['section'=4,'seq'=8] {'seq'}, dimensions={0} | all-to-all | bytes 5242880 | tf_op jit(solution)/shard_map/all_to_all | solution.py:286
  74.5 4.7 %all-to-all-start = ((bf16[8,2048,128]{2,1,0:T(8,128)(2,1)}), bf16[8,2048,128]{2,1,0:T(8,128)(2,1)}, u32[]{:S(2)}, u32[]{:S(2)}) async-start(bf16[8,2048,128]{2,1,0:T(8,128)(2,1)} %get-tuple-element.20), calls=%async_computation | async-start | bytes 8388608 | tf_op jit(solution)/shard_map/all_to_all | solution.py:286
  79.4 5.0 %shard_map.86 = (bf16[2176,128]{1,0:T(8,128)(2,1)S(1)}, bf16[2176,128]{1,0:T(8,128)(2,1)}, bf16[2176,128]{1,0:T(8,128)(2,1)}, bf16[2176,128]{1,0:T(8,128)(2,1)}) custom-call(f32[64]{0:T(128)S(1)} %divide_bitcast_fusion.gate_ref, s32[1]{0:T(128)} %bitcast.5.at_ref, bf16[128,8192]{1,0:T(8,128)(2,1)S(1)} %bitcast.67, bf16[128,8192]{1,0:T(8,128)(2,1)} %bitcast.79, ...), custom_call_target="tpu_custom_call" | custom-call | flops 4194304 | bytes 6291456 | tf_op jit(solution)/shard_map/pallas_call | solution.py:93
  84.8 1.7 collective-permute-start.8
  86.5 4.8 %shard_map.82 = (bf16[2176,128]{1,0:T(8,128)(2,1)S(1)}, bf16[2176,128]{1,0:T(8,128)(2,1)}, bf16[2176,128]{1,0:T(8,128)(2,1)}, bf16[2176,128]{1,0:T(8,128)(2,1)S(1)}) custom-call(f32[64]{0:T(128)S(1)} %divide_bitcast_fusion.gate_ref, s32[1]{0:T(128)} %bitcast.5.at_ref, bf16[128,8192]{1,0:T(8,128)(2,1)S(1)} %bitcast.68, bf16[128,8192]{1,0:T(8,128)(2,1)} %bitcast.80, ...), custom_call_target="tpu_custom_call" | custom-call | flops 4194304 | bytes 6291456 | tf_op jit(solution)/shard_map/pallas_call | solution.py:93
  92.6 1.7 collective-permute-start.1
  97.1 62.8 %collective-permute-done.8 = bf16[2176,128]{1,0:T(8,128)(2,1)} collective-permute-done((bf16[2176,128]{1,0:T(8,128)(2,1)}, bf16[2176,128]{1,0:T(8,128)(2,1)}, u32[]{:S(2)}, u32[]{:S(2)}) %collective-permute-start.8) | collective-permute-done | bytes 557088 | tf_op jit(solution)/shard_map/ppermute | solution.py:251
  160.0 11.9 %collective-permute-done.9 = bf16[2176,128]{1,0:T(8,128)(2,1)} collective-permute-done((bf16[2176,128]{1,0:T(8,128)(2,1)}, bf16[2176,128]{1,0:T(8,128)(2,1)}, u32[]{:S(2)}, u32[]{:S(2)}) %collective-permute-start.9) | collective-permute-done | bytes 557088 | tf_op jit(solution)/shard_map/ppermute | solution.py:251
  173.6 12.5 %collective-permute-done.1 = bf16[2176,128]{1,0:T(8,128)(2,1)} collective-permute-done((bf16[2176,128]{1,0:T(8,128)(2,1)}, bf16[2176,128]{1,0:T(8,128)(2,1)}, u32[]{:S(2)}, u32[]{:S(2)}) %collective-permute-start.1) | collective-permute-done | bytes 557088 | tf_op jit(solution)/shard_map/ppermute | solution.py:251
  186.2 11.0 %collective-permute-done.2 = bf16[2176,128]{1,0:T(8,128)(2,1)} collective-permute-done((bf16[2176,128]{1,0:T(8,128)(2,1)}, bf16[2176,128]{1,0:T(8,128)(2,1)}, u32[]{:S(2)}, u32[]{:S(2)}) %collective-permute-start.2) | collective-permute-done | bytes 557088 | tf_op jit(solution)/shard_map/ppermute | solution.py:251
  197.1 3.1 pad_maximum_fusion.query_ref.stat_ref
  200.3 4.3 %all-to-all-start.1 = ((bf16[8,768,128]{2,1,0:T(8,128)(2,1)}), bf16[8,768,128]{2,1,0:T(8,128)(2,1)}, u32[]{:S(2)}, u32[]{:S(2)}) async-start(bf16[8,768,128]{2,1,0:T(8,128)(2,1)} %copy-done.4), calls=%async_computation.1 | async-start | bytes 3145728 | tf_op jit(solution)/shard_map/all_to_all | solution.py:286
  206.2 37.2 %shard_map.84 = bf16[4,128,1024]{2,1,0:T(8,128)(2,1)S(1)} custom-call(s32[4,32]{1,0:T(4,128)S(1)} %select_reduce_fusion.1.picks_ref, s32[4,2]{1,0:T(4,128)S(1)} %stack.83.starts_ref, bf16[4,2176,128]{2,1,0:T(8,128)(2,1)S(1)} %copy-done.1, bf16[4,2176,128]{2,1,0:T(8,128)(2,1)S(1)} %copy-done.1, bf16[8,16,128,128]{3,2,1,0:T(8,128)(2,1)} %bitcast.16.memory_ref), custom_call_target="tpu_custom_call" | custom-call | flops 51539607552 | tf_op jit(solution)/shard_map/pallas_call | solution.py:199
  243.5 2.5 collective-permute-start.3
  246.2 2.5 collective-permute-start.5
  249.0 26.0 %shard_map.87.refs_0_ = f32[4,1024,128]{2,1,0:T(8,128)S(1)} custom-call(s32[4,32]{1,0:T(4,128)S(1)} %select_reduce_fusion.picks_ref, s32[4,2]{1,0:T(4,128)S(1)} %get-tuple-element.45.starts_ref, bf16[4,2176,128]{2,1,0:T(8,128)(2,1)S(1)} %pad_maximum_fusion.1.query_ref.stat_ref, bf16[4,2176,128]{2,1,0:T(8,128)(2,1)S(1)} %pad_maximum_fusion.1.query_ref.stat_ref, ...), custom_call_target="tpu_custom_call" | custom-call | flops 25769803776 | tf_op jit(solution)/shard_map/pallas_call | solution.py:199
  280.4 4.7 %shard_map.91 = bf16[1,128,1024]{2,1,0:T(8,128)(2,1)S(1)} custom-call(s32[4,32]{1,0:T(4,128)S(1)} %select_reduce_fusion.picks_ref, s32[4,2]{1,0:T(4,128)S(1)} %copy-done.5, bf16[4,2176,128]{2,1,0:T(8,128)(2,1)S(1)} %pad_maximum_fusion.1.query_ref.stat_ref, bf16[4,2176,128]{2,1,0:T(8,128)(2,1)S(1)} %pad_maximum_fusion.1.query_ref.stat_ref, ...), custom_call_target="tpu_custom_call" | custom-call | flops 3221225472 | tf_op jit(solution)/shard_map/pallas_call | solution.py:199
  285.1 5.6 %shard_map.90 = bf16[1,128,1024]{2,1,0:T(8,128)(2,1)S(1)} custom-call(s32[4,32]{1,0:T(4,128)S(1)} %select_reduce_fusion.picks_ref, s32[4,2]{1,0:T(4,128)S(1)} %copy-done.5, bf16[4,2176,128]{2,1,0:T(8,128)(2,1)S(1)} %pad_maximum_fusion.1.query_ref.stat_ref, bf16[4,2176,128]{2,1,0:T(8,128)(2,1)S(1)} %pad_maximum_fusion.1.query_ref.stat_ref, ...), custom_call_target="tpu_custom_call" | custom-call | flops 3221225472 | tf_op jit(solution)/shard_map/pallas_call | solution.py:199
  290.7 7.0 %shard_map.89 = bf16[1,128,1024]{2,1,0:T(8,128)(2,1)S(1)} custom-call(s32[4,32]{1,0:T(4,128)S(1)} %select_reduce_fusion.picks_ref, s32[4,2]{1,0:T(4,128)S(1)} %copy-done.5, bf16[4,2176,128]{2,1,0:T(8,128)(2,1)S(1)} %pad_maximum_fusion.1.query_ref.stat_ref, bf16[4,2176,128]{2,1,0:T(8,128)(2,1)S(1)} %pad_maximum_fusion.1.query_ref.stat_ref, ...), custom_call_target="tpu_custom_call" | custom-call | flops 3221225472 | tf_op jit(solution)/shard_map/pallas_call | solution.py:199
  297.7 6.0 %shard_map.88 = bf16[1,128,1024]{2,1,0:T(8,128)(2,1)S(1)} custom-call(s32[4,32]{1,0:T(4,128)S(1)} %select_reduce_fusion.picks_ref, s32[4,2]{1,0:T(4,128)S(1)} %copy-done.5, bf16[4,2176,128]{2,1,0:T(8,128)(2,1)S(1)} %pad_maximum_fusion.1.query_ref.stat_ref, bf16[4,2176,128]{2,1,0:T(8,128)(2,1)S(1)} %pad_maximum_fusion.1.query_ref.stat_ref, ...), custom_call_target="tpu_custom_call" | custom-call | flops 3221225472 | tf_op jit(solution)/shard_map/pallas_call | solution.py:199
  303.7 3.1 collective-permute-start.13
  306.8 2.9 collective-permute-start.12
  310.1 20.3 %collective-permute-done.10 = bf16[128,1024]{1,0:T(8,128)(2,1)S(1)} collective-permute-done((bf16[128,1024]{1,0:T(8,128)(2,1)S(1)}, bf16[128,1024]{1,0:T(8,128)(2,1)S(1)}, u32[]{:S(2)}, u32[]{:S(2)}) %collective-permute-start.10) | collective-permute-done | bytes 262176 | tf_op jit(solution)/shard_map/ppermute | solution.py:255
  (87 shorter events, 19.3 us)
Async XLA Ops:
  7.8 66.7 %copy-start.4 = (bf16[8,768,128]{2,1,0:T(8,128)(2,1)}, bf16[8,768,128]{2,1,0:T(8,128)(2,1)S(1)}, u32[]{:S(2)}) copy-start(bf16[8,768,128]{2,1,0:T(8,128)(2,1)S(1)} %get-tuple-element.25) | copy-start | bytes 4718596
  74.5 4.7 %copy-start.18 = (bf16[1,128,64]{1,2,0:T(8,128)(2,1)S(1)}, bf16[1,128,64]{1,2,0:T(8,128)(2,1)}, u32[]{:S(2)}) copy-start(bf16[1,128,64]{1,2,0:T(8,128)(2,1)} %param.11) | copy-start | bytes 49156
  74.5 4.9 %copy-start.19 = (f32[1,64]{1,0:T(1,128)S(1)}, f32[1,64]{1,0:T(1,128)}, u32[]{:S(2)}) copy-start(f32[1,64]{1,0:T(1,128)} %param.12) | copy-start | bytes 772
  74.5 4.9 %copy-start = (bf16[1,128,8192]{2,1,0:T(8,128)(2,1)S(1)}, bf16[1,128,8192]{2,1,0:T(8,128)(2,1)}, u32[]{:S(2)}) copy-start(bf16[1,128,8192]{2,1,0:T(8,128)(2,1)} %param.8) | copy-start | bytes 6291460
  74.5 125.7 %all-to-all-start = ((bf16[8,2048,128]{2,1,0:T(8,128)(2,1)}), bf16[8,2048,128]{2,1,0:T(8,128)(2,1)}, u32[]{:S(2)}, u32[]{:S(2)}) async-start(bf16[8,2048,128]{2,1,0:T(8,128)(2,1)} %get-tuple-element.20), calls=%async_computation | async-start | bytes 8388608 | tf_op jit(solution)/shard_map/all_to_all | solution.py:286
  84.5 12.4 %collective-permute-start.7 = (bf16[2176,128]{1,0:T(8,128)(2,1)}, bf16[2176,128]{1,0:T(8,128)(2,1)}, u32[]{:S(2)}, u32[]{:S(2)}) collective-permute-start(bf16[2176,128]{1,0:T(8,128)(2,1)} %get-tuple-element.22), channel_id=1, source_target_pairs={{0,1},{1,0},{2,3},{3,2},{4,5},{5,4},{6,7},{7,6},{8,9},{9,8},{10,11... | collective-permute-start | bytes 1671176 | tf_op jit(solution)/shard_map/ppermute | solution.py:251
  84.8 75.2 %collective-permute-start.8 = (bf16[2176,128]{1,0:T(8,128)(2,1)}, bf16[2176,128]{1,0:T(8,128)(2,1)}, u32[]{:S(2)}, u32[]{:S(2)}) collective-permute-start(bf16[2176,128]{1,0:T(8,128)(2,1)} %get-tuple-element.23), channel_id=1, source_target_pairs={{0,2},{1,3},{2,0},{3,1},{4,6},{5,7},{6,4},{7,5},{8,10},{9,11},{10,... | collective-permute-start | bytes 1671176 | tf_op jit(solution)/shard_map/ppermute | solution.py:251
  86.5 85.4 %collective-permute-start.9 = (bf16[2176,128]{1,0:T(8,128)(2,1)}, bf16[2176,128]{1,0:T(8,128)(2,1)}, u32[]{:S(2)}, u32[]{:S(2)}) collective-permute-start(bf16[2176,128]{1,0:T(8,128)(2,1)} %get-tuple-element.24), channel_id=1, source_target_pairs={{0,3},{1,2},{2,1},{3,0},{4,7},{5,6},{6,5},{7,4},{8,11},{9,10},{10,... | collective-permute-start | bytes 1671176 | tf_op jit(solution)/shard_map/ppermute | solution.py:251
  92.1 81.5 %collective-permute-start = (bf16[2176,128]{1,0:T(8,128)(2,1)}, bf16[2176,128]{1,0:T(8,128)(2,1)}, u32[]{:S(2)}, u32[]{:S(2)}) collective-permute-start(bf16[2176,128]{1,0:T(8,128)(2,1)} %get-tuple-element.17), channel_id=1, source_target_pairs={{0,1},{1,0},{2,3},{3,2},{4,5},{5,4},{6,7},{7,6},{8,9},{9,8},{10,11... | collective-permute-start | bytes 1671176 | tf_op jit(solution)/shard_map/ppermute | solution.py:251
  92.6 93.6 %collective-permute-start.1 = (bf16[2176,128]{1,0:T(8,128)(2,1)}, bf16[2176,128]{1,0:T(8,128)(2,1)}, u32[]{:S(2)}, u32[]{:S(2)}) collective-permute-start(bf16[2176,128]{1,0:T(8,128)(2,1)} %get-tuple-element.18), channel_id=1, source_target_pairs={{0,2},{1,3},{2,0},{3,1},{4,6},{5,7},{6,4},{7,5},{8,10},{9,11},{10,... | collective-permute-start | bytes 1671176 | tf_op jit(solution)/shard_map/ppermute | solution.py:251
  96.9 100.3 %collective-permute-start.2 = (bf16[2176,128]{1,0:T(8,128)(2,1)}, bf16[2176,128]{1,0:T(8,128)(2,1)}, u32[]{:S(2)}, u32[]{:S(2)}) collective-permute-start(bf16[2176,128]{1,0:T(8,128)(2,1)} %copy-done.6), channel_id=1, source_target_pairs={{0,3},{1,2},{2,1},{3,0},{4,7},{5,6},{6,5},{7,4},{8,11},{9,10},{10,... | collective-permute-start | bytes 1671176 | tf_op jit(solution)/shard_map/ppermute | solution.py:251
  200.3 77.8 %all-to-all-start.1 = ((bf16[8,768,128]{2,1,0:T(8,128)(2,1)}), bf16[8,768,128]{2,1,0:T(8,128)(2,1)}, u32[]{:S(2)}, u32[]{:S(2)}) async-start(bf16[8,768,128]{2,1,0:T(8,128)(2,1)} %copy-done.4), calls=%async_computation.1 | async-start | bytes 3145728 | tf_op jit(solution)/shard_map/all_to_all | solution.py:286
  243.5 32.9 %collective-permute-start.3 = (bf16[128,1024]{1,0:T(8,128)(2,1)S(1)}, bf16[128,1024]{1,0:T(8,128)(2,1)S(1)}, u32[]{:S(2)}, u32[]{:S(2)}) collective-permute-start(bf16[128,1024]{1,0:T(8,128)(2,1)S(1)} %get-tuple-element.34), channel_id=1, source_target_pairs={{0,24},{1,25},{2,26},{3,27},{4,28},{5,29},{6,30},{7,31},{8,0},{9,1... | collective-permute-start | bytes 786440 | tf_op jit(solution)/shard_map/ppermute | solution.py:255
  246.0 30.4 %collective-permute-start.4 = (bf16[128,1024]{1,0:T(8,128)(2,1)S(1)}, bf16[128,1024]{1,0:T(8,128)(2,1)S(1)}, u32[]{:S(2)}, u32[]{:S(2)}) collective-permute-start(bf16[128,1024]{1,0:T(8,128)(2,1)S(1)} %get-tuple-element.33), channel_id=1, source_target_pairs={{0,25},{1,24},{2,27},{3,26},{4,29},{5,28},{6,31},{7,30},{8,1},{9,0... | collective-permute-start | bytes 786440 | tf_op jit(solution)/shard_map/ppermute | solution.py:255
  246.2 30.2 %collective-permute-start.5 = (bf16[128,1024]{1,0:T(8,128)(2,1)S(1)}, bf16[128,1024]{1,0:T(8,128)(2,1)S(1)}, u32[]{:S(2)}, u32[]{:S(2)}) collective-permute-start(bf16[128,1024]{1,0:T(8,128)(2,1)S(1)} %get-tuple-element.32), channel_id=1, source_target_pairs={{0,26},{1,27},{2,24},{3,25},{4,30},{5,31},{6,28},{7,29},{8,2},{9,3... | collective-permute-start | bytes 786440 | tf_op jit(solution)/shard_map/ppermute | solution.py:255
  248.7 27.6 %collective-permute-start.6 = (bf16[128,1024]{1,0:T(8,128)(2,1)S(1)}, bf16[128,1024]{1,0:T(8,128)(2,1)S(1)}, u32[]{:S(2)}, u32[]{:S(2)}) collective-permute-start(bf16[128,1024]{1,0:T(8,128)(2,1)S(1)} %get-tuple-element.31), channel_id=1, source_target_pairs={{0,27},{1,26},{2,25},{3,24},{4,31},{5,30},{6,29},{7,28},{8,3},{9,2... | collective-permute-start | bytes 786440 | tf_op jit(solution)/shard_map/ppermute | solution.py:255
  303.7 6.2 %copy-start.11 = (bf16[128,1024]{1,0:T(8,128)(2,1)S(1)}, bf16[128,1024]{1,0:T(8,128)(2,1)}, u32[]{:S(2)}) copy-start(bf16[128,1024]{1,0:T(8,128)(2,1)} %copy-done.10) | copy-start | bytes 786436
  303.7 6.3 %copy-start.13 = (bf16[128,1024]{1,0:T(8,128)(2,1)S(1)}, bf16[128,1024]{1,0:T(8,128)(2,1)}, u32[]{:S(2)}) copy-start(bf16[128,1024]{1,0:T(8,128)(2,1)} %copy-done.12) | copy-start | bytes 786436
  303.7 6.3 %copy-start.15 = (bf16[128,1024]{1,0:T(8,128)(2,1)S(1)}, bf16[128,1024]{1,0:T(8,128)(2,1)}, u32[]{:S(2)}) copy-start(bf16[128,1024]{1,0:T(8,128)(2,1)} %copy-done.14) | copy-start | bytes 786436
  303.7 6.3 %copy-start.17 = (bf16[128,1024]{1,0:T(8,128)(2,1)S(1)}, bf16[128,1024]{1,0:T(8,128)(2,1)}, u32[]{:S(2)}) copy-start(bf16[128,1024]{1,0:T(8,128)(2,1)} %copy-done.16) | copy-start | bytes 786436
  303.7 26.8 %collective-permute-start.13 = (bf16[128,1024]{1,0:T(8,128)(2,1)S(1)}, bf16[128,1024]{1,0:T(8,128)(2,1)S(1)}, u32[]{:S(2)}, u32[]{:S(2)}) collective-permute-start(bf16[128,1024]{1,0:T(8,128)(2,1)S(1)} %bitcast.75), channel_id=1, source_target_pairs={{0,27},{1,26},{2,25},{3,24},{4,31},{5,30},{6,29},{7,28},{8,3},{9,2... | collective-permute-start | bytes 786440 | tf_op jit(solution)/shard_map/ppermute | solution.py:255
  306.8 23.6 %collective-permute-start.12 = (bf16[128,1024]{1,0:T(8,128)(2,1)S(1)}, bf16[128,1024]{1,0:T(8,128)(2,1)S(1)}, u32[]{:S(2)}, u32[]{:S(2)}) collective-permute-start(bf16[128,1024]{1,0:T(8,128)(2,1)S(1)} %bitcast.76), channel_id=1, source_target_pairs={{0,26},{1,27},{2,24},{3,25},{4,30},{5,31},{6,28},{7,29},{8,2},{9,3... | collective-permute-start | bytes 786440 | tf_op jit(solution)/shard_map/ppermute | solution.py:255
  309.7 20.7 %collective-permute-start.11 = (bf16[128,1024]{1,0:T(8,128)(2,1)S(1)}, bf16[128,1024]{1,0:T(8,128)(2,1)S(1)}, u32[]{:S(2)}, u32[]{:S(2)}) collective-permute-start(bf16[128,1024]{1,0:T(8,128)(2,1)S(1)} %bitcast.77), channel_id=1, source_target_pairs={{0,25},{1,24},{2,27},{3,26},{4,29},{5,28},{6,31},{7,30},{8,1},{9,0... | collective-permute-start | bytes 786440 | tf_op jit(solution)/shard_map/ppermute | solution.py:255
  309.7 20.7 %collective-permute-start.10 = (bf16[128,1024]{1,0:T(8,128)(2,1)S(1)}, bf16[128,1024]{1,0:T(8,128)(2,1)S(1)}, u32[]{:S(2)}, u32[]{:S(2)}) collective-permute-start(bf16[128,1024]{1,0:T(8,128)(2,1)S(1)} %bitcast.78), channel_id=1, source_target_pairs={{0,24},{1,25},{2,26},{3,27},{4,28},{5,29},{6,30},{7,31},{8,0},{9,1... | collective-permute-start | bytes 786440 | tf_op jit(solution)/shard_map/ppermute | solution.py:255
  (12 other events, 13.8 us)

commit v6 on v5

--- a/solution.py
+++ b/solution.py
@@ -218,7 +218,9 @@
 
 def after(value, *others):
     anywhere = pl.BlockSpec(memory_space=pl.ANY)
-    corners = [pl.BlockSpec((HINT, other.shape[1]), lambda i: (0, 0)) for other in others]
+    corners = [
+        pl.BlockSpec((1,) * (other.ndim - 2) + (HINT, 128), lambda i, count=other.ndim: (0,) * count) for other in others
+    ]
     return pl.pallas_call(
         lambda *refs: None,
         out_shape=jax.ShapeDtypeStruct(value.shape, value.dtype),
@@ -254,7 +256,7 @@
         pairs = [(s * seq + p, ((s - 1) % sections) * seq + (p ^ step)) for s in range(sections) for p in range(seq)]
         return lax.ppermute(value, ("section", "seq"), pairs)
 
-    cut = (5 * blocks + 7) // 8
+    cut = (3 * blocks + 3) // 4
     cuts = [[(0, blocks)]] * (own - 1) + [[(0, cut), (cut, blocks)]]
 
     def listed(i):
@@ -278,29 +280,36 @@
     gates = jax.nn.sigmoid(gate_logit[0])
     memories = list(pack(mem_keys[0], mem_values[0], seq, own, group, dim, cuts))
     out = jnp.zeros((rows, width), jnp.bfloat16)
-    before = []
+    before, worked, latest = [], [], None
     for i in range(own):
+        opened = gates if latest is None else after(gates, latest)
+        packed = prepare(grad_out[0], queries[0], mem_out[0], row_total[0], opened, at, kv_heads, dim, scale, own, i)
+        packed = jnp.stack([packed[0]] + [swapped(packed[x], x) for x in range(1, group)])
         pieces = []
         for _ in cuts[i]:
             piece = memories.pop(0)
-            pieces.append(lax.all_to_all(piece, "seq", split_axis=0, concat_axis=0, tiled=True))
-        packed = prepare(grad_out[0], queries[0], mem_out[0], row_total[0], gates, at, kv_heads, dim, scale, own, i)
-        packed = jnp.stack([packed[0]] + [swapped(packed[x], x) for x in range(1, group)])
+            piece = piece if latest is None else after(piece, latest)
+            latest = lax.all_to_all(piece, "seq", split_axis=0, concat_axis=0, tiled=True)
+            pieces.append(latest)
         picks, starts = listed(i)
         run = functools.partial(attend, packed, picks=picks, heads=heads, dim=dim, scale=scale)
         acc = None
         for j in range(len(pieces) - 1):
-            acc = run(pieces[j], acc, starts=starts[j], last=False)
-        ending = i == own - 1
-        if ending:
-            bounds = after(starts[-1], *before) if before else starts[-1]
-            results = [run(pieces[-1], acc, starts=bounds, last=True, only=x)[0] for x in range(group)]
+            acc = run(pieces[j], acc, starts=after(starts[j], *worked), last=False)
+            worked = [acc]
+        results = []
+        if i < own - 1:
+            done = run(pieces[-1], acc, starts=after(starts[-1], *worked), last=True)
+            worked = [done]
+            results = [delivered(done[x], x) for x in range(group)]
+            before += results
         else:
-            results = list(run(pieces[-1], acc, starts=starts[-1], last=True))
-        for x in range(group):
-            result = delivered(results[x], x)
-            if not ending:
-                before.append(result)
+            for x in range(group):
+                ready = before if x == 0 else results[x - 2:x - 1] if x > 1 else []
+                done = run(pieces[-1], acc, starts=after(starts[-1], *worked, *ready), last=True, only=x)
+                worked = [done]
+                results.append(delivered(done[0], x))
+        for x, result in enumerate(results):
             out = lax.dynamic_update_slice_in_dim(out, result, ((at ^ x) * own + i) * heads * dim, 1)
     return out[None]
 

time: 334 us -> 312 us (0.934)
  blocking collectives: 66.7 us -> 0 us
  local copies, waits for them, and re-layouts: 13.9 us -> 38.2 us
  waiting for transfers between devices: 119 us -> 132 us
  starting transfers between devices: 24.8 us -> 32.9 us
    all_to_all x1 -> x0, blocking collectives: 66.7 us -> none  [shards(): lax.all_to_all(piece, 'seq', split_axis=0, concat_axis=0, tiled=True)]
    ppermute x8, waiting for transfers between devices: 20.3 us -> 48.8 us  [delivered(): return lax.ppermute(value, ('section', 'seq'), pairs)]
    ppermute x6, waiting for transfers between devices: 98.3 us -> 83.2 us  [swapped(): return lax.ppermute(value, 'seq', [(p, p ^ step) for p in range(seq)])]
    unnamed x41 -> x70, local copies, waits for them, and re-layouts: 11.6 us -> 24.3 us
    dynamic_update_slice x8, local copies, waits for them, and re-layouts: 0.89 us -> 9.64 us  [shards(): lax.dynamic_update_slice_in_dim(out, result, ((at ^ x) * own + i) * heads...]
    all_to_all x2 -> x3, starting transfers between devices: 9 us -> 15.7 us  [shards(): lax.all_to_all(piece, 'seq', split_axis=0, concat_axis=0, tiled=True)]
    pallas_call x6, Pallas kernels: 86.4 us -> 80.3 us  [attend(): pl.pallas_call(functools.partial(attend_kernel, heads, dim, rows, scale,...]
    pallas_call x1 -> x9, Pallas kernels: 0.81 us -> 5.51 us  [after(): pl.pallas_call(lambda *refs: None, out_shape=jax.ShapeDtypeStruct(value.s...]
  transfers between devices with their start and end apart: 16 -> 17, of which waited for: 5 -> 6; matrix products, arithmetic and copies ran while one was open for 2% -> 7% of each run, Pallas kernels for 22% -> 28%
where the time goes in v6:
time: 312 us; the launch traced here: 310 us
  waiting for transfers between devices  132 us (42%)
  Pallas kernels  101 us (32%)
  local copies, waits for them, and re-layouts  38.2 us (12%)
  starting transfers between devices  32.9 us (11%)
  other arithmetic  6.29 us (2%)
    ppermute x6, waiting for transfers between devices, swapped(): return lax.ppermute(value, 'seq', [(p, p ^ step) for p in range(seq)])  83.2 us
    pallas_call x6, Pallas kernels, attend(): pl.pallas_call(functools.partial(attend_kernel, heads, dim, rows, scale,...  80.3 us
    ppermute x8, waiting for transfers between devices, delivered(): return lax.ppermute(value, ('section', 'seq'), pairs)  48.8 us
    unnamed x70, local copies, waits for them, and re-layouts  24.3 us
    all_to_all x3, starting transfers between devices, shards(): lax.all_to_all(piece, 'seq', split_axis=0, concat_axis=0, tiled=True)  15.7 us
    ppermute x8, starting transfers between devices, delivered(): return lax.ppermute(value, ('section', 'seq'), pairs)  13 us
    pallas_call x2, Pallas kernels, prepare(): pl.pallas_call(functools.partial(prepare_kernel, heads, dim, scale, own,...  9.98 us
    dynamic_update_slice x8, local copies, waits for them, and re-layouts, shards(): lax.dynamic_update_slice_in_dim(out, result, ((at ^ x) * own + i) * heads...  9.64 us
  transfers between devices with their start and end apart: 17, of which 6 were waited for; matrix products, arithmetic and copies ran while one was open for 7% of the time, Pallas kernels for 28%

profile of v6, /device:TPU:0, one launch (start us, length us, event | category | flops | bytes accessed | tf_op | source)
XLA Modules:
  0.0 310.2 jit_solution(12615258663444649356)
XLA Ops:
  3.2 4.7 %shard_map.84 = (bf16[8,2048,128]{2,1,0:T(8,128)(2,1)}, bf16[8,1536,128]{2,1,0:T(8,128)(2,1)}, bf16[8,512,128]{2,1,0:T(8,128)(2,1)S(1)}) custom-call(bf16[1024,1024]{1,0:T(8,128)(2,1)S(1)} %bitcast.69, bf16[1024,1024]{1,0:T(8,128)(2,1)S(1)} %bitcast.70), custom_call_target="tpu_custom_call" | custom-call | bytes 8388608 | tf_op jit(solution)/shard_map/pallas_call | solution.py:50
  8.9 6.5 %all-to-all-start = ((bf16[8,2048,128]{2,1,0:T(8,128)(2,1)}), bf16[8,2048,128]{2,1,0:T(8,128)(2,1)}, u32[]{:S(2)}, u32[]{:S(2)}) async-start(bf16[8,2048,128]{2,1,0:T(8,128)(2,1)} %get-tuple-element.20), calls=%async_computation | async-start | bytes 8388608 | tf_op jit(solution)/shard_map/all_to_all | solution.py:292
  15.5 5.0 %shard_map.83 = (bf16[2176,128]{1,0:T(8,128)(2,1)S(1)}, bf16[2176,128]{1,0:T(8,128)(2,1)}, bf16[2176,128]{1,0:T(8,128)(2,1)}, bf16[2176,128]{1,0:T(8,128)(2,1)}) custom-call(f32[64]{0:T(128)S(1)} %divide_bitcast_fusion.gate_ref.refs_0_, s32[1]{0:T(128)} %bitcast.5.at_ref, bf16[128,8192]{1,0:T(8,128)(2,1)S(1)} %bitcast.67, bf16[128,8192]{1,0:T(8,128)(2,1)} %bitcast.83, ...), custom_call_target="tpu_custom_call" | custom-call | flops 4194304 | bytes 6291456 | tf_op jit(solution)/shard_map/pallas_call | solution.py:93
  24.7 71.4 %collective-permute-done.1 = bf16[2176,128]{1,0:T(8,128)(2,1)} collective-permute-done((bf16[2176,128]{1,0:T(8,128)(2,1)}, bf16[2176,128]{1,0:T(8,128)(2,1)}, u32[]{:S(2)}, u32[]{:S(2)}) %collective-permute-start.1) | collective-permute-done | bytes 557088 | tf_op jit(solution)/shard_map/ppermute | solution.py:253
  96.1 11.8 %collective-permute-done.2 = bf16[2176,128]{1,0:T(8,128)(2,1)} collective-permute-done((bf16[2176,128]{1,0:T(8,128)(2,1)}, bf16[2176,128]{1,0:T(8,128)(2,1)}, u32[]{:S(2)}, u32[]{:S(2)}) %collective-permute-start.2) | collective-permute-done | bytes 557088 | tf_op jit(solution)/shard_map/ppermute | solution.py:253
  107.9 3.1 pad_maximum_fusion.query_ref.stat_ref
  111.6 5.6 %all-to-all-start.1 = ((bf16[8,1536,128]{2,1,0:T(8,128)(2,1)}), bf16[8,1536,128]{2,1,0:T(8,128)(2,1)}, u32[]{:S(2)}, u32[]{:S(2)}) async-start(bf16[8,1536,128]{2,1,0:T(8,128)(2,1)} %shard_map.89), calls=%async_computation.1 | async-start | bytes 6291456 | tf_op jit(solution)/shard_map/all_to_all | solution.py:292
  118.9 36.7 %shard_map.85.refs_1_ = bf16[4,128,1024]{2,1,0:T(8,128)(2,1)S(1)} custom-call(s32[4,32]{1,0:T(4,128)S(1)} %select_reduce_fusion.1.picks_ref, s32[4,2]{1,0:T(4,128)S(1)} %copy-done.25, bf16[4,2176,128]{2,1,0:T(8,128)(2,1)S(1)} %copy-done.8, bf16[4,2176,128]{2,1,0:T(8,128)(2,1)S(1)} %copy-done.8, bf16[8,16,128,128]{3,2,1,0:T(8,128)(2,1)} %bitcast.16.memory_ref), custom_call_target="tpu_custom_call" | custom-call | flops 51539607552 | tf_op jit(solution)/shard_map/pallas_call | solution.py:199
  156.6 2.4 collective-permute-start.3
  164.2 5.0 %shard_map.88 = (bf16[2176,128]{1,0:T(8,128)(2,1)S(1)}, bf16[2176,128]{1,0:T(8,128)(2,1)}, bf16[2176,128]{1,0:T(8,128)(2,1)}, bf16[2176,128]{1,0:T(8,128)(2,1)}) custom-call(f32[64]{0:T(128)S(1)} %copy-done.27, s32[1]{0:T(128)} %bitcast.5.at_ref, bf16[128,8192]{1,0:T(8,128)(2,1)S(1)} %bitcast.68, bf16[128,8192]{1,0:T(8,128)(2,1)} %bitcast.84, ...), custom_call_target="tpu_custom_call" | custom-call | flops 4194304 | bytes 6291456 | tf_op jit(solution)/shard_map/pallas_call | solution.py:93
  170.0 1.9 collective-permute-start.8
  172.6 2.2 collective-permute-start.5
  180.1 36.0 %collective-permute-done.5.refs_4_ = bf16[128,1024]{1,0:T(8,128)(2,1)S(1)} collective-permute-done((bf16[128,1024]{1,0:T(8,128)(2,1)}, bf16[128,1024]{1,0:T(8,128)(2,1)S(1)}, u32[]{:S(2)}, u32[]{:S(2)}) %collective-permute-start.5) | collective-permute-done | bytes 262176 | tf_op jit(solution)/shard_map/ppermute | solution.py:257
  216.9 4.4 %collective-permute-done.6.refs_5_ = bf16[128,1024]{1,0:T(8,128)(2,1)S(1)} collective-permute-done((bf16[128,1024]{1,0:T(8,128)(2,1)S(1)}, bf16[128,1024]{1,0:T(8,128)(2,1)S(1)}, u32[]{:S(2)}, u32[]{:S(2)}) %collective-permute-start.6) | collective-permute-done | bytes 262176 | tf_op jit(solution)/shard_map/ppermute | solution.py:257
  224.4 3.7 %all-to-all-start.2 = ((bf16[8,512,128]{2,1,0:T(8,128)(2,1)}), bf16[8,512,128]{2,1,0:T(8,128)(2,1)S(1)}, u32[]{:S(2)}, u32[]{:S(2)}) async-start(bf16[8,512,128]{2,1,0:T(8,128)(2,1)} %shard_map.92), calls=%async_computation.2 | async-start | bytes 2097152 | tf_op jit(solution)/shard_map/all_to_all | solution.py:292
  229.7 29.3 %shard_map.90.refs_1_.refs_0_ = f32[4,1024,128]{2,1,0:T(8,128)S(1)} custom-call(s32[4,32]{1,0:T(4,128)S(1)} %select_reduce_fusion.picks_ref, s32[4,2]{1,0:T(4,128)S(1)} %copy-done.21, bf16[4,2176,128]{2,1,0:T(8,128)(2,1)S(1)} %copy-done.3, bf16[4,2176,128]{2,1,0:T(8,128)(2,1)S(1)} %copy-done.3, bf16[8,12,128,128]{3,2,1,0:T(8,128)(2,1)} %bitcast.36.memory_ref), custom_call_target="tpu_custom_call" | custom-call | flops 38654705664 | tf_op jit(solution)/shard_map/pallas_call | solution.py:199
  265.0 3.7 %shard_map.93.refs_1_ = bf16[1,128,1024]{2,1,0:T(8,128)(2,1)S(1)} custom-call(s32[4,32]{1,0:T(4,128)S(1)} %select_reduce_fusion.picks_ref, s32[4,2]{1,0:T(4,128)S(1)} %copy-done.20, bf16[4,2176,128]{2,1,0:T(8,128)(2,1)S(1)} %copy-done.4, bf16[4,2176,128]{2,1,0:T(8,128)(2,1)S(1)} %copy-done.4, bf16[8,4,128,128]{3,2,1,0:T(8,128)(2,1)S(1)} %bitcast.71, ...), custom_call_target="tpu_custom_call" | custom-call | flops 3221225472 | tf_op jit(solution)/shard_map/pallas_call | solution.py:199
  270.0 2.7 collective-permute-start.10
  275.0 3.1 shard_map.95.refs_1_
  281.9 3.8 %shard_map.97.refs_1_ = bf16[1,128,1024]{2,1,0:T(8,128)(2,1)S(1)} custom-call(s32[4,32]{1,0:T(4,128)S(1)} %select_reduce_fusion.picks_ref, s32[4,2]{1,0:T(4,128)S(1)} %copy-done.23, bf16[4,2176,128]{2,1,0:T(8,128)(2,1)S(1)} %copy-done.6, bf16[4,2176,128]{2,1,0:T(8,128)(2,1)S(1)} %copy-done.6, bf16[8,4,128,128]{3,2,1,0:T(8,128)(2,1)S(1)} %bitcast.73, ...), custom_call_target="tpu_custom_call" | custom-call | flops 3221225472 | tf_op jit(solution)/shard_map/pallas_call | solution.py:199
  289.5 3.8 %shard_map.99 = bf16[1,128,1024]{2,1,0:T(8,128)(2,1)S(1)} custom-call(s32[4,32]{1,0:T(4,128)S(1)} %select_reduce_fusion.picks_ref, s32[4,2]{1,0:T(4,128)S(1)} %copy-done.22, bf16[4,2176,128]{2,1,0:T(8,128)(2,1)S(1)} %copy-done.7, bf16[4,2176,128]{2,1,0:T(8,128)(2,1)S(1)} %copy-done.7, bf16[8,4,128,128]{3,2,1,0:T(8,128)(2,1)S(1)} %bitcast.74, ...), custom_call_target="tpu_custom_call" | custom-call | flops 3221225472 | tf_op jit(solution)/shard_map/pallas_call | solution.py:199
  293.3 2.3 collective-permute-start.13
  295.6 1.8 collective-permute-start.12
  300.7 8.0 %collective-permute-done.12 = bf16[128,1024]{1,0:T(8,128)(2,1)S(1)} collective-permute-done((bf16[128,1024]{1,0:T(8,128)(2,1)S(1)}, bf16[128,1024]{1,0:T(8,128)(2,1)S(1)}, u32[]{:S(2)}, u32[]{:S(2)}) %collective-permute-start.12) | collective-permute-done | bytes 262176 | tf_op jit(solution)/shard_map/ppermute | solution.py:257
  (125 shorter events, 51.1 us)
Async XLA Ops:
  8.9 6.5 %copy-start.31 = (bf16[1,128,64]{1,2,0:T(8,128)(2,1)S(1)}, bf16[1,128,64]{1,2,0:T(8,128)(2,1)}, u32[]{:S(2)}) copy-start(bf16[1,128,64]{1,2,0:T(8,128)(2,1)} %param.11) | copy-start | bytes 49156
  8.9 6.6 %copy-start.32 = (f32[1,64]{1,0:T(1,128)S(1)}, f32[1,64]{1,0:T(1,128)}, u32[]{:S(2)}) copy-start(f32[1,64]{1,0:T(1,128)} %param.12) | copy-start | bytes 772
  8.9 6.6 %copy-start = (bf16[1,128,8192]{2,1,0:T(8,128)(2,1)S(1)}, bf16[1,128,8192]{2,1,0:T(8,128)(2,1)}, u32[]{:S(2)}) copy-start(bf16[1,128,8192]{2,1,0:T(8,128)(2,1)} %param.8) | copy-start | bytes 6291460
  8.9 102.1 %all-to-all-start = ((bf16[8,2048,128]{2,1,0:T(8,128)(2,1)}), bf16[8,2048,128]{2,1,0:T(8,128)(2,1)}, u32[]{:S(2)}, u32[]{:S(2)}) async-start(bf16[8,2048,128]{2,1,0:T(8,128)(2,1)} %get-tuple-element.20), calls=%async_computation | async-start | bytes 8388608 | tf_op jit(solution)/shard_map/all_to_all | solution.py:292
  20.5 4.2 %collective-permute-start = (bf16[2176,128]{1,0:T(8,128)(2,1)}, bf16[2176,128]{1,0:T(8,128)(2,1)}, u32[]{:S(2)}, u32[]{:S(2)}) collective-permute-start(bf16[2176,128]{1,0:T(8,128)(2,1)} %get-tuple-element.17), channel_id=1, source_target_pairs={{0,1},{1,0},{2,3},{3,2},{4,5},{5,4},{6,7},{7,6},{8,9},{9,8},{10,11... | collective-permute-start | bytes 1671176 | tf_op jit(solution)/shard_map/ppermute | solution.py:253
  21.0 75.1 %collective-permute-start.1 = (bf16[2176,128]{1,0:T(8,128)(2,1)}, bf16[2176,128]{1,0:T(8,128)(2,1)}, u32[]{:S(2)}, u32[]{:S(2)}) collective-permute-start(bf16[2176,128]{1,0:T(8,128)(2,1)} %get-tuple-element.18), channel_id=1, source_target_pairs={{0,2},{1,3},{2,0},{3,1},{4,6},{5,7},{6,4},{7,5},{8,10},{9,11},{10,... | collective-permute-start | bytes 1671176 | tf_op jit(solution)/shard_map/ppermute | solution.py:253
  22.7 85.2 %collective-permute-start.2 = (bf16[2176,128]{1,0:T(8,128)(2,1)}, bf16[2176,128]{1,0:T(8,128)(2,1)}, u32[]{:S(2)}, u32[]{:S(2)}) collective-permute-start(bf16[2176,128]{1,0:T(8,128)(2,1)} %get-tuple-element.19), channel_id=1, source_target_pairs={{0,3},{1,2},{2,1},{3,0},{4,7},{5,6},{6,5},{7,4},{8,11},{9,10},{10,... | collective-permute-start | bytes 1671176 | tf_op jit(solution)/shard_map/ppermute | solution.py:253
  111.6 112.1 %all-to-all-start.1 = ((bf16[8,1536,128]{2,1,0:T(8,128)(2,1)}), bf16[8,1536,128]{2,1,0:T(8,128)(2,1)}, u32[]{:S(2)}, u32[]{:S(2)}) async-start(bf16[8,1536,128]{2,1,0:T(8,128)(2,1)} %shard_map.89), calls=%async_computation.1 | async-start | bytes 6291456 | tf_op jit(solution)/shard_map/all_to_all | solution.py:292
  155.6 8.0 %copy-start.2 = (bf16[4,128,1024]{2,1,0:T(8,128)(2,1)}, bf16[4,128,1024]{2,1,0:T(8,128)(2,1)S(1)}, u32[]{:S(2)}) copy-start(bf16[4,128,1024]{2,1,0:T(8,128)(2,1)S(1)} %shard_map.85.refs_1_) | copy-start | bytes 3145732
  156.6 16.0 %collective-permute-start.3 = (bf16[128,1024]{1,0:T(8,128)(2,1)}, bf16[128,1024]{1,0:T(8,128)(2,1)}, u32[]{:S(2)}, u32[]{:S(2)}) collective-permute-start(bf16[128,1024]{1,0:T(8,128)(2,1)} %get-tuple-element.34), channel_id=1, source_target_pairs={{0,24},{1,25},{2,26},{3,27},{4,28},{5,29},{6,30},{7,31},{8,0},{9,1... | collective-permute-start | bytes 786440 | tf_op jit(solution)/shard_map/ppermute | solution.py:257
  159.7 18.4 %collective-permute-start.4 = (bf16[128,1024]{1,0:T(8,128)(2,1)}, bf16[128,1024]{1,0:T(8,128)(2,1)}, u32[]{:S(2)}, u32[]{:S(2)}) collective-permute-start(bf16[128,1024]{1,0:T(8,128)(2,1)} %get-tuple-element.33), channel_id=1, source_target_pairs={{0,25},{1,24},{2,27},{3,26},{4,29},{5,28},{6,31},{7,30},{8,1},{9,0... | collective-permute-start | bytes 786440 | tf_op jit(solution)/shard_map/ppermute | solution.py:257
  170.0 8.1 %copy-start.30 = (bf16[128,1024]{1,0:T(8,128)(2,1)S(1)}, bf16[128,1024]{1,0:T(8,128)(2,1)}, u32[]{:S(2)}) copy-start(bf16[128,1024]{1,0:T(8,128)(2,1)} %get-tuple-element.31) | copy-start | bytes 786436
  170.0 52.1 %collective-permute-start.7 = (bf16[2176,128]{1,0:T(8,128)(2,1)}, bf16[2176,128]{1,0:T(8,128)(2,1)S(1)}, u32[]{:S(2)}, u32[]{:S(2)}) collective-permute-start(bf16[2176,128]{1,0:T(8,128)(2,1)} %get-tuple-element.22), channel_id=1, source_target_pairs={{0,1},{1,0},{2,3},{3,2},{4,5},{5,4},{6,7},{7,6},{8,9},{9,8},{10,11... | collective-permute-start | bytes 1671176 | tf_op jit(solution)/shard_map/ppermute | solution.py:253
  170.0 52.1 %collective-permute-start.8 = (bf16[2176,128]{1,0:T(8,128)(2,1)}, bf16[2176,128]{1,0:T(8,128)(2,1)S(1)}, u32[]{:S(2)}, u32[]{:S(2)}) collective-permute-start(bf16[2176,128]{1,0:T(8,128)(2,1)} %get-tuple-element.23), channel_id=1, source_target_pairs={{0,2},{1,3},{2,0},{3,1},{4,6},{5,7},{6,4},{7,5},{8,10},{9,11},{10,... | collective-permute-start | bytes 1671176 | tf_op jit(solution)/shard_map/ppermute | solution.py:253
  171.9 50.1 %collective-permute-start.9 = (bf16[2176,128]{1,0:T(8,128)(2,1)}, bf16[2176,128]{1,0:T(8,128)(2,1)S(1)}, u32[]{:S(2)}, u32[]{:S(2)}) collective-permute-start(bf16[2176,128]{1,0:T(8,128)(2,1)} %get-tuple-element.24), channel_id=1, source_target_pairs={{0,3},{1,2},{2,1},{3,0},{4,7},{5,6},{6,5},{7,4},{8,11},{9,10},{10,... | collective-permute-start | bytes 1671176 | tf_op jit(solution)/shard_map/ppermute | solution.py:253
  172.6 49.4 %copy-start.14 = (bf16[2176,128]{1,0:T(8,128)(2,1)S(1)}, bf16[2176,128]{1,0:T(8,128)(2,1)}, u32[]{:S(2)}) copy-start(bf16[2176,128]{1,0:T(8,128)(2,1)} %copy-done.13) | copy-start | bytes 1671172
  172.6 43.5 %collective-permute-start.5 = (bf16[128,1024]{1,0:T(8,128)(2,1)}, bf16[128,1024]{1,0:T(8,128)(2,1)S(1)}, u32[]{:S(2)}, u32[]{:S(2)}) collective-permute-start(bf16[128,1024]{1,0:T(8,128)(2,1)} %get-tuple-element.32), channel_id=1, source_target_pairs={{0,26},{1,27},{2,24},{3,25},{4,30},{5,31},{6,28},{7,29},{8,2},{9,3... | collective-permute-start | bytes 786440 | tf_op jit(solution)/shard_map/ppermute | solution.py:257
  178.0 43.2 %collective-permute-start.6 = (bf16[128,1024]{1,0:T(8,128)(2,1)S(1)}, bf16[128,1024]{1,0:T(8,128)(2,1)S(1)}, u32[]{:S(2)}, u32[]{:S(2)}) collective-permute-start(bf16[128,1024]{1,0:T(8,128)(2,1)S(1)} %copy-done.30), channel_id=1, source_target_pairs={{0,27},{1,26},{2,25},{3,24},{4,31},{5,30},{6,29},{7,28},{8,3},{9,2... | collective-permute-start | bytes 786440 | tf_op jit(solution)/shard_map/ppermute | solution.py:257
  216.1 7.6 %copy-start.28 = (bf16[128,1024]{1,0:T(8,128)(2,1)}, bf16[128,1024]{1,0:T(8,128)(2,1)S(1)}, u32[]{:S(2)}) copy-start(bf16[128,1024]{1,0:T(8,128)(2,1)S(1)} %collective-permute-done.5.refs_4_) | copy-start | bytes 786436
  224.4 36.6 %all-to-all-start.2 = ((bf16[8,512,128]{2,1,0:T(8,128)(2,1)}), bf16[8,512,128]{2,1,0:T(8,128)(2,1)S(1)}, u32[]{:S(2)}, u32[]{:S(2)}) async-start(bf16[8,512,128]{2,1,0:T(8,128)(2,1)} %shard_map.92), calls=%async_computation.2 | async-start | bytes 2097152 | tf_op jit(solution)/shard_map/all_to_all | solution.py:292
  270.0 8.9 %collective-permute-start.10 = (bf16[128,1024]{1,0:T(8,128)(2,1)}, bf16[128,1024]{1,0:T(8,128)(2,1)}, u32[]{:S(2)}, u32[]{:S(2)}) collective-permute-start(bf16[128,1024]{1,0:T(8,128)(2,1)} %bitcast.80), channel_id=1, source_target_pairs={{0,24},{1,25},{2,26},{3,27},{4,28},{5,29},{6,30},{7,31},{8,0},{9,1... | collective-permute-start | bytes 786440 | tf_op jit(solution)/shard_map/ppermute | solution.py:257
  278.1 8.3 %collective-permute-start.11 = (bf16[128,1024]{1,0:T(8,128)(2,1)S(1)}, bf16[128,1024]{1,0:T(8,128)(2,1)}, u32[]{:S(2)}, u32[]{:S(2)}) collective-permute-start(bf16[128,1024]{1,0:T(8,128)(2,1)S(1)} %bitcast.81), channel_id=1, source_target_pairs={{0,25},{1,24},{2,27},{3,26},{4,29},{5,28},{6,31},{7,30},{8,1},{9,0... | collective-permute-start | bytes 786440 | tf_op jit(solution)/shard_map/ppermute | solution.py:257
  293.3 16.2 %collective-permute-start.13 = (bf16[128,1024]{1,0:T(8,128)(2,1)S(1)}, bf16[128,1024]{1,0:T(8,128)(2,1)S(1)}, u32[]{:S(2)}, u32[]{:S(2)}) collective-permute-start(bf16[128,1024]{1,0:T(8,128)(2,1)S(1)} %bitcast.82), channel_id=1, source_target_pairs={{0,27},{1,26},{2,25},{3,24},{4,31},{5,30},{6,29},{7,28},{8,3},{9,2... | collective-permute-start | bytes 786440 | tf_op jit(solution)/shard_map/ppermute | solution.py:257
  295.6 13.1 %collective-permute-start.12 = (bf16[128,1024]{1,0:T(8,128)(2,1)S(1)}, bf16[128,1024]{1,0:T(8,128)(2,1)S(1)}, u32[]{:S(2)}, u32[]{:S(2)}) collective-permute-start(bf16[128,1024]{1,0:T(8,128)(2,1)S(1)} %bitcast.79), channel_id=1, source_target_pairs={{0,26},{1,27},{2,24},{3,25},{4,30},{5,31},{6,28},{7,29},{8,2},{9,3... | collective-permute-start | bytes 786440 | tf_op jit(solution)/shard_map/ppermute | solution.py:257
  (26 other events, 48.5 us)

commit v7 on v6

--- a/solution.py
+++ b/solution.py
@@ -14,6 +14,7 @@
 MOST = 1 << 10
 HINT = 16
 VMEM_LIMIT = 48 * 1024 * 1024
+VMEM_MOST = 60 * 1024 * 1024
 
 NT = (((1,), (1,)), ((), ()))
 
@@ -211,9 +212,35 @@
             out_specs=out_spec,
             scratch_shapes=[pltpu.VMEM((width, dim), jnp.float32)] * 3,
         ),
-        compiler_params=pltpu.CompilerParams(vmem_limit_bytes=VMEM_LIMIT),
+        compiler_params=pltpu.CompilerParams(vmem_limit_bytes=VMEM_MOST),
         cost_estimate=pl.CostEstimate(flops=flops * 4, bytes_accessed=0, transcendentals=0),
     )(picks, starts, packed, packed, memory, *([] if fresh else [acc]))
+
+
+def assemble_kernel(own, group, at_ref, *refs):
+    pieces, out_ref = refs[:-1], refs[-1]
+    span = pieces[0].shape[1]
+    for index in range(own):
+        for x in range(group):
+            column = pl.multiple_of(((at_ref[0] ^ x) * own + index) * span, span)
+            out_ref[:, pl.ds(column, span)] = pieces[index * group + x][...]
+
+
+def assemble(pieces, at, own, group):
+    rows, span = pieces[0].shape
+    width = own * group * span
+    return pl.pallas_call(
+        functools.partial(assemble_kernel, own, group),
+        out_shape=jax.ShapeDtypeStruct((rows, width), pieces[0].dtype),
+        grid_spec=pltpu.PrefetchScalarGridSpec(
+            num_scalar_prefetch=1,
+            grid=(1,),
+            in_specs=[pl.BlockSpec((rows, span), lambda i, _: (0, 0))] * len(pieces),
+            out_specs=pl.BlockSpec((rows, width), lambda i, _: (0, 0)),
+        ),
+        compiler_params=pltpu.CompilerParams(vmem_limit_bytes=VMEM_LIMIT),
+        cost_estimate=pl.CostEstimate(flops=0, bytes_accessed=4 * rows * width, transcendentals=0),
+    )(at[None], *pieces)
 
 
 def after(value, *others):
@@ -279,12 +306,16 @@
 
     gates = jax.nn.sigmoid(gate_logit[0])
     memories = list(pack(mem_keys[0], mem_values[0], seq, own, group, dim, cuts))
-    out = jnp.zeros((rows, width), jnp.bfloat16)
-    before, worked, latest = [], [], None
-    for i in range(own):
+    gathered, worked, latest = [], [], None
+
+    def queries_of(i):
         opened = gates if latest is None else after(gates, latest)
         packed = prepare(grad_out[0], queries[0], mem_out[0], row_total[0], opened, at, kv_heads, dim, scale, own, i)
-        packed = jnp.stack([packed[0]] + [swapped(packed[x], x) for x in range(1, group)])
+        return [packed[0]] + [swapped(packed[x], x) for x in range(1, group)]
+
+    coming = queries_of(0)
+    for i in range(own):
+        packed = jnp.stack(coming)
         pieces = []
         for _ in cuts[i]:
             piece = memories.pop(0)
@@ -299,19 +330,19 @@
             worked = [acc]
         results = []
         if i < own - 1:
+            coming = queries_of(i + 1)
             done = run(pieces[-1], acc, starts=after(starts[-1], *worked), last=True)
             worked = [done]
+            done = after(done, *coming)
             results = [delivered(done[x], x) for x in range(group)]
-            before += results
         else:
             for x in range(group):
-                ready = before if x == 0 else results[x - 2:x - 1] if x > 1 else []
+                ready = gathered if x == 0 else results[x - 2:x - 1] if x > 1 else []
                 done = run(pieces[-1], acc, starts=after(starts[-1], *worked, *ready), last=True, only=x)
                 worked = [done]
                 results.append(delivered(done[0], x))
-        for x, result in enumerate(results):
-            out = lax.dynamic_update_slice_in_dim(out, result, ((at ^ x) * own + i) * heads * dim, 1)
-    return out[None]
+        gathered = gathered + results
+    return assemble(gathered, at, own, group)[None]
 
 
 def solution(mesh):

time: 312 us -> 291 us (0.933)
  local copies, waits for them, and re-layouts: 38.2 us -> 16.1 us
  waiting for transfers between devices: 132 us -> 119 us
  Pallas kernels: 101 us -> 112 us
    ppermute x8, waiting for transfers between devices: 48.8 us -> 8.24 us  [delivered(): return lax.ppermute(value, ('section', 'seq'), pairs)]
    ppermute x6, waiting for transfers between devices: 83.2 us -> 111 us  [swapped(): return lax.ppermute(value, 'seq', [(p, p ^ step) for p in range(seq)])]
    unnamed x70 -> x64, local copies, waits for them, and re-layouts: 24.3 us -> 12.3 us
    pallas_call x6, Pallas kernels: 80.3 us -> 90.5 us  [attend(): pl.pallas_call(functools.partial(attend_kernel, heads, dim, rows, scale,...]
    dynamic_update_slice x8 -> x0, local copies, waits for them, and re-layouts: 9.64 us -> none  [shards(): lax.dynamic_update_slice_in_dim(out, result, ((at ^ x) * own + i) * heads...]
    pallas_call x9 -> x10, Pallas kernels: 5.51 us -> 6.27 us  [after(): pl.pallas_call(lambda *refs: None, out_shape=jax.ShapeDtypeStruct(value.s...]
  transfers between devices with their start and end apart: 17 -> 17, of which waited for: 6 -> 5; matrix products, arithmetic and copies ran while one was open for 7% -> 5% of each run, Pallas kernels for 28% -> 35%
where the time goes in v7:
time: 291 us; the launch traced here: 289 us
  waiting for transfers between devices  119 us (41%)
  Pallas kernels  112 us (38%)
  starting transfers between devices  33.9 us (12%)
  local copies, waits for them, and re-layouts  16.1 us (6%)
  other arithmetic  7.43 us (3%)
    ppermute x6, waiting for transfers between devices, swapped(): return lax.ppermute(value, 'seq', [(p, p ^ step) for p in range(seq)])  111 us
    pallas_call x6, Pallas kernels, attend(): pl.pallas_call(functools.partial(attend_kernel, heads, dim, rows, scale,...  90.5 us
    ppermute x8, starting transfers between devices, delivered(): return lax.ppermute(value, ('section', 'seq'), pairs)  14.9 us
    all_to_all x3, starting transfers between devices, shards(): lax.all_to_all(piece, 'seq', split_axis=0, concat_axis=0, tiled=True)  14.8 us
    unnamed x64, local copies, waits for them, and re-layouts  12.3 us
    pallas_call x2, Pallas kernels, prepare(): pl.pallas_call(functools.partial(prepare_kernel, heads, dim, scale, own,...  9.46 us
    ppermute x8, waiting for transfers between devices, delivered(): return lax.ppermute(value, ('section', 'seq'), pairs)  8.24 us
    pallas_call x10, Pallas kernels, after(): pl.pallas_call(lambda *refs: None, out_shape=jax.ShapeDtypeStruct(value.s...  6.27 us
  transfers between devices with their start and end apart: 17, of which 5 were waited for; matrix products, arithmetic and copies ran while one was open for 5% of the time, Pallas kernels for 35%

profile of v7, /device:TPU:0, one launch (start us, length us, event | category | flops | bytes accessed | tf_op | source)
XLA Modules:
  0.0 289.4 jit_solution(4386342597291687372)
XLA Ops:
  3.2 4.7 %shard_map.84 = (bf16[8,2048,128]{2,1,0:T(8,128)(2,1)}, bf16[8,1536,128]{2,1,0:T(8,128)(2,1)}, bf16[8,512,128]{2,1,0:T(8,128)(2,1)S(1)}) custom-call(bf16[1024,1024]{1,0:T(8,128)(2,1)S(1)} %bitcast.55, bf16[1024,1024]{1,0:T(8,128)(2,1)S(1)} %bitcast.56), custom_call_target="tpu_custom_call" | custom-call | bytes 8388608 | tf_op jit(solution)/shard_map/pallas_call | solution.py:51
  8.9 6.5 %all-to-all-start = ((bf16[8,2048,128]{2,1,0:T(8,128)(2,1)}), bf16[8,2048,128]{2,1,0:T(8,128)(2,1)}, u32[]{:S(2)}, u32[]{:S(2)}) async-start(bf16[8,2048,128]{2,1,0:T(8,128)(2,1)} %get-tuple-element.20), calls=%async_computation | async-start | bytes 8388608 | tf_op jit(solution)/shard_map/all_to_all | solution.py:323
  15.5 4.8 %shard_map.83 = (bf16[2176,128]{1,0:T(8,128)(2,1)S(1)}, bf16[2176,128]{1,0:T(8,128)(2,1)S(1)}, bf16[2176,128]{1,0:T(8,128)(2,1)}, bf16[2176,128]{1,0:T(8,128)(2,1)}) custom-call(f32[64]{0:T(128)S(1)} %divide_bitcast_fusion.gate_ref.refs_0_, s32[1]{0:T(128)} %bitcast.at_ref, bf16[128,8192]{1,0:T(8,128)(2,1)S(1)} %bitcast.52, bf16[128,8192]{1,0:T(8,128)(2,1)} %bitcast.60, ...), custom_call_target="tpu_custom_call" | custom-call | flops 4194304 | bytes 6291456 | tf_op jit(solution)/shard_map/pallas_call | solution.py:94
  20.3 1.8 collective-permute-start.2
  28.7 67.5 %collective-permute-done.2 = bf16[2176,128]{1,0:T(8,128)(2,1)} collective-permute-done((bf16[2176,128]{1,0:T(8,128)(2,1)}, bf16[2176,128]{1,0:T(8,128)(2,1)}, u32[]{:S(2)}, u32[]{:S(2)}) %collective-permute-start.2) | collective-permute-done | bytes 557088 | tf_op jit(solution)/shard_map/ppermute | solution.py:280
  96.1 13.8 %collective-permute-done.1 = bf16[2176,128]{1,0:T(8,128)(2,1)} collective-permute-done((bf16[2176,128]{1,0:T(8,128)(2,1)}, bf16[2176,128]{1,0:T(8,128)(2,1)}, u32[]{:S(2)}, u32[]{:S(2)}) %collective-permute-start.1) | collective-permute-done | bytes 557088 | tf_op jit(solution)/shard_map/ppermute | solution.py:280
  110.0 3.1 %pad_maximum_fusion.query_ref.stat_ref = bf16[4,2176,128]{2,1,0:T(8,128)(2,1)} fusion(bf16[1,2176,128]{2,1,0:T(8,128)(2,1)} %bitcast.13, bf16[1,2176,128]{2,1,0:T(8,128)(2,1)} %bitcast.12, bf16[1,2176,128]{2,1,0:T(8,128)(2,1)} %bitcast.11, bf16[1,2176,128]{2,1,0:T(8,128)(2,1)S(1)} %bitcast.57), kind=kLoop, calls=%fused_computation | loop fusion | flops 3342336 | bytes 4456448 | tf_op jit(solution)/shard_map/stack | solution.py:318
  113.7 4.5 %all-to-all-start.1 = ((bf16[8,1536,128]{2,1,0:T(8,128)(2,1)}), bf16[8,1536,128]{2,1,0:T(8,128)(2,1)}, u32[]{:S(2)}, u32[]{:S(2)}) async-start(bf16[8,1536,128]{2,1,0:T(8,128)(2,1)} %shard_map.90), calls=%async_computation.1 | async-start | bytes 6291456 | tf_op jit(solution)/shard_map/all_to_all | solution.py:323
  119.5 4.6 %shard_map.87 = (bf16[2176,128]{1,0:T(8,128)(2,1)S(1)}, bf16[2176,128]{1,0:T(8,128)(2,1)}, bf16[2176,128]{1,0:T(8,128)(2,1)S(1)}, bf16[2176,128]{1,0:T(8,128)(2,1)S(1)}) custom-call(f32[64]{0:T(128)S(1)} %copy-done.19, s32[1]{0:T(128)} %bitcast.at_ref, bf16[128,8192]{1,0:T(8,128)(2,1)S(1)} %bitcast.53, bf16[128,8192]{1,0:T(8,128)(2,1)} %bitcast.61, ...), custom_call_target="tpu_custom_call" | custom-call | flops 4194304 | bytes 6291456 | tf_op jit(solution)/shard_map/pallas_call | solution.py:94
  125.4 1.7 collective-permute-start.4
  127.0 37.8 %shard_map.85.refs_0_.refs_1_ = bf16[4,128,1024]{2,1,0:T(8,128)(2,1)} custom-call(s32[4,32]{1,0:T(4,128)} %select_reduce_fusion.1.picks_ref, s32[4,2]{1,0:T(4,128)} %shard_map.82.starts_ref, bf16[4,2176,128]{2,1,0:T(8,128)(2,1)} %pad_maximum_fusion.query_ref.stat_ref, bf16[4,2176,128]{2,1,0:T(8,128)(2,1)} %pad_maximum_fusion.query_ref.stat_ref, ...), custom_call_target="tpu_custom_call" | custom-call | flops 51539607552 | tf_op jit(solution)/shard_map/pallas_call | solution.py:200
  165.5 16.5 %collective-permute-done.4.refs_3_ = bf16[2176,128]{1,0:T(8,128)(2,1)S(1)} collective-permute-done((bf16[2176,128]{1,0:T(8,128)(2,1)S(1)}, bf16[2176,128]{1,0:T(8,128)(2,1)S(1)}, u32[]{:S(2)}, u32[]{:S(2)}) %collective-permute-start.4) | collective-permute-done | bytes 557088 | tf_op jit(solution)/shard_map/ppermute | solution.py:280
  182.0 13.3 %collective-permute-done.5.refs_4_ = bf16[2176,128]{1,0:T(8,128)(2,1)S(1)} collective-permute-done((bf16[2176,128]{1,0:T(8,128)(2,1)S(1)}, bf16[2176,128]{1,0:T(8,128)(2,1)S(1)}, u32[]{:S(2)}, u32[]{:S(2)}) %collective-permute-start.5) | collective-permute-done | bytes 557088 | tf_op jit(solution)/shard_map/ppermute | solution.py:280
  196.9 2.1 slice_bitcast_fusion
  199.0 2.4 collective-permute-start.6
  206.7 3.9 %all-to-all-start.2 = ((bf16[8,512,128]{2,1,0:T(8,128)(2,1)}), bf16[8,512,128]{2,1,0:T(8,128)(2,1)S(1)}, u32[]{:S(2)}, u32[]{:S(2)}) async-start(bf16[8,512,128]{2,1,0:T(8,128)(2,1)} %shard_map.93), calls=%async_computation.2 | async-start | bytes 2097152 | tf_op jit(solution)/shard_map/all_to_all | solution.py:323
  210.5 33.0 %shard_map.91.refs_1_.refs_0_ = f32[4,1024,128]{2,1,0:T(8,128)} custom-call(s32[4,32]{1,0:T(4,128)} %select_reduce_fusion.picks_ref, s32[4,2]{1,0:T(4,128)} %shard_map.89.starts_ref, bf16[4,2176,128]{2,1,0:T(8,128)(2,1)} %pad_maximum_fusion.1.query_ref.stat_ref, bf16[4,2176,128]{2,1,0:T(8,128)(2,1)} %pad_maximum_fusion.1.query_ref.stat_ref, ...), custom_call_target="tpu_custom_call" | custom-call | flops 38654705664 | tf_op jit(solution)/shard_map/pallas_call | solution.py:200
  246.8 4.7 %shard_map.94.refs_1_ = bf16[1,128,1024]{2,1,0:T(8,128)(2,1)} custom-call(s32[4,32]{1,0:T(4,128)} %select_reduce_fusion.picks_ref, s32[4,2]{1,0:T(4,128)} %shard_map.92.starts_ref, bf16[4,2176,128]{2,1,0:T(8,128)(2,1)} %pad_maximum_fusion.1.query_ref.stat_ref, bf16[4,2176,128]{2,1,0:T(8,128)(2,1)} %pad_maximum_fusion.1.query_ref.stat_ref, ...), custom_call_target="tpu_custom_call" | custom-call | flops 3221225472 | tf_op jit(solution)/shard_map/pallas_call | solution.py:200
  252.1 3.3 %collective-permute-start.10 = (bf16[128,1024]{1,0:T(8,128)(2,1)}, bf16[128,1024]{1,0:T(8,128)(2,1)S(1)}, u32[]{:S(2)}, u32[]{:S(2)}) collective-permute-start(bf16[128,1024]{1,0:T(8,128)(2,1)} %bitcast.73), channel_id=1, source_target_pairs={{0,24},{1,25},{2,26},{3,27},{4,28},{5,29},{6,30},{7,31},{8,0},{9,1... | collective-permute-start | bytes 786440 | tf_op jit(solution)/shard_map/ppermute | solution.py:284
  255.5 5.2 %shard_map.96.refs_1_ = bf16[1,128,1024]{2,1,0:T(8,128)(2,1)} custom-call(s32[4,32]{1,0:T(4,128)} %select_reduce_fusion.picks_ref, s32[4,2]{1,0:T(4,128)} %shard_map.95.starts_ref, bf16[4,2176,128]{2,1,0:T(8,128)(2,1)} %pad_maximum_fusion.1.query_ref.stat_ref, bf16[4,2176,128]{2,1,0:T(8,128)(2,1)} %pad_maximum_fusion.1.query_ref.stat_ref, ...), custom_call_target="tpu_custom_call" | custom-call | flops 3221225472 | tf_op jit(solution)/shard_map/pallas_call | solution.py:200
  263.0 5.2 %shard_map.98.refs_1_ = bf16[1,128,1024]{2,1,0:T(8,128)(2,1)} custom-call(s32[4,32]{1,0:T(4,128)} %select_reduce_fusion.picks_ref, s32[4,2]{1,0:T(4,128)} %shard_map.97.starts_ref, bf16[4,2176,128]{2,1,0:T(8,128)(2,1)} %pad_maximum_fusion.1.query_ref.stat_ref, bf16[4,2176,128]{2,1,0:T(8,128)(2,1)} %pad_maximum_fusion.1.query_ref.stat_ref, ...), custom_call_target="tpu_custom_call" | custom-call | flops 3221225472 | tf_op jit(solution)/shard_map/pallas_call | solution.py:200
  268.2 4.3 %collective-permute-start.12 = (bf16[128,1024]{1,0:T(8,128)(2,1)}, bf16[128,1024]{1,0:T(8,128)(2,1)S(1)}, u32[]{:S(2)}, u32[]{:S(2)}) collective-permute-start(bf16[128,1024]{1,0:T(8,128)(2,1)} %bitcast.71), channel_id=1, source_target_pairs={{0,26},{1,27},{2,24},{3,25},{4,30},{5,31},{6,28},{7,29},{8,2},{9,3... | collective-permute-start | bytes 786440 | tf_op jit(solution)/shard_map/ppermute | solution.py:284
  273.9 4.6 %shard_map.100 = bf16[1,128,1024]{2,1,0:T(8,128)(2,1)} custom-call(s32[4,32]{1,0:T(4,128)} %select_reduce_fusion.picks_ref, s32[4,2]{1,0:T(4,128)} %shard_map.99.starts_ref, bf16[4,2176,128]{2,1,0:T(8,128)(2,1)} %pad_maximum_fusion.1.query_ref.stat_ref, bf16[4,2176,128]{2,1,0:T(8,128)(2,1)} %pad_maximum_fusion.1.query_ref.stat_ref, ...), custom_call_target="tpu_custom_call" | custom-call | flops 3221225472 | tf_op jit(solution)/shard_map/pallas_call | solution.py:200
  279.6 8.2 %collective-permute-done.13.refs_7_ = bf16[128,1024]{1,0:T(8,128)(2,1)S(1)} collective-permute-done((bf16[128,1024]{1,0:T(8,128)(2,1)}, bf16[128,1024]{1,0:T(8,128)(2,1)S(1)}, u32[]{:S(2)}, u32[]{:S(2)}) %collective-permute-start.13) | collective-permute-done | bytes 262176 | tf_op jit(solution)/shard_map/ppermute | solution.py:284
  (111 shorter events, 31.8 us)
Async XLA Ops:
  8.9 104.2 %all-to-all-start = ((bf16[8,2048,128]{2,1,0:T(8,128)(2,1)}), bf16[8,2048,128]{2,1,0:T(8,128)(2,1)}, u32[]{:S(2)}, u32[]{:S(2)}) async-start(bf16[8,2048,128]{2,1,0:T(8,128)(2,1)} %get-tuple-element.20), calls=%async_computation | async-start | bytes 8388608 | tf_op jit(solution)/shard_map/all_to_all | solution.py:323
  20.3 75.8 %collective-permute-start.2 = (bf16[2176,128]{1,0:T(8,128)(2,1)}, bf16[2176,128]{1,0:T(8,128)(2,1)}, u32[]{:S(2)}, u32[]{:S(2)}) collective-permute-start(bf16[2176,128]{1,0:T(8,128)(2,1)} %get-tuple-element.19), channel_id=1, source_target_pairs={{0,3},{1,2},{2,1},{3,0},{4,7},{5,6},{6,5},{7,4},{8,11},{9,10},{10,... | collective-permute-start | bytes 1671176 | tf_op jit(solution)/shard_map/ppermute | solution.py:280
  22.1 87.9 %collective-permute-start.1 = (bf16[2176,128]{1,0:T(8,128)(2,1)}, bf16[2176,128]{1,0:T(8,128)(2,1)}, u32[]{:S(2)}, u32[]{:S(2)}) collective-permute-start(bf16[2176,128]{1,0:T(8,128)(2,1)} %get-tuple-element.18), channel_id=1, source_target_pairs={{0,2},{1,3},{2,0},{3,1},{4,6},{5,7},{6,4},{7,5},{8,10},{9,11},{10,... | collective-permute-start | bytes 1671176 | tf_op jit(solution)/shard_map/ppermute | solution.py:280
  22.5 87.5 %collective-permute-start = (bf16[2176,128]{1,0:T(8,128)(2,1)S(1)}, bf16[2176,128]{1,0:T(8,128)(2,1)}, u32[]{:S(2)}, u32[]{:S(2)}) collective-permute-start(bf16[2176,128]{1,0:T(8,128)(2,1)S(1)} %get-tuple-element.17), channel_id=1, source_target_pairs={{0,1},{1,0},{2,3},{3,2},{4,5},{5,4},{6,7},{7,6},{8,9},{9,8},{10,11... | collective-permute-start | bytes 1671176 | tf_op jit(solution)/shard_map/ppermute | solution.py:280
  24.5 88.6 %copy-start.27 = (s32[4,2]{1,0:T(4,128)}, s32[4,2]{1,0:T(4,128)S(1)}, u32[]{:S(2)}) copy-start(s32[4,2]{1,0:T(4,128)S(1)} %get-tuple-element.46.refs_0_) | copy-start | bytes 100
  113.7 92.3 %all-to-all-start.1 = ((bf16[8,1536,128]{2,1,0:T(8,128)(2,1)}), bf16[8,1536,128]{2,1,0:T(8,128)(2,1)}, u32[]{:S(2)}, u32[]{:S(2)}) async-start(bf16[8,1536,128]{2,1,0:T(8,128)(2,1)} %shard_map.90), calls=%async_computation.1 | async-start | bytes 6291456 | tf_op jit(solution)/shard_map/all_to_all | solution.py:323
  125.0 40.5 %collective-permute-start.3 = (bf16[2176,128]{1,0:T(8,128)(2,1)}, bf16[2176,128]{1,0:T(8,128)(2,1)S(1)}, u32[]{:S(2)}, u32[]{:S(2)}) collective-permute-start(bf16[2176,128]{1,0:T(8,128)(2,1)} %get-tuple-element.22), channel_id=1, source_target_pairs={{0,1},{1,0},{2,3},{3,2},{4,5},{5,4},{6,7},{7,6},{8,9},{9,8},{10,11... | collective-permute-start | bytes 1671176 | tf_op jit(solution)/shard_map/ppermute | solution.py:280
  125.4 56.6 %collective-permute-start.4 = (bf16[2176,128]{1,0:T(8,128)(2,1)S(1)}, bf16[2176,128]{1,0:T(8,128)(2,1)S(1)}, u32[]{:S(2)}, u32[]{:S(2)}) collective-permute-start(bf16[2176,128]{1,0:T(8,128)(2,1)S(1)} %get-tuple-element.23), channel_id=1, source_target_pairs={{0,2},{1,3},{2,0},{3,1},{4,6},{5,7},{6,4},{7,5},{8,10},{9,11},{10,... | collective-permute-start | bytes 1671176 | tf_op jit(solution)/shard_map/ppermute | solution.py:280
  127.0 68.2 %collective-permute-start.5 = (bf16[2176,128]{1,0:T(8,128)(2,1)S(1)}, bf16[2176,128]{1,0:T(8,128)(2,1)S(1)}, u32[]{:S(2)}, u32[]{:S(2)}) collective-permute-start(bf16[2176,128]{1,0:T(8,128)(2,1)S(1)} %get-tuple-element.24), channel_id=1, source_target_pairs={{0,3},{1,2},{2,1},{3,0},{4,7},{5,6},{6,5},{7,4},{8,11},{9,10},{10,... | collective-permute-start | bytes 1671176 | tf_op jit(solution)/shard_map/ppermute | solution.py:280
  165.5 30.6 %copy-start.20 = (bf16[2176,128]{1,0:T(8,128)(2,1)}, bf16[2176,128]{1,0:T(8,128)(2,1)S(1)}, u32[]{:S(2)}) copy-start(bf16[2176,128]{1,0:T(8,128)(2,1)S(1)} %collective-permute-done.3.refs_2_) | copy-start | bytes 1671172
  199.0 44.5 %collective-permute-start.6 = (bf16[128,1024]{1,0:T(8,128)(2,1)}, bf16[128,1024]{1,0:T(8,128)(2,1)S(1)}, u32[]{:S(2)}, u32[]{:S(2)}) collective-permute-start(bf16[128,1024]{1,0:T(8,128)(2,1)} %get-tuple-element.34), channel_id=1, source_target_pairs={{0,24},{1,25},{2,26},{3,27},{4,28},{5,29},{6,30},{7,31},{8,0},{9,1... | collective-permute-start | bytes 786440 | tf_op jit(solution)/shard_map/ppermute | solution.py:284
  201.5 42.1 %collective-permute-start.7 = (bf16[128,1024]{1,0:T(8,128)(2,1)S(1)}, bf16[128,1024]{1,0:T(8,128)(2,1)S(1)}, u32[]{:S(2)}, u32[]{:S(2)}) collective-permute-start(bf16[128,1024]{1,0:T(8,128)(2,1)S(1)} %get-tuple-element.33), channel_id=1, source_target_pairs={{0,25},{1,24},{2,27},{3,26},{4,29},{5,28},{6,31},{7,30},{8,1},{9,0... | collective-permute-start | bytes 786440 | tf_op jit(solution)/shard_map/ppermute | solution.py:284
  201.6 41.9 %collective-permute-start.8 = (bf16[128,1024]{1,0:T(8,128)(2,1)S(1)}, bf16[128,1024]{1,0:T(8,128)(2,1)S(1)}, u32[]{:S(2)}, u32[]{:S(2)}) collective-permute-start(bf16[128,1024]{1,0:T(8,128)(2,1)S(1)} %get-tuple-element.32), channel_id=1, source_target_pairs={{0,26},{1,27},{2,24},{3,25},{4,30},{5,31},{6,28},{7,29},{8,2},{9,3... | collective-permute-start | bytes 786440 | tf_op jit(solution)/shard_map/ppermute | solution.py:284
  203.0 40.6 %collective-permute-start.9 = (bf16[128,1024]{1,0:T(8,128)(2,1)S(1)}, bf16[128,1024]{1,0:T(8,128)(2,1)S(1)}, u32[]{:S(2)}, u32[]{:S(2)}) collective-permute-start(bf16[128,1024]{1,0:T(8,128)(2,1)S(1)} %get-tuple-element.31), channel_id=1, source_target_pairs={{0,27},{1,26},{2,25},{3,24},{4,31},{5,30},{6,29},{7,28},{8,3},{9,2... | collective-permute-start | bytes 786440 | tf_op jit(solution)/shard_map/ppermute | solution.py:284
  206.7 39.1 %all-to-all-start.2 = ((bf16[8,512,128]{2,1,0:T(8,128)(2,1)}), bf16[8,512,128]{2,1,0:T(8,128)(2,1)S(1)}, u32[]{:S(2)}, u32[]{:S(2)}) async-start(bf16[8,512,128]{2,1,0:T(8,128)(2,1)} %shard_map.93), calls=%async_computation.2 | async-start | bytes 2097152 | tf_op jit(solution)/shard_map/all_to_all | solution.py:323
  252.1 9.5 %collective-permute-start.10 = (bf16[128,1024]{1,0:T(8,128)(2,1)}, bf16[128,1024]{1,0:T(8,128)(2,1)S(1)}, u32[]{:S(2)}, u32[]{:S(2)}) collective-permute-start(bf16[128,1024]{1,0:T(8,128)(2,1)} %bitcast.73), channel_id=1, source_target_pairs={{0,24},{1,25},{2,26},{3,27},{4,28},{5,29},{6,30},{7,31},{8,0},{9,1... | collective-permute-start | bytes 786440 | tf_op jit(solution)/shard_map/ppermute | solution.py:284
  260.7 11.8 %collective-permute-start.11 = (bf16[128,1024]{1,0:T(8,128)(2,1)}, bf16[128,1024]{1,0:T(8,128)(2,1)S(1)}, u32[]{:S(2)}, u32[]{:S(2)}) collective-permute-start(bf16[128,1024]{1,0:T(8,128)(2,1)} %bitcast.72), channel_id=1, source_target_pairs={{0,25},{1,24},{2,27},{3,26},{4,29},{5,28},{6,31},{7,30},{8,1},{9,0... | collective-permute-start | bytes 786440 | tf_op jit(solution)/shard_map/ppermute | solution.py:284
  268.2 11.4 %collective-permute-start.12 = (bf16[128,1024]{1,0:T(8,128)(2,1)}, bf16[128,1024]{1,0:T(8,128)(2,1)S(1)}, u32[]{:S(2)}, u32[]{:S(2)}) collective-permute-start(bf16[128,1024]{1,0:T(8,128)(2,1)} %bitcast.71), channel_id=1, source_target_pairs={{0,26},{1,27},{2,24},{3,25},{4,30},{5,31},{6,28},{7,29},{8,2},{9,3... | collective-permute-start | bytes 786440 | tf_op jit(solution)/shard_map/ppermute | solution.py:284
  273.8 14.0 %copy-start.9 = (bf16[128,1024]{1,0:T(8,128)(2,1)S(1)}, bf16[128,1024]{1,0:T(8,128)(2,1)}, u32[]{:S(2)}) copy-start(bf16[128,1024]{1,0:T(8,128)(2,1)} %copy-done.8) | copy-start | bytes 786436
  273.8 14.0 %copy-start.11 = (bf16[128,1024]{1,0:T(8,128)(2,1)S(1)}, bf16[128,1024]{1,0:T(8,128)(2,1)}, u32[]{:S(2)}) copy-start(bf16[128,1024]{1,0:T(8,128)(2,1)} %copy-done.10) | copy-start | bytes 786436
  273.8 14.0 %copy-start.13 = (bf16[128,1024]{1,0:T(8,128)(2,1)S(1)}, bf16[128,1024]{1,0:T(8,128)(2,1)}, u32[]{:S(2)}) copy-start(bf16[128,1024]{1,0:T(8,128)(2,1)} %copy-done.12) | copy-start | bytes 786436
  273.8 14.0 %copy-start.15 = (bf16[128,1024]{1,0:T(8,128)(2,1)S(1)}, bf16[128,1024]{1,0:T(8,128)(2,1)}, u32[]{:S(2)}) copy-start(bf16[128,1024]{1,0:T(8,128)(2,1)} %copy-done.14) | copy-start | bytes 786436
  273.9 14.0 %copy-start.17 = (bf16[128,1024]{1,0:T(8,128)(2,1)S(1)}, bf16[128,1024]{1,0:T(8,128)(2,1)}, u32[]{:S(2)}) copy-start(bf16[128,1024]{1,0:T(8,128)(2,1)} %copy-done.16) | copy-start | bytes 786436
  278.5 9.4 %collective-permute-start.13 = (bf16[128,1024]{1,0:T(8,128)(2,1)}, bf16[128,1024]{1,0:T(8,128)(2,1)S(1)}, u32[]{:S(2)}, u32[]{:S(2)}) collective-permute-start(bf16[128,1024]{1,0:T(8,128)(2,1)} %bitcast.77), channel_id=1, source_target_pairs={{0,27},{1,26},{2,25},{3,24},{4,31},{5,30},{6,29},{7,28},{8,3},{9,2... | collective-permute-start | bytes 786440 | tf_op jit(solution)/shard_map/ppermute | solution.py:284
  (23 other events, 95.7 us)

commit v8 on v7

--- a/solution.py
+++ b/solution.py
@@ -105,10 +105,11 @@
     )(gates, at[None], grad_out, queries, mem_out, row_total)
 
 
-def attend_kernel(heads, dim, rows, scale, fresh, last, first, picks_ref, starts_ref, query_ref, stat_ref, memory_ref, *refs):
-    acc_in = None if fresh else refs[0]
-    out_ref, log_ref, delta_ref, total = refs[-4:]
-    tile = first + pl.program_id(0)
+def attend_kernel(heads, dim, rows, scale, tiles, fresh, last, picks_ref, starts_ref, *refs):
+    packed_refs, memory_ref = refs[:tiles], refs[tiles]
+    acc_in = None if fresh else refs[tiles + 1]
+    out_ref, query_ref, log_ref, delta_ref, total = refs[-5:]
+    tile = pl.program_id(0)
     blocks = memory_ref.shape[1] // 2
     count = heads * rows
 
@@ -117,7 +118,13 @@
     else:
         total[...] = acc_in[0]
 
-    stats = stat_ref[0].astype(jnp.float32)
+    for x, packed in enumerate(packed_refs):
+
+        @pl.when(tile == x)
+        def _(packed=packed):
+            query_ref[...] = packed[...]
+
+    stats = query_ref[2 * count:, :].astype(jnp.float32)
     for h in range(heads):
         for target, first in ((delta_ref, h), (log_ref, heads + h)):
             terms = [stats[:, first + 2 * part * heads:first + 2 * part * heads + 1] for part in range(PARTS)]
@@ -143,8 +150,8 @@
 
         def products(side):
             keys, values = side
-            scores = lax.dot_general(query_ref[0, :count, :], keys, NT, preferred_element_type=jnp.float32)
-            grad_probs = lax.dot_general(query_ref[0, count:, :], values, NT, preferred_element_type=jnp.float32)
+            scores = lax.dot_general(query_ref[:count, :], keys, NT, preferred_element_type=jnp.float32)
+            grad_probs = lax.dot_general(query_ref[count:2 * count, :], values, NT, preferred_element_type=jnp.float32)
             return scores, grad_probs
 
         ahead = products(sides[0])
@@ -181,40 +188,37 @@
         out_ref[0] = total[...]
 
 
-def attend(packed, memory, acc, picks, starts, heads, dim, scale, last, only=None):
-    tiles, span, _ = packed.shape
+def attend(packed, memory, acc, picks, starts, heads, dim, scale, last):
+    tiles = len(packed)
+    span = packed[0].shape[0]
     rows = span // (2 * heads + 1)
     fresh = acc is None
     width = heads * rows
     holders = memory.shape[0]
     memory = memory.reshape(holders, -1, BLOCK, dim)
-    steps, first = (tiles, 0) if only is None else (1, only)
-    acc_spec = pl.BlockSpec((1, width, dim), lambda t, *_: (first + t, 0, 0))
+    acc_spec = pl.BlockSpec((1, width, dim), lambda t, *_: (t, 0, 0))
     if last:
-        out_shape = jax.ShapeDtypeStruct((steps, rows, heads * dim), jnp.bfloat16)
+        out_shape = jax.ShapeDtypeStruct((tiles, rows, heads * dim), jnp.bfloat16)
         out_spec = pl.BlockSpec((1, rows, heads * dim), lambda t, *_: (t, 0, 0))
     else:
         out_shape = jax.ShapeDtypeStruct((tiles, width, dim), jnp.float32)
         out_spec = acc_spec
-    flops = steps * holders * (memory.shape[1] // 4) * BLOCK * width * dim * 6
-    return pl.pallas_call(
-        functools.partial(attend_kernel, heads, dim, rows, scale, fresh, last, first),
+    flops = tiles * holders * memory.shape[1] * (BLOCK // 4) * width * dim * 6
+    return pl.pallas_call(
+        functools.partial(attend_kernel, heads, dim, rows, scale, tiles, fresh, last),
         out_shape=out_shape,
         grid_spec=pltpu.PrefetchScalarGridSpec(
             num_scalar_prefetch=2,
-            grid=(steps,),
-            in_specs=[
-                pl.BlockSpec((1, 2 * width, dim), lambda t, *_: (first + t, 0, 0)),
-                pl.BlockSpec((1, rows, dim), lambda t, *_: (first + t, 2 * heads, 0)),
-                pl.BlockSpec(memory.shape, lambda t, *_: (0, 0, 0, 0)),
-            ]
+            grid=(tiles,),
+            in_specs=[pl.BlockSpec((span, dim), lambda t, *_: (0, 0))] * tiles
+            + [pl.BlockSpec(memory.shape, lambda t, *_: (0, 0, 0, 0))]
             + ([] if fresh else [acc_spec]),
             out_specs=out_spec,
-            scratch_shapes=[pltpu.VMEM((width, dim), jnp.float32)] * 3,
+            scratch_shapes=[pltpu.VMEM((span, dim), jnp.bfloat16)] + [pltpu.VMEM((width, dim), jnp.float32)] * 3,
         ),
         compiler_params=pltpu.CompilerParams(vmem_limit_bytes=VMEM_MOST),
         cost_estimate=pl.CostEstimate(flops=flops * 4, bytes_accessed=0, transcendentals=0),
-    )(picks, starts, packed, packed, memory, *([] if fresh else [acc]))
+    )(picks, starts, *packed, memory, *([] if fresh else [acc]))
 
 
 def assemble_kernel(own, group, at_ref, *refs):
@@ -283,8 +287,8 @@
         pairs = [(s * seq + p, ((s - 1) % sections) * seq + (p ^ step)) for s in range(sections) for p in range(seq)]
         return lax.ppermute(value, ("section", "seq"), pairs)
 
-    cut = (3 * blocks + 3) // 4
-    cuts = [[(0, blocks)]] * (own - 1) + [[(0, cut), (cut, blocks)]]
+    marks = [0, (blocks + 1) // 2, blocks - max(blocks // 8, 1), blocks]
+    cuts = [[(0, blocks)]] * (own - 1) + [list(zip(marks[:-1], marks[1:]))]
 
     def listed(i):
         mine = lax.dynamic_index_in_dim(retrieved[0], at * own + i, 0, keepdims=False)
@@ -315,7 +319,7 @@
 
     coming = queries_of(0)
     for i in range(own):
-        packed = jnp.stack(coming)
+        packed = coming
         pieces = []
         for _ in cuts[i]:
             piece = memories.pop(0)
@@ -328,19 +332,14 @@
         for j in range(len(pieces) - 1):
             acc = run(pieces[j], acc, starts=after(starts[j], *worked), last=False)
             worked = [acc]
-        results = []
         if i < own - 1:
             coming = queries_of(i + 1)
-            done = run(pieces[-1], acc, starts=after(starts[-1], *worked), last=True)
-            worked = [done]
+        ready = [] if i < own - 1 else gathered
+        done = run(pieces[-1], acc, starts=after(starts[-1], *worked, *ready), last=True)
+        worked = [done]
+        if i < own - 1:
             done = after(done, *coming)
-            results = [delivered(done[x], x) for x in range(group)]
-        else:
-            for x in range(group):
-                ready = gathered if x == 0 else results[x - 2:x - 1] if x > 1 else []
-                done = run(pieces[-1], acc, starts=after(starts[-1], *worked, *ready), last=True, only=x)
-                worked = [done]
-                results.append(delivered(done[0], x))
+        results = [delivered(done[x], x) for x in range(group)]
         gathered = gathered + results
     return assemble(gathered, at, own, group)[None]
 

time: 291 us -> 322 us (1.11)
  blocking collectives: 0 us -> 100 us
  waiting for transfers between devices: 119 us -> 61.3 us
  local copies, waits for them, and re-layouts: 16.1 us -> 9.4 us
  other arithmetic: 7.43 us -> 2.7 us
    all_to_all x0 -> x1, blocking collectives: none -> 100 us  [shards(): lax.all_to_all(piece, 'seq', split_axis=0, concat_axis=0, tiled=True)]
    ppermute x6, waiting for transfers between devices: 111 us -> 14.1 us  [swapped(): return lax.ppermute(value, 'seq', [(p, p ^ step) for p in range(seq)])]
    all_to_all x3, waiting for transfers between devices: 0.01 us -> 27.1 us  [shards(): lax.all_to_all(piece, 'seq', split_axis=0, concat_axis=0, tiled=True)]
    ppermute x8, waiting for transfers between devices: 8.24 us -> 20 us  [delivered(): return lax.ppermute(value, ('section', 'seq'), pairs)]
    unnamed x64 -> x45, local copies, waits for them, and re-layouts: 12.3 us -> 5.01 us
    another operation x2 -> x0, other arithmetic: 4.75 us -> none  [shards(): packed = jnp.stack(coming)]
    ppermute x8, starting transfers between devices: 14.9 us -> 11 us  [delivered(): return lax.ppermute(value, ('section', 'seq'), pairs)]
    pallas_call x6 -> x4, Pallas kernels: 90.5 us -> 91.7 us  [attend(): pl.pallas_call(functools.partial(attend_kernel, heads, dim, rows, scale,...]
  transfers between devices with their start and end apart: 17 -> 17, of which waited for: 5 -> 5; matrix products, arithmetic and copies ran while one was open for 5% -> 2% of each run, Pallas kernels for 35% -> 30%
where the time goes in v8:
time: 322 us; the launch traced here: 320 us
  Pallas kernels  114 us (35%)
  blocking collectives  100 us (31%)
  waiting for transfers between devices  61.3 us (19%)
  starting transfers between devices  32.1 us (10%)
  local copies, waits for them, and re-layouts  9.4 us (3%)
    all_to_all x1, blocking collectives, shards(): lax.all_to_all(piece, 'seq', split_axis=0, concat_axis=0, tiled=True)  100 us
    pallas_call x4, Pallas kernels, attend(): pl.pallas_call(functools.partial(attend_kernel, heads, dim, rows, scale,...  91.7 us
    all_to_all x3, waiting for transfers between devices, shards(): lax.all_to_all(piece, 'seq', split_axis=0, concat_axis=0, tiled=True)  27.1 us
    ppermute x8, waiting for transfers between devices, delivered(): return lax.ppermute(value, ('section', 'seq'), pairs)  20 us
    all_to_all x3, starting transfers between devices, shards(): lax.all_to_all(piece, 'seq', split_axis=0, concat_axis=0, tiled=True)  15.2 us
    ppermute x6, waiting for transfers between devices, swapped(): return lax.ppermute(value, 'seq', [(p, p ^ step) for p in range(seq)])  14.1 us
    ppermute x8, starting transfers between devices, delivered(): return lax.ppermute(value, ('section', 'seq'), pairs)  11 us
    pallas_call x2, Pallas kernels, prepare(): pl.pallas_call(functools.partial(prepare_kernel, heads, dim, scale, own,...  9.41 us
  transfers between devices with their start and end apart: 17, of which 5 were waited for; matrix products, arithmetic and copies ran while one was open for 2% of the time, Pallas kernels for 30%

profile of v8, /device:TPU:0, one launch (start us, length us, event | category | flops | bytes accessed | tf_op | source)
XLA Modules:
  0.0 320.4 jit_solution(6952116831557043061)
XLA Ops:
  0.0 6.0 %shard_map.84 = (bf16[8,2048,128]{2,1,0:T(8,128)(2,1)}, bf16[8,1024,128]{2,1,0:T(8,128)(2,1)S(1)}, bf16[8,768,128]{2,1,0:T(8,128)(2,1)S(1)}, bf16[8,256,128]{2,1,0:T(8,128)(2,1)S(1)}) custom-call(bf16[1024,1024]{1,0:T(8,128)(2,1)} %bitcast.59, bf16[1024,1024]{1,0:T(8,128)(2,1)} %bitcast.60), custom_call_target="tpu_custom_call" | custom-call | bytes 8388608 | tf_op jit(solution)/shard_map/pallas_call | solution.py:51
  6.0 100.5 %all_to_all.20.refs_1_ = bf16[8,2048,128]{2,1,0:T(8,128)(2,1)} all-to-all(bf16[8,2048,128]{2,1,0:T(8,128)(2,1)} %get-tuple-element.21), channel_id=1, replica_groups=mesh['section'=4,'seq'=8] {'seq'}, dimensions={0} | all-to-all | bytes 8388608 | tf_op jit(solution)/shard_map/all_to_all | solution.py:327
  107.1 4.5 %all-to-all-start.1 = ((bf16[8,1024,128]{2,1,0:T(8,128)(2,1)}), bf16[8,1024,128]{2,1,0:T(8,128)(2,1)}, u32[]{:S(2)}, u32[]{:S(2)}) async-start(bf16[8,1024,128]{2,1,0:T(8,128)(2,1)} %shard_map.90), calls=%async_computation.1 | async-start | bytes 4194304 | tf_op jit(solution)/shard_map/all_to_all | solution.py:327
  111.8 4.6 %shard_map.83 = (bf16[2176,128]{1,0:T(8,128)(2,1)S(1)}, bf16[2176,128]{1,0:T(8,128)(2,1)}, bf16[2176,128]{1,0:T(8,128)(2,1)S(1)}, bf16[2176,128]{1,0:T(8,128)(2,1)S(1)}) custom-call(f32[64]{0:T(128)S(1)} %divide_bitcast_fusion.gate_ref.refs_0_, s32[1]{0:T(128)} %bitcast.at_ref, bf16[128,8192]{1,0:T(8,128)(2,1)S(1)} %bitcast.50, bf16[128,8192]{1,0:T(8,128)(2,1)} %bitcast.55, ...), custom_call_target="tpu_custom_call" | custom-call | flops 4194304 | bytes 6291456 | tf_op jit(solution)/shard_map/pallas_call | solution.py:94
  117.6 1.7 collective-permute-start.1
  125.1 4.8 %shard_map.87 = (bf16[2176,128]{1,0:T(8,128)(2,1)S(1)}, bf16[2176,128]{1,0:T(8,128)(2,1)}, bf16[2176,128]{1,0:T(8,128)(2,1)}, bf16[2176,128]{1,0:T(8,128)(2,1)S(1)}) custom-call(f32[64]{0:T(128)S(1)} %copy-done.14, s32[1]{0:T(128)} %bitcast.at_ref, bf16[128,8192]{1,0:T(8,128)(2,1)S(1)} %bitcast.51, bf16[128,8192]{1,0:T(8,128)(2,1)} %bitcast.56, ...), custom_call_target="tpu_custom_call" | custom-call | flops 4194304 | bytes 6291456 | tf_op jit(solution)/shard_map/pallas_call | solution.py:94
  132.0 1.7 collective-permute-start.4
  133.7 27.1 %all-to-all-done.1.refs_1_ = bf16[8,1024,128]{2,1,0:T(8,128)(2,1)} async-done(((bf16[8,1024,128]{2,1,0:T(8,128)(2,1)}), bf16[8,1024,128]{2,1,0:T(8,128)(2,1)}, u32[]{:S(2)}, u32[]{:S(2)}) %all-to-all-start.1) | async-done | bytes 2097184 | tf_op jit(solution)/shard_map/all_to_all | solution.py:327
  161.5 4.4 %all-to-all-start.2 = ((bf16[8,768,128]{2,1,0:T(8,128)(2,1)}), bf16[8,768,128]{2,1,0:T(8,128)(2,1)}, u32[]{:S(2)}, u32[]{:S(2)}) async-start(bf16[8,768,128]{2,1,0:T(8,128)(2,1)} %shard_map.93), calls=%async_computation.2 | async-start | bytes 3145728 | tf_op jit(solution)/shard_map/all_to_all | solution.py:327
  165.9 1.7 collective-permute-start.5
  167.7 6.4 %collective-permute-done.2.refs_3_ = bf16[2176,128]{1,0:T(8,128)(2,1)} collective-permute-done((bf16[2176,128]{1,0:T(8,128)(2,1)S(1)}, bf16[2176,128]{1,0:T(8,128)(2,1)}, u32[]{:S(2)}, u32[]{:S(2)}) %collective-permute-start.2) | collective-permute-done | bytes 557088 | tf_op jit(solution)/shard_map/ppermute | solution.py:284
  174.1 38.6 %shard_map.85.refs_0_.refs_1_ = bf16[4,128,1024]{2,1,0:T(8,128)(2,1)} custom-call(s32[4,32]{1,0:T(4,128)} %select_reduce_fusion.1.picks_ref, s32[4,2]{1,0:T(4,128)} %shard_map.82.starts_ref, bf16[2176,128]{1,0:T(8,128)(2,1)} %copy-done.15, bf16[2176,128]{1,0:T(8,128)(2,1)} %collective-permute-done.refs_1_, bf16[2176,128]{1,0:T(8,128)(2,1)} %collective-permute-done.1.refs_2_, ...), custom_call_target="tpu_custom_call" | custom-call | flops 51539607552 | tf_op jit(solution)/shard_map/pallas_call | solution.py:207
  213.4 7.7 %collective-permute-done.5.refs_4_.refs_3_ = bf16[2176,128]{1,0:T(8,128)(2,1)} collective-permute-done((bf16[2176,128]{1,0:T(8,128)(2,1)S(1)}, bf16[2176,128]{1,0:T(8,128)(2,1)}, u32[]{:S(2)}, u32[]{:S(2)}) %collective-permute-start.5) | collective-permute-done | bytes 557088 | tf_op jit(solution)/shard_map/ppermute | solution.py:284
  223.1 2.5 collective-permute-start.6
  225.8 1.4 collective-permute-start.8
  228.5 24.7 %shard_map.91.refs_1_.refs_5_ = f32[4,1024,128]{2,1,0:T(8,128)} custom-call(s32[4,32]{1,0:T(4,128)} %select_reduce_fusion.picks_ref, s32[4,2]{1,0:T(4,128)} %shard_map.89.starts_ref, bf16[2176,128]{1,0:T(8,128)(2,1)} %copy-done.12, bf16[2176,128]{1,0:T(8,128)(2,1)} %copy-done.18, bf16[2176,128]{1,0:T(8,128)(2,1)} %collective-permute-done.4.refs_3_.refs_2_, ...), custom_call_target="tpu_custom_call" | custom-call | flops 25769803776 | tf_op jit(solution)/shard_map/pallas_call | solution.py:207
  254.5 6.3 %all-to-all-start.3 = ((bf16[8,256,128]{2,1,0:T(8,128)(2,1)}), bf16[8,256,128]{2,1,0:T(8,128)(2,1)S(1)}, u32[]{:S(2)}, u32[]{:S(2)}) async-start(bf16[8,256,128]{2,1,0:T(8,128)(2,1)} %shard_map.96), calls=%async_computation.3 | async-start | bytes 1048576 | tf_op jit(solution)/shard_map/all_to_all | solution.py:327
  260.8 19.3 %shard_map.94.refs_1_.refs_5_ = f32[4,1024,128]{2,1,0:T(8,128)} custom-call(s32[4,32]{1,0:T(4,128)} %select_reduce_fusion.picks_ref, s32[4,2]{1,0:T(4,128)} %shard_map.92.starts_ref, bf16[2176,128]{1,0:T(8,128)(2,1)} %copy-done.12, bf16[2176,128]{1,0:T(8,128)(2,1)} %copy-done.18, bf16[2176,128]{1,0:T(8,128)(2,1)} %collective-permute-done.4.refs_3_.refs_2_, ...), custom_call_target="tpu_custom_call" | custom-call | flops 19327352832 | tf_op jit(solution)/shard_map/pallas_call | solution.py:207
  282.7 9.1 %shard_map.97 = bf16[4,128,1024]{2,1,0:T(8,128)(2,1)} custom-call(s32[4,32]{1,0:T(4,128)} %select_reduce_fusion.picks_ref, s32[4,2]{1,0:T(4,128)} %shard_map.95.starts_ref, bf16[2176,128]{1,0:T(8,128)(2,1)} %copy-done.12, bf16[2176,128]{1,0:T(8,128)(2,1)} %copy-done.18, bf16[2176,128]{1,0:T(8,128)(2,1)} %collective-permute-done.4.refs_3_.refs_2_, ...), custom_call_target="tpu_custom_call" | custom-call | flops 6442450944 | tf_op jit(solution)/shard_map/pallas_call | solution.py:207
  293.2 2.4 collective-permute-start.10
  295.5 3.3 %collective-permute-start.12 = (bf16[128,1024]{1,0:T(8,128)(2,1)S(1)}, bf16[128,1024]{1,0:T(8,128)(2,1)S(1)}, u32[]{:S(2)}, u32[]{:S(2)}) collective-permute-start(bf16[128,1024]{1,0:T(8,128)(2,1)S(1)} %get-tuple-element.37), channel_id=1, source_target_pairs={{0,26},{1,27},{2,24},{3,25},{4,30},{5,31},{6,28},{7,29},{8,2},{9,3... | collective-permute-start | bytes 786440 | tf_op jit(solution)/shard_map/ppermute | solution.py:288
  298.9 14.8 %collective-permute-done.10.refs_4_ = bf16[128,1024]{1,0:T(8,128)(2,1)S(1)} collective-permute-done((bf16[128,1024]{1,0:T(8,128)(2,1)S(1)}, bf16[128,1024]{1,0:T(8,128)(2,1)S(1)}, u32[]{:S(2)}, u32[]{:S(2)}) %collective-permute-start.10) | collective-permute-done | bytes 262176 | tf_op jit(solution)/shard_map/ppermute | solution.py:288
  313.6 5.2 %collective-permute-done.11.refs_5_ = bf16[128,1024]{1,0:T(8,128)(2,1)S(1)} collective-permute-done((bf16[128,1024]{1,0:T(8,128)(2,1)S(1)}, bf16[128,1024]{1,0:T(8,128)(2,1)S(1)}, u32[]{:S(2)}, u32[]{:S(2)}) %collective-permute-start.11) | collective-permute-done | bytes 262176 | tf_op jit(solution)/shard_map/ppermute | solution.py:288
  318.9 1.5 shard_map.98
  (90 shorter events, 20.0 us)
Async XLA Ops:
  6.0 100.5 %copy-start.1 = (bf16[8,1024,128]{2,1,0:T(8,128)(2,1)}, bf16[8,1024,128]{2,1,0:T(8,128)(2,1)S(1)}, u32[]{:S(2)}) copy-start(bf16[8,1024,128]{2,1,0:T(8,128)(2,1)S(1)} %get-tuple-element.26.refs_0_) | copy-start | bytes 6291460
  6.0 100.5 %copy-start.2 = (bf16[8,768,128]{2,1,0:T(8,128)(2,1)}, bf16[8,768,128]{2,1,0:T(8,128)(2,1)S(1)}, u32[]{:S(2)}) copy-start(bf16[8,768,128]{2,1,0:T(8,128)(2,1)S(1)} %get-tuple-element.27.refs_0_) | copy-start | bytes 4718596
  6.0 100.5 %copy-start.3 = (bf16[8,256,128]{2,1,0:T(8,128)(2,1)}, bf16[8,256,128]{2,1,0:T(8,128)(2,1)S(1)}, u32[]{:S(2)}) copy-start(bf16[8,256,128]{2,1,0:T(8,128)(2,1)S(1)} %get-tuple-element.28.refs_0_) | copy-start | bytes 1572868
  107.1 53.7 %all-to-all-start.1 = ((bf16[8,1024,128]{2,1,0:T(8,128)(2,1)}), bf16[8,1024,128]{2,1,0:T(8,128)(2,1)}, u32[]{:S(2)}, u32[]{:S(2)}) async-start(bf16[8,1024,128]{2,1,0:T(8,128)(2,1)} %shard_map.90), calls=%async_computation.1 | async-start | bytes 4194304 | tf_op jit(solution)/shard_map/all_to_all | solution.py:327
  117.3 48.6 %collective-permute-start = (bf16[2176,128]{1,0:T(8,128)(2,1)}, bf16[2176,128]{1,0:T(8,128)(2,1)}, u32[]{:S(2)}, u32[]{:S(2)}) collective-permute-start(bf16[2176,128]{1,0:T(8,128)(2,1)} %get-tuple-element.18), channel_id=1, source_target_pairs={{0,1},{1,0},{2,3},{3,2},{4,5},{5,4},{6,7},{7,6},{8,9},{9,8},{10,11... | collective-permute-start | bytes 1671176 | tf_op jit(solution)/shard_map/ppermute | solution.py:284
  117.6 50.0 %collective-permute-start.1 = (bf16[2176,128]{1,0:T(8,128)(2,1)S(1)}, bf16[2176,128]{1,0:T(8,128)(2,1)}, u32[]{:S(2)}, u32[]{:S(2)}) collective-permute-start(bf16[2176,128]{1,0:T(8,128)(2,1)S(1)} %get-tuple-element.19), channel_id=1, source_target_pairs={{0,2},{1,3},{2,0},{3,1},{4,6},{5,7},{6,4},{7,5},{8,10},{9,11},{10,... | collective-permute-start | bytes 1671176 | tf_op jit(solution)/shard_map/ppermute | solution.py:284
  119.3 54.7 %collective-permute-start.2 = (bf16[2176,128]{1,0:T(8,128)(2,1)S(1)}, bf16[2176,128]{1,0:T(8,128)(2,1)}, u32[]{:S(2)}, u32[]{:S(2)}) collective-permute-start(bf16[2176,128]{1,0:T(8,128)(2,1)S(1)} %get-tuple-element.20), channel_id=1, source_target_pairs={{0,3},{1,2},{2,1},{3,0},{4,7},{5,6},{6,5},{7,4},{8,11},{9,10},{10,... | collective-permute-start | bytes 1671176 | tf_op jit(solution)/shard_map/ppermute | solution.py:284
  131.6 81.8 %collective-permute-start.3 = (bf16[2176,128]{1,0:T(8,128)(2,1)}, bf16[2176,128]{1,0:T(8,128)(2,1)S(1)}, u32[]{:S(2)}, u32[]{:S(2)}) collective-permute-start(bf16[2176,128]{1,0:T(8,128)(2,1)} %get-tuple-element.23), channel_id=1, source_target_pairs={{0,1},{1,0},{2,3},{3,2},{4,5},{5,4},{6,7},{7,6},{8,9},{9,8},{10,11... | collective-permute-start | bytes 1671176 | tf_op jit(solution)/shard_map/ppermute | solution.py:284
  132.0 81.4 %collective-permute-start.4 = (bf16[2176,128]{1,0:T(8,128)(2,1)}, bf16[2176,128]{1,0:T(8,128)(2,1)}, u32[]{:S(2)}, u32[]{:S(2)}) collective-permute-start(bf16[2176,128]{1,0:T(8,128)(2,1)} %get-tuple-element.24), channel_id=1, source_target_pairs={{0,2},{1,3},{2,0},{3,1},{4,6},{5,7},{6,4},{7,5},{8,10},{9,11},{10,... | collective-permute-start | bytes 1671176 | tf_op jit(solution)/shard_map/ppermute | solution.py:284
  161.5 92.4 %all-to-all-start.2 = ((bf16[8,768,128]{2,1,0:T(8,128)(2,1)}), bf16[8,768,128]{2,1,0:T(8,128)(2,1)}, u32[]{:S(2)}, u32[]{:S(2)}) async-start(bf16[8,768,128]{2,1,0:T(8,128)(2,1)} %shard_map.93), calls=%async_computation.2 | async-start | bytes 3145728 | tf_op jit(solution)/shard_map/all_to_all | solution.py:327
  165.9 55.2 %collective-permute-start.5 = (bf16[2176,128]{1,0:T(8,128)(2,1)S(1)}, bf16[2176,128]{1,0:T(8,128)(2,1)}, u32[]{:S(2)}, u32[]{:S(2)}) collective-permute-start(bf16[2176,128]{1,0:T(8,128)(2,1)S(1)} %copy-done.17), channel_id=1, source_target_pairs={{0,3},{1,2},{2,1},{3,0},{4,7},{5,6},{6,5},{7,4},{8,11},{9,10},{10,... | collective-permute-start | bytes 1671176 | tf_op jit(solution)/shard_map/ppermute | solution.py:284
  223.1 57.0 %collective-permute-start.6 = (bf16[128,1024]{1,0:T(8,128)(2,1)S(1)}, bf16[128,1024]{1,0:T(8,128)(2,1)S(1)}, u32[]{:S(2)}, u32[]{:S(2)}) collective-permute-start(bf16[128,1024]{1,0:T(8,128)(2,1)S(1)} %get-tuple-element.43), channel_id=1, source_target_pairs={{0,24},{1,25},{2,26},{3,27},{4,28},{5,29},{6,30},{7,31},{8,0},{9,1... | collective-permute-start | bytes 786440 | tf_op jit(solution)/shard_map/ppermute | solution.py:288
  225.6 54.5 %collective-permute-start.7 = (bf16[128,1024]{1,0:T(8,128)(2,1)S(1)}, bf16[128,1024]{1,0:T(8,128)(2,1)S(1)}, u32[]{:S(2)}, u32[]{:S(2)}) collective-permute-start(bf16[128,1024]{1,0:T(8,128)(2,1)S(1)} %get-tuple-element.42), channel_id=1, source_target_pairs={{0,25},{1,24},{2,27},{3,26},{4,29},{5,28},{6,31},{7,30},{8,1},{9,0... | collective-permute-start | bytes 786440 | tf_op jit(solution)/shard_map/ppermute | solution.py:288
  225.8 54.3 %collective-permute-start.8 = (bf16[128,1024]{1,0:T(8,128)(2,1)S(1)}, bf16[128,1024]{1,0:T(8,128)(2,1)S(1)}, u32[]{:S(2)}, u32[]{:S(2)}) collective-permute-start(bf16[128,1024]{1,0:T(8,128)(2,1)S(1)} %get-tuple-element.41), channel_id=1, source_target_pairs={{0,26},{1,27},{2,24},{3,25},{4,30},{5,31},{6,28},{7,29},{8,2},{9,3... | collective-permute-start | bytes 786440 | tf_op jit(solution)/shard_map/ppermute | solution.py:288
  227.2 53.0 %collective-permute-start.9 = (bf16[128,1024]{1,0:T(8,128)(2,1)S(1)}, bf16[128,1024]{1,0:T(8,128)(2,1)S(1)}, u32[]{:S(2)}, u32[]{:S(2)}) collective-permute-start(bf16[128,1024]{1,0:T(8,128)(2,1)S(1)} %get-tuple-element.40), channel_id=1, source_target_pairs={{0,27},{1,26},{2,25},{3,24},{4,31},{5,30},{6,29},{7,28},{8,3},{9,2... | collective-permute-start | bytes 786440 | tf_op jit(solution)/shard_map/ppermute | solution.py:288
  254.5 27.3 %all-to-all-start.3 = ((bf16[8,256,128]{2,1,0:T(8,128)(2,1)}), bf16[8,256,128]{2,1,0:T(8,128)(2,1)S(1)}, u32[]{:S(2)}, u32[]{:S(2)}) async-start(bf16[8,256,128]{2,1,0:T(8,128)(2,1)} %shard_map.96), calls=%async_computation.3 | async-start | bytes 1048576 | tf_op jit(solution)/shard_map/all_to_all | solution.py:327
  291.8 27.1 %copy-start.5 = (bf16[128,1024]{1,0:T(8,128)(2,1)S(1)}, bf16[128,1024]{1,0:T(8,128)(2,1)}, u32[]{:S(2)}) copy-start(bf16[128,1024]{1,0:T(8,128)(2,1)} %copy-done.4) | copy-start | bytes 786436
  291.8 27.1 %copy-start.7 = (bf16[128,1024]{1,0:T(8,128)(2,1)S(1)}, bf16[128,1024]{1,0:T(8,128)(2,1)}, u32[]{:S(2)}) copy-start(bf16[128,1024]{1,0:T(8,128)(2,1)} %copy-done.6) | copy-start | bytes 786436
  291.8 27.1 %copy-start.9 = (bf16[128,1024]{1,0:T(8,128)(2,1)S(1)}, bf16[128,1024]{1,0:T(8,128)(2,1)}, u32[]{:S(2)}) copy-start(bf16[128,1024]{1,0:T(8,128)(2,1)} %copy-done.8) | copy-start | bytes 786436
  291.8 27.1 %copy-start.11 = (bf16[128,1024]{1,0:T(8,128)(2,1)S(1)}, bf16[128,1024]{1,0:T(8,128)(2,1)}, u32[]{:S(2)}) copy-start(bf16[128,1024]{1,0:T(8,128)(2,1)} %copy-done.10) | copy-start | bytes 786436
  293.2 20.5 %collective-permute-start.10 = (bf16[128,1024]{1,0:T(8,128)(2,1)S(1)}, bf16[128,1024]{1,0:T(8,128)(2,1)S(1)}, u32[]{:S(2)}, u32[]{:S(2)}) collective-permute-start(bf16[128,1024]{1,0:T(8,128)(2,1)S(1)} %get-tuple-element.39), channel_id=1, source_target_pairs={{0,24},{1,25},{2,26},{3,27},{4,28},{5,29},{6,30},{7,31},{8,0},{9,1... | collective-permute-start | bytes 786440 | tf_op jit(solution)/shard_map/ppermute | solution.py:288
  295.5 23.4 %collective-permute-start.11 = (bf16[128,1024]{1,0:T(8,128)(2,1)S(1)}, bf16[128,1024]{1,0:T(8,128)(2,1)S(1)}, u32[]{:S(2)}, u32[]{:S(2)}) collective-permute-start(bf16[128,1024]{1,0:T(8,128)(2,1)S(1)} %get-tuple-element.38), channel_id=1, source_target_pairs={{0,25},{1,24},{2,27},{3,26},{4,29},{5,28},{6,31},{7,30},{8,1},{9,0... | collective-permute-start | bytes 786440 | tf_op jit(solution)/shard_map/ppermute | solution.py:288
  295.5 23.4 %collective-permute-start.12 = (bf16[128,1024]{1,0:T(8,128)(2,1)S(1)}, bf16[128,1024]{1,0:T(8,128)(2,1)S(1)}, u32[]{:S(2)}, u32[]{:S(2)}) collective-permute-start(bf16[128,1024]{1,0:T(8,128)(2,1)S(1)} %get-tuple-element.37), channel_id=1, source_target_pairs={{0,26},{1,27},{2,24},{3,25},{4,30},{5,31},{6,28},{7,29},{8,2},{9,3... | collective-permute-start | bytes 786440 | tf_op jit(solution)/shard_map/ppermute | solution.py:288
  298.9 20.0 %collective-permute-start.13 = (bf16[128,1024]{1,0:T(8,128)(2,1)S(1)}, bf16[128,1024]{1,0:T(8,128)(2,1)S(1)}, u32[]{:S(2)}, u32[]{:S(2)}) collective-permute-start(bf16[128,1024]{1,0:T(8,128)(2,1)S(1)} %get-tuple-element.36), channel_id=1, source_target_pairs={{0,27},{1,26},{2,25},{3,24},{4,31},{5,30},{6,29},{7,28},{8,3},{9,2... | collective-permute-start | bytes 786440 | tf_op jit(solution)/shard_map/ppermute | solution.py:288
  (15 other events, 37.9 us)

commit v9 on v8

--- a/solution.py
+++ b/solution.py
@@ -108,7 +108,7 @@
 def attend_kernel(heads, dim, rows, scale, tiles, fresh, last, picks_ref, starts_ref, *refs):
     packed_refs, memory_ref = refs[:tiles], refs[tiles]
     acc_in = None if fresh else refs[tiles + 1]
-    out_ref, query_ref, log_ref, delta_ref, total = refs[-5:]
+    out_refs, (query_ref, log_ref, delta_ref, total) = refs[tiles + (1 if fresh else 2):-4], refs[-4:]
     tile = pl.program_id(0)
     blocks = memory_ref.shape[1] // 2
     count = heads * rows
@@ -124,11 +124,13 @@
         def _(packed=packed):
             query_ref[...] = packed[...]
 
-    stats = query_ref[2 * count:, :].astype(jnp.float32)
+    terms = query_ref[2 * count:, :].astype(jnp.float32)
+    stats = terms
+    for part in range(1, PARTS):
+        stats = stats + pltpu.roll(terms, dim - 2 * part * heads, 1)
     for h in range(heads):
-        for target, first in ((delta_ref, h), (log_ref, heads + h)):
-            terms = [stats[:, first + 2 * part * heads:first + 2 * part * heads + 1] for part in range(PARTS)]
-            target[h * rows:(h + 1) * rows, :] = jnp.broadcast_to(terms[0] + terms[1] + terms[2], (rows, dim))
+        for target, lane in ((delta_ref, h), (log_ref, heads + h)):
+            target[h * rows:(h + 1) * rows, :] = jnp.broadcast_to(stats[:, lane:lane + 1], (rows, dim))
 
     low = starts_ref[tile, 0]
     high = starts_ref[tile, 1]
@@ -181,11 +183,15 @@
     lax.fori_loop(0, full, many, 0)
     lax.fori_loop(0, (high - low - STEP * full + 1) // 2, few, 0)
 
-    if last:
-        for h in range(heads):
-            out_ref[0, :, h * dim:(h + 1) * dim] = total[h * rows:(h + 1) * rows, :].astype(jnp.bfloat16)
-    else:
-        out_ref[0] = total[...]
+    if not last:
+        out_refs[0][0] = total[...]
+        return
+    for x, out_ref in enumerate(out_refs):
+
+        @pl.when(tile == x)
+        def _(out_ref=out_ref):
+            for h in range(heads):
+                out_ref[:, h * dim:(h + 1) * dim] = total[h * rows:(h + 1) * rows, :].astype(jnp.bfloat16)
 
 
 def attend(packed, memory, acc, picks, starts, heads, dim, scale, last):
@@ -198,8 +204,8 @@
     memory = memory.reshape(holders, -1, BLOCK, dim)
     acc_spec = pl.BlockSpec((1, width, dim), lambda t, *_: (t, 0, 0))
     if last:
-        out_shape = jax.ShapeDtypeStruct((tiles, rows, heads * dim), jnp.bfloat16)
-        out_spec = pl.BlockSpec((1, rows, heads * dim), lambda t, *_: (t, 0, 0))
+        out_shape = [jax.ShapeDtypeStruct((rows, heads * dim), jnp.bfloat16)] * tiles
+        out_spec = [pl.BlockSpec((rows, heads * dim), lambda t, *_: (0, 0))] * tiles
     else:
         out_shape = jax.ShapeDtypeStruct((tiles, width, dim), jnp.float32)
         out_spec = acc_spec
@@ -287,8 +293,8 @@
         pairs = [(s * seq + p, ((s - 1) % sections) * seq + (p ^ step)) for s in range(sections) for p in range(seq)]
         return lax.ppermute(value, ("section", "seq"), pairs)
 
-    marks = [0, (blocks + 1) // 2, blocks - max(blocks // 8, 1), blocks]
-    cuts = [[(0, blocks)]] * (own - 1) + [list(zip(marks[:-1], marks[1:]))]
+    cut = (3 * blocks + 3) // 4
+    cuts = [[(0, blocks)]] * (own - 1) + [[(0, cut), (cut, blocks)]]
 
     def listed(i):
         mine = lax.dynamic_index_in_dim(retrieved[0], at * own + i, 0, keepdims=False)
@@ -310,7 +316,7 @@
 
     gates = jax.nn.sigmoid(gate_logit[0])
     memories = list(pack(mem_keys[0], mem_values[0], seq, own, group, dim, cuts))
-    gathered, worked, latest = [], [], None
+    gathered, worked, latest, held = [], [], None, []
 
     def queries_of(i):
         opened = gates if latest is None else after(gates, latest)
@@ -323,9 +329,10 @@
         pieces = []
         for _ in cuts[i]:
             piece = memories.pop(0)
-            piece = piece if latest is None else after(piece, latest)
+            piece = piece if latest is None else after(piece, latest, *held)
             latest = lax.all_to_all(piece, "seq", split_axis=0, concat_axis=0, tiled=True)
             pieces.append(latest)
+            held = packed
         picks, starts = listed(i)
         run = functools.partial(attend, packed, picks=picks, heads=heads, dim=dim, scale=scale)
         acc = None
@@ -336,9 +343,9 @@
             coming = queries_of(i + 1)
         ready = [] if i < own - 1 else gathered
         done = run(pieces[-1], acc, starts=after(starts[-1], *worked, *ready), last=True)
-        worked = [done]
+        worked = done[:1]
         if i < own - 1:
-            done = after(done, *coming)
+            done = [after(result, *coming) for result in done]
         results = [delivered(done[x], x) for x in range(group)]
         gathered = gathered + results
     return assemble(gathered, at, own, group)[None]

time: 322 us -> 284 us (0.88)
  blocking collectives: 100 us -> 0 us
  waiting for transfers between devices: 61.3 us -> 129 us
  Pallas kernels: 114 us -> 108 us
    all_to_all x1 -> x0, blocking collectives: 100 us -> none  [shards(): lax.all_to_all(piece, 'seq', split_axis=0, concat_axis=0, tiled=True)]
    ppermute x6, waiting for transfers between devices: 14.1 us -> 109 us  [swapped(): return lax.ppermute(value, 'seq', [(p, p ^ step) for p in range(seq)])]
    all_to_all x3, waiting for transfers between devices: 27.1 us -> 1.79 us  [shards(): lax.all_to_all(piece, 'seq', split_axis=0, concat_axis=0, tiled=True)]
    pallas_call x4 -> x3, Pallas kernels: 91.7 us -> 85.9 us  [attend(): pl.pallas_call(functools.partial(attend_kernel, heads, dim, rows, scale,...]
    unnamed x45 -> x43, local copies, waits for them, and re-layouts: 5.01 us -> 8.53 us
  transfers between devices with their start and end apart: 17 -> 17, of which waited for: 5 -> 7; matrix products, arithmetic and copies ran while one was open for 2% -> 2% of each run, Pallas kernels for 30% -> 30%
where the time goes in v9:
time: 284 us; the launch traced here: 282 us
  waiting for transfers between devices  129 us (45%)
  Pallas kernels  108 us (38%)
  starting transfers between devices  32 us (11%)
  local copies, waits for them, and re-layouts  10.3 us (4%)
    ppermute x6, waiting for transfers between devices, swapped(): return lax.ppermute(value, 'seq', [(p, p ^ step) for p in range(seq)])  109 us
    pallas_call x3, Pallas kernels, attend(): pl.pallas_call(functools.partial(attend_kernel, heads, dim, rows, scale,...  85.9 us
    ppermute x8, waiting for transfers between devices, delivered(): return lax.ppermute(value, ('section', 'seq'), pairs)  18.6 us
    all_to_all x3, starting transfers between devices, shards(): lax.all_to_all(piece, 'seq', split_axis=0, concat_axis=0, tiled=True)  14.8 us
    ppermute x8, starting transfers between devices, delivered(): return lax.ppermute(value, ('section', 'seq'), pairs)  12.9 us
    pallas_call x2, Pallas kernels, prepare(): pl.pallas_call(functools.partial(prepare_kernel, heads, dim, scale, own,...  9.24 us
    unnamed x43, local copies, waits for them, and re-layouts  8.53 us
    pallas_call x10, Pallas kernels, after(): pl.pallas_call(lambda *refs: None, out_shape=jax.ShapeDtypeStruct(value.s...  6.41 us
  transfers between devices with their start and end apart: 17, of which 7 were waited for; matrix products, arithmetic and copies ran while one was open for 2% of the time, Pallas kernels for 30%

profile of v9, /device:TPU:0, one launch (start us, length us, event | category | flops | bytes accessed | tf_op | source)
XLA Modules:
  0.0 282.3 jit_solution(17583207814662416317)
XLA Ops:
  0.0 1.6 copy-done.3
  1.6 1.6 copy-done.4
  3.2 4.8 %shard_map.84 = (bf16[8,2048,128]{2,1,0:T(8,128)(2,1)}, bf16[8,1536,128]{2,1,0:T(8,128)(2,1)}, bf16[8,512,128]{2,1,0:T(8,128)(2,1)S(1)}) custom-call(bf16[1024,1024]{1,0:T(8,128)(2,1)S(1)} %bitcast.34, bf16[1024,1024]{1,0:T(8,128)(2,1)S(1)} %bitcast.35), custom_call_target="tpu_custom_call" | custom-call | bytes 8388608 | tf_op jit(solution)/shard_map/pallas_call | solution.py:51
  8.9 6.5 %all-to-all-start = ((bf16[8,2048,128]{2,1,0:T(8,128)(2,1)}), bf16[8,2048,128]{2,1,0:T(8,128)(2,1)}, u32[]{:S(2)}, u32[]{:S(2)}) async-start(bf16[8,2048,128]{2,1,0:T(8,128)(2,1)} %get-tuple-element.28), calls=%async_computation | async-start | bytes 8388608 | tf_op jit(solution)/shard_map/all_to_all | solution.py:333
  15.6 4.6 %shard_map.83 = (bf16[2176,128]{1,0:T(8,128)(2,1)S(1)}, bf16[2176,128]{1,0:T(8,128)(2,1)}, bf16[2176,128]{1,0:T(8,128)(2,1)S(1)}, bf16[2176,128]{1,0:T(8,128)(2,1)S(1)}) custom-call(f32[64]{0:T(128)S(1)} %divide_bitcast_fusion.gate_ref.refs_0_, s32[1]{0:T(128)} %bitcast.at_ref, bf16[128,8192]{1,0:T(8,128)(2,1)S(1)} %bitcast.32, bf16[128,8192]{1,0:T(8,128)(2,1)} %bitcast.38, ...), custom_call_target="tpu_custom_call" | custom-call | flops 4194304 | bytes 6291456 | tf_op jit(solution)/shard_map/pallas_call | solution.py:94
  21.6 1.7 collective-permute-start.1
  25.4 70.7 %collective-permute-done.1.refs_2_.refs_4_ = bf16[2176,128]{1,0:T(8,128)(2,1)} collective-permute-done((bf16[2176,128]{1,0:T(8,128)(2,1)S(1)}, bf16[2176,128]{1,0:T(8,128)(2,1)}, u32[]{:S(2)}, u32[]{:S(2)}) %collective-permute-start.1) | collective-permute-done | bytes 557088 | tf_op jit(solution)/shard_map/ppermute | solution.py:290
  96.1 11.8 %collective-permute-done.2.refs_3_.refs_5_ = bf16[2176,128]{1,0:T(8,128)(2,1)} collective-permute-done((bf16[2176,128]{1,0:T(8,128)(2,1)S(1)}, bf16[2176,128]{1,0:T(8,128)(2,1)}, u32[]{:S(2)}, u32[]{:S(2)}) %collective-permute-start.2) | collective-permute-done | bytes 557088 | tf_op jit(solution)/shard_map/ppermute | solution.py:290
  107.8 1.8 all-to-all-done.refs_1_
  110.3 4.5 %all-to-all-start.1 = ((bf16[8,1536,128]{2,1,0:T(8,128)(2,1)}), bf16[8,1536,128]{2,1,0:T(8,128)(2,1)}, u32[]{:S(2)}, u32[]{:S(2)}) async-start(bf16[8,1536,128]{2,1,0:T(8,128)(2,1)} %shard_map.93), calls=%async_computation.1 | async-start | bytes 6291456 | tf_op jit(solution)/shard_map/all_to_all | solution.py:333
  118.4 4.6 %shard_map.87 = (bf16[2176,128]{1,0:T(8,128)(2,1)S(1)}, bf16[2176,128]{1,0:T(8,128)(2,1)}, bf16[2176,128]{1,0:T(8,128)(2,1)S(1)}, bf16[2176,128]{1,0:T(8,128)(2,1)S(1)}) custom-call(f32[64]{0:T(128)S(1)} %copy-done.15, s32[1]{0:T(128)} %bitcast.at_ref, bf16[128,8192]{1,0:T(8,128)(2,1)S(1)} %bitcast.33, bf16[128,8192]{1,0:T(8,128)(2,1)} %bitcast.39, ...), custom_call_target="tpu_custom_call" | custom-call | flops 4194304 | bytes 6291456 | tf_op jit(solution)/shard_map/pallas_call | solution.py:94
  124.3 1.7 collective-permute-start.4
  126.0 38.9 %shard_map.85 = (bf16[128,1024]{1,0:T(8,128)(2,1)}, bf16[128,1024]{1,0:T(8,128)(2,1)}, bf16[128,1024]{1,0:T(8,128)(2,1)}, bf16[128,1024]{1,0:T(8,128)(2,1)}) custom-call(s32[4,32]{1,0:T(4,128)} %select_reduce_fusion.1.picks_ref, s32[4,2]{1,0:T(4,128)} %shard_map.82.starts_ref, bf16[2176,128]{1,0:T(8,128)(2,1)} %copy-done.13, ...), custom_call_target="tpu_custom_call" | custom-call | flops 51539607552 | tf_op jit(solution)/shard_map/pallas_call | solution.py:213
  165.6 13.1 %collective-permute-done.4.refs_3_.refs_2_.refs_4_ = bf16[2176,128]{1,0:T(8,128)(2,1)S(1)} collective-permute-done((bf16[2176,128]{1,0:T(8,128)(2,1)S(1)}, bf16[2176,128]{1,0:T(8,128)(2,1)S(1)}, u32[]{:S(2)}, u32[]{:S(2)}) %collective-permute-start.4) | collective-permute-done | bytes 557088 | tf_op jit(solution)/shard_map/ppermute | solution.py:290
  178.6 13.4 %collective-permute-done.5.refs_4_.refs_3_.refs_5_ = bf16[2176,128]{1,0:T(8,128)(2,1)} collective-permute-done((bf16[2176,128]{1,0:T(8,128)(2,1)S(1)}, bf16[2176,128]{1,0:T(8,128)(2,1)}, u32[]{:S(2)}, u32[]{:S(2)}) %collective-permute-start.5) | collective-permute-done | bytes 557088 | tf_op jit(solution)/shard_map/ppermute | solution.py:290
  192.7 2.3 collective-permute-start.9
  195.7 1.5 collective-permute-start.8
  200.9 3.9 %all-to-all-start.2 = ((bf16[8,512,128]{2,1,0:T(8,128)(2,1)}), bf16[8,512,128]{2,1,0:T(8,128)(2,1)S(1)}, u32[]{:S(2)}, u32[]{:S(2)}) async-start(bf16[8,512,128]{2,1,0:T(8,128)(2,1)} %shard_map.96), calls=%async_computation.2 | async-start | bytes 2097152 | tf_op jit(solution)/shard_map/all_to_all | solution.py:333
  204.8 31.8 %shard_map.94.refs_1_.refs_5_ = f32[4,1024,128]{2,1,0:T(8,128)} custom-call(s32[4,32]{1,0:T(4,128)} %select_reduce_fusion.picks_ref, s32[4,2]{1,0:T(4,128)} %shard_map.92.starts_ref, bf16[2176,128]{1,0:T(8,128)(2,1)} %copy-done, bf16[2176,128]{1,0:T(8,128)(2,1)} %copy-done.16, bf16[2176,128]{1,0:T(8,128)(2,1)} %copy-done.17, ...), custom_call_target="tpu_custom_call" | custom-call | flops 38654705664 | tf_op jit(solution)/shard_map/pallas_call | solution.py:213
  239.3 15.2 %shard_map.97 = (bf16[128,1024]{1,0:T(8,128)(2,1)}, bf16[128,1024]{1,0:T(8,128)(2,1)}, bf16[128,1024]{1,0:T(8,128)(2,1)}, bf16[128,1024]{1,0:T(8,128)(2,1)}) custom-call(s32[4,32]{1,0:T(4,128)} %select_reduce_fusion.picks_ref, s32[4,2]{1,0:T(4,128)} %shard_map.95.starts_ref, bf16[2176,128]{1,0:T(8,128)(2,1)} %copy-done, bf16[2176,128]{1,0:T(8,128)(2,1)} %copy-done.16, ...), custom_call_target="tpu_custom_call" | custom-call | flops 12884901888 | tf_op jit(solution)/shard_map/pallas_call | solution.py:213
  254.5 3.3 %collective-permute-start.10 = (bf16[128,1024]{1,0:T(8,128)(2,1)}, bf16[128,1024]{1,0:T(8,128)(2,1)S(1)}, u32[]{:S(2)}, u32[]{:S(2)}) collective-permute-start(bf16[128,1024]{1,0:T(8,128)(2,1)} %get-tuple-element.39), channel_id=1, source_target_pairs={{0,24},{1,25},{2,26},{3,27},{4,28},{5,29},{6,30},{7,31},{8,0},{9,1... | collective-permute-start | bytes 786440 | tf_op jit(solution)/shard_map/ppermute | solution.py:294
  257.9 4.3 %collective-permute-start.12 = (bf16[128,1024]{1,0:T(8,128)(2,1)}, bf16[128,1024]{1,0:T(8,128)(2,1)S(1)}, u32[]{:S(2)}, u32[]{:S(2)}) collective-permute-start(bf16[128,1024]{1,0:T(8,128)(2,1)} %get-tuple-element.41), channel_id=1, source_target_pairs={{0,26},{1,27},{2,24},{3,25},{4,30},{5,31},{6,28},{7,29},{8,2},{9,3... | collective-permute-start | bytes 786440 | tf_op jit(solution)/shard_map/ppermute | solution.py:294
  262.2 13.4 %collective-permute-done.10.refs_4_ = bf16[128,1024]{1,0:T(8,128)(2,1)S(1)} collective-permute-done((bf16[128,1024]{1,0:T(8,128)(2,1)}, bf16[128,1024]{1,0:T(8,128)(2,1)S(1)}, u32[]{:S(2)}, u32[]{:S(2)}) %collective-permute-start.10) | collective-permute-done | bytes 262176 | tf_op jit(solution)/shard_map/ppermute | solution.py:294
  275.6 5.2 %collective-permute-done.11.refs_5_ = bf16[128,1024]{1,0:T(8,128)(2,1)S(1)} collective-permute-done((bf16[128,1024]{1,0:T(8,128)(2,1)}, bf16[128,1024]{1,0:T(8,128)(2,1)S(1)}, u32[]{:S(2)}, u32[]{:S(2)}) %collective-permute-start.11) | collective-permute-done | bytes 262176 | tf_op jit(solution)/shard_map/ppermute | solution.py:294
  (84 shorter events, 20.1 us)
Async XLA Ops:
  8.9 6.6 %copy-start.1 = (bf16[1,128,8192]{2,1,0:T(8,128)(2,1)S(1)}, bf16[1,128,8192]{2,1,0:T(8,128)(2,1)}, u32[]{:S(2)}) copy-start(bf16[1,128,8192]{2,1,0:T(8,128)(2,1)} %param.8) | copy-start | bytes 6291460
  8.9 100.7 %all-to-all-start = ((bf16[8,2048,128]{2,1,0:T(8,128)(2,1)}), bf16[8,2048,128]{2,1,0:T(8,128)(2,1)}, u32[]{:S(2)}, u32[]{:S(2)}) async-start(bf16[8,2048,128]{2,1,0:T(8,128)(2,1)} %get-tuple-element.28), calls=%async_computation | async-start | bytes 8388608 | tf_op jit(solution)/shard_map/all_to_all | solution.py:333
  21.1 4.3 %collective-permute-start = (bf16[2176,128]{1,0:T(8,128)(2,1)}, bf16[2176,128]{1,0:T(8,128)(2,1)}, u32[]{:S(2)}, u32[]{:S(2)}) collective-permute-start(bf16[2176,128]{1,0:T(8,128)(2,1)} %get-tuple-element.25), channel_id=1, source_target_pairs={{0,1},{1,0},{2,3},{3,2},{4,5},{5,4},{6,7},{7,6},{8,9},{9,8},{10,11... | collective-permute-start | bytes 1671176 | tf_op jit(solution)/shard_map/ppermute | solution.py:290
  21.6 74.5 %collective-permute-start.1 = (bf16[2176,128]{1,0:T(8,128)(2,1)S(1)}, bf16[2176,128]{1,0:T(8,128)(2,1)}, u32[]{:S(2)}, u32[]{:S(2)}) collective-permute-start(bf16[2176,128]{1,0:T(8,128)(2,1)S(1)} %get-tuple-element.26), channel_id=1, source_target_pairs={{0,2},{1,3},{2,0},{3,1},{4,6},{5,7},{6,4},{7,5},{8,10},{9,11},{10,... | collective-permute-start | bytes 1671176 | tf_op jit(solution)/shard_map/ppermute | solution.py:290
  23.2 84.6 %collective-permute-start.2 = (bf16[2176,128]{1,0:T(8,128)(2,1)S(1)}, bf16[2176,128]{1,0:T(8,128)(2,1)}, u32[]{:S(2)}, u32[]{:S(2)}) collective-permute-start(bf16[2176,128]{1,0:T(8,128)(2,1)S(1)} %get-tuple-element.27), channel_id=1, source_target_pairs={{0,3},{1,2},{2,1},{3,0},{4,7},{5,6},{6,5},{7,4},{8,11},{9,10},{10,... | collective-permute-start | bytes 1671176 | tf_op jit(solution)/shard_map/ppermute | solution.py:290
  110.3 89.8 %all-to-all-start.1 = ((bf16[8,1536,128]{2,1,0:T(8,128)(2,1)}), bf16[8,1536,128]{2,1,0:T(8,128)(2,1)}, u32[]{:S(2)}, u32[]{:S(2)}) async-start(bf16[8,1536,128]{2,1,0:T(8,128)(2,1)} %shard_map.93), calls=%async_computation.1 | async-start | bytes 6291456 | tf_op jit(solution)/shard_map/all_to_all | solution.py:333
  123.9 41.7 %collective-permute-start.3 = (bf16[2176,128]{1,0:T(8,128)(2,1)}, bf16[2176,128]{1,0:T(8,128)(2,1)S(1)}, u32[]{:S(2)}, u32[]{:S(2)}) collective-permute-start(bf16[2176,128]{1,0:T(8,128)(2,1)} %get-tuple-element.31), channel_id=1, source_target_pairs={{0,1},{1,0},{2,3},{3,2},{4,5},{5,4},{6,7},{7,6},{8,9},{9,8},{10,11... | collective-permute-start | bytes 1671176 | tf_op jit(solution)/shard_map/ppermute | solution.py:290
  124.3 54.4 %collective-permute-start.4 = (bf16[2176,128]{1,0:T(8,128)(2,1)S(1)}, bf16[2176,128]{1,0:T(8,128)(2,1)S(1)}, u32[]{:S(2)}, u32[]{:S(2)}) collective-permute-start(bf16[2176,128]{1,0:T(8,128)(2,1)S(1)} %get-tuple-element.32), channel_id=1, source_target_pairs={{0,2},{1,3},{2,0},{3,1},{4,6},{5,7},{6,4},{7,5},{8,10},{9,11},{10,... | collective-permute-start | bytes 1671176 | tf_op jit(solution)/shard_map/ppermute | solution.py:290
  125.9 66.0 %collective-permute-start.5 = (bf16[2176,128]{1,0:T(8,128)(2,1)S(1)}, bf16[2176,128]{1,0:T(8,128)(2,1)}, u32[]{:S(2)}, u32[]{:S(2)}) collective-permute-start(bf16[2176,128]{1,0:T(8,128)(2,1)S(1)} %get-tuple-element.33), channel_id=1, source_target_pairs={{0,3},{1,2},{2,1},{3,0},{4,7},{5,6},{6,5},{7,4},{8,11},{9,10},{10,... | collective-permute-start | bytes 1671176 | tf_op jit(solution)/shard_map/ppermute | solution.py:290
  165.6 26.4 %copy-start.16 = (bf16[2176,128]{1,0:T(8,128)(2,1)}, bf16[2176,128]{1,0:T(8,128)(2,1)S(1)}, u32[]{:S(2)}) copy-start(bf16[2176,128]{1,0:T(8,128)(2,1)S(1)} %collective-permute-done.3.refs_2_.refs_1_.refs_3_) | copy-start | bytes 1671172
  178.6 13.4 %copy-start.17 = (bf16[2176,128]{1,0:T(8,128)(2,1)}, bf16[2176,128]{1,0:T(8,128)(2,1)S(1)}, u32[]{:S(2)}) copy-start(bf16[2176,128]{1,0:T(8,128)(2,1)S(1)} %collective-permute-done.4.refs_3_.refs_2_.refs_4_) | copy-start | bytes 1671172
  192.7 43.9 %collective-permute-start.9 = (bf16[128,1024]{1,0:T(8,128)(2,1)}, bf16[128,1024]{1,0:T(8,128)(2,1)S(1)}, u32[]{:S(2)}, u32[]{:S(2)}) collective-permute-start(bf16[128,1024]{1,0:T(8,128)(2,1)} %shard_map.91), channel_id=1, source_target_pairs={{0,27},{1,26},{2,25},{3,24},{4,31},{5,30},{6,29},{7,28},{8,3},{9,2... | collective-permute-start | bytes 786440 | tf_op jit(solution)/shard_map/ppermute | solution.py:294
  195.7 40.9 %collective-permute-start.8 = (bf16[128,1024]{1,0:T(8,128)(2,1)}, bf16[128,1024]{1,0:T(8,128)(2,1)S(1)}, u32[]{:S(2)}, u32[]{:S(2)}) collective-permute-start(bf16[128,1024]{1,0:T(8,128)(2,1)} %shard_map.90), channel_id=1, source_target_pairs={{0,26},{1,27},{2,24},{3,25},{4,30},{5,31},{6,28},{7,29},{8,2},{9,3... | collective-permute-start | bytes 786440 | tf_op jit(solution)/shard_map/ppermute | solution.py:294
  197.9 38.7 %collective-permute-start.7 = (bf16[128,1024]{1,0:T(8,128)(2,1)}, bf16[128,1024]{1,0:T(8,128)(2,1)S(1)}, u32[]{:S(2)}, u32[]{:S(2)}) collective-permute-start(bf16[128,1024]{1,0:T(8,128)(2,1)} %shard_map.89), channel_id=1, source_target_pairs={{0,25},{1,24},{2,27},{3,26},{4,29},{5,28},{6,31},{7,30},{8,1},{9,0... | collective-permute-start | bytes 786440 | tf_op jit(solution)/shard_map/ppermute | solution.py:294
  199.6 37.0 %collective-permute-start.6 = (bf16[128,1024]{1,0:T(8,128)(2,1)}, bf16[128,1024]{1,0:T(8,128)(2,1)S(1)}, u32[]{:S(2)}, u32[]{:S(2)}) collective-permute-start(bf16[128,1024]{1,0:T(8,128)(2,1)} %shard_map.88), channel_id=1, source_target_pairs={{0,24},{1,25},{2,26},{3,27},{4,28},{5,29},{6,30},{7,31},{8,0},{9,1... | collective-permute-start | bytes 786440 | tf_op jit(solution)/shard_map/ppermute | solution.py:294
  200.9 37.4 %all-to-all-start.2 = ((bf16[8,512,128]{2,1,0:T(8,128)(2,1)}), bf16[8,512,128]{2,1,0:T(8,128)(2,1)S(1)}, u32[]{:S(2)}, u32[]{:S(2)}) async-start(bf16[8,512,128]{2,1,0:T(8,128)(2,1)} %shard_map.96), calls=%async_computation.2 | async-start | bytes 2097152 | tf_op jit(solution)/shard_map/all_to_all | solution.py:333
  239.3 41.5 %copy-start.6 = (bf16[128,1024]{1,0:T(8,128)(2,1)S(1)}, bf16[128,1024]{1,0:T(8,128)(2,1)}, u32[]{:S(2)}) copy-start(bf16[128,1024]{1,0:T(8,128)(2,1)} %copy-done.5) | copy-start | bytes 786436
  239.3 41.5 %copy-start.8 = (bf16[128,1024]{1,0:T(8,128)(2,1)S(1)}, bf16[128,1024]{1,0:T(8,128)(2,1)}, u32[]{:S(2)}) copy-start(bf16[128,1024]{1,0:T(8,128)(2,1)} %copy-done.7) | copy-start | bytes 786436
  239.3 41.5 %copy-start.10 = (bf16[128,1024]{1,0:T(8,128)(2,1)S(1)}, bf16[128,1024]{1,0:T(8,128)(2,1)}, u32[]{:S(2)}) copy-start(bf16[128,1024]{1,0:T(8,128)(2,1)} %copy-done.9) | copy-start | bytes 786436
  239.3 41.5 %copy-start.12 = (bf16[128,1024]{1,0:T(8,128)(2,1)S(1)}, bf16[128,1024]{1,0:T(8,128)(2,1)}, u32[]{:S(2)}) copy-start(bf16[128,1024]{1,0:T(8,128)(2,1)} %copy-done.11) | copy-start | bytes 786436
  254.5 21.0 %collective-permute-start.10 = (bf16[128,1024]{1,0:T(8,128)(2,1)}, bf16[128,1024]{1,0:T(8,128)(2,1)S(1)}, u32[]{:S(2)}, u32[]{:S(2)}) collective-permute-start(bf16[128,1024]{1,0:T(8,128)(2,1)} %get-tuple-element.39), channel_id=1, source_target_pairs={{0,24},{1,25},{2,26},{3,27},{4,28},{5,29},{6,30},{7,31},{8,0},{9,1... | collective-permute-start | bytes 786440 | tf_op jit(solution)/shard_map/ppermute | solution.py:294
  257.8 22.9 %collective-permute-start.11 = (bf16[128,1024]{1,0:T(8,128)(2,1)}, bf16[128,1024]{1,0:T(8,128)(2,1)S(1)}, u32[]{:S(2)}, u32[]{:S(2)}) collective-permute-start(bf16[128,1024]{1,0:T(8,128)(2,1)} %get-tuple-element.40), channel_id=1, source_target_pairs={{0,25},{1,24},{2,27},{3,26},{4,29},{5,28},{6,31},{7,30},{8,1},{9,0... | collective-permute-start | bytes 786440 | tf_op jit(solution)/shard_map/ppermute | solution.py:294
  257.9 22.9 %collective-permute-start.12 = (bf16[128,1024]{1,0:T(8,128)(2,1)}, bf16[128,1024]{1,0:T(8,128)(2,1)S(1)}, u32[]{:S(2)}, u32[]{:S(2)}) collective-permute-start(bf16[128,1024]{1,0:T(8,128)(2,1)} %get-tuple-element.41), channel_id=1, source_target_pairs={{0,26},{1,27},{2,24},{3,25},{4,30},{5,31},{6,28},{7,29},{8,2},{9,3... | collective-permute-start | bytes 786440 | tf_op jit(solution)/shard_map/ppermute | solution.py:294
  262.2 18.6 %collective-permute-start.13 = (bf16[128,1024]{1,0:T(8,128)(2,1)}, bf16[128,1024]{1,0:T(8,128)(2,1)S(1)}, u32[]{:S(2)}, u32[]{:S(2)}) collective-permute-start(bf16[128,1024]{1,0:T(8,128)(2,1)} %get-tuple-element.42), channel_id=1, source_target_pairs={{0,27},{1,26},{2,25},{3,24},{4,31},{5,30},{6,29},{7,28},{8,3},{9,2... | collective-permute-start | bytes 786440 | tf_op jit(solution)/shard_map/ppermute | solution.py:294
  (14 other events, 28.5 us)

commit v10 on v9

--- a/solution.py
+++ b/solution.py
@@ -29,34 +29,42 @@
 
 
 def pack_kernel(own, group, cuts, keys_ref, values_ref, *outs):
-    dim = outs[0].shape[2]
+    dim = outs[0].shape[3]
+    block = pl.program_id(0)
     at = 0
     for index, pieces in enumerate(cuts):
         for low, high in pieces:
-            out = outs[at]
+
+            @pl.when((block >= low) & (block < high))
+            def _(out=outs[at], index=index):
+                for device in range(out.shape[0]):
+                    head = device % group * own + index
+                    for half, source in enumerate((keys_ref, values_ref)):
+                        out[device, half] = source[:, head * dim:(head + 1) * dim]
+
             at += 1
-            rows = (high - low) * BLOCK
-            for device in range(out.shape[0]):
-                head = device % group * own + index
-                for half, source in enumerate((keys_ref, values_ref)):
-                    out[device, half * rows:(half + 1) * rows, :] = source[
-                        low * BLOCK:high * BLOCK, head * dim:(head + 1) * dim
-                    ]
 
 
 def pack(mem_keys, mem_values, seq, own, group, dim, cuts):
     mem_dev, width = mem_keys.shape
-    whole = pl.BlockSpec((mem_dev, width), lambda i: (0, 0))
-    shapes = [(seq, 2 * (high - low) * BLOCK, dim) for pieces in cuts for low, high in pieces]
-    return pl.pallas_call(
+    rows = pl.BlockSpec((BLOCK, width), lambda i: (i, 0))
+    spans = [span for pieces in cuts for span in pieces]
+
+    def place(low, high):
+        return pl.BlockSpec((seq, 2, BLOCK, dim), lambda i: (0, 0, jnp.clip(i - low, 0, high - low - 1), 0))
+
+    outs = pl.pallas_call(
         functools.partial(pack_kernel, own, group, cuts),
-        out_shape=[jax.ShapeDtypeStruct(shape, mem_keys.dtype) for shape in shapes],
-        grid=(1,),
-        in_specs=[whole, whole],
-        out_specs=[pl.BlockSpec(shape, lambda i: (0, 0, 0)) for shape in shapes],
-        compiler_params=pltpu.CompilerParams(vmem_limit_bytes=VMEM_LIMIT),
+        out_shape=[
+            jax.ShapeDtypeStruct((seq, 2, (high - low) * BLOCK, dim), mem_keys.dtype) for low, high in spans
+        ],
+        grid=(mem_dev // BLOCK,),
+        in_specs=[rows, rows],
+        out_specs=[place(low, high) for low, high in spans],
+        compiler_params=pltpu.CompilerParams(vmem_limit_bytes=VMEM_MOST),
         cost_estimate=pl.CostEstimate(flops=0, bytes_accessed=8 * mem_dev * width, transcendentals=0),
     )(mem_keys, mem_values)
+    return [out.reshape(seq, -1, dim) for out in outs]
 
 
 def prepare_kernel(heads, dim, scale, own, index, gate_ref, at_ref, grad_ref, query_ref, out_ref, total_ref, *packed_refs):
@@ -293,7 +301,7 @@
         pairs = [(s * seq + p, ((s - 1) % sections) * seq + (p ^ step)) for s in range(sections) for p in range(seq)]
         return lax.ppermute(value, ("section", "seq"), pairs)
 
-    cut = (3 * blocks + 3) // 4
+    cut = (5 * blocks + 7) // 8
     cuts = [[(0, blocks)]] * (own - 1) + [[(0, cut), (cut, blocks)]]
 
     def listed(i):
@@ -341,11 +349,9 @@
             worked = [acc]
         if i < own - 1:
             coming = queries_of(i + 1)
-        ready = [] if i < own - 1 else gathered
+        ready = coming[:1] if i < own - 1 else gathered
         done = run(pieces[-1], acc, starts=after(starts[-1], *worked, *ready), last=True)
         worked = done[:1]
-        if i < own - 1:
-            done = [after(result, *coming) for result in done]
         results = [delivered(done[x], x) for x in range(group)]
         gathered = gathered + results
     return assemble(gathered, at, own, group)[None]

time: 284 us -> 273 us (0.961)
  waiting for transfers between devices: 129 us -> 119 us
  local copies, waits for them, and re-layouts: 10.3 us -> 6.27 us
    ppermute x6, waiting for transfers between devices: 109 us -> 90.8 us  [swapped(): return lax.ppermute(value, 'seq', [(p, p ^ step) for p in range(seq)])]
    all_to_all x3, waiting for transfers between devices: 1.79 us -> 9 us  [shards(): lax.all_to_all(piece, 'seq', split_axis=0, concat_axis=0, tiled=True)]
    unnamed x43 -> x35, local copies, waits for them, and re-layouts: 8.53 us -> 4.53 us
    pallas_call x1, Pallas kernels: 4.77 us -> 7.72 us  [pack(): pl.pallas_call(functools.partial(pack_kernel, own, group, cuts), out_shap...]
    pallas_call x10 -> x6, Pallas kernels: 6.41 us -> 4.2 us  [after(): pl.pallas_call(lambda *refs: None, out_shape=jax.ShapeDtypeStruct(value.s...]
  transfers between devices with their start and end apart: 17 -> 17, of which waited for: 7 -> 8; matrix products, arithmetic and copies ran while one was open for 2% -> 2% of each run, Pallas kernels for 30% -> 30%
where the time goes in v10:
time: 273 us; the launch traced here: 272 us
  waiting for transfers between devices  119 us (44%)
  Pallas kernels  110 us (40%)
  starting transfers between devices  33.5 us (12%)
  local copies, waits for them, and re-layouts  6.27 us (2%)
  other arithmetic  2.73 us (1%)
    ppermute x6, waiting for transfers between devices, swapped(): return lax.ppermute(value, 'seq', [(p, p ^ step) for p in range(seq)])  90.8 us
    pallas_call x3, Pallas kernels, attend(): pl.pallas_call(functools.partial(attend_kernel, heads, dim, rows, scale,...  87.1 us
    ppermute x8, waiting for transfers between devices, delivered(): return lax.ppermute(value, ('section', 'seq'), pairs)  19.6 us
    all_to_all x3, starting transfers between devices, shards(): lax.all_to_all(piece, 'seq', split_axis=0, concat_axis=0, tiled=True)  15 us
    ppermute x8, starting transfers between devices, delivered(): return lax.ppermute(value, ('section', 'seq'), pairs)  14.3 us
    pallas_call x2, Pallas kernels, prepare(): pl.pallas_call(functools.partial(prepare_kernel, heads, dim, scale, own,...  9.24 us
    all_to_all x3, waiting for transfers between devices, shards(): lax.all_to_all(piece, 'seq', split_axis=0, concat_axis=0, tiled=True)  9 us
    pallas_call x1, Pallas kernels, pack(): pl.pallas_call(functools.partial(pack_kernel, own, group, cuts), out_shap...  7.72 us
  transfers between devices with their start and end apart: 17, of which 8 were waited for; matrix products, arithmetic and copies ran while one was open for 2% of the time, Pallas kernels for 30%

profile of v10, /device:TPU:0, one launch (start us, length us, event | category | flops | bytes accessed | tf_op | source)
XLA Modules:
  0.0 271.8 jit_solution(15519063503374121067)
XLA Ops:
  0.0 7.7 %shard_map.82 = (bf16[8,2,1024,128]{3,2,1,0:T(8,128)(2,1)}, bf16[8,2,640,128]{3,2,1,0:T(8,128)(2,1)}, bf16[8,2,384,128]{3,2,1,0:T(8,128)(2,1)}) custom-call(bf16[1024,1024]{1,0:T(8,128)(2,1)} %bitcast.46, bf16[1024,1024]{1,0:T(8,128)(2,1)} %bitcast.47), custom_call_target="tpu_custom_call" | custom-call | bytes 8388608 | tf_op jit(solution)/shard_map/pallas_call | solution.py:56
  7.7 6.5 %all-to-all-start = ((bf16[8,2048,128]{2,1,0:T(8,128)(2,1)}), bf16[8,2048,128]{2,1,0:T(8,128)(2,1)}, u32[]{:S(2)}, u32[]{:S(2)}) async-start(bf16[8,2048,128]{2,1,0:T(8,128)(2,1)} %bitcast.45), calls=%async_computation | async-start | bytes 8388608 | tf_op jit(solution)/shard_map/all_to_all | solution.py:341
  14.4 4.6 %shard_map.86 = (bf16[2176,128]{1,0:T(8,128)(2,1)S(1)}, bf16[2176,128]{1,0:T(8,128)(2,1)}, bf16[2176,128]{1,0:T(8,128)(2,1)S(1)}, bf16[2176,128]{1,0:T(8,128)(2,1)S(1)}) custom-call(f32[64]{0:T(128)S(1)} %divide_bitcast_fusion.refs_0_.gate_ref, s32[1]{0:T(128)} %bitcast.at_ref, bf16[128,8192]{1,0:T(8,128)(2,1)S(1)} %bitcast.35, bf16[128,8192]{1,0:T(8,128)(2,1)} %bitcast.40, ...), custom_call_target="tpu_custom_call" | custom-call | flops 4194304 | bytes 6291456 | tf_op jit(solution)/shard_map/pallas_call | solution.py:102
  20.3 1.7 collective-permute-start.1
  25.9 69.0 %collective-permute-done.1.refs_2_.refs_4_ = bf16[2176,128]{1,0:T(8,128)(2,1)} collective-permute-done((bf16[2176,128]{1,0:T(8,128)(2,1)S(1)}, bf16[2176,128]{1,0:T(8,128)(2,1)}, u32[]{:S(2)}, u32[]{:S(2)}) %collective-permute-start.1) | collective-permute-done | bytes 557088 | tf_op jit(solution)/shard_map/ppermute | solution.py:298
  94.9 11.8 %collective-permute-done.2.refs_3_.refs_5_ = bf16[2176,128]{1,0:T(8,128)(2,1)} collective-permute-done((bf16[2176,128]{1,0:T(8,128)(2,1)S(1)}, bf16[2176,128]{1,0:T(8,128)(2,1)}, u32[]{:S(2)}, u32[]{:S(2)}) %collective-permute-start.2) | collective-permute-done | bytes 557088 | tf_op jit(solution)/shard_map/ppermute | solution.py:298
  106.6 1.8 all-to-all-done.refs_1_
  109.1 4.4 %all-to-all-start.1 = ((bf16[8,1280,128]{2,1,0:T(8,128)(2,1)}), bf16[8,1280,128]{2,1,0:T(8,128)(2,1)}, u32[]{:S(2)}, u32[]{:S(2)}) async-start(bf16[8,1280,128]{2,1,0:T(8,128)(2,1)} %shard_map.89), calls=%async_computation.1 | async-start | bytes 5242880 | tf_op jit(solution)/shard_map/all_to_all | solution.py:341
  114.8 4.6 %shard_map.84 = (bf16[2176,128]{1,0:T(8,128)(2,1)S(1)}, bf16[2176,128]{1,0:T(8,128)(2,1)}, bf16[2176,128]{1,0:T(8,128)(2,1)S(1)}, bf16[2176,128]{1,0:T(8,128)(2,1)S(1)}) custom-call(f32[64]{0:T(128)S(1)} %copy-done.12, s32[1]{0:T(128)} %bitcast.at_ref, bf16[128,8192]{1,0:T(8,128)(2,1)S(1)} %bitcast.36, bf16[128,8192]{1,0:T(8,128)(2,1)} %bitcast.41, ...), custom_call_target="tpu_custom_call" | custom-call | flops 4194304 | bytes 6291456 | tf_op jit(solution)/shard_map/pallas_call | solution.py:102
  120.6 1.7 collective-permute-start.8
  123.5 39.0 %shard_map.87 = (bf16[128,1024]{1,0:T(8,128)(2,1)}, bf16[128,1024]{1,0:T(8,128)(2,1)}, bf16[128,1024]{1,0:T(8,128)(2,1)}, bf16[128,1024]{1,0:T(8,128)(2,1)}) custom-call(s32[4,32]{1,0:T(4,128)} %select_reduce_fusion.1.picks_ref, s32[4,2]{1,0:T(4,128)} %shard_map.85.starts_ref, bf16[2176,128]{1,0:T(8,128)(2,1)} %copy-done.10, ...), custom_call_target="tpu_custom_call" | custom-call | flops 51539607552 | tf_op jit(solution)/shard_map/pallas_call | solution.py:221
  162.5 2.4 collective-permute-start.3
  166.0 2.6 collective-permute-start.5
  168.9 3.7 %collective-permute-start.6 = (bf16[128,1024]{1,0:T(8,128)(2,1)}, bf16[128,1024]{1,0:T(8,128)(2,1)S(1)}, u32[]{:S(2)}, u32[]{:S(2)}) collective-permute-start(bf16[128,1024]{1,0:T(8,128)(2,1)} %get-tuple-element.33), channel_id=1, source_target_pairs={{0,27},{1,26},{2,25},{3,24},{4,31},{5,30},{6,29},{7,28},{8,3},{9,2... | collective-permute-start | bytes 786440 | tf_op jit(solution)/shard_map/ppermute | solution.py:302
  172.6 9.7 %collective-permute-done.9.refs_3_.refs_5_ = bf16[2176,128]{1,0:T(8,128)(2,1)} collective-permute-done((bf16[2176,128]{1,0:T(8,128)(2,1)S(1)}, bf16[2176,128]{1,0:T(8,128)(2,1)}, u32[]{:S(2)}, u32[]{:S(2)}) %collective-permute-start.9) | collective-permute-done | bytes 557088 | tf_op jit(solution)/shard_map/ppermute | solution.py:298
  183.0 4.1 %all-to-all-start.2 = ((bf16[8,768,128]{2,1,0:T(8,128)(2,1)}), bf16[8,768,128]{2,1,0:T(8,128)(2,1)S(1)}, u32[]{:S(2)}, u32[]{:S(2)}) async-start(bf16[8,768,128]{2,1,0:T(8,128)(2,1)} %shard_map.92), calls=%async_computation.2 | async-start | bytes 3145728 | tf_op jit(solution)/shard_map/all_to_all | solution.py:341
  187.1 28.8 %shard_map.90.refs_1_.refs_5_ = f32[4,1024,128]{2,1,0:T(8,128)} custom-call(s32[4,32]{1,0:T(4,128)} %select_reduce_fusion.picks_ref, s32[4,2]{1,0:T(4,128)} %shard_map.88.starts_ref, bf16[2176,128]{1,0:T(8,128)(2,1)} %copy-done.1, bf16[2176,128]{1,0:T(8,128)(2,1)} %copy-done.14, bf16[2176,128]{1,0:T(8,128)(2,1)} %collective-permute-done.8.refs_2_.refs_4_, ...), custom_call_target="tpu_custom_call" | custom-call | flops 32212254720 | tf_op jit(solution)/shard_map/pallas_call | solution.py:221
  217.7 7.2 %all-to-all-done.2 = bf16[8,768,128]{2,1,0:T(8,128)(2,1)S(1)} async-done(((bf16[8,768,128]{2,1,0:T(8,128)(2,1)}), bf16[8,768,128]{2,1,0:T(8,128)(2,1)S(1)}, u32[]{:S(2)}, u32[]{:S(2)}) %all-to-all-start.2) | async-done | bytes 1572896 | tf_op jit(solution)/shard_map/all_to_all | solution.py:341
  224.9 1.2 copy-done.13
  226.1 19.4 %shard_map.93 = (bf16[128,1024]{1,0:T(8,128)(2,1)}, bf16[128,1024]{1,0:T(8,128)(2,1)}, bf16[128,1024]{1,0:T(8,128)(2,1)}, bf16[128,1024]{1,0:T(8,128)(2,1)}) custom-call(s32[4,32]{1,0:T(4,128)} %select_reduce_fusion.picks_ref, s32[4,2]{1,0:T(4,128)} %shard_map.91.starts_ref, bf16[2176,128]{1,0:T(8,128)(2,1)} %copy-done.1, bf16[2176,128]{1,0:T(8,128)(2,1)} %copy-done.14, ...), custom_call_target="tpu_custom_call" | custom-call | flops 19327352832 | tf_op jit(solution)/shard_map/pallas_call | solution.py:221
  245.5 4.3 %collective-permute-start.10 = (bf16[128,1024]{1,0:T(8,128)(2,1)}, bf16[128,1024]{1,0:T(8,128)(2,1)S(1)}, u32[]{:S(2)}, u32[]{:S(2)}) collective-permute-start(bf16[128,1024]{1,0:T(8,128)(2,1)} %get-tuple-element.39), channel_id=1, source_target_pairs={{0,24},{1,25},{2,26},{3,27},{4,28},{5,29},{6,30},{7,31},{8,0},{9,1... | collective-permute-start | bytes 786440 | tf_op jit(solution)/shard_map/ppermute | solution.py:302
  250.8 16.8 %collective-permute-done.10.refs_4_ = bf16[128,1024]{1,0:T(8,128)(2,1)S(1)} collective-permute-done((bf16[128,1024]{1,0:T(8,128)(2,1)}, bf16[128,1024]{1,0:T(8,128)(2,1)S(1)}, u32[]{:S(2)}, u32[]{:S(2)}) %collective-permute-start.10) | collective-permute-done | bytes 262176 | tf_op jit(solution)/shard_map/ppermute | solution.py:302
  267.5 2.8 %collective-permute-done.11.refs_5_ = bf16[128,1024]{1,0:T(8,128)(2,1)S(1)} collective-permute-done((bf16[128,1024]{1,0:T(8,128)(2,1)}, bf16[128,1024]{1,0:T(8,128)(2,1)S(1)}, u32[]{:S(2)}, u32[]{:S(2)}) %collective-permute-start.11) | collective-permute-done | bytes 262176 | tf_op jit(solution)/shard_map/ppermute | solution.py:302
  270.4 1.5 shard_map.94
  (72 shorter events, 14.6 us)
Async XLA Ops:
  7.7 6.6 %copy-start.16 = (f32[1,64]{1,0:T(1,128)S(1)}, f32[1,64]{1,0:T(1,128)}, u32[]{:S(2)}) copy-start(f32[1,64]{1,0:T(1,128)} %param.12) | copy-start | bytes 772
  7.7 6.6 %copy-start = (bf16[1,128,8192]{2,1,0:T(8,128)(2,1)S(1)}, bf16[1,128,8192]{2,1,0:T(8,128)(2,1)}, u32[]{:S(2)}) copy-start(bf16[1,128,8192]{2,1,0:T(8,128)(2,1)} %param.8) | copy-start | bytes 6291460
  7.7 100.7 %all-to-all-start = ((bf16[8,2048,128]{2,1,0:T(8,128)(2,1)}), bf16[8,2048,128]{2,1,0:T(8,128)(2,1)}, u32[]{:S(2)}, u32[]{:S(2)}) async-start(bf16[8,2048,128]{2,1,0:T(8,128)(2,1)} %bitcast.45), calls=%async_computation | async-start | bytes 8388608 | tf_op jit(solution)/shard_map/all_to_all | solution.py:341
  19.8 6.1 %collective-permute-start = (bf16[2176,128]{1,0:T(8,128)(2,1)}, bf16[2176,128]{1,0:T(8,128)(2,1)}, u32[]{:S(2)}, u32[]{:S(2)}) collective-permute-start(bf16[2176,128]{1,0:T(8,128)(2,1)} %get-tuple-element.27), channel_id=1, source_target_pairs={{0,1},{1,0},{2,3},{3,2},{4,5},{5,4},{6,7},{7,6},{8,9},{9,8},{10,11... | collective-permute-start | bytes 1671176 | tf_op jit(solution)/shard_map/ppermute | solution.py:298
  20.3 74.6 %collective-permute-start.1 = (bf16[2176,128]{1,0:T(8,128)(2,1)S(1)}, bf16[2176,128]{1,0:T(8,128)(2,1)}, u32[]{:S(2)}, u32[]{:S(2)}) collective-permute-start(bf16[2176,128]{1,0:T(8,128)(2,1)S(1)} %get-tuple-element.28), channel_id=1, source_target_pairs={{0,2},{1,3},{2,0},{3,1},{4,6},{5,7},{6,4},{7,5},{8,10},{9,11},{10,... | collective-permute-start | bytes 1671176 | tf_op jit(solution)/shard_map/ppermute | solution.py:298
  22.0 84.6 %collective-permute-start.2 = (bf16[2176,128]{1,0:T(8,128)(2,1)S(1)}, bf16[2176,128]{1,0:T(8,128)(2,1)}, u32[]{:S(2)}, u32[]{:S(2)}) collective-permute-start(bf16[2176,128]{1,0:T(8,128)(2,1)S(1)} %get-tuple-element.29), channel_id=1, source_target_pairs={{0,3},{1,2},{2,1},{3,0},{4,7},{5,6},{6,5},{7,4},{8,11},{9,10},{10,... | collective-permute-start | bytes 1671176 | tf_op jit(solution)/shard_map/ppermute | solution.py:298
  109.1 73.1 %all-to-all-start.1 = ((bf16[8,1280,128]{2,1,0:T(8,128)(2,1)}), bf16[8,1280,128]{2,1,0:T(8,128)(2,1)}, u32[]{:S(2)}, u32[]{:S(2)}) async-start(bf16[8,1280,128]{2,1,0:T(8,128)(2,1)} %shard_map.89), calls=%async_computation.1 | async-start | bytes 5242880 | tf_op jit(solution)/shard_map/all_to_all | solution.py:341
  120.2 45.8 %collective-permute-start.7 = (bf16[2176,128]{1,0:T(8,128)(2,1)}, bf16[2176,128]{1,0:T(8,128)(2,1)S(1)}, u32[]{:S(2)}, u32[]{:S(2)}) collective-permute-start(bf16[2176,128]{1,0:T(8,128)(2,1)} %get-tuple-element.34), channel_id=1, source_target_pairs={{0,1},{1,0},{2,3},{3,2},{4,5},{5,4},{6,7},{7,6},{8,9},{9,8},{10,11... | collective-permute-start | bytes 1671176 | tf_op jit(solution)/shard_map/ppermute | solution.py:298
  120.6 48.3 %collective-permute-start.8 = (bf16[2176,128]{1,0:T(8,128)(2,1)S(1)}, bf16[2176,128]{1,0:T(8,128)(2,1)}, u32[]{:S(2)}, u32[]{:S(2)}) collective-permute-start(bf16[2176,128]{1,0:T(8,128)(2,1)S(1)} %get-tuple-element.35), channel_id=1, source_target_pairs={{0,2},{1,3},{2,0},{3,1},{4,6},{5,7},{6,4},{7,5},{8,10},{9,11},{10,... | collective-permute-start | bytes 1671176 | tf_op jit(solution)/shard_map/ppermute | solution.py:298
  122.3 60.0 %collective-permute-start.9 = (bf16[2176,128]{1,0:T(8,128)(2,1)S(1)}, bf16[2176,128]{1,0:T(8,128)(2,1)}, u32[]{:S(2)}, u32[]{:S(2)}) collective-permute-start(bf16[2176,128]{1,0:T(8,128)(2,1)S(1)} %get-tuple-element.36), channel_id=1, source_target_pairs={{0,3},{1,2},{2,1},{3,0},{4,7},{5,6},{6,5},{7,4},{8,11},{9,10},{10,... | collective-permute-start | bytes 1671176 | tf_op jit(solution)/shard_map/ppermute | solution.py:298
  162.5 53.4 %collective-permute-start.3 = (bf16[128,1024]{1,0:T(8,128)(2,1)}, bf16[128,1024]{1,0:T(8,128)(2,1)S(1)}, u32[]{:S(2)}, u32[]{:S(2)}) collective-permute-start(bf16[128,1024]{1,0:T(8,128)(2,1)} %get-tuple-element.30.refs_1_), channel_id=1, source_target_pairs={{0,24},{1,25},{2,26},{3,27},{4,28},{5,29},{6,30},{7,31},{8,0},{9,1... | collective-permute-start | bytes 786440 | tf_op jit(solution)/shard_map/ppermute | solution.py:302
  165.7 50.3 %collective-permute-start.4 = (bf16[128,1024]{1,0:T(8,128)(2,1)}, bf16[128,1024]{1,0:T(8,128)(2,1)S(1)}, u32[]{:S(2)}, u32[]{:S(2)}) collective-permute-start(bf16[128,1024]{1,0:T(8,128)(2,1)} %get-tuple-element.31), channel_id=1, source_target_pairs={{0,25},{1,24},{2,27},{3,26},{4,29},{5,28},{6,31},{7,30},{8,1},{9,0... | collective-permute-start | bytes 786440 | tf_op jit(solution)/shard_map/ppermute | solution.py:302
  166.0 16.3 %copy-start.14 = (bf16[2176,128]{1,0:T(8,128)(2,1)}, bf16[2176,128]{1,0:T(8,128)(2,1)S(1)}, u32[]{:S(2)}) copy-start(bf16[2176,128]{1,0:T(8,128)(2,1)S(1)} %collective-permute-done.7.refs_1_.refs_3_) | copy-start | bytes 1671172
  166.0 50.0 %collective-permute-start.5 = (bf16[128,1024]{1,0:T(8,128)(2,1)}, bf16[128,1024]{1,0:T(8,128)(2,1)S(1)}, u32[]{:S(2)}, u32[]{:S(2)}) collective-permute-start(bf16[128,1024]{1,0:T(8,128)(2,1)} %get-tuple-element.32), channel_id=1, source_target_pairs={{0,26},{1,27},{2,24},{3,25},{4,30},{5,31},{6,28},{7,29},{8,2},{9,3... | collective-permute-start | bytes 786440 | tf_op jit(solution)/shard_map/ppermute | solution.py:302
  168.9 47.1 %collective-permute-start.6 = (bf16[128,1024]{1,0:T(8,128)(2,1)}, bf16[128,1024]{1,0:T(8,128)(2,1)S(1)}, u32[]{:S(2)}, u32[]{:S(2)}) collective-permute-start(bf16[128,1024]{1,0:T(8,128)(2,1)} %get-tuple-element.33), channel_id=1, source_target_pairs={{0,27},{1,26},{2,25},{3,24},{4,31},{5,30},{6,29},{7,28},{8,3},{9,2... | collective-permute-start | bytes 786440 | tf_op jit(solution)/shard_map/ppermute | solution.py:302
  183.0 41.9 %all-to-all-start.2 = ((bf16[8,768,128]{2,1,0:T(8,128)(2,1)}), bf16[8,768,128]{2,1,0:T(8,128)(2,1)S(1)}, u32[]{:S(2)}, u32[]{:S(2)}) async-start(bf16[8,768,128]{2,1,0:T(8,128)(2,1)} %shard_map.92), calls=%async_computation.2 | async-start | bytes 3145728 | tf_op jit(solution)/shard_map/all_to_all | solution.py:341
  226.1 44.2 %copy-start.3 = (bf16[128,1024]{1,0:T(8,128)(2,1)S(1)}, bf16[128,1024]{1,0:T(8,128)(2,1)}, u32[]{:S(2)}) copy-start(bf16[128,1024]{1,0:T(8,128)(2,1)} %copy-done.2) | copy-start | bytes 786436
  226.1 44.2 %copy-start.5 = (bf16[128,1024]{1,0:T(8,128)(2,1)S(1)}, bf16[128,1024]{1,0:T(8,128)(2,1)}, u32[]{:S(2)}) copy-start(bf16[128,1024]{1,0:T(8,128)(2,1)} %copy-done.4) | copy-start | bytes 786436
  226.1 44.3 %copy-start.7 = (bf16[128,1024]{1,0:T(8,128)(2,1)S(1)}, bf16[128,1024]{1,0:T(8,128)(2,1)}, u32[]{:S(2)}) copy-start(bf16[128,1024]{1,0:T(8,128)(2,1)} %copy-done.6) | copy-start | bytes 786436
  226.1 44.3 %copy-start.9 = (bf16[128,1024]{1,0:T(8,128)(2,1)S(1)}, bf16[128,1024]{1,0:T(8,128)(2,1)}, u32[]{:S(2)}) copy-start(bf16[128,1024]{1,0:T(8,128)(2,1)} %copy-done.8) | copy-start | bytes 786436
  245.5 22.1 %collective-permute-start.10 = (bf16[128,1024]{1,0:T(8,128)(2,1)}, bf16[128,1024]{1,0:T(8,128)(2,1)S(1)}, u32[]{:S(2)}, u32[]{:S(2)}) collective-permute-start(bf16[128,1024]{1,0:T(8,128)(2,1)} %get-tuple-element.39), channel_id=1, source_target_pairs={{0,24},{1,25},{2,26},{3,27},{4,28},{5,29},{6,30},{7,31},{8,0},{9,1... | collective-permute-start | bytes 786440 | tf_op jit(solution)/shard_map/ppermute | solution.py:302
  249.8 20.5 %collective-permute-start.11 = (bf16[128,1024]{1,0:T(8,128)(2,1)}, bf16[128,1024]{1,0:T(8,128)(2,1)S(1)}, u32[]{:S(2)}, u32[]{:S(2)}) collective-permute-start(bf16[128,1024]{1,0:T(8,128)(2,1)} %get-tuple-element.40), channel_id=1, source_target_pairs={{0,25},{1,24},{2,27},{3,26},{4,29},{5,28},{6,31},{7,30},{8,1},{9,0... | collective-permute-start | bytes 786440 | tf_op jit(solution)/shard_map/ppermute | solution.py:302
  249.8 20.5 %collective-permute-start.12 = (bf16[128,1024]{1,0:T(8,128)(2,1)}, bf16[128,1024]{1,0:T(8,128)(2,1)S(1)}, u32[]{:S(2)}, u32[]{:S(2)}) collective-permute-start(bf16[128,1024]{1,0:T(8,128)(2,1)} %get-tuple-element.41), channel_id=1, source_target_pairs={{0,26},{1,27},{2,24},{3,25},{4,30},{5,31},{6,28},{7,29},{8,2},{9,3... | collective-permute-start | bytes 786440 | tf_op jit(solution)/shard_map/ppermute | solution.py:302
  249.8 20.5 %collective-permute-start.13 = (bf16[128,1024]{1,0:T(8,128)(2,1)}, bf16[128,1024]{1,0:T(8,128)(2,1)S(1)}, u32[]{:S(2)}, u32[]{:S(2)}) collective-permute-start(bf16[128,1024]{1,0:T(8,128)(2,1)} %get-tuple-element.42), channel_id=1, source_target_pairs={{0,27},{1,26},{2,25},{3,24},{4,31},{5,30},{6,29},{7,28},{8,3},{9,2... | collective-permute-start | bytes 786440 | tf_op jit(solution)/shard_map/ppermute | solution.py:302
  (10 other events, 18.0 us)

commit v11 on v10

--- a/solution.py
+++ b/solution.py
@@ -10,7 +10,7 @@
 
 BLOCK = 128
 PARTS = 3
-STEP = 4
+STEPS = (8, 4)
 MOST = 1 << 10
 HINT = 16
 VMEM_LIMIT = 48 * 1024 * 1024
@@ -28,42 +28,40 @@
     return terms
 
 
-def pack_kernel(own, group, cuts, keys_ref, values_ref, *outs):
+def pack_kernel(own, group, index, spans, at_ref, keys_ref, values_ref, *outs):
     dim = outs[0].shape[3]
     block = pl.program_id(0)
-    at = 0
-    for index, pieces in enumerate(cuts):
-        for low, high in pieces:
-
-            @pl.when((block >= low) & (block < high))
-            def _(out=outs[at], index=index):
-                for device in range(out.shape[0]):
-                    head = device % group * own + index
-                    for half, source in enumerate((keys_ref, values_ref)):
-                        out[device, half] = source[:, head * dim:(head + 1) * dim]
-
-            at += 1
-
-
-def pack(mem_keys, mem_values, seq, own, group, dim, cuts):
+    for (low, high), out in zip(spans, outs):
+
+        @pl.when((block >= low) & (block < high))
+        def _(out=out):
+            for device in range(out.shape[0]):
+                head = device % group * own + index
+                for half, source in enumerate((keys_ref, values_ref)):
+                    out[device, half] = source[:, head * dim:(head + 1) * dim]
+
+
+def pack(mem_keys, mem_values, at, seq, own, group, dim, index, spans):
     mem_dev, width = mem_keys.shape
-    rows = pl.BlockSpec((BLOCK, width), lambda i: (i, 0))
-    spans = [span for pieces in cuts for span in pieces]
+    rows = pl.BlockSpec((BLOCK, width), lambda i, _: (i, 0))
 
     def place(low, high):
-        return pl.BlockSpec((seq, 2, BLOCK, dim), lambda i: (0, 0, jnp.clip(i - low, 0, high - low - 1), 0))
+        return pl.BlockSpec((seq, 2, BLOCK, dim), lambda i, _: (0, 0, jnp.clip(i - low, 0, high - low - 1), 0))
 
     outs = pl.pallas_call(
-        functools.partial(pack_kernel, own, group, cuts),
+        functools.partial(pack_kernel, own, group, index, spans),
         out_shape=[
             jax.ShapeDtypeStruct((seq, 2, (high - low) * BLOCK, dim), mem_keys.dtype) for low, high in spans
         ],
-        grid=(mem_dev // BLOCK,),
-        in_specs=[rows, rows],
-        out_specs=[place(low, high) for low, high in spans],
+        grid_spec=pltpu.PrefetchScalarGridSpec(
+            num_scalar_prefetch=1,
+            grid=(mem_dev // BLOCK,),
+            in_specs=[rows, rows],
+            out_specs=[place(low, high) for low, high in spans],
+        ),
         compiler_params=pltpu.CompilerParams(vmem_limit_bytes=VMEM_MOST),
-        cost_estimate=pl.CostEstimate(flops=0, bytes_accessed=8 * mem_dev * width, transcendentals=0),
-    )(mem_keys, mem_values)
+        cost_estimate=pl.CostEstimate(flops=0, bytes_accessed=8 * mem_dev * width // own, transcendentals=0),
+    )(at, mem_keys, mem_values)
     return [out.reshape(seq, -1, dim) for out in outs]
 
 
@@ -113,11 +111,12 @@
     )(gates, at[None], grad_out, queries, mem_out, row_total)
 
 
-def attend_kernel(heads, dim, rows, scale, tiles, fresh, last, picks_ref, starts_ref, *refs):
+def attend_kernel(heads, dim, rows, scale, first, tiles, fresh, last, picks_ref, starts_ref, *refs):
     packed_refs, memory_ref = refs[:tiles], refs[tiles]
     acc_in = None if fresh else refs[tiles + 1]
     out_refs, (query_ref, log_ref, delta_ref, total) = refs[tiles + (1 if fresh else 2):-4], refs[-4:]
-    tile = pl.program_id(0)
+    step = pl.program_id(0)
+    tile = first + step
     blocks = memory_ref.shape[1] // 2
     count = heads * rows
 
@@ -128,7 +127,7 @@
 
     for x, packed in enumerate(packed_refs):
 
-        @pl.when(tile == x)
+        @pl.when(step == x)
         def _(packed=packed):
             query_ref[...] = packed[...]
 
@@ -178,31 +177,34 @@
             gained = part if gained is None else gained + part
         total[...] += gained
 
-    full = (high - low) // STEP
-
-    def many(turn, carry):
-        add(low + STEP * turn, STEP, False)
+    for number in STEPS:
+        full = (high - low) // number
+
+        def many(turn, carry, low=low, number=number):
+            add(low + number * turn, number, False)
+            return carry
+
+        lax.fori_loop(0, full, many, 0)
+        low = low + number * full
+
+    def few(turn, carry):
+        add(low + 2 * turn, 2, True)
         return carry
 
-    def few(turn, carry):
-        add(low + STEP * full + 2 * turn, 2, True)
-        return carry
-
-    lax.fori_loop(0, full, many, 0)
-    lax.fori_loop(0, (high - low - STEP * full + 1) // 2, few, 0)
+    lax.fori_loop(0, (high - low + 1) // 2, few, 0)
 
     if not last:
         out_refs[0][0] = total[...]
         return
     for x, out_ref in enumerate(out_refs):
 
-        @pl.when(tile == x)
+        @pl.when(step == x)
         def _(out_ref=out_ref):
             for h in range(heads):
                 out_ref[:, h * dim:(h + 1) * dim] = total[h * rows:(h + 1) * rows, :].astype(jnp.bfloat16)
 
 
-def attend(packed, memory, acc, picks, starts, heads, dim, scale, last):
+def attend(packed, memory, acc, picks, starts, heads, dim, scale, last, first=0):
     tiles = len(packed)
     span = packed[0].shape[0]
     rows = span // (2 * heads + 1)
@@ -210,7 +212,7 @@
     width = heads * rows
     holders = memory.shape[0]
     memory = memory.reshape(holders, -1, BLOCK, dim)
-    acc_spec = pl.BlockSpec((1, width, dim), lambda t, *_: (t, 0, 0))
+    acc_spec = pl.BlockSpec((1, width, dim), lambda t, *_: (first + t, 0, 0))
     if last:
         out_shape = [jax.ShapeDtypeStruct((rows, heads * dim), jnp.bfloat16)] * tiles
         out_spec = [pl.BlockSpec((rows, heads * dim), lambda t, *_: (0, 0))] * tiles
@@ -219,7 +221,7 @@
         out_spec = acc_spec
     flops = tiles * holders * memory.shape[1] * (BLOCK // 4) * width * dim * 6
     return pl.pallas_call(
-        functools.partial(attend_kernel, heads, dim, rows, scale, tiles, fresh, last),
+        functools.partial(attend_kernel, heads, dim, rows, scale, first, tiles, fresh, last),
         out_shape=out_shape,
         grid_spec=pltpu.PrefetchScalarGridSpec(
             num_scalar_prefetch=2,
@@ -323,15 +325,21 @@
         ]
 
     gates = jax.nn.sigmoid(gate_logit[0])
-    memories = list(pack(mem_keys[0], mem_values[0], seq, own, group, dim, cuts))
     gathered, worked, latest, held = [], [], None, []
 
-    def queries_of(i):
+    def memory_of(i, hint):
+        return pack(mem_keys[0], mem_values[0], hint, seq, own, group, dim, i, cuts[i])
+
+    def queries_of(i, memories):
         opened = gates if latest is None else after(gates, latest)
         packed = prepare(grad_out[0], queries[0], mem_out[0], row_total[0], opened, at, kv_heads, dim, scale, own, i)
-        return [packed[0]] + [swapped(packed[x], x) for x in range(1, group)]
-
-    coming = queries_of(0)
+        if i + 1 < own:
+            memories += memory_of(i + 1, after(at[None], packed[0]))
+        sent = [after(packed[x], *memories[len(cuts[i]):]) if i + 1 < own else packed[x] for x in range(group)]
+        return [packed[0]] + [swapped(sent[x], x) for x in range(1, group)]
+
+    memories = memory_of(0, at[None])
+    coming = queries_of(0, memories)
     for i in range(own):
         packed = coming
         pieces = []
@@ -342,19 +350,27 @@
             pieces.append(latest)
             held = packed
         picks, starts = listed(i)
-        run = functools.partial(attend, packed, picks=picks, heads=heads, dim=dim, scale=scale)
+        run = functools.partial(attend, picks=picks, heads=heads, dim=dim, scale=scale)
         acc = None
         for j in range(len(pieces) - 1):
-            acc = run(pieces[j], acc, starts=after(starts[j], *worked), last=False)
+            acc = run(packed, pieces[j], acc, starts=after(starts[j], *worked), last=False)
             worked = [acc]
         if i < own - 1:
-            coming = queries_of(i + 1)
-        ready = coming[:1] if i < own - 1 else gathered
-        done = run(pieces[-1], acc, starts=after(starts[-1], *worked, *ready), last=True)
-        worked = done[:1]
-        results = [delivered(done[x], x) for x in range(group)]
-        gathered = gathered + results
-    return assemble(gathered, at, own, group)[None]
+            coming = queries_of(i + 1, memories)
+            done = run(packed, pieces[-1], acc, starts=after(starts[-1], *worked, coming[0]), last=True)
+            worked = done[:1]
+            gathered += [delivered(done[x], x) for x in range(group)]
+            continue
+        results, half = [], group // 2
+        for low, high in ((0, half), (half, group)):
+            bounds = after(starts[-1], *worked, *([] if low else gathered))
+            done = run(packed[low:high], pieces[-1], acc, starts=bounds, last=True, first=low)
+            worked = done[:1]
+            for x in range(low, high):
+                result = done[x - low]
+                result = after(result, results[x - half]) if low else result
+                results.append(delivered(result, x))
+    return assemble(gathered + results, at, own, group)[None]
 
 
 def solution(mesh):

time: 273 us -> 273 us (level)
  waiting for transfers between devices: 119 us -> 101 us
  Pallas kernels: 110 us -> 119 us
  local copies, waits for them, and re-layouts: 6.27 us -> 13.7 us
    ppermute x8, waiting for transfers between devices: 19.6 us -> 9.37 us  [delivered(): return lax.ppermute(value, ('section', 'seq'), pairs)]
    ppermute x6, waiting for transfers between devices: 90.8 us -> 81.8 us  [swapped(): return lax.ppermute(value, 'seq', [(p, p ^ step) for p in range(seq)])]
    unnamed x35 -> x56, local copies, waits for them, and re-layouts: 4.53 us -> 11.9 us
    pallas_call x1 -> x2, Pallas kernels: 7.72 us -> 14.3 us  [pack(): pl.pallas_call(functools.partial(pack_kernel, own, group, index, spans),...]
    pallas_call x6 -> x13, Pallas kernels: 4.2 us -> 9.44 us  [after(): pl.pallas_call(lambda *refs: None, out_shape=jax.ShapeDtypeStruct(value.s...]
    pallas_call x3 -> x4, Pallas kernels: 87.1 us -> 85.6 us  [attend(): pl.pallas_call(functools.partial(attend_kernel, heads, dim, rows, scale,...]
  transfers between devices with their start and end apart: 17 -> 17, of which waited for: 8 -> 7; matrix products, arithmetic and copies ran while one was open for 2% -> 2% of each run, Pallas kernels for 30% -> 36%
where the time goes in v11:
time: 273 us; the launch traced here: 270 us
  Pallas kernels  119 us (44%)
  waiting for transfers between devices  101 us (37%)
  starting transfers between devices  33.9 us (12%)
  local copies, waits for them, and re-layouts  13.7 us (5%)
    pallas_call x4, Pallas kernels, attend(): pl.pallas_call(functools.partial(attend_kernel, heads, dim, rows, scale,...  85.6 us
    ppermute x6, waiting for transfers between devices, swapped(): return lax.ppermute(value, 'seq', [(p, p ^ step) for p in range(seq)])  81.8 us
    all_to_all x3, starting transfers between devices, shards(): lax.all_to_all(piece, 'seq', split_axis=0, concat_axis=0, tiled=True)  15.4 us
    ppermute x8, starting transfers between devices, delivered(): return lax.ppermute(value, ('section', 'seq'), pairs)  14.3 us
    pallas_call x2, Pallas kernels, pack(): pl.pallas_call(functools.partial(pack_kernel, own, group, index, spans),...  14.3 us
    unnamed x56, local copies, waits for them, and re-layouts  11.9 us
    pallas_call x13, Pallas kernels, after(): pl.pallas_call(lambda *refs: None, out_shape=jax.ShapeDtypeStruct(value.s...  9.44 us
    all_to_all x3, waiting for transfers between devices, shards(): lax.all_to_all(piece, 'seq', split_axis=0, concat_axis=0, tiled=True)  9.43 us
  transfers between devices with their start and end apart: 17, of which 7 were waited for; matrix products, arithmetic and copies ran while one was open for 2% of the time, Pallas kernels for 36%

profile of v11, /device:TPU:0, one launch (start us, length us, event | category | flops | bytes accessed | tf_op | source)
XLA Modules:
  0.0 270.5 jit_solution(4257380867679458425)
XLA Ops:
  0.0 6.8 %shard_map.82 = bf16[8,2,1024,128]{3,2,1,0:T(8,128)(2,1)} custom-call(s32[1]{0:T(128)} %bitcast.at_ref, bf16[1024,1024]{1,0:T(8,128)(2,1)} %bitcast.52, bf16[1024,1024]{1,0:T(8,128)(2,1)} %bitcast.54), custom_call_target="tpu_custom_call" | custom-call | bytes 4194304 | tf_op jit(solution)/shard_map/pallas_call | solution.py:51
  6.8 6.5 %all-to-all-start = ((bf16[8,2048,128]{2,1,0:T(8,128)(2,1)}), bf16[8,2048,128]{2,1,0:T(8,128)(2,1)}, u32[]{:S(2)}, u32[]{:S(2)}) async-start(bf16[8,2048,128]{2,1,0:T(8,128)(2,1)} %bitcast.47), calls=%async_computation | async-start | bytes 8388608 | tf_op jit(solution)/shard_map/all_to_all | solution.py:349
  13.4 4.0 %shard_map.86 = (bf16[2176,128]{1,0:T(8,128)(2,1)S(1)}, bf16[2176,128]{1,0:T(8,128)(2,1)S(1)}, bf16[2176,128]{1,0:T(8,128)(2,1)S(1)}, bf16[2176,128]{1,0:T(8,128)(2,1)S(1)}) custom-call(f32[64]{0:T(128)S(1)} %divide_bitcast_fusion.refs_0_.gate_ref, s32[1]{0:T(128)} %bitcast.at_ref, bf16[128,8192]{1,0:T(8,128)(2,1)S(1)} %bitcast.35, ...), custom_call_target="tpu_custom_call" | custom-call | flops 4194304 | bytes 6291456 | tf_op jit(solution)/shard_map/pallas_call | solution.py:100
  21.9 7.6 %shard_map.88 = (bf16[8,2,640,128]{3,2,1,0:T(8,128)(2,1)}, bf16[8,2,384,128]{3,2,1,0:T(8,128)(2,1)}) custom-call(s32[1]{0:T(128)} %shard_map.87.at_ref, bf16[1024,1024]{1,0:T(8,128)(2,1)} %bitcast.53, bf16[1024,1024]{1,0:T(8,128)(2,1)} %bitcast.55), custom_call_target="tpu_custom_call" | custom-call | bytes 4194304 | tf_op jit(solution)/shard_map/pallas_call | solution.py:51
  30.1 1.8 collective-permute-start.2
  37.9 56.1 %collective-permute-done.2.refs_3_.refs_5_ = bf16[2176,128]{1,0:T(8,128)(2,1)S(1)} collective-permute-done((bf16[2176,128]{1,0:T(8,128)(2,1)}, bf16[2176,128]{1,0:T(8,128)(2,1)S(1)}, u32[]{:S(2)}, u32[]{:S(2)}) %collective-permute-start.2) | collective-permute-done | bytes 557088 | tf_op jit(solution)/shard_map/ppermute | solution.py:300
  94.0 13.7 %collective-permute-done.1.refs_2_.refs_4_ = bf16[2176,128]{1,0:T(8,128)(2,1)S(1)} collective-permute-done((bf16[2176,128]{1,0:T(8,128)(2,1)}, bf16[2176,128]{1,0:T(8,128)(2,1)S(1)}, u32[]{:S(2)}, u32[]{:S(2)}) %collective-permute-start.1) | collective-permute-done | bytes 557088 | tf_op jit(solution)/shard_map/ppermute | solution.py:300
  109.3 4.4 %all-to-all-start.1 = ((bf16[8,1280,128]{2,1,0:T(8,128)(2,1)}), bf16[8,1280,128]{2,1,0:T(8,128)(2,1)}, u32[]{:S(2)}, u32[]{:S(2)}) async-start(bf16[8,1280,128]{2,1,0:T(8,128)(2,1)} %shard_map.94), calls=%async_computation.1 | async-start | bytes 5242880 | tf_op jit(solution)/shard_map/all_to_all | solution.py:349
  115.0 4.6 %shard_map.84 = (bf16[2176,128]{1,0:T(8,128)(2,1)S(1)}, bf16[2176,128]{1,0:T(8,128)(2,1)}, bf16[2176,128]{1,0:T(8,128)(2,1)S(1)}, bf16[2176,128]{1,0:T(8,128)(2,1)S(1)}) custom-call(f32[64]{0:T(128)S(1)} %copy-done.19, s32[1]{0:T(128)} %bitcast.at_ref, bf16[128,8192]{1,0:T(8,128)(2,1)S(1)} %bitcast.36, bf16[128,8192]{1,0:T(8,128)(2,1)} %bitcast.49, ...), custom_call_target="tpu_custom_call" | custom-call | flops 4194304 | bytes 6291456 | tf_op jit(solution)/shard_map/pallas_call | solution.py:100
  123.8 36.1 %shard_map.92 = (bf16[128,1024]{1,0:T(8,128)(2,1)}, bf16[128,1024]{1,0:T(8,128)(2,1)}, bf16[128,1024]{1,0:T(8,128)(2,1)}, bf16[128,1024]{1,0:T(8,128)(2,1)}) custom-call(s32[4,32]{1,0:T(4,128)} %select_reduce_fusion.1.picks_ref, s32[4,2]{1,0:T(4,128)} %shard_map.85.starts_ref, bf16[2176,128]{1,0:T(8,128)(2,1)} %copy-done.1, ...), custom_call_target="tpu_custom_call" | custom-call | flops 51539607552 | tf_op jit(solution)/shard_map/pallas_call | solution.py:223
  160.0 2.5 collective-permute-start.3
  164.3 2.6 collective-permute-start.5
  166.8 2.2 collective-permute-done.8.refs_2_.refs_4_.refs_0_
  169.1 3.6 %collective-permute-start.6 = (bf16[128,1024]{1,0:T(8,128)(2,1)}, bf16[128,1024]{1,0:T(8,128)(2,1)S(1)}, u32[]{:S(2)}, u32[]{:S(2)}) collective-permute-start(bf16[128,1024]{1,0:T(8,128)(2,1)} %get-tuple-element.33), channel_id=1, source_target_pairs={{0,27},{1,26},{2,25},{3,24},{4,31},{5,30},{6,29},{7,28},{8,3},{9,2... | collective-permute-start | bytes 786440 | tf_op jit(solution)/shard_map/ppermute | solution.py:304
  172.7 9.8 %collective-permute-done.9.refs_3_.refs_5_.refs_1_ = bf16[2176,128]{1,0:T(8,128)(2,1)} collective-permute-done((bf16[2176,128]{1,0:T(8,128)(2,1)S(1)}, bf16[2176,128]{1,0:T(8,128)(2,1)}, u32[]{:S(2)}, u32[]{:S(2)}) %collective-permute-start.9) | collective-permute-done | bytes 557088 | tf_op jit(solution)/shard_map/ppermute | solution.py:300
  183.1 4.5 %all-to-all-start.2 = ((bf16[8,768,128]{2,1,0:T(8,128)(2,1)}), bf16[8,768,128]{2,1,0:T(8,128)(2,1)}, u32[]{:S(2)}, u32[]{:S(2)}) async-start(bf16[8,768,128]{2,1,0:T(8,128)(2,1)} %shard_map.97), calls=%async_computation.2 | async-start | bytes 3145728 | tf_op jit(solution)/shard_map/all_to_all | solution.py:349
  187.6 26.2 %shard_map.95.refs_1_.refs_3_ = f32[4,1024,128]{2,1,0:T(8,128)} custom-call(s32[4,32]{1,0:T(4,128)} %select_reduce_fusion.picks_ref, s32[4,2]{1,0:T(4,128)} %shard_map.93.starts_ref, bf16[2176,128]{1,0:T(8,128)(2,1)} %copy-done.2, bf16[2176,128]{1,0:T(8,128)(2,1)} %copy-done.23, bf16[2176,128]{1,0:T(8,128)(2,1)} %copy-done.22, ...), custom_call_target="tpu_custom_call" | custom-call | flops 32212254720 | tf_op jit(solution)/shard_map/pallas_call | solution.py:223
  216.2 9.4 %all-to-all-done.2 = bf16[8,768,128]{2,1,0:T(8,128)(2,1)} async-done(((bf16[8,768,128]{2,1,0:T(8,128)(2,1)}), bf16[8,768,128]{2,1,0:T(8,128)(2,1)}, u32[]{:S(2)}, u32[]{:S(2)}) %all-to-all-start.2) | async-done | bytes 1572896 | tf_op jit(solution)/shard_map/all_to_all | solution.py:349
  225.6 11.7 %shard_map.98 = (bf16[128,1024]{1,0:T(8,128)(2,1)}, bf16[128,1024]{1,0:T(8,128)(2,1)}) custom-call(s32[4,32]{1,0:T(4,128)} %select_reduce_fusion.picks_ref, s32[4,2]{1,0:T(4,128)} %shard_map.96.starts_ref, bf16[2176,128]{1,0:T(8,128)(2,1)} %copy-done.2, bf16[2176,128]{1,0:T(8,128)(2,1)} %copy-done.23, bf16[8,6,128,128]{3,2,1,0:T(8,128)(2,1)} %bitcast.24.refs_2_, ...), custom_call_target="tpu_custom_call" | custom-call | flops 9663676416 | tf_op jit(solution)/shard_map/pallas_call | solution.py:223
  238.0 3.3 %collective-permute-start.10 = (bf16[128,1024]{1,0:T(8,128)(2,1)}, bf16[128,1024]{1,0:T(8,128)(2,1)S(1)}, u32[]{:S(2)}, u32[]{:S(2)}) collective-permute-start(bf16[128,1024]{1,0:T(8,128)(2,1)} %get-tuple-element.37.refs_1_), channel_id=1, source_target_pairs={{0,24},{1,25},{2,26},{3,27},{4,28},{5,29},{6,30},{7,31},{8,0},{9,1... | collective-permute-start | bytes 786440 | tf_op jit(solution)/shard_map/ppermute | solution.py:304
  241.4 11.6 %shard_map.100 = (bf16[128,1024]{1,0:T(8,128)(2,1)}, bf16[128,1024]{1,0:T(8,128)(2,1)}) custom-call(s32[4,32]{1,0:T(4,128)} %select_reduce_fusion.picks_ref, s32[4,2]{1,0:T(4,128)} %shard_map.99.starts_ref, bf16[2176,128]{1,0:T(8,128)(2,1)} %copy-done.22, bf16[2176,128]{1,0:T(8,128)(2,1)} %collective-permute-done.9.refs_3_.refs_5_.refs_1_, ...), custom_call_target="tpu_custom_call" | custom-call | flops 9663676416 | tf_op jit(solution)/shard_map/pallas_call | solution.py:223
  255.7 2.0 collective-permute-start.12
  257.7 6.4 %collective-permute-done.13.refs_7_ = bf16[128,1024]{1,0:T(8,128)(2,1)S(1)} collective-permute-done((bf16[128,1024]{1,0:T(8,128)(2,1)}, bf16[128,1024]{1,0:T(8,128)(2,1)S(1)}, u32[]{:S(2)}, u32[]{:S(2)}) %collective-permute-start.13) | collective-permute-done | bytes 262176 | tf_op jit(solution)/shard_map/ppermute | solution.py:304
  264.1 3.0 %collective-permute-done.12.refs_6_ = bf16[128,1024]{1,0:T(8,128)(2,1)S(1)} collective-permute-done((bf16[128,1024]{1,0:T(8,128)(2,1)}, bf16[128,1024]{1,0:T(8,128)(2,1)S(1)}, u32[]{:S(2)}, u32[]{:S(2)}) %collective-permute-start.12) | collective-permute-done | bytes 262176 | tf_op jit(solution)/shard_map/ppermute | solution.py:304
  (102 shorter events, 30.0 us)
Async XLA Ops:
  6.8 101.0 %all-to-all-start = ((bf16[8,2048,128]{2,1,0:T(8,128)(2,1)}), bf16[8,2048,128]{2,1,0:T(8,128)(2,1)}, u32[]{:S(2)}, u32[]{:S(2)}) async-start(bf16[8,2048,128]{2,1,0:T(8,128)(2,1)} %bitcast.47), calls=%async_computation | async-start | bytes 8388608 | tf_op jit(solution)/shard_map/all_to_all | solution.py:349
  30.1 63.9 %collective-permute-start.2 = (bf16[2176,128]{1,0:T(8,128)(2,1)}, bf16[2176,128]{1,0:T(8,128)(2,1)S(1)}, u32[]{:S(2)}, u32[]{:S(2)}) collective-permute-start(bf16[2176,128]{1,0:T(8,128)(2,1)} %shard_map.91), channel_id=1, source_target_pairs={{0,3},{1,2},{2,1},{3,0},{4,7},{5,6},{6,5},{7,4},{8,11},{9,10},{10,... | collective-permute-start | bytes 1671176 | tf_op jit(solution)/shard_map/ppermute | solution.py:300
  32.6 75.2 %collective-permute-start.1 = (bf16[2176,128]{1,0:T(8,128)(2,1)}, bf16[2176,128]{1,0:T(8,128)(2,1)S(1)}, u32[]{:S(2)}, u32[]{:S(2)}) collective-permute-start(bf16[2176,128]{1,0:T(8,128)(2,1)} %shard_map.90), channel_id=1, source_target_pairs={{0,2},{1,3},{2,0},{3,1},{4,6},{5,7},{6,4},{7,5},{8,10},{9,11},{10,... | collective-permute-start | bytes 1671176 | tf_op jit(solution)/shard_map/ppermute | solution.py:300
  33.6 74.2 %collective-permute-start = (bf16[2176,128]{1,0:T(8,128)(2,1)}, bf16[2176,128]{1,0:T(8,128)(2,1)}, u32[]{:S(2)}, u32[]{:S(2)}) collective-permute-start(bf16[2176,128]{1,0:T(8,128)(2,1)} %shard_map.89), channel_id=1, source_target_pairs={{0,1},{1,0},{2,3},{3,2},{4,5},{5,4},{6,7},{7,6},{8,9},{9,8},{10,11... | collective-permute-start | bytes 1671176 | tf_op jit(solution)/shard_map/ppermute | solution.py:300
  35.5 73.7 %copy-start.24 = (s32[4,2]{1,0:T(4,128)}, s32[4,2]{1,0:T(4,128)S(1)}, u32[]{:S(2)}) copy-start(s32[4,2]{1,0:T(4,128)S(1)} %get-tuple-element.56.refs_0_) | copy-start | bytes 100
  94.0 13.7 %copy-start.20 = (bf16[2176,128]{1,0:T(8,128)(2,1)}, bf16[2176,128]{1,0:T(8,128)(2,1)S(1)}, u32[]{:S(2)}) copy-start(bf16[2176,128]{1,0:T(8,128)(2,1)S(1)} %collective-permute-done.2.refs_3_.refs_5_) | copy-start | bytes 1671172
  109.3 73.2 %all-to-all-start.1 = ((bf16[8,1280,128]{2,1,0:T(8,128)(2,1)}), bf16[8,1280,128]{2,1,0:T(8,128)(2,1)}, u32[]{:S(2)}, u32[]{:S(2)}) async-start(bf16[8,1280,128]{2,1,0:T(8,128)(2,1)} %shard_map.94), calls=%async_computation.1 | async-start | bytes 5242880 | tf_op jit(solution)/shard_map/all_to_all | solution.py:349
  120.5 43.0 %collective-permute-start.7 = (bf16[2176,128]{1,0:T(8,128)(2,1)}, bf16[2176,128]{1,0:T(8,128)(2,1)S(1)}, u32[]{:S(2)}, u32[]{:S(2)}) collective-permute-start(bf16[2176,128]{1,0:T(8,128)(2,1)} %get-tuple-element.34), channel_id=1, source_target_pairs={{0,1},{1,0},{2,3},{3,2},{4,5},{5,4},{6,7},{7,6},{8,9},{9,8},{10,11... | collective-permute-start | bytes 1671176 | tf_op jit(solution)/shard_map/ppermute | solution.py:300
  120.9 48.2 %collective-permute-start.8 = (bf16[2176,128]{1,0:T(8,128)(2,1)S(1)}, bf16[2176,128]{1,0:T(8,128)(2,1)S(1)}, u32[]{:S(2)}, u32[]{:S(2)}) collective-permute-start(bf16[2176,128]{1,0:T(8,128)(2,1)S(1)} %get-tuple-element.35), channel_id=1, source_target_pairs={{0,2},{1,3},{2,0},{3,1},{4,6},{5,7},{6,4},{7,5},{8,10},{9,11},{10,... | collective-permute-start | bytes 1671176 | tf_op jit(solution)/shard_map/ppermute | solution.py:300
  122.6 59.9 %collective-permute-start.9 = (bf16[2176,128]{1,0:T(8,128)(2,1)S(1)}, bf16[2176,128]{1,0:T(8,128)(2,1)}, u32[]{:S(2)}, u32[]{:S(2)}) collective-permute-start(bf16[2176,128]{1,0:T(8,128)(2,1)S(1)} %get-tuple-element.36), channel_id=1, source_target_pairs={{0,3},{1,2},{2,1},{3,0},{4,7},{5,6},{6,5},{7,4},{8,11},{9,10},{10,... | collective-permute-start | bytes 1671176 | tf_op jit(solution)/shard_map/ppermute | solution.py:300
  160.0 53.8 %collective-permute-start.3 = (bf16[128,1024]{1,0:T(8,128)(2,1)}, bf16[128,1024]{1,0:T(8,128)(2,1)S(1)}, u32[]{:S(2)}, u32[]{:S(2)}) collective-permute-start(bf16[128,1024]{1,0:T(8,128)(2,1)} %get-tuple-element.30.refs_1_), channel_id=1, source_target_pairs={{0,24},{1,25},{2,26},{3,27},{4,28},{5,29},{6,30},{7,31},{8,0},{9,1... | collective-permute-start | bytes 786440 | tf_op jit(solution)/shard_map/ppermute | solution.py:304
  163.2 50.6 %collective-permute-start.4 = (bf16[128,1024]{1,0:T(8,128)(2,1)}, bf16[128,1024]{1,0:T(8,128)(2,1)S(1)}, u32[]{:S(2)}, u32[]{:S(2)}) collective-permute-start(bf16[128,1024]{1,0:T(8,128)(2,1)} %get-tuple-element.31), channel_id=1, source_target_pairs={{0,25},{1,24},{2,27},{3,26},{4,29},{5,28},{6,31},{7,30},{8,1},{9,0... | collective-permute-start | bytes 786440 | tf_op jit(solution)/shard_map/ppermute | solution.py:304
  164.3 49.5 %collective-permute-start.5 = (bf16[128,1024]{1,0:T(8,128)(2,1)}, bf16[128,1024]{1,0:T(8,128)(2,1)S(1)}, u32[]{:S(2)}, u32[]{:S(2)}) collective-permute-start(bf16[128,1024]{1,0:T(8,128)(2,1)} %get-tuple-element.32), channel_id=1, source_target_pairs={{0,26},{1,27},{2,24},{3,25},{4,30},{5,31},{6,28},{7,29},{8,2},{9,3... | collective-permute-start | bytes 786440 | tf_op jit(solution)/shard_map/ppermute | solution.py:304
  169.1 13.4 %copy-start.22 = (bf16[2176,128]{1,0:T(8,128)(2,1)}, bf16[2176,128]{1,0:T(8,128)(2,1)S(1)}, u32[]{:S(2)}) copy-start(bf16[2176,128]{1,0:T(8,128)(2,1)S(1)} %collective-permute-done.8.refs_2_.refs_4_.refs_0_) | copy-start | bytes 1671172
  169.1 44.8 %collective-permute-start.6 = (bf16[128,1024]{1,0:T(8,128)(2,1)}, bf16[128,1024]{1,0:T(8,128)(2,1)S(1)}, u32[]{:S(2)}, u32[]{:S(2)}) collective-permute-start(bf16[128,1024]{1,0:T(8,128)(2,1)} %get-tuple-element.33), channel_id=1, source_target_pairs={{0,27},{1,26},{2,25},{3,24},{4,31},{5,30},{6,29},{7,28},{8,3},{9,2... | collective-permute-start | bytes 786440 | tf_op jit(solution)/shard_map/ppermute | solution.py:304
  183.1 42.5 %all-to-all-start.2 = ((bf16[8,768,128]{2,1,0:T(8,128)(2,1)}), bf16[8,768,128]{2,1,0:T(8,128)(2,1)}, u32[]{:S(2)}, u32[]{:S(2)}) async-start(bf16[8,768,128]{2,1,0:T(8,128)(2,1)} %shard_map.97), calls=%async_computation.2 | async-start | bytes 3145728 | tf_op jit(solution)/shard_map/all_to_all | solution.py:349
  238.0 16.4 %collective-permute-start.10 = (bf16[128,1024]{1,0:T(8,128)(2,1)}, bf16[128,1024]{1,0:T(8,128)(2,1)S(1)}, u32[]{:S(2)}, u32[]{:S(2)}) collective-permute-start(bf16[128,1024]{1,0:T(8,128)(2,1)} %get-tuple-element.37.refs_1_), channel_id=1, source_target_pairs={{0,24},{1,25},{2,26},{3,27},{4,28},{5,29},{6,30},{7,31},{8,0},{9,1... | collective-permute-start | bytes 786440 | tf_op jit(solution)/shard_map/ppermute | solution.py:304
  241.3 25.8 %copy-start.4 = (bf16[128,1024]{1,0:T(8,128)(2,1)S(1)}, bf16[128,1024]{1,0:T(8,128)(2,1)}, u32[]{:S(2)}) copy-start(bf16[128,1024]{1,0:T(8,128)(2,1)} %copy-done.3) | copy-start | bytes 786436
  241.3 25.8 %copy-start.6 = (bf16[128,1024]{1,0:T(8,128)(2,1)S(1)}, bf16[128,1024]{1,0:T(8,128)(2,1)}, u32[]{:S(2)}) copy-start(bf16[128,1024]{1,0:T(8,128)(2,1)} %copy-done.5) | copy-start | bytes 786436
  241.3 25.8 %copy-start.8 = (bf16[128,1024]{1,0:T(8,128)(2,1)S(1)}, bf16[128,1024]{1,0:T(8,128)(2,1)}, u32[]{:S(2)}) copy-start(bf16[128,1024]{1,0:T(8,128)(2,1)} %copy-done.7) | copy-start | bytes 786436
  241.3 25.8 %copy-start.10 = (bf16[128,1024]{1,0:T(8,128)(2,1)S(1)}, bf16[128,1024]{1,0:T(8,128)(2,1)}, u32[]{:S(2)}) copy-start(bf16[128,1024]{1,0:T(8,128)(2,1)} %copy-done.9) | copy-start | bytes 786436
  241.3 11.6 %collective-permute-start.11 = (bf16[128,1024]{1,0:T(8,128)(2,1)}, bf16[128,1024]{1,0:T(8,128)(2,1)S(1)}, u32[]{:S(2)}, u32[]{:S(2)}) collective-permute-start(bf16[128,1024]{1,0:T(8,128)(2,1)} %get-tuple-element.38), channel_id=1, source_target_pairs={{0,25},{1,24},{2,27},{3,26},{4,29},{5,28},{6,31},{7,30},{8,1},{9,0... | collective-permute-start | bytes 786440 | tf_op jit(solution)/shard_map/ppermute | solution.py:304
  254.3 9.8 %collective-permute-start.13 = (bf16[128,1024]{1,0:T(8,128)(2,1)}, bf16[128,1024]{1,0:T(8,128)(2,1)S(1)}, u32[]{:S(2)}, u32[]{:S(2)}) collective-permute-start(bf16[128,1024]{1,0:T(8,128)(2,1)} %shard_map.102), channel_id=1, source_target_pairs={{0,27},{1,26},{2,25},{3,24},{4,31},{5,30},{6,29},{7,28},{8,3},{9,2... | collective-permute-start | bytes 786440 | tf_op jit(solution)/shard_map/ppermute | solution.py:304
  255.7 11.3 %collective-permute-start.12 = (bf16[128,1024]{1,0:T(8,128)(2,1)}, bf16[128,1024]{1,0:T(8,128)(2,1)S(1)}, u32[]{:S(2)}, u32[]{:S(2)}) collective-permute-start(bf16[128,1024]{1,0:T(8,128)(2,1)} %shard_map.101), channel_id=1, source_target_pairs={{0,26},{1,27},{2,24},{3,25},{4,30},{5,31},{6,28},{7,29},{8,2},{9,3... | collective-permute-start | bytes 786440 | tf_op jit(solution)/shard_map/ppermute | solution.py:304
  (20 other events, 36.6 us)

commit v12 on v11

--- a/solution.py
+++ b/solution.py
@@ -303,7 +303,7 @@
         pairs = [(s * seq + p, ((s - 1) % sections) * seq + (p ^ step)) for s in range(sections) for p in range(seq)]
         return lax.ppermute(value, ("section", "seq"), pairs)
 
-    cut = (5 * blocks + 7) // 8
+    cut = (3 * blocks + 3) // 4
     cuts = [[(0, blocks)]] * (own - 1) + [[(0, cut), (cut, blocks)]]
 
     def listed(i):
@@ -330,16 +330,19 @@
     def memory_of(i, hint):
         return pack(mem_keys[0], mem_values[0], hint, seq, own, group, dim, i, cuts[i])
 
-    def queries_of(i, memories):
-        opened = gates if latest is None else after(gates, latest)
-        packed = prepare(grad_out[0], queries[0], mem_out[0], row_total[0], opened, at, kv_heads, dim, scale, own, i)
-        if i + 1 < own:
-            memories += memory_of(i + 1, after(at[None], packed[0]))
-        sent = [after(packed[x], *memories[len(cuts[i]):]) if i + 1 < own else packed[x] for x in range(group)]
+    def queries_of(i):
+        return prepare(grad_out[0], queries[0], mem_out[0], row_total[0], gates, at, kv_heads, dim, scale, own, i)
+
+    def exchanged(packed, *first):
+        sent = [after(value, *first) if first else value for value in packed]
         return [packed[0]] + [swapped(sent[x], x) for x in range(1, group)]
 
     memories = memory_of(0, at[None])
-    coming = queries_of(0, memories)
+    asked = [queries_of(0)]
+    for i in range(1, own):
+        memories += memory_of(i, after(at[None], asked[-1][0]))
+        asked.append(queries_of(i))
+    coming = exchanged(asked[0], *memories[len(cuts[0]):], *[value[0] for value in asked[1:]])
     for i in range(own):
         packed = coming
         pieces = []
@@ -356,20 +359,20 @@
             acc = run(packed, pieces[j], acc, starts=after(starts[j], *worked), last=False)
             worked = [acc]
         if i < own - 1:
-            coming = queries_of(i + 1, memories)
-            done = run(packed, pieces[-1], acc, starts=after(starts[-1], *worked, coming[0]), last=True)
+            coming = exchanged(asked[i + 1], latest)
+            done = run(packed, pieces[-1], acc, starts=after(starts[-1], *worked), last=True)
             worked = done[:1]
             gathered += [delivered(done[x], x) for x in range(group)]
             continue
-        results, half = [], group // 2
-        for low, high in ((0, half), (half, group)):
-            bounds = after(starts[-1], *worked, *([] if low else gathered))
+        results, half = [None] * group, group // 2
+        for low, high in ((half, group), (0, half)):
+            bounds = after(starts[-1], *worked, *(gathered if low else []))
             done = run(packed[low:high], pieces[-1], acc, starts=bounds, last=True, first=low)
             worked = done[:1]
             for x in range(low, high):
                 result = done[x - low]
-                result = after(result, results[x - half]) if low else result
-                results.append(delivered(result, x))
+                result = result if low else after(result, results[x + half])
+                results[x] = delivered(result, x)
     return assemble(gathered + results, at, own, group)[None]
 
 

time: 273 us -> 276 us (1.011)
  local copies, waits for them, and re-layouts: 13.7 us -> 16.6 us
    all_to_all x3, waiting for transfers between devices: 9.43 us -> 0.01 us  [shards(): lax.all_to_all(piece, 'seq', split_axis=0, concat_axis=0, tiled=True)]
    ppermute x6, waiting for transfers between devices: 81.8 us -> 89.2 us  [swapped(): return lax.ppermute(value, 'seq', [(p, p ^ step) for p in range(seq)])]
    ppermute x8, waiting for transfers between devices: 9.37 us -> 13 us  [delivered(): return lax.ppermute(value, ('section', 'seq'), pairs)]
    unnamed x56 -> x64, local copies, waits for them, and re-layouts: 11.9 us -> 14.9 us
    pallas_call x13 -> x15, Pallas kernels: 9.44 us -> 10.2 us  [after(): pl.pallas_call(lambda *refs: None, out_shape=jax.ShapeDtypeStruct(value.s...]
where the time goes in v12:
time: 276 us; the launch traced here: 274 us
  Pallas kernels  117 us (42%)
  waiting for transfers between devices  102 us (37%)
  starting transfers between devices  35.4 us (13%)
  local copies, waits for them, and re-layouts  16.6 us (6%)
    ppermute x6, waiting for transfers between devices, swapped(): return lax.ppermute(value, 'seq', [(p, p ^ step) for p in range(seq)])  89.2 us
    pallas_call x4, Pallas kernels, attend(): pl.pallas_call(functools.partial(attend_kernel, heads, dim, rows, scale,...  83.3 us
    ppermute x8, starting transfers between devices, delivered(): return lax.ppermute(value, ('section', 'seq'), pairs)  16.2 us
    all_to_all x3, starting transfers between devices, shards(): lax.all_to_all(piece, 'seq', split_axis=0, concat_axis=0, tiled=True)  15 us
    unnamed x64, local copies, waits for them, and re-layouts  14.9 us
    pallas_call x2, Pallas kernels, pack(): pl.pallas_call(functools.partial(pack_kernel, own, group, index, spans),...  14.2 us
    ppermute x8, waiting for transfers between devices, delivered(): return lax.ppermute(value, ('section', 'seq'), pairs)  13 us
    pallas_call x15, Pallas kernels, after(): pl.pallas_call(lambda *refs: None, out_shape=jax.ShapeDtypeStruct(value.s...  10.2 us
  transfers between devices with their start and end apart: 17, of which 7 were waited for; matrix products, arithmetic and copies ran while one was open for 2% of the time, Pallas kernels for 36%

profile of v12, /device:TPU:0, one launch (start us, length us, event | category | flops | bytes accessed | tf_op | source)
XLA Modules:
  0.0 274.3 jit_solution(17344423255395989476)
XLA Ops:
  0.0 6.7 %shard_map.90 = bf16[8,2,1024,128]{3,2,1,0:T(8,128)(2,1)} custom-call(s32[1]{0:T(128)} %bitcast.at_ref, bf16[1024,1024]{1,0:T(8,128)(2,1)} %bitcast.52, bf16[1024,1024]{1,0:T(8,128)(2,1)} %bitcast.54), custom_call_target="tpu_custom_call" | custom-call | bytes 4194304 | tf_op jit(solution)/shard_map/pallas_call | solution.py:51
  6.7 6.5 %all-to-all-start = ((bf16[8,2048,128]{2,1,0:T(8,128)(2,1)}), bf16[8,2048,128]{2,1,0:T(8,128)(2,1)}, u32[]{:S(2)}, u32[]{:S(2)}) async-start(bf16[8,2048,128]{2,1,0:T(8,128)(2,1)} %bitcast.47), calls=%async_computation | async-start | bytes 8388608 | tf_op jit(solution)/shard_map/all_to_all | solution.py:352
  13.3 4.0 %shard_map.83 = (bf16[2176,128]{1,0:T(8,128)(2,1)S(1)}, bf16[2176,128]{1,0:T(8,128)(2,1)S(1)}, bf16[2176,128]{1,0:T(8,128)(2,1)S(1)}, bf16[2176,128]{1,0:T(8,128)(2,1)S(1)}) custom-call(f32[64]{0:T(128)S(1)} %divide_bitcast_fusion.gate_ref, s32[1]{0:T(128)} %bitcast.at_ref, bf16[128,8192]{1,0:T(8,128)(2,1)S(1)} %bitcast.35, bf16[128,8192]{1,0:T(8,128)(2,1)} %bitcast.48, ...), custom_call_target="tpu_custom_call" | custom-call | flops 4194304 | bytes 6291456 | tf_op jit(solution)/shard_map/pallas_call | solution.py:100
  21.8 7.5 %shard_map.85 = (bf16[8,2,768,128]{3,2,1,0:T(8,128)(2,1)}, bf16[8,2,256,128]{3,2,1,0:T(8,128)(2,1)}) custom-call(s32[1]{0:T(128)} %shard_map.84.at_ref, bf16[1024,1024]{1,0:T(8,128)(2,1)} %bitcast.53, bf16[1024,1024]{1,0:T(8,128)(2,1)} %bitcast.55), custom_call_target="tpu_custom_call" | custom-call | bytes 4194304 | tf_op jit(solution)/shard_map/pallas_call | solution.py:51
  29.3 4.0 %shard_map.86 = (bf16[2176,128]{1,0:T(8,128)(2,1)S(1)}, bf16[2176,128]{1,0:T(8,128)(2,1)S(1)}, bf16[2176,128]{1,0:T(8,128)(2,1)S(1)}, bf16[2176,128]{1,0:T(8,128)(2,1)S(1)}) custom-call(f32[64]{0:T(128)S(1)} %divide_bitcast_fusion.gate_ref, s32[1]{0:T(128)} %bitcast.at_ref, bf16[128,8192]{1,0:T(8,128)(2,1)S(1)} %bitcast.36, bf16[128,8192]{1,0:T(8,128)(2,1)} %bitcast.49, ...), custom_call_target="tpu_custom_call" | custom-call | flops 4194304 | bytes 6291456 | tf_op jit(solution)/shard_map/pallas_call | solution.py:100
  37.3 1.8 collective-permute-start.2
  43.9 50.1 %collective-permute-done.2.refs_3_.refs_5_ = bf16[2176,128]{1,0:T(8,128)(2,1)S(1)} collective-permute-done((bf16[2176,128]{1,0:T(8,128)(2,1)}, bf16[2176,128]{1,0:T(8,128)(2,1)S(1)}, u32[]{:S(2)}, u32[]{:S(2)}) %collective-permute-start.2) | collective-permute-done | bytes 557088 | tf_op jit(solution)/shard_map/ppermute | solution.py:300
  93.9 13.7 %collective-permute-done.1.refs_2_.refs_4_ = bf16[2176,128]{1,0:T(8,128)(2,1)S(1)} collective-permute-done((bf16[2176,128]{1,0:T(8,128)(2,1)}, bf16[2176,128]{1,0:T(8,128)(2,1)S(1)}, u32[]{:S(2)}, u32[]{:S(2)}) %collective-permute-start.1) | collective-permute-done | bytes 557088 | tf_op jit(solution)/shard_map/ppermute | solution.py:300
  109.4 4.4 %all-to-all-start.1 = ((bf16[8,1536,128]{2,1,0:T(8,128)(2,1)}), bf16[8,1536,128]{2,1,0:T(8,128)(2,1)}, u32[]{:S(2)}, u32[]{:S(2)}) async-start(bf16[8,1536,128]{2,1,0:T(8,128)(2,1)} %shard_map.96), calls=%async_computation.1 | async-start | bytes 6291456 | tf_op jit(solution)/shard_map/all_to_all | solution.py:352
  119.8 36.1 %shard_map.91 = (bf16[128,1024]{1,0:T(8,128)(2,1)}, bf16[128,1024]{1,0:T(8,128)(2,1)}, bf16[128,1024]{1,0:T(8,128)(2,1)}, bf16[128,1024]{1,0:T(8,128)(2,1)}) custom-call(s32[4,32]{1,0:T(4,128)} %select_reduce_fusion.1.picks_ref, s32[4,2]{1,0:T(4,128)} %shard_map.82.starts_ref, bf16[2176,128]{1,0:T(8,128)(2,1)} %copy-done.2, bf16[2176,128]{1,0:T(8,128)(2,1)} %copy-done.24, ...), custom_call_target="tpu_custom_call" | custom-call | flops 51539607552 | tf_op jit(solution)/shard_map/pallas_call | solution.py:223
  155.9 2.5 collective-permute-start.3
  159.4 2.6 collective-permute-start.5
  162.0 15.8 %collective-permute-done.8.refs_2_.refs_4_.refs_0_ = bf16[2176,128]{1,0:T(8,128)(2,1)S(1)} collective-permute-done((bf16[2176,128]{1,0:T(8,128)(2,1)}, bf16[2176,128]{1,0:T(8,128)(2,1)S(1)}, u32[]{:S(2)}, u32[]{:S(2)}) %collective-permute-start.8) | collective-permute-done | bytes 557088 | tf_op jit(solution)/shard_map/ppermute | solution.py:300
  177.8 3.5 %collective-permute-start.6 = (bf16[128,1024]{1,0:T(8,128)(2,1)}, bf16[128,1024]{1,0:T(8,128)(2,1)S(1)}, u32[]{:S(2)}, u32[]{:S(2)}) collective-permute-start(bf16[128,1024]{1,0:T(8,128)(2,1)} %get-tuple-element.33), channel_id=1, source_target_pairs={{0,27},{1,26},{2,25},{3,24},{4,31},{5,30},{6,29},{7,28},{8,3},{9,2... | collective-permute-start | bytes 786440 | tf_op jit(solution)/shard_map/ppermute | solution.py:304
  181.3 9.7 %collective-permute-done.9.refs_3_.refs_5_.refs_1_ = bf16[2176,128]{1,0:T(8,128)(2,1)S(1)} collective-permute-done((bf16[2176,128]{1,0:T(8,128)(2,1)}, bf16[2176,128]{1,0:T(8,128)(2,1)S(1)}, u32[]{:S(2)}, u32[]{:S(2)}) %collective-permute-start.9) | collective-permute-done | bytes 557088 | tf_op jit(solution)/shard_map/ppermute | solution.py:300
  192.5 4.1 %all-to-all-start.2 = ((bf16[8,512,128]{2,1,0:T(8,128)(2,1)}), bf16[8,512,128]{2,1,0:T(8,128)(2,1)S(1)}, u32[]{:S(2)}, u32[]{:S(2)}) async-start(bf16[8,512,128]{2,1,0:T(8,128)(2,1)} %shard_map.99), calls=%async_computation.2 | async-start | bytes 2097152 | tf_op jit(solution)/shard_map/all_to_all | solution.py:352
  196.6 29.6 %shard_map.97.refs_1_.refs_3_ = f32[4,1024,128]{2,1,0:T(8,128)} custom-call(s32[4,32]{1,0:T(4,128)} %select_reduce_fusion.picks_ref, s32[4,2]{1,0:T(4,128)} %shard_map.92.starts_ref, bf16[2176,128]{1,0:T(8,128)(2,1)} %copy-done, bf16[2176,128]{1,0:T(8,128)(2,1)} %copy-done.25, bf16[2176,128]{1,0:T(8,128)(2,1)} %copy-done.26, bf16[2176,128]{1,0:T(8,128)(2,1)} %copy-done.27, ...), custom_call_target="tpu_custom_call" | custom-call | flops 38654705664 | tf_op jit(solution)/shard_map/pallas_call | solution.py:223
  229.6 9.5 %shard_map.100 = (bf16[128,1024]{1,0:T(8,128)(2,1)}, bf16[128,1024]{1,0:T(8,128)(2,1)}) custom-call(s32[4,32]{1,0:T(4,128)} %select_reduce_fusion.picks_ref, s32[4,2]{1,0:T(4,128)} %shard_map.98.starts_ref, bf16[2176,128]{1,0:T(8,128)(2,1)} %copy-done.26, bf16[2176,128]{1,0:T(8,128)(2,1)} %copy-done.27, bf16[8,4,128,128]{3,2,1,0:T(8,128)(2,1)} %bitcast.56, ...), custom_call_target="tpu_custom_call" | custom-call | flops 6442450944 | tf_op jit(solution)/shard_map/pallas_call | solution.py:223
  239.8 4.9 %collective-permute-start.10 = (bf16[128,1024]{1,0:T(8,128)(2,1)}, bf16[128,1024]{1,0:T(8,128)(2,1)S(1)}, u32[]{:S(2)}, u32[]{:S(2)}) collective-permute-start(bf16[128,1024]{1,0:T(8,128)(2,1)} %get-tuple-element.37.refs_1_), channel_id=1, source_target_pairs={{0,26},{1,27},{2,24},{3,25},{4,30},{5,31},{6,28},{7,29},{8,2},{9,3... | collective-permute-start | bytes 786440 | tf_op jit(solution)/shard_map/ppermute | solution.py:304
  244.8 8.0 %shard_map.102 = (bf16[128,1024]{1,0:T(8,128)(2,1)}, bf16[128,1024]{1,0:T(8,128)(2,1)}) custom-call(s32[4,32]{1,0:T(4,128)} %select_reduce_fusion.picks_ref, s32[4,2]{1,0:T(4,128)} %shard_map.101.starts_ref, bf16[2176,128]{1,0:T(8,128)(2,1)} %copy-done, bf16[2176,128]{1,0:T(8,128)(2,1)} %copy-done.25, bf16[8,4,128,128]{3,2,1,0:T(8,128)(2,1)} %bitcast.57, ...), custom_call_target="tpu_custom_call" | custom-call | flops 6442450944 | tf_op jit(solution)/shard_map/pallas_call | solution.py:223
  252.8 2.3 collective-permute-done.12.refs_1_.refs_7_
  256.5 2.3 collective-permute-start.13
  260.3 5.4 %collective-permute-done.13.refs_5_ = bf16[128,1024]{1,0:T(8,128)(2,1)S(1)} collective-permute-done((bf16[128,1024]{1,0:T(8,128)(2,1)}, bf16[128,1024]{1,0:T(8,128)(2,1)S(1)}, u32[]{:S(2)}, u32[]{:S(2)}) %collective-permute-start.13) | collective-permute-done | bytes 262176 | tf_op jit(solution)/shard_map/ppermute | solution.py:304
  265.7 5.2 %collective-permute-done.11.refs_4_ = bf16[128,1024]{1,0:T(8,128)(2,1)S(1)} collective-permute-done((bf16[128,1024]{1,0:T(8,128)(2,1)}, bf16[128,1024]{1,0:T(8,128)(2,1)S(1)}, u32[]{:S(2)}, u32[]{:S(2)}) %collective-permute-start.11) | collective-permute-done | bytes 262176 | tf_op jit(solution)/shard_map/ppermute | solution.py:304
  (112 shorter events, 33.9 us)
Async XLA Ops:
  6.7 101.0 %all-to-all-start = ((bf16[8,2048,128]{2,1,0:T(8,128)(2,1)}), bf16[8,2048,128]{2,1,0:T(8,128)(2,1)}, u32[]{:S(2)}, u32[]{:S(2)}) async-start(bf16[8,2048,128]{2,1,0:T(8,128)(2,1)} %bitcast.47), calls=%async_computation | async-start | bytes 8388608 | tf_op jit(solution)/shard_map/all_to_all | solution.py:352
  37.3 56.7 %collective-permute-start.2 = (bf16[2176,128]{1,0:T(8,128)(2,1)}, bf16[2176,128]{1,0:T(8,128)(2,1)S(1)}, u32[]{:S(2)}, u32[]{:S(2)}) collective-permute-start(bf16[2176,128]{1,0:T(8,128)(2,1)} %shard_map.89), channel_id=1, source_target_pairs={{0,3},{1,2},{2,1},{3,0},{4,7},{5,6},{6,5},{7,4},{8,11},{9,10},{10,... | collective-permute-start | bytes 1671176 | tf_op jit(solution)/shard_map/ppermute | solution.py:300
  39.7 68.0 %collective-permute-start.1 = (bf16[2176,128]{1,0:T(8,128)(2,1)}, bf16[2176,128]{1,0:T(8,128)(2,1)S(1)}, u32[]{:S(2)}, u32[]{:S(2)}) collective-permute-start(bf16[2176,128]{1,0:T(8,128)(2,1)} %shard_map.88), channel_id=1, source_target_pairs={{0,2},{1,3},{2,0},{3,1},{4,6},{5,7},{6,4},{7,5},{8,10},{9,11},{10,... | collective-permute-start | bytes 1671176 | tf_op jit(solution)/shard_map/ppermute | solution.py:300
  40.8 66.9 %collective-permute-start = (bf16[2176,128]{1,0:T(8,128)(2,1)}, bf16[2176,128]{1,0:T(8,128)(2,1)S(1)}, u32[]{:S(2)}, u32[]{:S(2)}) collective-permute-start(bf16[2176,128]{1,0:T(8,128)(2,1)} %shard_map.87), channel_id=1, source_target_pairs={{0,1},{1,0},{2,3},{3,2},{4,5},{5,4},{6,7},{7,6},{8,9},{9,8},{10,11... | collective-permute-start | bytes 1671176 | tf_op jit(solution)/shard_map/ppermute | solution.py:300
  43.3 66.1 %copy-start.28 = (s32[4,2]{1,0:T(4,128)}, s32[4,2]{1,0:T(4,128)S(1)}, u32[]{:S(2)}) copy-start(s32[4,2]{1,0:T(4,128)S(1)} %get-tuple-element.56.refs_0_) | copy-start | bytes 100
  93.9 13.7 %copy-start.22 = (bf16[2176,128]{1,0:T(8,128)(2,1)}, bf16[2176,128]{1,0:T(8,128)(2,1)S(1)}, u32[]{:S(2)}) copy-start(bf16[2176,128]{1,0:T(8,128)(2,1)S(1)} %collective-permute-done.2.refs_3_.refs_5_) | copy-start | bytes 1671172
  109.4 81.5 %all-to-all-start.1 = ((bf16[8,1536,128]{2,1,0:T(8,128)(2,1)}), bf16[8,1536,128]{2,1,0:T(8,128)(2,1)}, u32[]{:S(2)}, u32[]{:S(2)}) async-start(bf16[8,1536,128]{2,1,0:T(8,128)(2,1)} %shard_map.96), calls=%async_computation.1 | async-start | bytes 6291456 | tf_op jit(solution)/shard_map/all_to_all | solution.py:352
  116.4 43.0 %collective-permute-start.7 = (bf16[2176,128]{1,0:T(8,128)(2,1)}, bf16[2176,128]{1,0:T(8,128)(2,1)S(1)}, u32[]{:S(2)}, u32[]{:S(2)}) collective-permute-start(bf16[2176,128]{1,0:T(8,128)(2,1)} %shard_map.93), channel_id=1, source_target_pairs={{0,1},{1,0},{2,3},{3,2},{4,5},{5,4},{6,7},{7,6},{8,9},{9,8},{10,11... | collective-permute-start | bytes 1671176 | tf_op jit(solution)/shard_map/ppermute | solution.py:300
  117.5 60.3 %collective-permute-start.8 = (bf16[2176,128]{1,0:T(8,128)(2,1)}, bf16[2176,128]{1,0:T(8,128)(2,1)S(1)}, u32[]{:S(2)}, u32[]{:S(2)}) collective-permute-start(bf16[2176,128]{1,0:T(8,128)(2,1)} %shard_map.94), channel_id=1, source_target_pairs={{0,2},{1,3},{2,0},{3,1},{4,6},{5,7},{6,4},{7,5},{8,10},{9,11},{10,... | collective-permute-start | bytes 1671176 | tf_op jit(solution)/shard_map/ppermute | solution.py:300
  119.8 71.1 %collective-permute-start.9 = (bf16[2176,128]{1,0:T(8,128)(2,1)}, bf16[2176,128]{1,0:T(8,128)(2,1)S(1)}, u32[]{:S(2)}, u32[]{:S(2)}) collective-permute-start(bf16[2176,128]{1,0:T(8,128)(2,1)} %shard_map.95), channel_id=1, source_target_pairs={{0,3},{1,2},{2,1},{3,0},{4,7},{5,6},{6,5},{7,4},{8,11},{9,10},{10,... | collective-permute-start | bytes 1671176 | tf_op jit(solution)/shard_map/ppermute | solution.py:300
  155.9 70.3 %collective-permute-start.3 = (bf16[128,1024]{1,0:T(8,128)(2,1)}, bf16[128,1024]{1,0:T(8,128)(2,1)S(1)}, u32[]{:S(2)}, u32[]{:S(2)}) collective-permute-start(bf16[128,1024]{1,0:T(8,128)(2,1)} %get-tuple-element.30.refs_1_), channel_id=1, source_target_pairs={{0,24},{1,25},{2,26},{3,27},{4,28},{5,29},{6,30},{7,31},{8,0},{9,1... | collective-permute-start | bytes 786440 | tf_op jit(solution)/shard_map/ppermute | solution.py:304
  159.1 67.1 %collective-permute-start.4 = (bf16[128,1024]{1,0:T(8,128)(2,1)}, bf16[128,1024]{1,0:T(8,128)(2,1)S(1)}, u32[]{:S(2)}, u32[]{:S(2)}) collective-permute-start(bf16[128,1024]{1,0:T(8,128)(2,1)} %get-tuple-element.31), channel_id=1, source_target_pairs={{0,25},{1,24},{2,27},{3,26},{4,29},{5,28},{6,31},{7,30},{8,1},{9,0... | collective-permute-start | bytes 786440 | tf_op jit(solution)/shard_map/ppermute | solution.py:304
  159.4 31.5 %copy-start.25 = (bf16[2176,128]{1,0:T(8,128)(2,1)}, bf16[2176,128]{1,0:T(8,128)(2,1)S(1)}, u32[]{:S(2)}) copy-start(bf16[2176,128]{1,0:T(8,128)(2,1)S(1)} %collective-permute-done.7.refs_1_.refs_3_) | copy-start | bytes 1671172
  159.4 66.8 %collective-permute-start.5 = (bf16[128,1024]{1,0:T(8,128)(2,1)}, bf16[128,1024]{1,0:T(8,128)(2,1)S(1)}, u32[]{:S(2)}, u32[]{:S(2)}) collective-permute-start(bf16[128,1024]{1,0:T(8,128)(2,1)} %get-tuple-element.32), channel_id=1, source_target_pairs={{0,26},{1,27},{2,24},{3,25},{4,30},{5,31},{6,28},{7,29},{8,2},{9,3... | collective-permute-start | bytes 786440 | tf_op jit(solution)/shard_map/ppermute | solution.py:304
  177.8 48.5 %collective-permute-start.6 = (bf16[128,1024]{1,0:T(8,128)(2,1)}, bf16[128,1024]{1,0:T(8,128)(2,1)S(1)}, u32[]{:S(2)}, u32[]{:S(2)}) collective-permute-start(bf16[128,1024]{1,0:T(8,128)(2,1)} %get-tuple-element.33), channel_id=1, source_target_pairs={{0,27},{1,26},{2,25},{3,24},{4,31},{5,30},{6,29},{7,28},{8,3},{9,2... | collective-permute-start | bytes 786440 | tf_op jit(solution)/shard_map/ppermute | solution.py:304
  192.5 36.1 %all-to-all-start.2 = ((bf16[8,512,128]{2,1,0:T(8,128)(2,1)}), bf16[8,512,128]{2,1,0:T(8,128)(2,1)S(1)}, u32[]{:S(2)}, u32[]{:S(2)}) async-start(bf16[8,512,128]{2,1,0:T(8,128)(2,1)} %shard_map.99), calls=%async_computation.2 | async-start | bytes 2097152 | tf_op jit(solution)/shard_map/all_to_all | solution.py:352
  239.8 19.0 %collective-permute-start.10 = (bf16[128,1024]{1,0:T(8,128)(2,1)}, bf16[128,1024]{1,0:T(8,128)(2,1)S(1)}, u32[]{:S(2)}, u32[]{:S(2)}) collective-permute-start(bf16[128,1024]{1,0:T(8,128)(2,1)} %get-tuple-element.37.refs_1_), channel_id=1, source_target_pairs={{0,26},{1,27},{2,24},{3,25},{4,30},{5,31},{6,28},{7,29},{8,2},{9,3... | collective-permute-start | bytes 786440 | tf_op jit(solution)/shard_map/ppermute | solution.py:304
  244.7 26.2 %copy-start.4 = (bf16[128,1024]{1,0:T(8,128)(2,1)S(1)}, bf16[128,1024]{1,0:T(8,128)(2,1)}, u32[]{:S(2)}) copy-start(bf16[128,1024]{1,0:T(8,128)(2,1)} %copy-done.3) | copy-start | bytes 786436
  244.7 26.2 %copy-start.6 = (bf16[128,1024]{1,0:T(8,128)(2,1)S(1)}, bf16[128,1024]{1,0:T(8,128)(2,1)}, u32[]{:S(2)}) copy-start(bf16[128,1024]{1,0:T(8,128)(2,1)} %copy-done.5) | copy-start | bytes 786436
  244.7 26.2 %copy-start.8 = (bf16[128,1024]{1,0:T(8,128)(2,1)S(1)}, bf16[128,1024]{1,0:T(8,128)(2,1)}, u32[]{:S(2)}) copy-start(bf16[128,1024]{1,0:T(8,128)(2,1)} %copy-done.7) | copy-start | bytes 786436
  244.7 26.2 %copy-start.10 = (bf16[128,1024]{1,0:T(8,128)(2,1)S(1)}, bf16[128,1024]{1,0:T(8,128)(2,1)}, u32[]{:S(2)}) copy-start(bf16[128,1024]{1,0:T(8,128)(2,1)} %copy-done.9) | copy-start | bytes 786436
  244.7 10.4 %collective-permute-start.12 = (bf16[128,1024]{1,0:T(8,128)(2,1)}, bf16[128,1024]{1,0:T(8,128)(2,1)S(1)}, u32[]{:S(2)}, u32[]{:S(2)}) collective-permute-start(bf16[128,1024]{1,0:T(8,128)(2,1)} %get-tuple-element.40), channel_id=1, source_target_pairs={{0,27},{1,26},{2,25},{3,24},{4,31},{5,30},{6,29},{7,28},{8,3},{9,2... | collective-permute-start | bytes 786440 | tf_op jit(solution)/shard_map/ppermute | solution.py:304
  256.5 9.2 %collective-permute-start.13 = (bf16[128,1024]{1,0:T(8,128)(2,1)}, bf16[128,1024]{1,0:T(8,128)(2,1)S(1)}, u32[]{:S(2)}, u32[]{:S(2)}) collective-permute-start(bf16[128,1024]{1,0:T(8,128)(2,1)} %shard_map.104), channel_id=1, source_target_pairs={{0,25},{1,24},{2,27},{3,26},{4,29},{5,28},{6,31},{7,30},{8,1},{9,0... | collective-permute-start | bytes 786440 | tf_op jit(solution)/shard_map/ppermute | solution.py:304
  260.1 10.8 %collective-permute-start.11 = (bf16[128,1024]{1,0:T(8,128)(2,1)}, bf16[128,1024]{1,0:T(8,128)(2,1)S(1)}, u32[]{:S(2)}, u32[]{:S(2)}) collective-permute-start(bf16[128,1024]{1,0:T(8,128)(2,1)} %shard_map.103), channel_id=1, source_target_pairs={{0,24},{1,25},{2,26},{3,27},{4,28},{5,29},{6,30},{7,31},{8,0},{9,1... | collective-permute-start | bytes 786440 | tf_op jit(solution)/shard_map/ppermute | solution.py:304
  (24 other events, 49.5 us)

commit v13 on v12

--- a/solution.py
+++ b/solution.py
@@ -303,11 +303,17 @@
         pairs = [(s * seq + p, ((s - 1) % sections) * seq + (p ^ step)) for s in range(sections) for p in range(seq)]
         return lax.ppermute(value, ("section", "seq"), pairs)
 
-    cut = (3 * blocks + 3) // 4
+    cut = (5 * blocks + 7) // 8
     cuts = [[(0, blocks)]] * (own - 1) + [[(0, cut), (cut, blocks)]]
 
+    moved = own > 1
+    chosen = retrieved[0]
+    if moved:
+        chosen = delivered(chosen, 0)
+
     def listed(i):
-        mine = lax.dynamic_index_in_dim(retrieved[0], at * own + i, 0, keepdims=False)
+        source = chosen if i == own - 1 else retrieved[0]
+        mine = lax.dynamic_index_in_dim(source, at * own + i, 0, keepdims=False)
         mine = jnp.stack(
             [lax.dynamic_index_in_dim(mine, home * group + (at ^ x), 0, keepdims=False) for x in range(group)]
         )
@@ -343,6 +349,8 @@
         memories += memory_of(i, after(at[None], asked[-1][0]))
         asked.append(queries_of(i))
     coming = exchanged(asked[0], *memories[len(cuts[0]):], *[value[0] for value in asked[1:]])
+    if moved:
+        memories[-len(cuts[-1]):] = [delivered(value, 0) for value in memories[-len(cuts[-1]):]]
     for i in range(own):
         packed = coming
         pieces = []
@@ -359,7 +367,10 @@
             acc = run(packed, pieces[j], acc, starts=after(starts[j], *worked), last=False)
             worked = [acc]
         if i < own - 1:
-            coming = exchanged(asked[i + 1], latest)
+            if i == own - 2:
+                coming = [delivered(after(value, latest), x) for x, value in enumerate(asked[i + 1])]
+            else:
+                coming = exchanged(asked[i + 1], latest)
             done = run(packed, pieces[-1], acc, starts=after(starts[-1], *worked), last=True)
             worked = done[:1]
             gathered += [delivered(done[x], x) for x in range(group)]
@@ -371,8 +382,12 @@
             worked = done[:1]
             for x in range(low, high):
                 result = done[x - low]
-                result = result if low else after(result, results[x + half])
-                results[x] = delivered(result, x)
+                if not moved:
+                    results[x] = delivered(result if low else after(result, results[x + half]), x)
+                elif x:
+                    results[x] = swapped(result if low else after(result, *results[half:]), x)
+                else:
+                    results[x] = result
     return assemble(gathered + results, at, own, group)[None]
 
 

time: 276 us -> 286 us (1.036)
  waiting for transfers between devices: 102 us -> 108 us
  starting transfers between devices: 35.4 us -> 39.5 us
    ppermute x6, waiting for transfers between devices: 89.2 us -> 1.87 us  [swapped(): return lax.ppermute(value, 'seq', [(p, p ^ step) for p in range(seq)])]
    ppermute x8 -> x11, waiting for transfers between devices: 13 us -> 97.3 us  [delivered(): return lax.ppermute(value, ('section', 'seq'), pairs)]
    all_to_all x3, waiting for transfers between devices: 0.01 us -> 9.24 us  [shards(): lax.all_to_all(piece, 'seq', split_axis=0, concat_axis=0, tiled=True)]
    ppermute x8 -> x11, starting transfers between devices: 16.2 us -> 19.3 us  [delivered(): return lax.ppermute(value, ('section', 'seq'), pairs)]
    unnamed x64 -> x70, local copies, waits for them, and re-layouts: 14.9 us -> 15.4 us
  transfers between devices with their start and end apart: 17 -> 20, of which waited for: 7 -> 6; matrix products, arithmetic and copies ran while one was open for 2% -> 2% of each run, Pallas kernels for 36% -> 34%
where the time goes in v13:
time: 286 us; the launch traced here: 285 us
  Pallas kernels  118 us (41%)
  waiting for transfers between devices  108 us (38%)
  starting transfers between devices  39.5 us (14%)
  local copies, waits for them, and re-layouts  16.3 us (6%)
    ppermute x11, waiting for transfers between devices, delivered(): return lax.ppermute(value, ('section', 'seq'), pairs)  97.3 us
    pallas_call x4, Pallas kernels, attend(): pl.pallas_call(functools.partial(attend_kernel, heads, dim, rows, scale,...  83.8 us
    ppermute x11, starting transfers between devices, delivered(): return lax.ppermute(value, ('section', 'seq'), pairs)  19.3 us
    unnamed x70, local copies, waits for them, and re-layouts  15.4 us
    all_to_all x3, starting transfers between devices, shards(): lax.all_to_all(piece, 'seq', split_axis=0, concat_axis=0, tiled=True)  15.3 us
    pallas_call x2, Pallas kernels, pack(): pl.pallas_call(functools.partial(pack_kernel, own, group, index, spans),...  14.3 us
    pallas_call x15, Pallas kernels, after(): pl.pallas_call(lambda *refs: None, out_shape=jax.ShapeDtypeStruct(value.s...  10.2 us
    all_to_all x3, waiting for transfers between devices, shards(): lax.all_to_all(piece, 'seq', split_axis=0, concat_axis=0, tiled=True)  9.24 us
  transfers between devices with their start and end apart: 20, of which 6 were waited for; matrix products, arithmetic and copies ran while one was open for 2% of the time, Pallas kernels for 34%

profile of v13, /device:TPU:0, one launch (start us, length us, event | category | flops | bytes accessed | tf_op | source)
XLA Modules:
  0.0 285.0 jit_solution(3541634315809087878)
XLA Ops:
  0.0 6.7 %shard_map.90 = bf16[8,2,1024,128]{3,2,1,0:T(8,128)(2,1)} custom-call(s32[1]{0:T(128)} %bitcast.at_ref, bf16[1024,1024]{1,0:T(8,128)(2,1)} %bitcast.53, bf16[1024,1024]{1,0:T(8,128)(2,1)} %bitcast.55), custom_call_target="tpu_custom_call" | custom-call | bytes 4194304 | tf_op jit(solution)/shard_map/pallas_call | solution.py:51
  6.7 6.5 %all-to-all-start = ((bf16[8,2048,128]{2,1,0:T(8,128)(2,1)}), bf16[8,2048,128]{2,1,0:T(8,128)(2,1)}, u32[]{:S(2)}, u32[]{:S(2)}) async-start(bf16[8,2048,128]{2,1,0:T(8,128)(2,1)} %bitcast.44), calls=%async_computation | async-start | bytes 8388608 | tf_op jit(solution)/shard_map/all_to_all | solution.py:360
  13.3 4.0 %shard_map.83 = (bf16[2176,128]{1,0:T(8,128)(2,1)S(1)}, bf16[2176,128]{1,0:T(8,128)(2,1)S(1)}, bf16[2176,128]{1,0:T(8,128)(2,1)S(1)}, bf16[2176,128]{1,0:T(8,128)(2,1)S(1)}) custom-call(f32[64]{0:T(128)S(1)} %divide_bitcast_fusion.gate_ref, s32[1]{0:T(128)} %bitcast.at_ref, bf16[128,8192]{1,0:T(8,128)(2,1)S(1)} %bitcast.36, bf16[128,8192]{1,0:T(8,128)(2,1)} %bitcast.49, ...), custom_call_target="tpu_custom_call" | custom-call | flops 4194304 | bytes 6291456 | tf_op jit(solution)/shard_map/pallas_call | solution.py:100
  21.8 7.6 %shard_map.85 = (bf16[8,2,640,128]{3,2,1,0:T(8,128)(2,1)}, bf16[8,2,384,128]{3,2,1,0:T(8,128)(2,1)}) custom-call(s32[1]{0:T(128)} %shard_map.84.at_ref, bf16[1024,1024]{1,0:T(8,128)(2,1)} %bitcast.54, bf16[1024,1024]{1,0:T(8,128)(2,1)} %bitcast.56), custom_call_target="tpu_custom_call" | custom-call | bytes 4194304 | tf_op jit(solution)/shard_map/pallas_call | solution.py:51
  29.4 2.4 collective-permute-start.12
  32.4 4.0 %shard_map.86 = (bf16[2176,128]{1,0:T(8,128)(2,1)S(1)}, bf16[2176,128]{1,0:T(8,128)(2,1)S(1)}, bf16[2176,128]{1,0:T(8,128)(2,1)S(1)}, bf16[2176,128]{1,0:T(8,128)(2,1)S(1)}) custom-call(f32[64]{0:T(128)S(1)} %divide_bitcast_fusion.gate_ref, s32[1]{0:T(128)} %bitcast.at_ref, bf16[128,8192]{1,0:T(8,128)(2,1)S(1)} %bitcast.37, bf16[128,8192]{1,0:T(8,128)(2,1)} %bitcast.50, ...), custom_call_target="tpu_custom_call" | custom-call | flops 4194304 | bytes 6291456 | tf_op jit(solution)/shard_map/pallas_call | solution.py:100
  43.1 1.4 collective-permute-start.7
  45.8 77.5 %collective-permute-done.7 = s32[8,8,32]{2,1,0:T(8,128)S(1)} collective-permute-done((s32[8,8,32]{2,1,0:T(8,128)S(1)}, s32[8,8,32]{2,1,0:T(8,128)S(1)}, u32[]{:S(2)}, u32[]{:S(2)}) %collective-permute-start.7) | collective-permute-done | bytes 8224 | tf_op jit(solution)/shard_map/ppermute | solution.py:304
  128.8 4.9 %all-to-all-start.1 = ((bf16[8,1280,128]{2,1,0:T(8,128)(2,1)}), bf16[8,1280,128]{2,1,0:T(8,128)(2,1)}, u32[]{:S(2)}, u32[]{:S(2)}) async-start(bf16[8,1280,128]{2,1,0:T(8,128)(2,1)} %shard_map.97), calls=%async_computation.1 | async-start | bytes 5242880 | tf_op jit(solution)/shard_map/all_to_all | solution.py:360
  134.3 4.8 %collective-permute-start.10 = (bf16[2176,128]{1,0:T(8,128)(2,1)}, bf16[2176,128]{1,0:T(8,128)(2,1)S(1)}, u32[]{:S(2)}, u32[]{:S(2)}) collective-permute-start(bf16[2176,128]{1,0:T(8,128)(2,1)} %shard_map.95), channel_id=1, source_target_pairs={{0,26},{1,27},{2,24},{3,25},{4,30},{5,31},{6,28},{7,29},{8,2},{9,3... | collective-permute-start | bytes 1671176 | tf_op jit(solution)/shard_map/ppermute | solution.py:304
  142.5 36.1 %shard_map.91 = (bf16[128,1024]{1,0:T(8,128)(2,1)}, bf16[128,1024]{1,0:T(8,128)(2,1)}, bf16[128,1024]{1,0:T(8,128)(2,1)}, bf16[128,1024]{1,0:T(8,128)(2,1)}) custom-call(s32[4,32]{1,0:T(4,128)} %select_reduce_fusion.1.picks_ref, s32[4,2]{1,0:T(4,128)} %shard_map.82.starts_ref, bf16[2176,128]{1,0:T(8,128)(2,1)} %copy-done.2, bf16[2176,128]{1,0:T(8,128)(2,1)} %copy-done.25, ...), custom_call_target="tpu_custom_call" | custom-call | flops 51539607552 | tf_op jit(solution)/shard_map/pallas_call | solution.py:223
  179.3 2.4 collective-permute-start.3
  181.7 7.4 %collective-permute-done.10.refs_2_.refs_4_.refs_0_ = bf16[2176,128]{1,0:T(8,128)(2,1)S(1)} collective-permute-done((bf16[2176,128]{1,0:T(8,128)(2,1)}, bf16[2176,128]{1,0:T(8,128)(2,1)S(1)}, u32[]{:S(2)}, u32[]{:S(2)}) %collective-permute-start.10) | collective-permute-done | bytes 557088 | tf_op jit(solution)/shard_map/ppermute | solution.py:304
  189.2 2.7 collective-permute-start.4
  191.9 12.4 %collective-permute-done.11.refs_3_.refs_5_.refs_1_ = bf16[2176,128]{1,0:T(8,128)(2,1)S(1)} collective-permute-done((bf16[2176,128]{1,0:T(8,128)(2,1)}, bf16[2176,128]{1,0:T(8,128)(2,1)S(1)}, u32[]{:S(2)}, u32[]{:S(2)}) %collective-permute-start.11) | collective-permute-done | bytes 557088 | tf_op jit(solution)/shard_map/ppermute | solution.py:304
  205.3 2.5 collective-permute-start.6
  209.3 4.0 %all-to-all-start.2 = ((bf16[8,768,128]{2,1,0:T(8,128)(2,1)}), bf16[8,768,128]{2,1,0:T(8,128)(2,1)S(1)}, u32[]{:S(2)}, u32[]{:S(2)}) async-start(bf16[8,768,128]{2,1,0:T(8,128)(2,1)} %shard_map.100), calls=%async_computation.2 | async-start | bytes 3145728 | tf_op jit(solution)/shard_map/all_to_all | solution.py:360
  213.3 26.3 %shard_map.98.refs_1_.refs_3_ = f32[4,1024,128]{2,1,0:T(8,128)} custom-call(s32[4,32]{1,0:T(4,128)} %select_reduce_fusion.picks_ref, s32[4,2]{1,0:T(4,128)} %shard_map.92.starts_ref, bf16[2176,128]{1,0:T(8,128)(2,1)} %copy-done.26, bf16[2176,128]{1,0:T(8,128)(2,1)} %copy-done.28, bf16[2176,128]{1,0:T(8,128)(2,1)} %copy-done.27, ...), custom_call_target="tpu_custom_call" | custom-call | flops 32212254720 | tf_op jit(solution)/shard_map/pallas_call | solution.py:223
  241.9 9.2 %all-to-all-done.2 = bf16[8,768,128]{2,1,0:T(8,128)(2,1)S(1)} async-done(((bf16[8,768,128]{2,1,0:T(8,128)(2,1)}), bf16[8,768,128]{2,1,0:T(8,128)(2,1)S(1)}, u32[]{:S(2)}, u32[]{:S(2)}) %all-to-all-start.2) | async-done | bytes 1572896 | tf_op jit(solution)/shard_map/all_to_all | solution.py:360
  252.3 11.1 %shard_map.101 = (bf16[128,1024]{1,0:T(8,128)(2,1)}, bf16[128,1024]{1,0:T(8,128)(2,1)}) custom-call(s32[4,32]{1,0:T(4,128)} %select_reduce_fusion.picks_ref, s32[4,2]{1,0:T(4,128)} %shard_map.99.starts_ref, bf16[2176,128]{1,0:T(8,128)(2,1)} %copy-done.27, bf16[2176,128]{1,0:T(8,128)(2,1)} %copy-done.29, bf16[8,6,128,128]{3,2,1,0:T(8,128)(2,1)} %bitcast.57, ...), custom_call_target="tpu_custom_call" | custom-call | flops 9663676416 | tf_op jit(solution)/shard_map/pallas_call | solution.py:223
  264.8 10.3 %shard_map.103 = (bf16[128,1024]{1,0:T(8,128)(2,1)}, bf16[128,1024]{1,0:T(8,128)(2,1)}) custom-call(s32[4,32]{1,0:T(4,128)} %select_reduce_fusion.picks_ref, s32[4,2]{1,0:T(4,128)} %shard_map.102.starts_ref, bf16[2176,128]{1,0:T(8,128)(2,1)} %copy-done.26, bf16[2176,128]{1,0:T(8,128)(2,1)} %copy-done.28, bf16[8,6,128,128]{3,2,1,0:T(8,128)(2,1)} %bitcast.58, ...), custom_call_target="tpu_custom_call" | custom-call | flops 9663676416 | tf_op jit(solution)/shard_map/pallas_call | solution.py:223
  276.9 2.3 collective-permute-start.16
  279.3 1.4 collective-permute-done.16.refs_5_
  283.5 1.5 shard_map.105
  (125 shorter events, 35.3 us)
Async XLA Ops:
  6.7 120.2 %all-to-all-start = ((bf16[8,2048,128]{2,1,0:T(8,128)(2,1)}), bf16[8,2048,128]{2,1,0:T(8,128)(2,1)}, u32[]{:S(2)}, u32[]{:S(2)}) async-start(bf16[8,2048,128]{2,1,0:T(8,128)(2,1)} %bitcast.44), calls=%async_computation | async-start | bytes 8388608 | tf_op jit(solution)/shard_map/all_to_all | solution.py:360
  29.4 97.5 %collective-permute-start.12 = (bf16[8,1280,128]{2,1,0:T(8,128)(2,1)}, bf16[8,1280,128]{2,1,0:T(8,128)(2,1)}, u32[]{:S(2)}, u32[]{:S(2)}) collective-permute-start(bf16[8,1280,128]{2,1,0:T(8,128)(2,1)} %bitcast.40), channel_id=1, source_target_pairs={{0,24},{1,25},{2,26},{3,27},{4,28},{5,29},{6,30},{7,31},{8,0},{9,1... | collective-permute-start | bytes 7864328 | tf_op jit(solution)/shard_map/ppermute | solution.py:304
  31.8 147.5 %collective-permute-start.13 = (bf16[8,768,128]{2,1,0:T(8,128)(2,1)}, bf16[8,768,128]{2,1,0:T(8,128)(2,1)}, u32[]{:S(2)}, u32[]{:S(2)}) collective-permute-start(bf16[8,768,128]{2,1,0:T(8,128)(2,1)} %bitcast.45), channel_id=1, source_target_pairs={{0,24},{1,25},{2,26},{3,27},{4,28},{5,29},{6,30},{7,31},{8,0},{9,1... | collective-permute-start | bytes 4718600 | tf_op jit(solution)/shard_map/ppermute | solution.py:304
  40.3 86.5 %collective-permute-start.2 = (bf16[2176,128]{1,0:T(8,128)(2,1)}, bf16[2176,128]{1,0:T(8,128)(2,1)S(1)}, u32[]{:S(2)}, u32[]{:S(2)}) collective-permute-start(bf16[2176,128]{1,0:T(8,128)(2,1)} %shard_map.89), channel_id=1, source_target_pairs={{0,3},{1,2},{2,1},{3,0},{4,7},{5,6},{6,5},{7,4},{8,11},{9,10},{10,... | collective-permute-start | bytes 1671176 | tf_op jit(solution)/shard_map/ppermute | solution.py:300
  42.3 84.6 %collective-permute-start.1 = (bf16[2176,128]{1,0:T(8,128)(2,1)}, bf16[2176,128]{1,0:T(8,128)(2,1)S(1)}, u32[]{:S(2)}, u32[]{:S(2)}) collective-permute-start(bf16[2176,128]{1,0:T(8,128)(2,1)} %shard_map.88), channel_id=1, source_target_pairs={{0,2},{1,3},{2,0},{3,1},{4,6},{5,7},{6,4},{7,5},{8,10},{9,11},{10,... | collective-permute-start | bytes 1671176 | tf_op jit(solution)/shard_map/ppermute | solution.py:300
  43.1 80.2 %collective-permute-start.7 = (s32[8,8,32]{2,1,0:T(8,128)S(1)}, s32[8,8,32]{2,1,0:T(8,128)S(1)}, u32[]{:S(2)}, u32[]{:S(2)}) collective-permute-start(s32[8,8,32]{2,1,0:T(8,128)S(1)} %bitcast.62), channel_id=1, source_target_pairs={{0,24},{1,25},{2,26},{3,27},{4,28},{5,29},{6,30},{7,31},{8,0},{9,1... | collective-permute-start | bytes 24584 | tf_op jit(solution)/shard_map/ppermute | solution.py:304
  123.3 3.6 %collective-permute-start = (bf16[2176,128]{1,0:T(8,128)(2,1)}, bf16[2176,128]{1,0:T(8,128)(2,1)S(1)}, u32[]{:S(2)}, u32[]{:S(2)}) collective-permute-start(bf16[2176,128]{1,0:T(8,128)(2,1)} %shard_map.87), channel_id=1, source_target_pairs={{0,1},{1,0},{2,3},{3,2},{4,5},{5,4},{6,7},{7,6},{8,9},{9,8},{10,11... | collective-permute-start | bytes 1671176 | tf_op jit(solution)/shard_map/ppermute | solution.py:300
  128.8 79.1 %all-to-all-start.1 = ((bf16[8,1280,128]{2,1,0:T(8,128)(2,1)}), bf16[8,1280,128]{2,1,0:T(8,128)(2,1)}, u32[]{:S(2)}, u32[]{:S(2)}) async-start(bf16[8,1280,128]{2,1,0:T(8,128)(2,1)} %shard_map.97), calls=%async_computation.1 | async-start | bytes 5242880 | tf_op jit(solution)/shard_map/all_to_all | solution.py:360
  134.3 54.9 %collective-permute-start.10 = (bf16[2176,128]{1,0:T(8,128)(2,1)}, bf16[2176,128]{1,0:T(8,128)(2,1)S(1)}, u32[]{:S(2)}, u32[]{:S(2)}) collective-permute-start(bf16[2176,128]{1,0:T(8,128)(2,1)} %shard_map.95), channel_id=1, source_target_pairs={{0,26},{1,27},{2,24},{3,25},{4,30},{5,31},{6,28},{7,29},{8,2},{9,3... | collective-permute-start | bytes 1671176 | tf_op jit(solution)/shard_map/ppermute | solution.py:304
  139.8 64.5 %collective-permute-start.11 = (bf16[2176,128]{1,0:T(8,128)(2,1)}, bf16[2176,128]{1,0:T(8,128)(2,1)S(1)}, u32[]{:S(2)}, u32[]{:S(2)}) collective-permute-start(bf16[2176,128]{1,0:T(8,128)(2,1)} %shard_map.96), channel_id=1, source_target_pairs={{0,27},{1,26},{2,25},{3,24},{4,31},{5,30},{6,29},{7,28},{8,3},{9,2... | collective-permute-start | bytes 1671176 | tf_op jit(solution)/shard_map/ppermute | solution.py:304
  140.5 64.9 %collective-permute-start.8 = (bf16[2176,128]{1,0:T(8,128)(2,1)}, bf16[2176,128]{1,0:T(8,128)(2,1)S(1)}, u32[]{:S(2)}, u32[]{:S(2)}) collective-permute-start(bf16[2176,128]{1,0:T(8,128)(2,1)} %shard_map.93), channel_id=1, source_target_pairs={{0,24},{1,25},{2,26},{3,27},{4,28},{5,29},{6,30},{7,31},{8,0},{9,1... | collective-permute-start | bytes 1671176 | tf_op jit(solution)/shard_map/ppermute | solution.py:304
  142.4 65.5 %collective-permute-start.9 = (bf16[2176,128]{1,0:T(8,128)(2,1)}, bf16[2176,128]{1,0:T(8,128)(2,1)S(1)}, u32[]{:S(2)}, u32[]{:S(2)}) collective-permute-start(bf16[2176,128]{1,0:T(8,128)(2,1)} %shard_map.94), channel_id=1, source_target_pairs={{0,25},{1,24},{2,27},{3,26},{4,29},{5,28},{6,31},{7,30},{8,1},{9,0... | collective-permute-start | bytes 1671176 | tf_op jit(solution)/shard_map/ppermute | solution.py:304
  179.3 60.3 %collective-permute-start.3 = (bf16[128,1024]{1,0:T(8,128)(2,1)}, bf16[128,1024]{1,0:T(8,128)(2,1)S(1)}, u32[]{:S(2)}, u32[]{:S(2)}) collective-permute-start(bf16[128,1024]{1,0:T(8,128)(2,1)} %get-tuple-element.30.refs_1_), channel_id=1, source_target_pairs={{0,24},{1,25},{2,26},{3,27},{4,28},{5,29},{6,30},{7,31},{8,0},{9,1... | collective-permute-start | bytes 786440 | tf_op jit(solution)/shard_map/ppermute | solution.py:304
  189.2 18.7 %copy-start.27 = (bf16[2176,128]{1,0:T(8,128)(2,1)}, bf16[2176,128]{1,0:T(8,128)(2,1)S(1)}, u32[]{:S(2)}) copy-start(bf16[2176,128]{1,0:T(8,128)(2,1)S(1)} %collective-permute-done.10.refs_2_.refs_4_.refs_0_) | copy-start | bytes 1671172
  189.2 50.4 %collective-permute-start.4 = (bf16[128,1024]{1,0:T(8,128)(2,1)}, bf16[128,1024]{1,0:T(8,128)(2,1)S(1)}, u32[]{:S(2)}, u32[]{:S(2)}) collective-permute-start(bf16[128,1024]{1,0:T(8,128)(2,1)} %get-tuple-element.31), channel_id=1, source_target_pairs={{0,25},{1,24},{2,27},{3,26},{4,29},{5,28},{6,31},{7,30},{8,1},{9,0... | collective-permute-start | bytes 786440 | tf_op jit(solution)/shard_map/ppermute | solution.py:304
  204.3 35.3 %collective-permute-start.5 = (bf16[128,1024]{1,0:T(8,128)(2,1)}, bf16[128,1024]{1,0:T(8,128)(2,1)S(1)}, u32[]{:S(2)}, u32[]{:S(2)}) collective-permute-start(bf16[128,1024]{1,0:T(8,128)(2,1)} %get-tuple-element.32), channel_id=1, source_target_pairs={{0,26},{1,27},{2,24},{3,25},{4,30},{5,31},{6,28},{7,29},{8,2},{9,3... | collective-permute-start | bytes 786440 | tf_op jit(solution)/shard_map/ppermute | solution.py:304
  205.3 34.3 %collective-permute-start.6 = (bf16[128,1024]{1,0:T(8,128)(2,1)}, bf16[128,1024]{1,0:T(8,128)(2,1)S(1)}, u32[]{:S(2)}, u32[]{:S(2)}) collective-permute-start(bf16[128,1024]{1,0:T(8,128)(2,1)} %get-tuple-element.33), channel_id=1, source_target_pairs={{0,27},{1,26},{2,25},{3,24},{4,31},{5,30},{6,29},{7,28},{8,3},{9,2... | collective-permute-start | bytes 786440 | tf_op jit(solution)/shard_map/ppermute | solution.py:304
  209.3 41.8 %all-to-all-start.2 = ((bf16[8,768,128]{2,1,0:T(8,128)(2,1)}), bf16[8,768,128]{2,1,0:T(8,128)(2,1)S(1)}, u32[]{:S(2)}, u32[]{:S(2)}) async-start(bf16[8,768,128]{2,1,0:T(8,128)(2,1)} %shard_map.100), calls=%async_computation.2 | async-start | bytes 3145728 | tf_op jit(solution)/shard_map/all_to_all | solution.py:360
  264.1 10.9 %collective-permute-start.14 = (bf16[128,1024]{1,0:T(8,128)(2,1)}, bf16[128,1024]{1,0:T(8,128)(2,1)S(1)}, u32[]{:S(2)}, u32[]{:S(2)}) collective-permute-start(bf16[128,1024]{1,0:T(8,128)(2,1)} %get-tuple-element.37.refs_1_), channel_id=1, source_target_pairs={{0,2},{1,3},{2,0},{3,1},{4,6},{5,7},{6,4},{7,5},{8,10},{9,11},{10,... | collective-permute-start | bytes 786440 | tf_op jit(solution)/shard_map/ppermute | solution.py:300
  264.1 16.5 %copy-start.4 = (bf16[128,1024]{1,0:T(8,128)(2,1)S(1)}, bf16[128,1024]{1,0:T(8,128)(2,1)}, u32[]{:S(2)}) copy-start(bf16[128,1024]{1,0:T(8,128)(2,1)} %copy-done.3) | copy-start | bytes 786436
  264.1 16.5 %copy-start.6 = (bf16[128,1024]{1,0:T(8,128)(2,1)S(1)}, bf16[128,1024]{1,0:T(8,128)(2,1)}, u32[]{:S(2)}) copy-start(bf16[128,1024]{1,0:T(8,128)(2,1)} %copy-done.5) | copy-start | bytes 786436
  264.1 16.5 %copy-start.8 = (bf16[128,1024]{1,0:T(8,128)(2,1)S(1)}, bf16[128,1024]{1,0:T(8,128)(2,1)}, u32[]{:S(2)}) copy-start(bf16[128,1024]{1,0:T(8,128)(2,1)} %copy-done.7) | copy-start | bytes 786436
  264.2 11.4 %collective-permute-start.15 = (bf16[128,1024]{1,0:T(8,128)(2,1)}, bf16[128,1024]{1,0:T(8,128)(2,1)S(1)}, u32[]{:S(2)}, u32[]{:S(2)}) collective-permute-start(bf16[128,1024]{1,0:T(8,128)(2,1)} %get-tuple-element.40), channel_id=1, source_target_pairs={{0,3},{1,2},{2,1},{3,0},{4,7},{5,6},{6,5},{7,4},{8,11},{9,10},{10,... | collective-permute-start | bytes 786440 | tf_op jit(solution)/shard_map/ppermute | solution.py:300
  276.9 3.7 %collective-permute-start.16 = (bf16[128,1024]{1,0:T(8,128)(2,1)}, bf16[128,1024]{1,0:T(8,128)(2,1)S(1)}, u32[]{:S(2)}, u32[]{:S(2)}) collective-permute-start(bf16[128,1024]{1,0:T(8,128)(2,1)} %shard_map.104), channel_id=1, source_target_pairs={{0,1},{1,0},{2,3},{3,2},{4,5},{5,4},{6,7},{7,6},{8,9},{9,8},{10,11... | collective-permute-start | bytes 786440 | tf_op jit(solution)/shard_map/ppermute | solution.py:300
  (30 other events, 67.0 us)

commit v14 on v13

--- a/solution.py
+++ b/solution.py
@@ -28,7 +28,33 @@
     return terms
 
 
-def pack_kernel(own, group, index, spans, at_ref, keys_ref, values_ref, *outs):
+def narrow_kernel(own, index, at_ref, keys_ref, values_ref, out_ref):
+    group, _, dim = out_ref.shape[1:]
+    for device in range(group):
+        head = device * own + index
+        out_ref[0, device] = keys_ref[:, head * dim:(head + 1) * dim]
+        out_ref[1, device] = values_ref[:, head * dim:(head + 1) * dim]
+
+
+def narrow(mem_keys, mem_values, hint, own, group, dim, index):
+    mem_dev, width = mem_keys.shape
+    rows = pl.BlockSpec((BLOCK, width), lambda i, _: (i, 0))
+    return pl.pallas_call(
+        functools.partial(narrow_kernel, own, index),
+        out_shape=jax.ShapeDtypeStruct((2, group, mem_dev, dim), mem_keys.dtype),
+        grid_spec=pltpu.PrefetchScalarGridSpec(
+            num_scalar_prefetch=1,
+            grid=(mem_dev // BLOCK,),
+            in_specs=[rows, rows],
+            out_specs=pl.BlockSpec((2, group, BLOCK, dim), lambda i, _: (0, 0, i, 0)),
+        ),
+        compiler_params=pltpu.CompilerParams(vmem_limit_bytes=VMEM_MOST),
+        cost_estimate=pl.CostEstimate(flops=0, bytes_accessed=6 * mem_dev * width // own, transcendentals=0),
+    )(hint, mem_keys, mem_values)
+
+
+def pack_kernel(own, group, index, spans, wide, *refs):
+    sources, outs = refs[:2 if wide else 1], refs[2 if wide else 1:]
     dim = outs[0].shape[3]
     block = pl.program_id(0)
     for (low, high), out in zip(spans, outs):
@@ -37,31 +63,35 @@
         def _(out=out):
             for device in range(out.shape[0]):
                 head = device % group * own + index
-                for half, source in enumerate((keys_ref, values_ref)):
-                    out[device, half] = source[:, head * dim:(head + 1) * dim]
-
-
-def pack(mem_keys, mem_values, at, seq, own, group, dim, index, spans):
-    mem_dev, width = mem_keys.shape
-    rows = pl.BlockSpec((BLOCK, width), lambda i, _: (i, 0))
+                for half in range(2):
+                    if wide:
+                        out[device, half] = sources[half][:, head * dim:(head + 1) * dim]
+                    else:
+                        out[device, half] = sources[0][half, device % group]
+
+
+def pack(sources, seq, own, group, dim, index, spans):
+    wide = len(sources) == 2
+    mem_dev = sources[0].shape[0 if wide else 2]
+    if wide:
+        specs = [pl.BlockSpec((BLOCK, source.shape[1]), lambda i: (i, 0)) for source in sources]
+    else:
+        specs = [pl.BlockSpec((2, group, BLOCK, dim), lambda i: (0, 0, i, 0))]
 
     def place(low, high):
-        return pl.BlockSpec((seq, 2, BLOCK, dim), lambda i, _: (0, 0, jnp.clip(i - low, 0, high - low - 1), 0))
+        return pl.BlockSpec((seq, 2, BLOCK, dim), lambda i: (0, 0, jnp.clip(i - low, 0, high - low - 1), 0))
 
     outs = pl.pallas_call(
-        functools.partial(pack_kernel, own, group, index, spans),
+        functools.partial(pack_kernel, own, group, index, spans, wide),
         out_shape=[
-            jax.ShapeDtypeStruct((seq, 2, (high - low) * BLOCK, dim), mem_keys.dtype) for low, high in spans
+            jax.ShapeDtypeStruct((seq, 2, (high - low) * BLOCK, dim), sources[0].dtype) for low, high in spans
         ],
-        grid_spec=pltpu.PrefetchScalarGridSpec(
-            num_scalar_prefetch=1,
-            grid=(mem_dev // BLOCK,),
-            in_specs=[rows, rows],
-            out_specs=[place(low, high) for low, high in spans],
-        ),
+        grid=(mem_dev // BLOCK,),
+        in_specs=specs,
+        out_specs=[place(low, high) for low, high in spans],
         compiler_params=pltpu.CompilerParams(vmem_limit_bytes=VMEM_MOST),
-        cost_estimate=pl.CostEstimate(flops=0, bytes_accessed=8 * mem_dev * width // own, transcendentals=0),
-    )(at, mem_keys, mem_values)
+        cost_estimate=pl.CostEstimate(flops=0, bytes_accessed=8 * mem_dev * dim * group, transcendentals=0),
+    )(*sources)
     return [out.reshape(seq, -1, dim) for out in outs]
 
 
@@ -333,8 +363,8 @@
     gates = jax.nn.sigmoid(gate_logit[0])
     gathered, worked, latest, held = [], [], None, []
 
-    def memory_of(i, hint):
-        return pack(mem_keys[0], mem_values[0], hint, seq, own, group, dim, i, cuts[i])
+    def memory_of(i, sources):
+        return pack(sources, seq, own, group, dim, i, cuts[i])
 
     def queries_of(i):
         return prepare(grad_out[0], queries[0], mem_out[0], row_total[0], gates, at, kv_heads, dim, scale, own, i)
@@ -343,14 +373,15 @@
         sent = [after(value, *first) if first else value for value in packed]
         return [packed[0]] + [swapped(sent[x], x) for x in range(1, group)]
 
-    memories = memory_of(0, at[None])
+    memories = memory_of(0, [mem_keys[0], mem_values[0]])
     asked = [queries_of(0)]
+    ready = []
     for i in range(1, own):
-        memories += memory_of(i, after(at[None], asked[-1][0]))
+        rows_of = narrow(mem_keys[0], mem_values[0], after(at[None], asked[-1][0]), own, group, dim, i)
         asked.append(queries_of(i))
-    coming = exchanged(asked[0], *memories[len(cuts[0]):], *[value[0] for value in asked[1:]])
-    if moved:
-        memories[-len(cuts[-1]):] = [delivered(value, 0) for value in memories[-len(cuts[-1]):]]
+        ready += [rows_of, asked[i][0]]
+        memories += memory_of(i, [delivered(rows_of, 0) if i == own - 1 else rows_of])
+    coming = exchanged(asked[0], *ready)
     for i in range(own):
         packed = coming
         pieces = []
@@ -371,7 +402,7 @@
                 coming = [delivered(after(value, latest), x) for x, value in enumerate(asked[i + 1])]
             else:
                 coming = exchanged(asked[i + 1], latest)
-            done = run(packed, pieces[-1], acc, starts=after(starts[-1], *worked), last=True)
+            done = run(packed, pieces[-1], acc, starts=after(starts[-1], *worked, memories[0]), last=True)
             worked = done[:1]
             gathered += [delivered(done[x], x) for x in range(group)]
             continue

time: 286 us -> 260 us (0.909)
  waiting for transfers between devices: 108 us -> 81.1 us
  Pallas kernels: 118 us -> 126 us
  starting transfers between devices: 39.5 us -> 32.8 us
    ppermute x11 -> x10, waiting for transfers between devices: 97.3 us -> 34.4 us  [delivered(): return lax.ppermute(value, ('section', 'seq'), pairs)]
    all_to_all x3, waiting for transfers between devices: 9.24 us -> 44.6 us  [shards(): lax.all_to_all(piece, 'seq', split_axis=0, concat_axis=0, tiled=True)]
    pallas_call x2 -> x3, Pallas kernels: 14.3 us -> 20 us  [the longest x2 13.3 us: pack(): pl.pallas_call(functools.partial(pack_kernel, own, group, index, spans, w...]
    ppermute x11 -> x10, starting transfers between devices: 19.3 us -> 13.8 us  [delivered(): return lax.ppermute(value, ('section', 'seq'), pairs)]
    unnamed x70 -> x66, local copies, waits for them, and re-layouts: 15.4 us -> 14.7 us
  transfers between devices with their start and end apart: 20 -> 19, of which waited for: 6 -> 6; matrix products, arithmetic and copies ran while one was open for 2% -> 2% of each run, Pallas kernels for 34% -> 41%
where the time goes in v14:
time: 260 us; the launch traced here: 258 us
  Pallas kernels  126 us (48%)
  waiting for transfers between devices  81.1 us (31%)
  starting transfers between devices  32.8 us (13%)
  local copies, waits for them, and re-layouts  15.6 us (6%)
  other arithmetic  2.65 us (1%)
    pallas_call x4, Pallas kernels, attend(): pl.pallas_call(functools.partial(attend_kernel, heads, dim, rows, scale,...  85.1 us
    all_to_all x3, waiting for transfers between devices, shards(): lax.all_to_all(piece, 'seq', split_axis=0, concat_axis=0, tiled=True)  44.6 us
    ppermute x10, waiting for transfers between devices, delivered(): return lax.ppermute(value, ('section', 'seq'), pairs)  34.4 us
    unnamed x66, local copies, waits for them, and re-layouts  14.7 us
    all_to_all x3, starting transfers between devices, shards(): lax.all_to_all(piece, 'seq', split_axis=0, concat_axis=0, tiled=True)  14.6 us
    ppermute x10, starting transfers between devices, delivered(): return lax.ppermute(value, ('section', 'seq'), pairs)  13.8 us
    pallas_call x2, Pallas kernels, pack(): pl.pallas_call(functools.partial(pack_kernel, own, group, index, spans, w...  13.3 us
    pallas_call x15, Pallas kernels, after(): pl.pallas_call(lambda *refs: None, out_shape=jax.ShapeDtypeStruct(value.s...  11 us
  transfers between devices with their start and end apart: 19, of which 6 were waited for; matrix products, arithmetic and copies ran while one was open for 2% of the time, Pallas kernels for 41%

profile of v14, /device:TPU:0, one launch (start us, length us, event | category | flops | bytes accessed | tf_op | source)
XLA Modules:
  0.0 258.0 jit_solution(8182064919501531293)
XLA Ops:
  0.0 6.8 %shard_map.91 = bf16[8,2,1024,128]{3,2,1,0:T(8,128)(2,1)} custom-call(bf16[1024,1024]{1,0:T(8,128)(2,1)} %bitcast.43, bf16[1024,1024]{1,0:T(8,128)(2,1)} %bitcast.45), custom_call_target="tpu_custom_call" | custom-call | bytes 4194304 | tf_op jit(solution)/shard_map/pallas_call | solution.py:84
  6.9 6.5 %all-to-all-start = ((bf16[8,2048,128]{2,1,0:T(8,128)(2,1)}), bf16[8,2048,128]{2,1,0:T(8,128)(2,1)}, u32[]{:S(2)}, u32[]{:S(2)}) async-start(bf16[8,2048,128]{2,1,0:T(8,128)(2,1)} %bitcast.42), calls=%async_computation | async-start | bytes 8388608 | tf_op jit(solution)/shard_map/all_to_all | solution.py:391
  13.5 4.0 %shard_map.82 = (bf16[2176,128]{1,0:T(8,128)(2,1)S(1)}, bf16[2176,128]{1,0:T(8,128)(2,1)S(1)}, bf16[2176,128]{1,0:T(8,128)(2,1)S(1)}, bf16[2176,128]{1,0:T(8,128)(2,1)S(1)}) custom-call(f32[64]{0:T(128)S(1)} %divide_bitcast_fusion.gate_ref, s32[1]{0:T(128)} %bitcast.at_ref, bf16[128,8192]{1,0:T(8,128)(2,1)S(1)} %bitcast.36, bf16[128,8192]{1,0:T(8,128)(2,1)} %bitcast.47, ...), custom_call_target="tpu_custom_call" | custom-call | flops 4194304 | bytes 6291456 | tf_op jit(solution)/shard_map/pallas_call | solution.py:130
  21.9 6.7 %shard_map.84.refs_1_ = bf16[2,4,1024,128]{3,2,1,0:T(8,128)(2,1)} custom-call(s32[1]{0:T(128)} %shard_map.83.at_ref, bf16[1024,1024]{1,0:T(8,128)(2,1)} %bitcast.44, bf16[1024,1024]{1,0:T(8,128)(2,1)} %bitcast.46), custom_call_target="tpu_custom_call" | custom-call | bytes 3145728 | tf_op jit(solution)/shard_map/pallas_call | solution.py:42
  28.6 2.4 collective-permute-start
  31.6 4.0 %shard_map.87 = (bf16[2176,128]{1,0:T(8,128)(2,1)S(1)}, bf16[2176,128]{1,0:T(8,128)(2,1)S(1)}, bf16[2176,128]{1,0:T(8,128)(2,1)S(1)}, bf16[2176,128]{1,0:T(8,128)(2,1)S(1)}) custom-call(f32[64]{0:T(128)S(1)} %divide_bitcast_fusion.gate_ref, s32[1]{0:T(128)} %bitcast.at_ref, bf16[128,8192]{1,0:T(8,128)(2,1)S(1)} %bitcast.37, bf16[128,8192]{1,0:T(8,128)(2,1)} %bitcast.48, ...), custom_call_target="tpu_custom_call" | custom-call | flops 4194304 | bytes 6291456 | tf_op jit(solution)/shard_map/pallas_call | solution.py:130
  40.3 2.0 collective-permute-start.2
  43.2 34.4 %collective-permute-done.8 = s32[8,8,32]{2,1,0:T(8,128)S(1)} collective-permute-done((s32[8,8,32]{2,1,0:T(8,128)S(1)}, s32[8,8,32]{2,1,0:T(8,128)S(1)}, u32[]{:S(2)}, u32[]{:S(2)}) %collective-permute-start.8) | collective-permute-done | bytes 8224 | tf_op jit(solution)/shard_map/ppermute | solution.py:334
  81.1 6.4 %shard_map.85 = (bf16[8,2,640,128]{3,2,1,0:T(8,128)(2,1)}, bf16[8,2,384,128]{3,2,1,0:T(8,128)(2,1)}) custom-call(bf16[2,4,1024,128]{3,2,1,0:T(8,128)(2,1)} %collective-permute-done.refs_0_), custom_call_target="tpu_custom_call" | custom-call | bytes 4194304 | tf_op jit(solution)/shard_map/pallas_call | solution.py:84
  88.8 18.8 %all-to-all-done.refs_1_ = bf16[8,2048,128]{2,1,0:T(8,128)(2,1)} async-done(((bf16[8,2048,128]{2,1,0:T(8,128)(2,1)}), bf16[8,2048,128]{2,1,0:T(8,128)(2,1)}, u32[]{:S(2)}, u32[]{:S(2)}) %all-to-all-start) | async-done | bytes 4194336 | tf_op jit(solution)/shard_map/all_to_all | solution.py:391
  108.2 2.4 collective-permute-start.9
  113.1 2.8 %collective-permute-start.12 = (bf16[2176,128]{1,0:T(8,128)(2,1)}, bf16[2176,128]{1,0:T(8,128)(2,1)}, u32[]{:S(2)}, u32[]{:S(2)}) collective-permute-start(bf16[2176,128]{1,0:T(8,128)(2,1)} %shard_map.97), channel_id=1, source_target_pairs={{0,27},{1,26},{2,25},{3,24},{4,31},{5,30},{6,29},{7,28},{8,3},{9,2... | collective-permute-start | bytes 1671176 | tf_op jit(solution)/shard_map/ppermute | solution.py:334
  117.5 4.4 %all-to-all-start.1 = ((bf16[8,1280,128]{2,1,0:T(8,128)(2,1)}), bf16[8,1280,128]{2,1,0:T(8,128)(2,1)}, u32[]{:S(2)}, u32[]{:S(2)}) async-start(bf16[8,1280,128]{2,1,0:T(8,128)(2,1)} %shard_map.98), calls=%async_computation.1 | async-start | bytes 5242880 | tf_op jit(solution)/shard_map/all_to_all | solution.py:391
  121.9 36.1 %shard_map.92 = (bf16[128,1024]{1,0:T(8,128)(2,1)}, bf16[128,1024]{1,0:T(8,128)(2,1)}, bf16[128,1024]{1,0:T(8,128)(2,1)}, bf16[128,1024]{1,0:T(8,128)(2,1)}) custom-call(s32[4,32]{1,0:T(4,128)} %select_reduce_fusion.1.picks_ref, s32[4,2]{1,0:T(4,128)} %shard_map.86.starts_ref, bf16[2176,128]{1,0:T(8,128)(2,1)} %copy-done.2, bf16[2176,128]{1,0:T(8,128)(2,1)} %copy-done.24, ...), custom_call_target="tpu_custom_call" | custom-call | flops 51539607552 | tf_op jit(solution)/shard_map/pallas_call | solution.py:253
  158.1 2.5 collective-permute-start.4
  161.4 2.5 collective-permute-start.6
  164.3 19.1 %all-to-all-done.1.refs_1_ = bf16[8,1280,128]{2,1,0:T(8,128)(2,1)} async-done(((bf16[8,1280,128]{2,1,0:T(8,128)(2,1)}), bf16[8,1280,128]{2,1,0:T(8,128)(2,1)}, u32[]{:S(2)}, u32[]{:S(2)}) %all-to-all-start.1) | async-done | bytes 2621472 | tf_op jit(solution)/shard_map/all_to_all | solution.py:391
  184.1 3.8 %all-to-all-start.2 = ((bf16[8,768,128]{2,1,0:T(8,128)(2,1)}), bf16[8,768,128]{2,1,0:T(8,128)(2,1)S(1)}, u32[]{:S(2)}, u32[]{:S(2)}) async-start(bf16[8,768,128]{2,1,0:T(8,128)(2,1)} %shard_map.101), calls=%async_computation.2 | async-start | bytes 3145728 | tf_op jit(solution)/shard_map/all_to_all | solution.py:391
  187.9 28.4 %shard_map.99.refs_1_.refs_3_ = f32[4,1024,128]{2,1,0:T(8,128)} custom-call(s32[4,32]{1,0:T(4,128)} %select_reduce_fusion.picks_ref, s32[4,2]{1,0:T(4,128)} %shard_map.93.starts_ref, bf16[2176,128]{1,0:T(8,128)(2,1)} %copy-done.27, bf16[2176,128]{1,0:T(8,128)(2,1)} %collective-permute-done.10.refs_1_.refs_3_, ...), custom_call_target="tpu_custom_call" | custom-call | flops 32212254720 | tf_op jit(solution)/shard_map/pallas_call | solution.py:253
  218.8 6.7 %all-to-all-done.2 = bf16[8,768,128]{2,1,0:T(8,128)(2,1)S(1)} async-done(((bf16[8,768,128]{2,1,0:T(8,128)(2,1)}), bf16[8,768,128]{2,1,0:T(8,128)(2,1)S(1)}, u32[]{:S(2)}, u32[]{:S(2)}) %all-to-all-start.2) | async-done | bytes 1572896 | tf_op jit(solution)/shard_map/all_to_all | solution.py:391
  226.7 10.5 %shard_map.102 = (bf16[128,1024]{1,0:T(8,128)(2,1)}, bf16[128,1024]{1,0:T(8,128)(2,1)}) custom-call(s32[4,32]{1,0:T(4,128)} %select_reduce_fusion.picks_ref, s32[4,2]{1,0:T(4,128)} %shard_map.100.starts_ref, bf16[2176,128]{1,0:T(8,128)(2,1)} %collective-permute-done.11.refs_2_.refs_4_.refs_0_, ...), custom_call_target="tpu_custom_call" | custom-call | flops 9663676416 | tf_op jit(solution)/shard_map/pallas_call | solution.py:253
  238.5 10.0 %shard_map.104 = (bf16[128,1024]{1,0:T(8,128)(2,1)}, bf16[128,1024]{1,0:T(8,128)(2,1)}) custom-call(s32[4,32]{1,0:T(4,128)} %select_reduce_fusion.picks_ref, s32[4,2]{1,0:T(4,128)} %shard_map.103.starts_ref, bf16[2176,128]{1,0:T(8,128)(2,1)} %copy-done.27, bf16[2176,128]{1,0:T(8,128)(2,1)} %collective-permute-done.10.refs_1_.refs_3_, ...), custom_call_target="tpu_custom_call" | custom-call | flops 9663676416 | tf_op jit(solution)/shard_map/pallas_call | solution.py:253
  250.7 1.7 collective-permute-start.15
  256.6 1.5 shard_map.106
  (120 shorter events, 33.2 us)
Async XLA Ops:
  6.9 100.7 %all-to-all-start = ((bf16[8,2048,128]{2,1,0:T(8,128)(2,1)}), bf16[8,2048,128]{2,1,0:T(8,128)(2,1)}, u32[]{:S(2)}, u32[]{:S(2)}) async-start(bf16[8,2048,128]{2,1,0:T(8,128)(2,1)} %bitcast.42), calls=%async_computation | async-start | bytes 8388608 | tf_op jit(solution)/shard_map/all_to_all | solution.py:391
  28.6 52.5 %collective-permute-start = (bf16[2,4,1024,128]{3,2,1,0:T(8,128)(2,1)}, bf16[2,4,1024,128]{3,2,1,0:T(8,128)(2,1)}, u32[]{:S(2)}, u32[]{:S(2)}) collective-permute-start(bf16[2,4,1024,128]{3,2,1,0:T(8,128)(2,1)} %shard_map.84.refs_1_), channel_id=1, source_target_pairs={{0,24},{1,25},{2,26},{3,27},{4,28},{5,29},{6,30},{7,31},{8,0},{9,1... | collective-permute-start | bytes 6291464 | tf_op jit(solution)/shard_map/ppermute | solution.py:334
  31.1 46.5 %collective-permute-start.8 = (s32[8,8,32]{2,1,0:T(8,128)S(1)}, s32[8,8,32]{2,1,0:T(8,128)S(1)}, u32[]{:S(2)}, u32[]{:S(2)}) collective-permute-start(s32[8,8,32]{2,1,0:T(8,128)S(1)} %bitcast.57), channel_id=1, source_target_pairs={{0,24},{1,25},{2,26},{3,27},{4,28},{5,29},{6,30},{7,31},{8,0},{9,1... | collective-permute-start | bytes 24584 | tf_op jit(solution)/shard_map/ppermute | solution.py:334
  39.6 73.2 %collective-permute-start.1 = (bf16[2176,128]{1,0:T(8,128)(2,1)}, bf16[2176,128]{1,0:T(8,128)(2,1)S(1)}, u32[]{:S(2)}, u32[]{:S(2)}) collective-permute-start(bf16[2176,128]{1,0:T(8,128)(2,1)} %shard_map.88), channel_id=1, source_target_pairs={{0,1},{1,0},{2,3},{3,2},{4,5},{5,4},{6,7},{7,6},{8,9},{9,8},{10,11... | collective-permute-start | bytes 1671176 | tf_op jit(solution)/shard_map/ppermute | solution.py:330
  40.3 72.8 %collective-permute-start.2 = (bf16[2176,128]{1,0:T(8,128)(2,1)}, bf16[2176,128]{1,0:T(8,128)(2,1)S(1)}, u32[]{:S(2)}, u32[]{:S(2)}) collective-permute-start(bf16[2176,128]{1,0:T(8,128)(2,1)} %shard_map.89), channel_id=1, source_target_pairs={{0,2},{1,3},{2,0},{3,1},{4,6},{5,7},{6,4},{7,5},{8,10},{9,11},{10,... | collective-permute-start | bytes 1671176 | tf_op jit(solution)/shard_map/ppermute | solution.py:330
  43.0 72.9 %collective-permute-start.3 = (bf16[2176,128]{1,0:T(8,128)(2,1)}, bf16[2176,128]{1,0:T(8,128)(2,1)S(1)}, u32[]{:S(2)}, u32[]{:S(2)}) collective-permute-start(bf16[2176,128]{1,0:T(8,128)(2,1)} %shard_map.90), channel_id=1, source_target_pairs={{0,3},{1,2},{2,1},{3,0},{4,7},{5,6},{6,5},{7,4},{8,11},{9,10},{10,... | collective-permute-start | bytes 1671176 | tf_op jit(solution)/shard_map/ppermute | solution.py:330
  108.2 53.0 %collective-permute-start.9 = (bf16[2176,128]{1,0:T(8,128)(2,1)}, bf16[2176,128]{1,0:T(8,128)(2,1)S(1)}, u32[]{:S(2)}, u32[]{:S(2)}) collective-permute-start(bf16[2176,128]{1,0:T(8,128)(2,1)} %shard_map.94), channel_id=1, source_target_pairs={{0,24},{1,25},{2,26},{3,27},{4,28},{5,29},{6,30},{7,31},{8,0},{9,1... | collective-permute-start | bytes 1671176 | tf_op jit(solution)/shard_map/ppermute | solution.py:334
  111.4 50.1 %collective-permute-start.10 = (bf16[2176,128]{1,0:T(8,128)(2,1)}, bf16[2176,128]{1,0:T(8,128)(2,1)}, u32[]{:S(2)}, u32[]{:S(2)}) collective-permute-start(bf16[2176,128]{1,0:T(8,128)(2,1)} %shard_map.95), channel_id=1, source_target_pairs={{0,25},{1,24},{2,27},{3,26},{4,29},{5,28},{6,31},{7,30},{8,1},{9,0... | collective-permute-start | bytes 1671176 | tf_op jit(solution)/shard_map/ppermute | solution.py:334
  113.1 50.9 %collective-permute-start.11 = (bf16[2176,128]{1,0:T(8,128)(2,1)S(1)}, bf16[2176,128]{1,0:T(8,128)(2,1)}, u32[]{:S(2)}, u32[]{:S(2)}) collective-permute-start(bf16[2176,128]{1,0:T(8,128)(2,1)S(1)} %copy-done.20), channel_id=1, source_target_pairs={{0,26},{1,27},{2,24},{3,25},{4,30},{5,31},{6,28},{7,29},{8,2},{9,3... | collective-permute-start | bytes 1671176 | tf_op jit(solution)/shard_map/ppermute | solution.py:334
  113.1 51.2 %collective-permute-start.12 = (bf16[2176,128]{1,0:T(8,128)(2,1)}, bf16[2176,128]{1,0:T(8,128)(2,1)}, u32[]{:S(2)}, u32[]{:S(2)}) collective-permute-start(bf16[2176,128]{1,0:T(8,128)(2,1)} %shard_map.97), channel_id=1, source_target_pairs={{0,27},{1,26},{2,25},{3,24},{4,31},{5,30},{6,29},{7,28},{8,3},{9,2... | collective-permute-start | bytes 1671176 | tf_op jit(solution)/shard_map/ppermute | solution.py:334
  117.5 65.9 %all-to-all-start.1 = ((bf16[8,1280,128]{2,1,0:T(8,128)(2,1)}), bf16[8,1280,128]{2,1,0:T(8,128)(2,1)}, u32[]{:S(2)}, u32[]{:S(2)}) async-start(bf16[8,1280,128]{2,1,0:T(8,128)(2,1)} %shard_map.98), calls=%async_computation.1 | async-start | bytes 5242880 | tf_op jit(solution)/shard_map/all_to_all | solution.py:391
  158.1 58.3 %collective-permute-start.4 = (bf16[128,1024]{1,0:T(8,128)(2,1)}, bf16[128,1024]{1,0:T(8,128)(2,1)S(1)}, u32[]{:S(2)}, u32[]{:S(2)}) collective-permute-start(bf16[128,1024]{1,0:T(8,128)(2,1)} %get-tuple-element.29.refs_1_), channel_id=1, source_target_pairs={{0,24},{1,25},{2,26},{3,27},{4,28},{5,29},{6,30},{7,31},{8,0},{9,1... | collective-permute-start | bytes 786440 | tf_op jit(solution)/shard_map/ppermute | solution.py:334
  161.2 22.2 %copy-start.27 = (bf16[2176,128]{1,0:T(8,128)(2,1)}, bf16[2176,128]{1,0:T(8,128)(2,1)S(1)}, u32[]{:S(2)}) copy-start(bf16[2176,128]{1,0:T(8,128)(2,1)S(1)} %collective-permute-done.9.refs_0_.refs_2_) | copy-start | bytes 1671172
  161.2 55.1 %collective-permute-start.5 = (bf16[128,1024]{1,0:T(8,128)(2,1)}, bf16[128,1024]{1,0:T(8,128)(2,1)S(1)}, u32[]{:S(2)}, u32[]{:S(2)}) collective-permute-start(bf16[128,1024]{1,0:T(8,128)(2,1)} %get-tuple-element.30), channel_id=1, source_target_pairs={{0,25},{1,24},{2,27},{3,26},{4,29},{5,28},{6,31},{7,30},{8,1},{9,0... | collective-permute-start | bytes 786440 | tf_op jit(solution)/shard_map/ppermute | solution.py:334
  161.4 54.9 %collective-permute-start.6 = (bf16[128,1024]{1,0:T(8,128)(2,1)}, bf16[128,1024]{1,0:T(8,128)(2,1)S(1)}, u32[]{:S(2)}, u32[]{:S(2)}) collective-permute-start(bf16[128,1024]{1,0:T(8,128)(2,1)} %get-tuple-element.31), channel_id=1, source_target_pairs={{0,26},{1,27},{2,24},{3,25},{4,30},{5,31},{6,28},{7,29},{8,2},{9,3... | collective-permute-start | bytes 786440 | tf_op jit(solution)/shard_map/ppermute | solution.py:334
  164.0 52.4 %collective-permute-start.7 = (bf16[128,1024]{1,0:T(8,128)(2,1)}, bf16[128,1024]{1,0:T(8,128)(2,1)S(1)}, u32[]{:S(2)}, u32[]{:S(2)}) collective-permute-start(bf16[128,1024]{1,0:T(8,128)(2,1)} %get-tuple-element.32), channel_id=1, source_target_pairs={{0,27},{1,26},{2,25},{3,24},{4,31},{5,30},{6,29},{7,28},{8,3},{9,2... | collective-permute-start | bytes 786440 | tf_op jit(solution)/shard_map/ppermute | solution.py:334
  184.1 41.3 %all-to-all-start.2 = ((bf16[8,768,128]{2,1,0:T(8,128)(2,1)}), bf16[8,768,128]{2,1,0:T(8,128)(2,1)S(1)}, u32[]{:S(2)}, u32[]{:S(2)}) async-start(bf16[8,768,128]{2,1,0:T(8,128)(2,1)} %shard_map.101), calls=%async_computation.2 | async-start | bytes 3145728 | tf_op jit(solution)/shard_map/all_to_all | solution.py:391
  237.8 10.7 %collective-permute-start.13 = (bf16[128,1024]{1,0:T(8,128)(2,1)}, bf16[128,1024]{1,0:T(8,128)(2,1)S(1)}, u32[]{:S(2)}, u32[]{:S(2)}) collective-permute-start(bf16[128,1024]{1,0:T(8,128)(2,1)} %get-tuple-element.37.refs_1_), channel_id=1, source_target_pairs={{0,2},{1,3},{2,0},{3,1},{4,6},{5,7},{6,4},{7,5},{8,10},{9,11},{10,... | collective-permute-start | bytes 786440 | tf_op jit(solution)/shard_map/ppermute | solution.py:330
  237.8 15.9 %copy-start.4 = (bf16[128,1024]{1,0:T(8,128)(2,1)S(1)}, bf16[128,1024]{1,0:T(8,128)(2,1)}, u32[]{:S(2)}) copy-start(bf16[128,1024]{1,0:T(8,128)(2,1)} %copy-done.3) | copy-start | bytes 786436
  237.8 15.9 %copy-start.6 = (bf16[128,1024]{1,0:T(8,128)(2,1)S(1)}, bf16[128,1024]{1,0:T(8,128)(2,1)}, u32[]{:S(2)}) copy-start(bf16[128,1024]{1,0:T(8,128)(2,1)} %copy-done.5) | copy-start | bytes 786436
  237.8 15.9 %copy-start.8 = (bf16[128,1024]{1,0:T(8,128)(2,1)S(1)}, bf16[128,1024]{1,0:T(8,128)(2,1)}, u32[]{:S(2)}) copy-start(bf16[128,1024]{1,0:T(8,128)(2,1)} %copy-done.7) | copy-start | bytes 786436
  237.8 15.9 %copy-start.10 = (bf16[128,1024]{1,0:T(8,128)(2,1)S(1)}, bf16[128,1024]{1,0:T(8,128)(2,1)}, u32[]{:S(2)}) copy-start(bf16[128,1024]{1,0:T(8,128)(2,1)} %copy-done.9) | copy-start | bytes 786436
  237.9 11.4 %collective-permute-start.14 = (bf16[128,1024]{1,0:T(8,128)(2,1)}, bf16[128,1024]{1,0:T(8,128)(2,1)S(1)}, u32[]{:S(2)}, u32[]{:S(2)}) collective-permute-start(bf16[128,1024]{1,0:T(8,128)(2,1)} %get-tuple-element.40), channel_id=1, source_target_pairs={{0,3},{1,2},{2,1},{3,0},{4,7},{5,6},{6,5},{7,4},{8,11},{9,10},{10,... | collective-permute-start | bytes 786440 | tf_op jit(solution)/shard_map/ppermute | solution.py:330
  250.7 3.0 %collective-permute-start.15 = (bf16[128,1024]{1,0:T(8,128)(2,1)}, bf16[128,1024]{1,0:T(8,128)(2,1)S(1)}, u32[]{:S(2)}, u32[]{:S(2)}) collective-permute-start(bf16[128,1024]{1,0:T(8,128)(2,1)} %shard_map.105), channel_id=1, source_target_pairs={{0,1},{1,0},{2,3},{3,2},{4,5},{5,4},{6,7},{7,6},{8,9},{9,8},{10,11... | collective-permute-start | bytes 786440 | tf_op jit(solution)/shard_map/ppermute | solution.py:330
  (27 other events, 61.7 us)

commit v15 on v14

--- a/solution.py
+++ b/solution.py
@@ -279,16 +279,17 @@
 def assemble(pieces, at, own, group):
     rows, span = pieces[0].shape
     width = own * group * span
+    part = rows // 4
     return pl.pallas_call(
         functools.partial(assemble_kernel, own, group),
         out_shape=jax.ShapeDtypeStruct((rows, width), pieces[0].dtype),
         grid_spec=pltpu.PrefetchScalarGridSpec(
             num_scalar_prefetch=1,
-            grid=(1,),
-            in_specs=[pl.BlockSpec((rows, span), lambda i, _: (0, 0))] * len(pieces),
-            out_specs=pl.BlockSpec((rows, width), lambda i, _: (0, 0)),
+            grid=(rows // part,),
+            in_specs=[pl.BlockSpec((part, span), lambda i, _: (i, 0))] * len(pieces),
+            out_specs=pl.BlockSpec((part, width), lambda i, _: (i, 0)),
         ),
-        compiler_params=pltpu.CompilerParams(vmem_limit_bytes=VMEM_LIMIT),
+        compiler_params=pltpu.CompilerParams(vmem_limit_bytes=VMEM_MOST),
         cost_estimate=pl.CostEstimate(flops=0, bytes_accessed=4 * rows * width, transcendentals=0),
     )(at[None], *pieces)
 
@@ -369,19 +370,15 @@
     def queries_of(i):
         return prepare(grad_out[0], queries[0], mem_out[0], row_total[0], gates, at, kv_heads, dim, scale, own, i)
 
-    def exchanged(packed, *first):
-        sent = [after(value, *first) if first else value for value in packed]
-        return [packed[0]] + [swapped(sent[x], x) for x in range(1, group)]
+    def exchanged(packed):
+        return [packed[0]] + [swapped(packed[x], x) for x in range(1, group)]
 
     memories = memory_of(0, [mem_keys[0], mem_values[0]])
-    asked = [queries_of(0)]
-    ready = []
+    asked = [queries_of(i) for i in range(own)]
     for i in range(1, own):
-        rows_of = narrow(mem_keys[0], mem_values[0], after(at[None], asked[-1][0]), own, group, dim, i)
-        asked.append(queries_of(i))
-        ready += [rows_of, asked[i][0]]
+        rows_of = narrow(mem_keys[0], mem_values[0], after(at[None], asked[i][0]), own, group, dim, i)
         memories += memory_of(i, [delivered(rows_of, 0) if i == own - 1 else rows_of])
-    coming = exchanged(asked[0], *ready)
+    coming = exchanged(asked[0])
     for i in range(own):
         packed = coming
         pieces = []
@@ -399,9 +396,9 @@
             worked = [acc]
         if i < own - 1:
             if i == own - 2:
-                coming = [delivered(after(value, latest), x) for x, value in enumerate(asked[i + 1])]
+                coming = [delivered(value, x) for x, value in enumerate(asked[i + 1])]
             else:
-                coming = exchanged(asked[i + 1], latest)
+                coming = exchanged(asked[i + 1])
             done = run(packed, pieces[-1], acc, starts=after(starts[-1], *worked, memories[0]), last=True)
             worked = done[:1]
             gathered += [delivered(done[x], x) for x in range(group)]

time: 260 us -> 262 us (level)
  waiting for transfers between devices: 81.1 us -> 88.7 us
  local copies, waits for them, and re-layouts: 15.6 us -> 10.6 us
  Pallas kernels: 126 us -> 123 us
  starting transfers between devices: 32.8 us -> 35.6 us
    all_to_all x3, waiting for transfers between devices: 44.6 us -> 27 us  [shards(): lax.all_to_all(piece, 'seq', split_axis=0, concat_axis=0, tiled=True)]
    ppermute x10, waiting for transfers between devices: 34.4 us -> 48 us  [delivered(): return lax.ppermute(value, ('section', 'seq'), pairs)]
    ppermute x6, waiting for transfers between devices: 2.14 us -> 13.7 us  [swapped(): return lax.ppermute(value, 'seq', [(p, p ^ step) for p in range(seq)])]
    unnamed x66 -> x48, local copies, waits for them, and re-layouts: 14.7 us -> 9.75 us
    pallas_call x15 -> x8, Pallas kernels: 11 us -> 6.15 us  [after(): pl.pallas_call(lambda *refs: None, out_shape=jax.ShapeDtypeStruct(value.s...]
  transfers between devices with their start and end apart: 19 -> 19, of which waited for: 6 -> 6; matrix products, arithmetic and copies ran while one was open for 2% -> 2% of each run, Pallas kernels for 41% -> 38%
where the time goes in v15:
time: 262 us; the launch traced here: 260 us
  Pallas kernels  123 us (47%)
  waiting for transfers between devices  88.7 us (34%)
  starting transfers between devices  35.6 us (14%)
  local copies, waits for them, and re-layouts  10.6 us (4%)
  other arithmetic  2.65 us (1%)
    pallas_call x4, Pallas kernels, attend(): pl.pallas_call(functools.partial(attend_kernel, heads, dim, rows, scale,...  84 us
    ppermute x10, waiting for transfers between devices, delivered(): return lax.ppermute(value, ('section', 'seq'), pairs)  48 us
    all_to_all x3, waiting for transfers between devices, shards(): lax.all_to_all(piece, 'seq', split_axis=0, concat_axis=0, tiled=True)  27 us
    ppermute x10, starting transfers between devices, delivered(): return lax.ppermute(value, ('section', 'seq'), pairs)  16.1 us
    all_to_all x3, starting transfers between devices, shards(): lax.all_to_all(piece, 'seq', split_axis=0, concat_axis=0, tiled=True)  14.6 us
    ppermute x6, waiting for transfers between devices, swapped(): return lax.ppermute(value, 'seq', [(p, p ^ step) for p in range(seq)])  13.7 us
    pallas_call x2, Pallas kernels, pack(): pl.pallas_call(functools.partial(pack_kernel, own, group, index, spans, w...  13 us
    unnamed x48, local copies, waits for them, and re-layouts  9.75 us
  transfers between devices with their start and end apart: 19, of which 6 were waited for; matrix products, arithmetic and copies ran while one was open for 2% of the time, Pallas kernels for 38%

profile of v15, /device:TPU:0, one launch (start us, length us, event | category | flops | bytes accessed | tf_op | source)
XLA Modules:
  0.0 260.4 jit_solution(10657264417258993647)
XLA Ops:
  0.0 6.7 %shard_map.88 = bf16[8,2,1024,128]{3,2,1,0:T(8,128)(2,1)} custom-call(bf16[1024,1024]{1,0:T(8,128)(2,1)} %bitcast.43, bf16[1024,1024]{1,0:T(8,128)(2,1)} %bitcast.45), custom_call_target="tpu_custom_call" | custom-call | bytes 4194304 | tf_op jit(solution)/shard_map/pallas_call | solution.py:84
  6.7 6.5 %all-to-all-start = ((bf16[8,2048,128]{2,1,0:T(8,128)(2,1)}), bf16[8,2048,128]{2,1,0:T(8,128)(2,1)}, u32[]{:S(2)}, u32[]{:S(2)}) async-start(bf16[8,2048,128]{2,1,0:T(8,128)(2,1)} %bitcast.42), calls=%async_computation | async-start | bytes 8388608 | tf_op jit(solution)/shard_map/all_to_all | solution.py:388
  13.3 4.0 %shard_map.82 = (bf16[2176,128]{1,0:T(8,128)(2,1)S(1)}, bf16[2176,128]{1,0:T(8,128)(2,1)S(1)}, bf16[2176,128]{1,0:T(8,128)(2,1)S(1)}, bf16[2176,128]{1,0:T(8,128)(2,1)S(1)}) custom-call(f32[64]{0:T(128)S(1)} %divide_bitcast_fusion.gate_ref, s32[1]{0:T(128)} %bitcast.at_ref, bf16[128,8192]{1,0:T(8,128)(2,1)S(1)} %bitcast.36, bf16[128,8192]{1,0:T(8,128)(2,1)} %bitcast.47, ...), custom_call_target="tpu_custom_call" | custom-call | flops 4194304 | bytes 6291456 | tf_op jit(solution)/shard_map/pallas_call | solution.py:130
  21.0 6.9 %shard_map.84 = bf16[2,4,1024,128]{3,2,1,0:T(8,128)(2,1)} custom-call(s32[1]{0:T(128)} %shard_map.83.at_ref, bf16[1024,1024]{1,0:T(8,128)(2,1)} %bitcast.44, bf16[1024,1024]{1,0:T(8,128)(2,1)} %bitcast.46), custom_call_target="tpu_custom_call" | custom-call | bytes 3145728 | tf_op jit(solution)/shard_map/pallas_call | solution.py:42
  27.9 2.4 collective-permute-start
  32.3 4.8 %shard_map.87 = (bf16[2176,128]{1,0:T(8,128)(2,1)S(1)}, bf16[2176,128]{1,0:T(8,128)(2,1)}, bf16[2176,128]{1,0:T(8,128)(2,1)}, bf16[2176,128]{1,0:T(8,128)(2,1)S(1)}) custom-call(f32[64]{0:T(128)S(1)} %divide_bitcast_fusion.gate_ref, s32[1]{0:T(128)} %bitcast.at_ref, bf16[128,8192]{1,0:T(8,128)(2,1)S(1)} %bitcast.37, bf16[128,8192]{1,0:T(8,128)(2,1)} %bitcast.48, ...), custom_call_target="tpu_custom_call" | custom-call | flops 4194304 | bytes 6291456 | tf_op jit(solution)/shard_map/pallas_call | solution.py:130
  38.8 2.0 collective-permute-start.2
  40.8 47.9 %collective-permute-done.8 = s32[8,8,32]{2,1,0:T(8,128)S(1)} collective-permute-done((s32[8,8,32]{2,1,0:T(8,128)S(1)}, s32[8,8,32]{2,1,0:T(8,128)S(1)}, u32[]{:S(2)}, u32[]{:S(2)}) %collective-permute-start.8) | collective-permute-done | bytes 8224 | tf_op jit(solution)/shard_map/ppermute | solution.py:335
  92.9 4.0 %collective-permute-start.10 = (bf16[2176,128]{1,0:T(8,128)(2,1)}, bf16[2176,128]{1,0:T(8,128)(2,1)}, u32[]{:S(2)}, u32[]{:S(2)}) collective-permute-start(bf16[2176,128]{1,0:T(8,128)(2,1)} %copy-done.6), channel_id=1, source_target_pairs={{0,25},{1,24},{2,27},{3,26},{4,29},{5,28},{6,31},{7,30},{8,1},{9,0... | collective-permute-start | bytes 1671176 | tf_op jit(solution)/shard_map/ppermute | solution.py:335
  97.0 6.3 %shard_map.85 = (bf16[8,2,640,128]{3,2,1,0:T(8,128)(2,1)}, bf16[8,2,384,128]{3,2,1,0:T(8,128)(2,1)}) custom-call(bf16[2,4,1024,128]{3,2,1,0:T(8,128)(2,1)} %collective-permute-done.refs_0_), custom_call_target="tpu_custom_call" | custom-call | bytes 4194304 | tf_op jit(solution)/shard_map/pallas_call | solution.py:84
  106.2 11.0 %collective-permute-done.3.refs_3_.refs_5_ = bf16[2176,128]{1,0:T(8,128)(2,1)S(1)} collective-permute-done((bf16[2176,128]{1,0:T(8,128)(2,1)}, bf16[2176,128]{1,0:T(8,128)(2,1)S(1)}, u32[]{:S(2)}, u32[]{:S(2)}) %collective-permute-start.3) | collective-permute-done | bytes 557088 | tf_op jit(solution)/shard_map/ppermute | solution.py:331
  118.8 4.4 %all-to-all-start.1 = ((bf16[8,1280,128]{2,1,0:T(8,128)(2,1)}), bf16[8,1280,128]{2,1,0:T(8,128)(2,1)}, u32[]{:S(2)}, u32[]{:S(2)}) async-start(bf16[8,1280,128]{2,1,0:T(8,128)(2,1)} %shard_map.91), calls=%async_computation.1 | async-start | bytes 5242880 | tf_op jit(solution)/shard_map/all_to_all | solution.py:388
  123.3 36.1 %shard_map.89 = (bf16[128,1024]{1,0:T(8,128)(2,1)}, bf16[128,1024]{1,0:T(8,128)(2,1)}, bf16[128,1024]{1,0:T(8,128)(2,1)}, bf16[128,1024]{1,0:T(8,128)(2,1)}) custom-call(s32[4,32]{1,0:T(4,128)} %select_reduce_fusion.1.picks_ref, s32[4,2]{1,0:T(4,128)} %shard_map.86.starts_ref, bf16[2176,128]{1,0:T(8,128)(2,1)} %copy-done.1, bf16[2176,128]{1,0:T(8,128)(2,1)} %copy-done.15, ...), custom_call_target="tpu_custom_call" | custom-call | flops 51539607552 | tf_op jit(solution)/shard_map/pallas_call | solution.py:253
  159.4 2.9 %collective-permute-start.4 = (bf16[128,1024]{1,0:T(8,128)(2,1)}, bf16[128,1024]{1,0:T(8,128)(2,1)S(1)}, u32[]{:S(2)}, u32[]{:S(2)}) collective-permute-start(bf16[128,1024]{1,0:T(8,128)(2,1)} %get-tuple-element.29.refs_1_), channel_id=1, source_target_pairs={{0,24},{1,25},{2,26},{3,27},{4,28},{5,29},{6,30},{7,31},{8,0},{9,1... | collective-permute-start | bytes 786440 | tf_op jit(solution)/shard_map/ppermute | solution.py:335
  163.0 2.8 %collective-permute-start.6 = (bf16[128,1024]{1,0:T(8,128)(2,1)}, bf16[128,1024]{1,0:T(8,128)(2,1)S(1)}, u32[]{:S(2)}, u32[]{:S(2)}) collective-permute-start(bf16[128,1024]{1,0:T(8,128)(2,1)} %get-tuple-element.31), channel_id=1, source_target_pairs={{0,26},{1,27},{2,24},{3,25},{4,30},{5,31},{6,28},{7,29},{8,2},{9,3... | collective-permute-start | bytes 786440 | tf_op jit(solution)/shard_map/ppermute | solution.py:335
  166.1 17.6 %all-to-all-done.1.refs_1_ = bf16[8,1280,128]{2,1,0:T(8,128)(2,1)} async-done(((bf16[8,1280,128]{2,1,0:T(8,128)(2,1)}), bf16[8,1280,128]{2,1,0:T(8,128)(2,1)}, u32[]{:S(2)}, u32[]{:S(2)}) %all-to-all-start.1) | async-done | bytes 2621472 | tf_op jit(solution)/shard_map/all_to_all | solution.py:388
  184.4 3.8 %all-to-all-start.2 = ((bf16[8,768,128]{2,1,0:T(8,128)(2,1)}), bf16[8,768,128]{2,1,0:T(8,128)(2,1)S(1)}, u32[]{:S(2)}, u32[]{:S(2)}) async-start(bf16[8,768,128]{2,1,0:T(8,128)(2,1)} %shard_map.94), calls=%async_computation.2 | async-start | bytes 3145728 | tf_op jit(solution)/shard_map/all_to_all | solution.py:388
  188.1 25.7 %shard_map.92.refs_1_.refs_3_ = f32[4,1024,128]{2,1,0:T(8,128)} custom-call(s32[4,32]{1,0:T(4,128)} %select_reduce_fusion.picks_ref, s32[4,2]{1,0:T(4,128)} %shard_map.90.starts_ref, bf16[2176,128]{1,0:T(8,128)(2,1)} %collective-permute-done.9.refs_0_.refs_2_, bf16[2176,128]{1,0:T(8,128)(2,1)} %collective-permute-done.10.refs_1_.refs_3_, ...), custom_call_target="tpu_custom_call" | custom-call | flops 32212254720 | tf_op jit(solution)/shard_map/pallas_call | solution.py:253
  216.3 9.4 %all-to-all-done.2 = bf16[8,768,128]{2,1,0:T(8,128)(2,1)S(1)} async-done(((bf16[8,768,128]{2,1,0:T(8,128)(2,1)}), bf16[8,768,128]{2,1,0:T(8,128)(2,1)S(1)}, u32[]{:S(2)}, u32[]{:S(2)}) %all-to-all-start.2) | async-done | bytes 1572896 | tf_op jit(solution)/shard_map/all_to_all | solution.py:388
  226.9 10.7 %shard_map.95 = (bf16[128,1024]{1,0:T(8,128)(2,1)}, bf16[128,1024]{1,0:T(8,128)(2,1)}) custom-call(s32[4,32]{1,0:T(4,128)} %select_reduce_fusion.picks_ref, s32[4,2]{1,0:T(4,128)} %shard_map.93.starts_ref, bf16[2176,128]{1,0:T(8,128)(2,1)} %collective-permute-done.11.refs_2_.refs_4_.refs_0_, ...), custom_call_target="tpu_custom_call" | custom-call | flops 9663676416 | tf_op jit(solution)/shard_map/pallas_call | solution.py:253
  238.3 2.1 collective-permute-start.14
  240.4 11.4 %shard_map.97 = (bf16[128,1024]{1,0:T(8,128)(2,1)}, bf16[128,1024]{1,0:T(8,128)(2,1)}) custom-call(s32[4,32]{1,0:T(4,128)} %select_reduce_fusion.picks_ref, s32[4,2]{1,0:T(4,128)} %shard_map.96.starts_ref, bf16[2176,128]{1,0:T(8,128)(2,1)} %collective-permute-done.9.refs_0_.refs_2_, bf16[2176,128]{1,0:T(8,128)(2,1)} %collective-permute-done.10.refs_1_.refs_3_, ...), custom_call_target="tpu_custom_call" | custom-call | flops 9663676416 | tf_op jit(solution)/shard_map/pallas_call | solution.py:253
  254.3 1.6 collective-permute-done.15.refs_5_
  256.7 3.8 %shard_map.99 = bf16[128,8192]{1,0:T(8,128)(2,1)} custom-call(s32[1]{0:T(128)} %bitcast.at_ref, bf16[128,1024]{1,0:T(8,128)(2,1)} %copy-done.9, bf16[128,1024]{1,0:T(8,128)(2,1)} %copy-done.10, bf16[128,1024]{1,0:T(8,128)(2,1)} %copy-done.11, bf16[128,1024]{1,0:T(8,128)(2,1)} %copy-done.12, bf16[128,1024]{1,0:T(8,128)(2,1)} %get-tuple-element.38.refs_4_, ...), custom_call_target="tpu_custom_call" | custom-call | bytes 4194304 | tf_op jit(solution)/shard_map/pallas_call | solution.py:283
  (95 shorter events, 25.2 us)
Async XLA Ops:
  6.7 110.5 %all-to-all-start = ((bf16[8,2048,128]{2,1,0:T(8,128)(2,1)}), bf16[8,2048,128]{2,1,0:T(8,128)(2,1)}, u32[]{:S(2)}, u32[]{:S(2)}) async-start(bf16[8,2048,128]{2,1,0:T(8,128)(2,1)} %bitcast.42), calls=%async_computation | async-start | bytes 8388608 | tf_op jit(solution)/shard_map/all_to_all | solution.py:388
  21.0 9.9 %copy-start.21 = (s32[1,8,8,32]{3,2,1,0:T(8,128)S(1)}, s32[1,8,8,32]{3,2,1,0:T(8,128)}, u32[]{:S(2)}) copy-start(s32[1,8,8,32]{3,2,1,0:T(8,128)} %param.15) | copy-start | bytes 24580
  27.9 65.1 %collective-permute-start = (bf16[2,4,1024,128]{3,2,1,0:T(8,128)(2,1)}, bf16[2,4,1024,128]{3,2,1,0:T(8,128)(2,1)}, u32[]{:S(2)}, u32[]{:S(2)}) collective-permute-start(bf16[2,4,1024,128]{3,2,1,0:T(8,128)(2,1)} %shard_map.84), channel_id=1, source_target_pairs={{0,24},{1,25},{2,26},{3,27},{4,28},{5,29},{6,30},{7,31},{8,0},{9,1... | collective-permute-start | bytes 6291464 | tf_op jit(solution)/shard_map/ppermute | solution.py:335
  30.3 132.7 %collective-permute-start.9 = (bf16[2176,128]{1,0:T(8,128)(2,1)S(1)}, bf16[2176,128]{1,0:T(8,128)(2,1)}, u32[]{:S(2)}, u32[]{:S(2)}) collective-permute-start(bf16[2176,128]{1,0:T(8,128)(2,1)S(1)} %copy-done.3), channel_id=1, source_target_pairs={{0,24},{1,25},{2,26},{3,27},{4,28},{5,29},{6,30},{7,31},{8,0},{9,1... | collective-permute-start | bytes 1671176 | tf_op jit(solution)/shard_map/ppermute | solution.py:335
  30.8 57.9 %collective-permute-start.8 = (s32[8,8,32]{2,1,0:T(8,128)S(1)}, s32[8,8,32]{2,1,0:T(8,128)S(1)}, u32[]{:S(2)}, u32[]{:S(2)}) collective-permute-start(s32[8,8,32]{2,1,0:T(8,128)S(1)} %bitcast.57), channel_id=1, source_target_pairs={{0,24},{1,25},{2,26},{3,27},{4,28},{5,29},{6,30},{7,31},{8,0},{9,1... | collective-permute-start | bytes 24584 | tf_op jit(solution)/shard_map/ppermute | solution.py:335
  38.7 65.8 %collective-permute-start.1 = (bf16[2176,128]{1,0:T(8,128)(2,1)}, bf16[2176,128]{1,0:T(8,128)(2,1)S(1)}, u32[]{:S(2)}, u32[]{:S(2)}) collective-permute-start(bf16[2176,128]{1,0:T(8,128)(2,1)} %get-tuple-element.26), channel_id=1, source_target_pairs={{0,1},{1,0},{2,3},{3,2},{4,5},{5,4},{6,7},{7,6},{8,9},{9,8},{10,11... | collective-permute-start | bytes 1671176 | tf_op jit(solution)/shard_map/ppermute | solution.py:331
  38.8 65.8 %collective-permute-start.2 = (bf16[2176,128]{1,0:T(8,128)(2,1)}, bf16[2176,128]{1,0:T(8,128)(2,1)S(1)}, u32[]{:S(2)}, u32[]{:S(2)}) collective-permute-start(bf16[2176,128]{1,0:T(8,128)(2,1)} %get-tuple-element.27), channel_id=1, source_target_pairs={{0,2},{1,3},{2,0},{3,1},{4,6},{5,7},{6,4},{7,5},{8,10},{9,11},{10,... | collective-permute-start | bytes 1671176 | tf_op jit(solution)/shard_map/ppermute | solution.py:331
  88.7 28.5 %collective-permute-start.3 = (bf16[2176,128]{1,0:T(8,128)(2,1)}, bf16[2176,128]{1,0:T(8,128)(2,1)S(1)}, u32[]{:S(2)}, u32[]{:S(2)}) collective-permute-start(bf16[2176,128]{1,0:T(8,128)(2,1)} %copy-done.7), channel_id=1, source_target_pairs={{0,3},{1,2},{2,1},{3,0},{4,7},{5,6},{6,5},{7,4},{8,11},{9,10},{10,... | collective-permute-start | bytes 1671176 | tf_op jit(solution)/shard_map/ppermute | solution.py:331
  90.6 13.9 %copy-start.19 = (s32[4,2]{1,0:T(4,128)}, s32[4,2]{1,0:T(4,128)S(1)}, u32[]{:S(2)}) copy-start(s32[4,2]{1,0:T(4,128)S(1)} %get-tuple-element.56.refs_0_) | copy-start | bytes 100
  92.9 11.6 %copy-start.5 = (bf16[2176,128]{1,0:T(8,128)(2,1)S(1)}, bf16[2176,128]{1,0:T(8,128)(2,1)}, u32[]{:S(2)}) copy-start(bf16[2176,128]{1,0:T(8,128)(2,1)} %copy-done.4) | copy-start | bytes 1671172
  92.9 70.1 %collective-permute-start.10 = (bf16[2176,128]{1,0:T(8,128)(2,1)}, bf16[2176,128]{1,0:T(8,128)(2,1)}, u32[]{:S(2)}, u32[]{:S(2)}) collective-permute-start(bf16[2176,128]{1,0:T(8,128)(2,1)} %copy-done.6), channel_id=1, source_target_pairs={{0,25},{1,24},{2,27},{3,26},{4,29},{5,28},{6,31},{7,30},{8,1},{9,0... | collective-permute-start | bytes 1671176 | tf_op jit(solution)/shard_map/ppermute | solution.py:335
  104.5 12.7 %copy-start.15 = (bf16[2176,128]{1,0:T(8,128)(2,1)}, bf16[2176,128]{1,0:T(8,128)(2,1)S(1)}, u32[]{:S(2)}) copy-start(bf16[2176,128]{1,0:T(8,128)(2,1)S(1)} %collective-permute-done.1.refs_1_.refs_3_) | copy-start | bytes 1671172
  104.5 61.3 %collective-permute-start.11 = (bf16[2176,128]{1,0:T(8,128)(2,1)S(1)}, bf16[2176,128]{1,0:T(8,128)(2,1)}, u32[]{:S(2)}, u32[]{:S(2)}) collective-permute-start(bf16[2176,128]{1,0:T(8,128)(2,1)S(1)} %copy-done.5), channel_id=1, source_target_pairs={{0,26},{1,27},{2,24},{3,25},{4,30},{5,31},{6,28},{7,29},{8,2},{9,3... | collective-permute-start | bytes 1671176 | tf_op jit(solution)/shard_map/ppermute | solution.py:335
  104.6 12.7 %copy-start.16 = (bf16[2176,128]{1,0:T(8,128)(2,1)}, bf16[2176,128]{1,0:T(8,128)(2,1)S(1)}, u32[]{:S(2)}) copy-start(bf16[2176,128]{1,0:T(8,128)(2,1)S(1)} %collective-permute-done.2.refs_2_.refs_4_) | copy-start | bytes 1671172
  104.6 61.5 %collective-permute-start.12 = (bf16[2176,128]{1,0:T(8,128)(2,1)S(1)}, bf16[2176,128]{1,0:T(8,128)(2,1)}, u32[]{:S(2)}, u32[]{:S(2)}) collective-permute-start(bf16[2176,128]{1,0:T(8,128)(2,1)S(1)} %get-tuple-element.35), channel_id=1, source_target_pairs={{0,27},{1,26},{2,25},{3,24},{4,31},{5,30},{6,29},{7,28},{8,3},{9,2... | collective-permute-start | bytes 1671176 | tf_op jit(solution)/shard_map/ppermute | solution.py:335
  118.8 64.8 %all-to-all-start.1 = ((bf16[8,1280,128]{2,1,0:T(8,128)(2,1)}), bf16[8,1280,128]{2,1,0:T(8,128)(2,1)}, u32[]{:S(2)}, u32[]{:S(2)}) async-start(bf16[8,1280,128]{2,1,0:T(8,128)(2,1)} %shard_map.91), calls=%async_computation.1 | async-start | bytes 5242880 | tf_op jit(solution)/shard_map/all_to_all | solution.py:388
  159.4 54.5 %collective-permute-start.4 = (bf16[128,1024]{1,0:T(8,128)(2,1)}, bf16[128,1024]{1,0:T(8,128)(2,1)S(1)}, u32[]{:S(2)}, u32[]{:S(2)}) collective-permute-start(bf16[128,1024]{1,0:T(8,128)(2,1)} %get-tuple-element.29.refs_1_), channel_id=1, source_target_pairs={{0,24},{1,25},{2,26},{3,27},{4,28},{5,29},{6,30},{7,31},{8,0},{9,1... | collective-permute-start | bytes 786440 | tf_op jit(solution)/shard_map/ppermute | solution.py:335
  163.0 50.9 %collective-permute-start.5 = (bf16[128,1024]{1,0:T(8,128)(2,1)}, bf16[128,1024]{1,0:T(8,128)(2,1)S(1)}, u32[]{:S(2)}, u32[]{:S(2)}) collective-permute-start(bf16[128,1024]{1,0:T(8,128)(2,1)} %get-tuple-element.30), channel_id=1, source_target_pairs={{0,25},{1,24},{2,27},{3,26},{4,29},{5,28},{6,31},{7,30},{8,1},{9,0... | collective-permute-start | bytes 786440 | tf_op jit(solution)/shard_map/ppermute | solution.py:335
  163.0 50.9 %collective-permute-start.6 = (bf16[128,1024]{1,0:T(8,128)(2,1)}, bf16[128,1024]{1,0:T(8,128)(2,1)S(1)}, u32[]{:S(2)}, u32[]{:S(2)}) collective-permute-start(bf16[128,1024]{1,0:T(8,128)(2,1)} %get-tuple-element.31), channel_id=1, source_target_pairs={{0,26},{1,27},{2,24},{3,25},{4,30},{5,31},{6,28},{7,29},{8,2},{9,3... | collective-permute-start | bytes 786440 | tf_op jit(solution)/shard_map/ppermute | solution.py:335
  165.8 48.1 %collective-permute-start.7 = (bf16[128,1024]{1,0:T(8,128)(2,1)}, bf16[128,1024]{1,0:T(8,128)(2,1)S(1)}, u32[]{:S(2)}, u32[]{:S(2)}) collective-permute-start(bf16[128,1024]{1,0:T(8,128)(2,1)} %get-tuple-element.32), channel_id=1, source_target_pairs={{0,27},{1,26},{2,25},{3,24},{4,31},{5,30},{6,29},{7,28},{8,3},{9,2... | collective-permute-start | bytes 786440 | tf_op jit(solution)/shard_map/ppermute | solution.py:335
  184.4 41.3 %all-to-all-start.2 = ((bf16[8,768,128]{2,1,0:T(8,128)(2,1)}), bf16[8,768,128]{2,1,0:T(8,128)(2,1)S(1)}, u32[]{:S(2)}, u32[]{:S(2)}) async-start(bf16[8,768,128]{2,1,0:T(8,128)(2,1)} %shard_map.94), calls=%async_computation.2 | async-start | bytes 3145728 | tf_op jit(solution)/shard_map/all_to_all | solution.py:388
  238.3 13.5 %collective-permute-start.13 = (bf16[128,1024]{1,0:T(8,128)(2,1)}, bf16[128,1024]{1,0:T(8,128)(2,1)S(1)}, u32[]{:S(2)}, u32[]{:S(2)}) collective-permute-start(bf16[128,1024]{1,0:T(8,128)(2,1)} %get-tuple-element.37.refs_1_), channel_id=1, source_target_pairs={{0,2},{1,3},{2,0},{3,1},{4,6},{5,7},{6,4},{7,5},{8,10},{9,11},{10,... | collective-permute-start | bytes 786440 | tf_op jit(solution)/shard_map/ppermute | solution.py:331
  238.3 14.5 %collective-permute-start.14 = (bf16[128,1024]{1,0:T(8,128)(2,1)}, bf16[128,1024]{1,0:T(8,128)(2,1)S(1)}, u32[]{:S(2)}, u32[]{:S(2)}) collective-permute-start(bf16[128,1024]{1,0:T(8,128)(2,1)} %get-tuple-element.40), channel_id=1, source_target_pairs={{0,3},{1,2},{2,1},{3,0},{4,7},{5,6},{6,5},{7,4},{8,11},{9,10},{10,... | collective-permute-start | bytes 786440 | tf_op jit(solution)/shard_map/ppermute | solution.py:331
  254.2 1.7 collective-permute-start.15
  (18 other events, 40.7 us)

commit v16 on v15

--- a/solution.py
+++ b/solution.py
@@ -340,7 +340,8 @@
     moved = own > 1
     chosen = retrieved[0]
     if moved:
-        chosen = delivered(chosen, 0)
+        of_all = lax.all_gather(chosen, "section")
+        chosen = lax.dynamic_index_in_dim(of_all, (lax.axis_index("section") + 1) % sections, 0, keepdims=False)
 
     def listed(i):
         source = chosen if i == own - 1 else retrieved[0]

time: 262 us -> 253 us (0.966)
  waiting for transfers between devices: 88.7 us -> 29.6 us
  blocking collectives: 0 us -> 54 us
    all_gather x0 -> x1, blocking collectives: none -> 54 us  [shards(): of_all = lax.all_gather(chosen, 'section')]
    ppermute x10 -> x9, waiting for transfers between devices: 48 us -> 0.02 us  [delivered(): return lax.ppermute(value, ('section', 'seq'), pairs)]
    ppermute x6, waiting for transfers between devices: 13.7 us -> 2.41 us  [swapped(): return lax.ppermute(value, 'seq', [(p, p ^ step) for p in range(seq)])]
    ppermute x10 -> x9, starting transfers between devices: 16.1 us -> 13 us  [delivered(): return lax.ppermute(value, ('section', 'seq'), pairs)]
    unnamed x48 -> x46, local copies, waits for them, and re-layouts: 9.75 us -> 9 us
  transfers between devices with their start and end apart: 19 -> 18, of which waited for: 6 -> 4; matrix products, arithmetic and copies ran while one was open for 2% -> 2% of each run, Pallas kernels for 38% -> 40%
where the time goes in v16:
time: 253 us; the launch traced here: 251 us
  Pallas kernels  121 us (48%)
  blocking collectives  54 us (21%)
  starting transfers between devices  33.3 us (13%)
  waiting for transfers between devices  29.6 us (12%)
  local copies, waits for them, and re-layouts  9.9 us (4%)
  other arithmetic  2.67 us (1%)
    pallas_call x4, Pallas kernels, attend(): pl.pallas_call(functools.partial(attend_kernel, heads, dim, rows, scale,...  82.7 us
    all_gather x1, blocking collectives, shards(): of_all = lax.all_gather(chosen, 'section')  54 us
    all_to_all x3, waiting for transfers between devices, shards(): lax.all_to_all(piece, 'seq', split_axis=0, concat_axis=0, tiled=True)  27.2 us
    all_to_all x3, starting transfers between devices, shards(): lax.all_to_all(piece, 'seq', split_axis=0, concat_axis=0, tiled=True)  16 us
    pallas_call x2, Pallas kernels, pack(): pl.pallas_call(functools.partial(pack_kernel, own, group, index, spans, w...  13.1 us
    ppermute x9, starting transfers between devices, delivered(): return lax.ppermute(value, ('section', 'seq'), pairs)  13 us
    unnamed x46, local copies, waits for them, and re-layouts  9 us
    pallas_call x2, Pallas kernels, prepare(): pl.pallas_call(functools.partial(prepare_kernel, heads, dim, scale, own,...  8.97 us
  transfers between devices with their start and end apart: 18, of which 4 were waited for; matrix products, arithmetic and copies ran while one was open for 2% of the time, Pallas kernels for 40%

profile of v16, /device:TPU:0, one launch (start us, length us, event | category | flops | bytes accessed | tf_op | source)
XLA Modules:
  0.0 251.1 jit_solution(5595549263228991104)
XLA Ops:
  0.0 6.7 %shard_map.88 = bf16[8,2,1024,128]{3,2,1,0:T(8,128)(2,1)} custom-call(bf16[1024,1024]{1,0:T(8,128)(2,1)} %bitcast.42, bf16[1024,1024]{1,0:T(8,128)(2,1)} %bitcast.44), custom_call_target="tpu_custom_call" | custom-call | bytes 4194304 | tf_op jit(solution)/shard_map/pallas_call | solution.py:84
  6.7 6.5 %all-to-all-start = ((bf16[8,2048,128]{2,1,0:T(8,128)(2,1)}), bf16[8,2048,128]{2,1,0:T(8,128)(2,1)}, u32[]{:S(2)}, u32[]{:S(2)}) async-start(bf16[8,2048,128]{2,1,0:T(8,128)(2,1)} %bitcast.41), calls=%async_computation | async-start | bytes 8388608 | tf_op jit(solution)/shard_map/all_to_all | solution.py:389
  13.3 4.0 %shard_map.82 = (bf16[2176,128]{1,0:T(8,128)(2,1)S(1)}, bf16[2176,128]{1,0:T(8,128)(2,1)S(1)}, bf16[2176,128]{1,0:T(8,128)(2,1)S(1)}, bf16[2176,128]{1,0:T(8,128)(2,1)S(1)}) custom-call(f32[64]{0:T(128)S(1)} %divide_bitcast_fusion.gate_ref, s32[1]{0:T(128)} %bitcast.at_ref, bf16[128,8192]{1,0:T(8,128)(2,1)S(1)} %bitcast.35, bf16[128,8192]{1,0:T(8,128)(2,1)} %bitcast.46, ...), custom_call_target="tpu_custom_call" | custom-call | flops 4194304 | bytes 6291456 | tf_op jit(solution)/shard_map/pallas_call | solution.py:130
  21.0 6.9 %shard_map.84 = bf16[2,4,1024,128]{3,2,1,0:T(8,128)(2,1)} custom-call(s32[1]{0:T(128)} %shard_map.83.at_ref, bf16[1024,1024]{1,0:T(8,128)(2,1)} %bitcast.43, bf16[1024,1024]{1,0:T(8,128)(2,1)} %bitcast.45), custom_call_target="tpu_custom_call" | custom-call | bytes 3145728 | tf_op jit(solution)/shard_map/pallas_call | solution.py:42
  27.8 2.4 collective-permute-start
  30.8 5.0 %shard_map.87 = (bf16[2176,128]{1,0:T(8,128)(2,1)S(1)}, bf16[2176,128]{1,0:T(8,128)(2,1)}, bf16[2176,128]{1,0:T(8,128)(2,1)}, bf16[2176,128]{1,0:T(8,128)(2,1)}) custom-call(f32[64]{0:T(128)S(1)} %divide_bitcast_fusion.gate_ref, s32[1]{0:T(128)} %bitcast.at_ref, bf16[128,8192]{1,0:T(8,128)(2,1)S(1)} %bitcast.36, bf16[128,8192]{1,0:T(8,128)(2,1)} %bitcast.47, ...), custom_call_target="tpu_custom_call" | custom-call | flops 4194304 | bytes 6291456 | tf_op jit(solution)/shard_map/pallas_call | solution.py:130
  36.6 2.0 collective-permute-start.2
  38.8 54.0 %all_gather.3 = s32[4,8,8,32]{3,2,1,0:T(8,128)S(1)} all-gather(s32[1,8,8,32]{3,2,1,0:T(8,128)S(1)} %copy-done.18), channel_id=1, replica_groups=mesh['section'=4,'seq'=8] {'section'}, dimensions={0}, use_global_device_ids=true | all-gather | bytes 40960 | tf_op jit(solution)/shard_map/all_gather | solution.py:343
  96.8 6.4 %shard_map.85 = (bf16[8,2,640,128]{3,2,1,0:T(8,128)(2,1)}, bf16[8,2,384,128]{3,2,1,0:T(8,128)(2,1)}) custom-call(bf16[2,4,1024,128]{3,2,1,0:T(8,128)(2,1)} %collective-permute-done.refs_0_), custom_call_target="tpu_custom_call" | custom-call | bytes 4194304 | tf_op jit(solution)/shard_map/pallas_call | solution.py:84
  104.5 2.8 %collective-permute-start.10 = (bf16[2176,128]{1,0:T(8,128)(2,1)S(1)}, bf16[2176,128]{1,0:T(8,128)(2,1)}, u32[]{:S(2)}, u32[]{:S(2)}) collective-permute-start(bf16[2176,128]{1,0:T(8,128)(2,1)S(1)} %copy-done.5), channel_id=1, source_target_pairs={{0,26},{1,27},{2,24},{3,25},{4,30},{5,31},{6,28},{7,29},{8,2},{9,3... | collective-permute-start | bytes 1671176 | tf_op jit(solution)/shard_map/ppermute | solution.py:335
  107.3 1.4 collective-permute-start.11
  110.3 4.7 %all-to-all-start.1 = ((bf16[8,1280,128]{2,1,0:T(8,128)(2,1)}), bf16[8,1280,128]{2,1,0:T(8,128)(2,1)}, u32[]{:S(2)}, u32[]{:S(2)}) async-start(bf16[8,1280,128]{2,1,0:T(8,128)(2,1)} %shard_map.91), calls=%async_computation.1 | async-start | bytes 5242880 | tf_op jit(solution)/shard_map/all_to_all | solution.py:389
  115.0 36.2 %shard_map.89 = (bf16[128,1024]{1,0:T(8,128)(2,1)}, bf16[128,1024]{1,0:T(8,128)(2,1)}, bf16[128,1024]{1,0:T(8,128)(2,1)}, bf16[128,1024]{1,0:T(8,128)(2,1)}) custom-call(s32[4,32]{1,0:T(4,128)} %select_reduce_fusion.1.picks_ref, s32[4,2]{1,0:T(4,128)} %shard_map.86.starts_ref, bf16[2176,128]{1,0:T(8,128)(2,1)} %copy-done.1, bf16[2176,128]{1,0:T(8,128)(2,1)} %copy-done.14, ...), custom_call_target="tpu_custom_call" | custom-call | flops 51539607552 | tf_op jit(solution)/shard_map/pallas_call | solution.py:253
  152.6 1.3 collective-permute-start.5
  153.9 2.4 collective-permute-start.6
  157.2 18.0 %all-to-all-done.1.refs_1_ = bf16[8,1280,128]{2,1,0:T(8,128)(2,1)} async-done(((bf16[8,1280,128]{2,1,0:T(8,128)(2,1)}), bf16[8,1280,128]{2,1,0:T(8,128)(2,1)}, u32[]{:S(2)}, u32[]{:S(2)}) %all-to-all-start.1) | async-done | bytes 2621472 | tf_op jit(solution)/shard_map/all_to_all | solution.py:389
  175.9 4.7 %all-to-all-start.2 = ((bf16[8,768,128]{2,1,0:T(8,128)(2,1)}), bf16[8,768,128]{2,1,0:T(8,128)(2,1)S(1)}, u32[]{:S(2)}, u32[]{:S(2)}) async-start(bf16[8,768,128]{2,1,0:T(8,128)(2,1)} %shard_map.94), calls=%async_computation.2 | async-start | bytes 3145728 | tf_op jit(solution)/shard_map/all_to_all | solution.py:389
  180.7 26.3 %shard_map.92.refs_1_.refs_3_ = f32[4,1024,128]{2,1,0:T(8,128)} custom-call(s32[4,32]{1,0:T(4,128)} %select_reduce_fusion.picks_ref, s32[4,2]{1,0:T(4,128)} %shard_map.90.starts_ref, bf16[2176,128]{1,0:T(8,128)(2,1)} %collective-permute-done.8.refs_0_.refs_2_, bf16[2176,128]{1,0:T(8,128)(2,1)} %collective-permute-done.9.refs_1_.refs_3_, ...), custom_call_target="tpu_custom_call" | custom-call | flops 32212254720 | tf_op jit(solution)/shard_map/pallas_call | solution.py:253
  209.3 9.1 %all-to-all-done.2 = bf16[8,768,128]{2,1,0:T(8,128)(2,1)S(1)} async-done(((bf16[8,768,128]{2,1,0:T(8,128)(2,1)}), bf16[8,768,128]{2,1,0:T(8,128)(2,1)S(1)}, u32[]{:S(2)}, u32[]{:S(2)}) %all-to-all-start.2) | async-done | bytes 1572896 | tf_op jit(solution)/shard_map/all_to_all | solution.py:389
  219.7 10.3 %shard_map.95 = (bf16[128,1024]{1,0:T(8,128)(2,1)}, bf16[128,1024]{1,0:T(8,128)(2,1)}) custom-call(s32[4,32]{1,0:T(4,128)} %select_reduce_fusion.picks_ref, s32[4,2]{1,0:T(4,128)} %shard_map.93.starts_ref, bf16[2176,128]{1,0:T(8,128)(2,1)} %collective-permute-done.10.refs_2_.refs_4_.refs_0_, ...), custom_call_target="tpu_custom_call" | custom-call | flops 9663676416 | tf_op jit(solution)/shard_map/pallas_call | solution.py:253
  231.3 10.0 %shard_map.97 = (bf16[128,1024]{1,0:T(8,128)(2,1)}, bf16[128,1024]{1,0:T(8,128)(2,1)}) custom-call(s32[4,32]{1,0:T(4,128)} %select_reduce_fusion.picks_ref, s32[4,2]{1,0:T(4,128)} %shard_map.96.starts_ref, bf16[2176,128]{1,0:T(8,128)(2,1)} %collective-permute-done.8.refs_0_.refs_2_, bf16[2176,128]{1,0:T(8,128)(2,1)} %collective-permute-done.9.refs_1_.refs_3_, ...), custom_call_target="tpu_custom_call" | custom-call | flops 9663676416 | tf_op jit(solution)/shard_map/pallas_call | solution.py:253
  243.7 1.5 collective-permute-start.14
  245.2 1.4 collective-permute-done.14.refs_5_
  247.3 3.8 %shard_map.99 = bf16[128,8192]{1,0:T(8,128)(2,1)} custom-call(s32[1]{0:T(128)} %bitcast.at_ref, bf16[128,1024]{1,0:T(8,128)(2,1)} %copy-done.8, bf16[128,1024]{1,0:T(8,128)(2,1)} %copy-done.9, bf16[128,1024]{1,0:T(8,128)(2,1)} %copy-done.10, bf16[128,1024]{1,0:T(8,128)(2,1)} %copy-done.11, bf16[128,1024]{1,0:T(8,128)(2,1)} %get-tuple-element.38.refs_4_, ...), custom_call_target="tpu_custom_call" | custom-call | bytes 4194304 | tf_op jit(solution)/shard_map/pallas_call | solution.py:283
  (92 shorter events, 23.2 us)
Async XLA Ops:
  6.7 6.6 %copy-start.21 = (f32[1,64]{1,0:T(1,128)S(1)}, f32[1,64]{1,0:T(1,128)}, u32[]{:S(2)}) copy-start(f32[1,64]{1,0:T(1,128)} %param.12) | copy-start | bytes 772
  6.7 6.6 %copy-start = (bf16[1,128,8192]{2,1,0:T(8,128)(2,1)S(1)}, bf16[1,128,8192]{2,1,0:T(8,128)(2,1)}, u32[]{:S(2)}) copy-start(bf16[1,128,8192]{2,1,0:T(8,128)(2,1)} %param.8) | copy-start | bytes 6291460
  6.7 102.0 %all-to-all-start = ((bf16[8,2048,128]{2,1,0:T(8,128)(2,1)}), bf16[8,2048,128]{2,1,0:T(8,128)(2,1)}, u32[]{:S(2)}, u32[]{:S(2)}) async-start(bf16[8,2048,128]{2,1,0:T(8,128)(2,1)} %bitcast.41), calls=%async_computation | async-start | bytes 8388608 | tf_op jit(solution)/shard_map/all_to_all | solution.py:389
  21.0 9.3 %copy-start.3 = (bf16[2176,128]{1,0:T(8,128)(2,1)S(1)}, bf16[2176,128]{1,0:T(8,128)(2,1)}, u32[]{:S(2)}) copy-start(bf16[2176,128]{1,0:T(8,128)(2,1)} %copy-done.2) | copy-start | bytes 1671172
  27.8 11.0 %copy-start.18 = (s32[1,8,8,32]{3,2,1,0:T(8,128)S(1)}, s32[1,8,8,32]{3,2,1,0:T(8,128)}, u32[]{:S(2)}) copy-start(s32[1,8,8,32]{3,2,1,0:T(8,128)} %param.15) | copy-start | bytes 24580
  27.8 68.5 %collective-permute-start = (bf16[2,4,1024,128]{3,2,1,0:T(8,128)(2,1)}, bf16[2,4,1024,128]{3,2,1,0:T(8,128)(2,1)}, u32[]{:S(2)}, u32[]{:S(2)}) collective-permute-start(bf16[2,4,1024,128]{3,2,1,0:T(8,128)(2,1)} %shard_map.84), channel_id=1, source_target_pairs={{0,24},{1,25},{2,26},{3,27},{4,28},{5,29},{6,30},{7,31},{8,0},{9,1... | collective-permute-start | bytes 6291464 | tf_op jit(solution)/shard_map/ppermute | solution.py:335
  30.3 122.3 %collective-permute-start.8 = (bf16[2176,128]{1,0:T(8,128)(2,1)S(1)}, bf16[2176,128]{1,0:T(8,128)(2,1)}, u32[]{:S(2)}, u32[]{:S(2)}) collective-permute-start(bf16[2176,128]{1,0:T(8,128)(2,1)S(1)} %copy-done.3), channel_id=1, source_target_pairs={{0,24},{1,25},{2,26},{3,27},{4,28},{5,29},{6,30},{7,31},{8,0},{9,1... | collective-permute-start | bytes 1671176 | tf_op jit(solution)/shard_map/ppermute | solution.py:335
  36.6 67.9 %collective-permute-start.1 = (bf16[2176,128]{1,0:T(8,128)(2,1)}, bf16[2176,128]{1,0:T(8,128)(2,1)S(1)}, u32[]{:S(2)}, u32[]{:S(2)}) collective-permute-start(bf16[2176,128]{1,0:T(8,128)(2,1)} %get-tuple-element.26), channel_id=1, source_target_pairs={{0,1},{1,0},{2,3},{3,2},{4,5},{5,4},{6,7},{7,6},{8,9},{9,8},{10,11... | collective-permute-start | bytes 1671176 | tf_op jit(solution)/shard_map/ppermute | solution.py:331
  36.6 70.7 %collective-permute-start.2 = (bf16[2176,128]{1,0:T(8,128)(2,1)}, bf16[2176,128]{1,0:T(8,128)(2,1)S(1)}, u32[]{:S(2)}, u32[]{:S(2)}) collective-permute-start(bf16[2176,128]{1,0:T(8,128)(2,1)} %get-tuple-element.27), channel_id=1, source_target_pairs={{0,2},{1,3},{2,0},{3,1},{4,6},{5,7},{6,4},{7,5},{8,10},{9,11},{10,... | collective-permute-start | bytes 1671176 | tf_op jit(solution)/shard_map/ppermute | solution.py:331
  38.6 70.1 %collective-permute-start.3 = (bf16[2176,128]{1,0:T(8,128)(2,1)}, bf16[2176,128]{1,0:T(8,128)(2,1)S(1)}, u32[]{:S(2)}, u32[]{:S(2)}) collective-permute-start(bf16[2176,128]{1,0:T(8,128)(2,1)} %get-tuple-element.28), channel_id=1, source_target_pairs={{0,3},{1,2},{2,1},{3,0},{4,7},{5,6},{6,5},{7,4},{8,11},{9,10},{10,... | collective-permute-start | bytes 1671176 | tf_op jit(solution)/shard_map/ppermute | solution.py:331
  93.9 10.6 %copy-start.19 = (s32[4,2]{1,0:T(4,128)}, s32[4,2]{1,0:T(4,128)S(1)}, u32[]{:S(2)}) copy-start(s32[4,2]{1,0:T(4,128)S(1)} %get-tuple-element.56.refs_0_) | copy-start | bytes 100
  96.3 8.1 %copy-start.5 = (bf16[2176,128]{1,0:T(8,128)(2,1)S(1)}, bf16[2176,128]{1,0:T(8,128)(2,1)}, u32[]{:S(2)}) copy-start(bf16[2176,128]{1,0:T(8,128)(2,1)} %copy-done.4) | copy-start | bytes 1671172
  96.3 57.6 %collective-permute-start.9 = (bf16[2176,128]{1,0:T(8,128)(2,1)}, bf16[2176,128]{1,0:T(8,128)(2,1)}, u32[]{:S(2)}, u32[]{:S(2)}) collective-permute-start(bf16[2176,128]{1,0:T(8,128)(2,1)} %copy-done.6), channel_id=1, source_target_pairs={{0,25},{1,24},{2,27},{3,26},{4,29},{5,28},{6,31},{7,30},{8,1},{9,0... | collective-permute-start | bytes 1671176 | tf_op jit(solution)/shard_map/ppermute | solution.py:335
  104.5 51.8 %collective-permute-start.10 = (bf16[2176,128]{1,0:T(8,128)(2,1)S(1)}, bf16[2176,128]{1,0:T(8,128)(2,1)}, u32[]{:S(2)}, u32[]{:S(2)}) collective-permute-start(bf16[2176,128]{1,0:T(8,128)(2,1)S(1)} %copy-done.5), channel_id=1, source_target_pairs={{0,26},{1,27},{2,24},{3,25},{4,30},{5,31},{6,28},{7,29},{8,2},{9,3... | collective-permute-start | bytes 1671176 | tf_op jit(solution)/shard_map/ppermute | solution.py:335
  107.3 49.9 %collective-permute-start.11 = (bf16[2176,128]{1,0:T(8,128)(2,1)S(1)}, bf16[2176,128]{1,0:T(8,128)(2,1)}, u32[]{:S(2)}, u32[]{:S(2)}) collective-permute-start(bf16[2176,128]{1,0:T(8,128)(2,1)S(1)} %get-tuple-element.35), channel_id=1, source_target_pairs={{0,27},{1,26},{2,25},{3,24},{4,31},{5,30},{6,29},{7,28},{8,3},{9,2... | collective-permute-start | bytes 1671176 | tf_op jit(solution)/shard_map/ppermute | solution.py:335
  110.3 64.9 %all-to-all-start.1 = ((bf16[8,1280,128]{2,1,0:T(8,128)(2,1)}), bf16[8,1280,128]{2,1,0:T(8,128)(2,1)}, u32[]{:S(2)}, u32[]{:S(2)}) async-start(bf16[8,1280,128]{2,1,0:T(8,128)(2,1)} %shard_map.91), calls=%async_computation.1 | async-start | bytes 5242880 | tf_op jit(solution)/shard_map/all_to_all | solution.py:389
  151.2 55.8 %collective-permute-start.4 = (bf16[128,1024]{1,0:T(8,128)(2,1)}, bf16[128,1024]{1,0:T(8,128)(2,1)S(1)}, u32[]{:S(2)}, u32[]{:S(2)}) collective-permute-start(bf16[128,1024]{1,0:T(8,128)(2,1)} %get-tuple-element.29.refs_1_), channel_id=1, source_target_pairs={{0,24},{1,25},{2,26},{3,27},{4,28},{5,29},{6,30},{7,31},{8,0},{9,1... | collective-permute-start | bytes 786440 | tf_op jit(solution)/shard_map/ppermute | solution.py:335
  152.6 54.4 %collective-permute-start.5 = (bf16[128,1024]{1,0:T(8,128)(2,1)}, bf16[128,1024]{1,0:T(8,128)(2,1)S(1)}, u32[]{:S(2)}, u32[]{:S(2)}) collective-permute-start(bf16[128,1024]{1,0:T(8,128)(2,1)} %get-tuple-element.30), channel_id=1, source_target_pairs={{0,25},{1,24},{2,27},{3,26},{4,29},{5,28},{6,31},{7,30},{8,1},{9,0... | collective-permute-start | bytes 786440 | tf_op jit(solution)/shard_map/ppermute | solution.py:335
  153.9 53.1 %collective-permute-start.6 = (bf16[128,1024]{1,0:T(8,128)(2,1)}, bf16[128,1024]{1,0:T(8,128)(2,1)S(1)}, u32[]{:S(2)}, u32[]{:S(2)}) collective-permute-start(bf16[128,1024]{1,0:T(8,128)(2,1)} %get-tuple-element.31), channel_id=1, source_target_pairs={{0,26},{1,27},{2,24},{3,25},{4,30},{5,31},{6,28},{7,29},{8,2},{9,3... | collective-permute-start | bytes 786440 | tf_op jit(solution)/shard_map/ppermute | solution.py:335
  156.3 50.7 %collective-permute-start.7 = (bf16[128,1024]{1,0:T(8,128)(2,1)}, bf16[128,1024]{1,0:T(8,128)(2,1)S(1)}, u32[]{:S(2)}, u32[]{:S(2)}) collective-permute-start(bf16[128,1024]{1,0:T(8,128)(2,1)} %get-tuple-element.32), channel_id=1, source_target_pairs={{0,27},{1,26},{2,25},{3,24},{4,31},{5,30},{6,29},{7,28},{8,3},{9,2... | collective-permute-start | bytes 786440 | tf_op jit(solution)/shard_map/ppermute | solution.py:335
  175.9 42.6 %all-to-all-start.2 = ((bf16[8,768,128]{2,1,0:T(8,128)(2,1)}), bf16[8,768,128]{2,1,0:T(8,128)(2,1)S(1)}, u32[]{:S(2)}, u32[]{:S(2)}) async-start(bf16[8,768,128]{2,1,0:T(8,128)(2,1)} %shard_map.94), calls=%async_computation.2 | async-start | bytes 3145728 | tf_op jit(solution)/shard_map/all_to_all | solution.py:389
  230.6 10.7 %collective-permute-start.12 = (bf16[128,1024]{1,0:T(8,128)(2,1)}, bf16[128,1024]{1,0:T(8,128)(2,1)S(1)}, u32[]{:S(2)}, u32[]{:S(2)}) collective-permute-start(bf16[128,1024]{1,0:T(8,128)(2,1)} %get-tuple-element.37.refs_1_), channel_id=1, source_target_pairs={{0,2},{1,3},{2,0},{3,1},{4,6},{5,7},{6,4},{7,5},{8,10},{9,11},{10,... | collective-permute-start | bytes 786440 | tf_op jit(solution)/shard_map/ppermute | solution.py:331
  230.6 11.7 %collective-permute-start.13 = (bf16[128,1024]{1,0:T(8,128)(2,1)}, bf16[128,1024]{1,0:T(8,128)(2,1)S(1)}, u32[]{:S(2)}, u32[]{:S(2)}) collective-permute-start(bf16[128,1024]{1,0:T(8,128)(2,1)} %get-tuple-element.40), channel_id=1, source_target_pairs={{0,3},{1,2},{2,1},{3,0},{4,7},{5,6},{6,5},{7,4},{8,11},{9,10},{10,... | collective-permute-start | bytes 786440 | tf_op jit(solution)/shard_map/ppermute | solution.py:331
  243.7 2.9 %collective-permute-start.14 = (bf16[128,1024]{1,0:T(8,128)(2,1)}, bf16[128,1024]{1,0:T(8,128)(2,1)S(1)}, u32[]{:S(2)}, u32[]{:S(2)}) collective-permute-start(bf16[128,1024]{1,0:T(8,128)(2,1)} %shard_map.98), channel_id=1, source_target_pairs={{0,1},{1,0},{2,3},{3,2},{4,5},{5,4},{6,7},{7,6},{8,9},{9,8},{10,11... | collective-permute-start | bytes 786440 | tf_op jit(solution)/shard_map/ppermute | solution.py:331
  (16 other events, 23.1 us)

commit v17 on v16

--- a/solution.py
+++ b/solution.py
@@ -334,7 +334,7 @@
         pairs = [(s * seq + p, ((s - 1) % sections) * seq + (p ^ step)) for s in range(sections) for p in range(seq)]
         return lax.ppermute(value, ("section", "seq"), pairs)
 
-    cut = (5 * blocks + 7) // 8
+    cut = (3 * blocks + 3) // 4
     cuts = [[(0, blocks)]] * (own - 1) + [[(0, cut), (cut, blocks)]]
 
     moved = own > 1

time: 253 us -> 258 us (1.020)
  local copies, waits for them, and re-layouts: 9.9 us -> 13.4 us
    unnamed x46 -> x47, local copies, waits for them, and re-layouts: 9 us -> 12.6 us
  transfers between devices with their start and end apart: 18 -> 18, of which waited for: 4 -> 3; matrix products, arithmetic and copies ran while one was open for 2% -> 3% of each run, Pallas kernels for 40% -> 39%
where the time goes in v17:
time: 258 us
  Pallas kernels  122 us (47%)
  blocking collectives  54 us (21%)
  starting transfers between devices  34.4 us (13%)
  waiting for transfers between devices  31.2 us (12%)
  local copies, waits for them, and re-layouts  13.4 us (5%)
  other arithmetic  2.7 us (1%)
    pallas_call x4, Pallas kernels, attend(): pl.pallas_call(functools.partial(attend_kernel, heads, dim, rows, scale,...  83.4 us
    all_gather x1, blocking collectives, shards(): of_all = lax.all_gather(chosen, 'section')  54 us
    all_to_all x3, waiting for transfers between devices, shards(): lax.all_to_all(piece, 'seq', split_axis=0, concat_axis=0, tiled=True)  26.6 us
    all_to_all x3, starting transfers between devices, shards(): lax.all_to_all(piece, 'seq', split_axis=0, concat_axis=0, tiled=True)  14.9 us
    ppermute x9, starting transfers between devices, delivered(): return lax.ppermute(value, ('section', 'seq'), pairs)  13.1 us
    pallas_call x2, Pallas kernels, pack(): pl.pallas_call(functools.partial(pack_kernel, own, group, index, spans, w...  13 us
    unnamed x47, local copies, waits for them, and re-layouts  12.6 us
    pallas_call x2, Pallas kernels, prepare(): pl.pallas_call(functools.partial(prepare_kernel, heads, dim, scale, own,...  8.95 us
  transfers between devices with their start and end apart: 18, of which 3 were waited for; matrix products, arithmetic and copies ran while one was open for 3% of the time, Pallas kernels for 39%

profile of v17, /device:TPU:0, one launch (start us, length us, event | category | flops | bytes accessed | tf_op | source)
XLA Modules:
  0.0 258.0 jit_solution(11669860993163576325)
XLA Ops:
  0.0 6.7 %shard_map.88 = bf16[8,2,1024,128]{3,2,1,0:T(8,128)(2,1)} custom-call(bf16[1024,1024]{1,0:T(8,128)(2,1)} %bitcast.42, bf16[1024,1024]{1,0:T(8,128)(2,1)} %bitcast.44), custom_call_target="tpu_custom_call" | custom-call | bytes 4194304 | tf_op jit(solution)/shard_map/pallas_call | solution.py:84
  6.7 6.5 %all-to-all-start = ((bf16[8,2048,128]{2,1,0:T(8,128)(2,1)}), bf16[8,2048,128]{2,1,0:T(8,128)(2,1)}, u32[]{:S(2)}, u32[]{:S(2)}) async-start(bf16[8,2048,128]{2,1,0:T(8,128)(2,1)} %bitcast.39), calls=%async_computation | async-start | bytes 8388608 | tf_op jit(solution)/shard_map/all_to_all | solution.py:389
  13.3 4.0 %shard_map.82 = (bf16[2176,128]{1,0:T(8,128)(2,1)S(1)}, bf16[2176,128]{1,0:T(8,128)(2,1)S(1)}, bf16[2176,128]{1,0:T(8,128)(2,1)S(1)}, bf16[2176,128]{1,0:T(8,128)(2,1)S(1)}) custom-call(f32[64]{0:T(128)S(1)} %divide_bitcast_fusion.gate_ref, s32[1]{0:T(128)} %bitcast.at_ref, bf16[128,8192]{1,0:T(8,128)(2,1)S(1)} %bitcast.35, bf16[128,8192]{1,0:T(8,128)(2,1)} %bitcast.46, ...), custom_call_target="tpu_custom_call" | custom-call | flops 4194304 | bytes 6291456 | tf_op jit(solution)/shard_map/pallas_call | solution.py:130
  21.0 6.7 %shard_map.84 = bf16[2,4,1024,128]{3,2,1,0:T(8,128)(2,1)} custom-call(s32[1]{0:T(128)} %shard_map.83.at_ref, bf16[1024,1024]{1,0:T(8,128)(2,1)} %bitcast.43, bf16[1024,1024]{1,0:T(8,128)(2,1)} %bitcast.45), custom_call_target="tpu_custom_call" | custom-call | bytes 3145728 | tf_op jit(solution)/shard_map/pallas_call | solution.py:42
  27.7 2.4 collective-permute-start
  30.7 5.0 %shard_map.87 = (bf16[2176,128]{1,0:T(8,128)(2,1)S(1)}, bf16[2176,128]{1,0:T(8,128)(2,1)}, bf16[2176,128]{1,0:T(8,128)(2,1)}, bf16[2176,128]{1,0:T(8,128)(2,1)}) custom-call(f32[64]{0:T(128)S(1)} %divide_bitcast_fusion.gate_ref, s32[1]{0:T(128)} %bitcast.at_ref, bf16[128,8192]{1,0:T(8,128)(2,1)S(1)} %bitcast.36, bf16[128,8192]{1,0:T(8,128)(2,1)} %bitcast.47, ...), custom_call_target="tpu_custom_call" | custom-call | flops 4194304 | bytes 6291456 | tf_op jit(solution)/shard_map/pallas_call | solution.py:130
  36.5 2.0 collective-permute-start.2
  38.7 54.0 %all_gather.3 = s32[4,8,8,32]{3,2,1,0:T(8,128)S(1)} all-gather(s32[1,8,8,32]{3,2,1,0:T(8,128)S(1)} %copy-done.18), channel_id=1, replica_groups=mesh['section'=4,'seq'=8] {'section'}, dimensions={0}, use_global_device_ids=true | all-gather | bytes 40960 | tf_op jit(solution)/shard_map/all_gather | solution.py:343
  95.2 6.3 %shard_map.85 = (bf16[8,2,768,128]{3,2,1,0:T(8,128)(2,1)}, bf16[8,2,256,128]{3,2,1,0:T(8,128)(2,1)}) custom-call(bf16[2,4,1024,128]{3,2,1,0:T(8,128)(2,1)} %collective-permute-done.refs_0_), custom_call_target="tpu_custom_call" | custom-call | bytes 4194304 | tf_op jit(solution)/shard_map/pallas_call | solution.py:84
  101.5 3.8 %copy.35.refs_0_ = bf16[8,1536,128]{2,1,0:T(8,128)(2,1)} copy(bf16[8,1536,128]{2,1,0:T(8,128)(2,1)} %bitcast.40) | data formatting | bytes 6291456
  105.4 2.8 %collective-permute-start.10 = (bf16[2176,128]{1,0:T(8,128)(2,1)S(1)}, bf16[2176,128]{1,0:T(8,128)(2,1)}, u32[]{:S(2)}, u32[]{:S(2)}) collective-permute-start(bf16[2176,128]{1,0:T(8,128)(2,1)S(1)} %copy-done.5), channel_id=1, source_target_pairs={{0,26},{1,27},{2,24},{3,25},{4,30},{5,31},{6,28},{7,29},{8,2},{9,3... | collective-permute-start | bytes 1671176 | tf_op jit(solution)/shard_map/ppermute | solution.py:335
  111.2 4.7 %all-to-all-start.1 = ((bf16[8,1536,128]{2,1,0:T(8,128)(2,1)}), bf16[8,1536,128]{2,1,0:T(8,128)(2,1)}, u32[]{:S(2)}, u32[]{:S(2)}) async-start(bf16[8,1536,128]{2,1,0:T(8,128)(2,1)} %shard_map.91), calls=%async_computation.1 | async-start | bytes 6291456 | tf_op jit(solution)/shard_map/all_to_all | solution.py:389
  118.8 36.2 %shard_map.89 = (bf16[128,1024]{1,0:T(8,128)(2,1)}, bf16[128,1024]{1,0:T(8,128)(2,1)}, bf16[128,1024]{1,0:T(8,128)(2,1)}, bf16[128,1024]{1,0:T(8,128)(2,1)}) custom-call(s32[4,32]{1,0:T(4,128)} %select_reduce_fusion.1.picks_ref, s32[4,2]{1,0:T(4,128)} %shard_map.86.starts_ref, bf16[2176,128]{1,0:T(8,128)(2,1)} %copy-done.1, bf16[2176,128]{1,0:T(8,128)(2,1)} %copy-done.14, ...), custom_call_target="tpu_custom_call" | custom-call | flops 51539607552 | tf_op jit(solution)/shard_map/pallas_call | solution.py:253
  157.8 2.4 collective-permute-start.6
  161.1 26.6 %all-to-all-done.1.refs_1_ = bf16[8,1536,128]{2,1,0:T(8,128)(2,1)} async-done(((bf16[8,1536,128]{2,1,0:T(8,128)(2,1)}), bf16[8,1536,128]{2,1,0:T(8,128)(2,1)}, u32[]{:S(2)}, u32[]{:S(2)}) %all-to-all-start.1) | async-done | bytes 3145760 | tf_op jit(solution)/shard_map/all_to_all | solution.py:389
  188.4 3.7 %all-to-all-start.2 = ((bf16[8,512,128]{2,1,0:T(8,128)(2,1)}), bf16[8,512,128]{2,1,0:T(8,128)(2,1)S(1)}, u32[]{:S(2)}, u32[]{:S(2)}) async-start(bf16[8,512,128]{2,1,0:T(8,128)(2,1)} %shard_map.94), calls=%async_computation.2 | async-start | bytes 2097152 | tf_op jit(solution)/shard_map/all_to_all | solution.py:389
  192.2 29.6 %shard_map.92.refs_1_.refs_3_ = f32[4,1024,128]{2,1,0:T(8,128)} custom-call(s32[4,32]{1,0:T(4,128)} %select_reduce_fusion.picks_ref, s32[4,2]{1,0:T(4,128)} %shard_map.90.starts_ref, bf16[2176,128]{1,0:T(8,128)(2,1)} %collective-permute-done.8.refs_0_.refs_2_, bf16[2176,128]{1,0:T(8,128)(2,1)} %collective-permute-done.9.refs_1_.refs_3_, ...), custom_call_target="tpu_custom_call" | custom-call | flops 38654705664 | tf_op jit(solution)/shard_map/pallas_call | solution.py:253
  225.1 8.8 %shard_map.95 = (bf16[128,1024]{1,0:T(8,128)(2,1)}, bf16[128,1024]{1,0:T(8,128)(2,1)}) custom-call(s32[4,32]{1,0:T(4,128)} %select_reduce_fusion.picks_ref, s32[4,2]{1,0:T(4,128)} %shard_map.93.starts_ref, bf16[2176,128]{1,0:T(8,128)(2,1)} %collective-permute-done.10.refs_2_.refs_4_.refs_0_, ...), custom_call_target="tpu_custom_call" | custom-call | flops 6442450944 | tf_op jit(solution)/shard_map/pallas_call | solution.py:253
  234.6 2.8 %collective-permute-start.12 = (bf16[128,1024]{1,0:T(8,128)(2,1)}, bf16[128,1024]{1,0:T(8,128)(2,1)S(1)}, u32[]{:S(2)}, u32[]{:S(2)}) collective-permute-start(bf16[128,1024]{1,0:T(8,128)(2,1)} %get-tuple-element.37.refs_1_), channel_id=1, source_target_pairs={{0,2},{1,3},{2,0},{3,1},{4,6},{5,7},{6,4},{7,5},{8,10},{9,11},{10,... | collective-permute-start | bytes 786440 | tf_op jit(solution)/shard_map/ppermute | solution.py:331
  237.4 1.4 collective-permute-start.13
  238.9 8.7 %shard_map.97 = (bf16[128,1024]{1,0:T(8,128)(2,1)}, bf16[128,1024]{1,0:T(8,128)(2,1)}) custom-call(s32[4,32]{1,0:T(4,128)} %select_reduce_fusion.picks_ref, s32[4,2]{1,0:T(4,128)} %shard_map.96.starts_ref, bf16[2176,128]{1,0:T(8,128)(2,1)} %collective-permute-done.8.refs_0_.refs_2_, bf16[2176,128]{1,0:T(8,128)(2,1)} %collective-permute-done.9.refs_1_.refs_3_, ...), custom_call_target="tpu_custom_call" | custom-call | flops 6442450944 | tf_op jit(solution)/shard_map/pallas_call | solution.py:253
  247.6 2.8 %collective-permute-done.13.refs_2_.refs_7_ = bf16[128,1024]{1,0:T(8,128)(2,1)S(1)} collective-permute-done((bf16[128,1024]{1,0:T(8,128)(2,1)}, bf16[128,1024]{1,0:T(8,128)(2,1)S(1)}, u32[]{:S(2)}, u32[]{:S(2)}) %collective-permute-start.13) | collective-permute-done | bytes 262176 | tf_op jit(solution)/shard_map/ppermute | solution.py:331
  251.8 1.7 collective-permute-done.14.refs_5_
  254.3 3.8 %shard_map.99 = bf16[128,8192]{1,0:T(8,128)(2,1)} custom-call(s32[1]{0:T(128)} %bitcast.at_ref, bf16[128,1024]{1,0:T(8,128)(2,1)} %copy-done.7, bf16[128,1024]{1,0:T(8,128)(2,1)} %copy-done.8, bf16[128,1024]{1,0:T(8,128)(2,1)} %copy-done.9, bf16[128,1024]{1,0:T(8,128)(2,1)} %copy-done.10, bf16[128,1024]{1,0:T(8,128)(2,1)} %get-tuple-element.38.refs_4_, ...), custom_call_target="tpu_custom_call" | custom-call | bytes 4194304 | tf_op jit(solution)/shard_map/pallas_call | solution.py:283
  (93 shorter events, 24.0 us)
Async XLA Ops:
  6.7 6.5 %copy-start.20 = (bf16[1,128,64]{1,2,0:T(8,128)(2,1)S(1)}, bf16[1,128,64]{1,2,0:T(8,128)(2,1)}, u32[]{:S(2)}) copy-start(bf16[1,128,64]{1,2,0:T(8,128)(2,1)} %param.11) | copy-start | bytes 49156
  6.7 6.6 %copy-start.21 = (f32[1,64]{1,0:T(1,128)S(1)}, f32[1,64]{1,0:T(1,128)}, u32[]{:S(2)}) copy-start(f32[1,64]{1,0:T(1,128)} %param.12) | copy-start | bytes 772
  6.7 6.6 %copy-start = (bf16[1,128,8192]{2,1,0:T(8,128)(2,1)S(1)}, bf16[1,128,8192]{2,1,0:T(8,128)(2,1)}, u32[]{:S(2)}) copy-start(bf16[1,128,8192]{2,1,0:T(8,128)(2,1)} %param.8) | copy-start | bytes 6291460
  6.7 103.0 %all-to-all-start = ((bf16[8,2048,128]{2,1,0:T(8,128)(2,1)}), bf16[8,2048,128]{2,1,0:T(8,128)(2,1)}, u32[]{:S(2)}, u32[]{:S(2)}) async-start(bf16[8,2048,128]{2,1,0:T(8,128)(2,1)} %bitcast.39), calls=%async_computation | async-start | bytes 8388608 | tf_op jit(solution)/shard_map/all_to_all | solution.py:389
  21.0 9.2 %copy-start.3 = (bf16[2176,128]{1,0:T(8,128)(2,1)S(1)}, bf16[2176,128]{1,0:T(8,128)(2,1)}, u32[]{:S(2)}) copy-start(bf16[2176,128]{1,0:T(8,128)(2,1)} %copy-done.2) | copy-start | bytes 1671172
  27.7 10.9 %copy-start.18 = (s32[1,8,8,32]{3,2,1,0:T(8,128)S(1)}, s32[1,8,8,32]{3,2,1,0:T(8,128)}, u32[]{:S(2)}) copy-start(s32[1,8,8,32]{3,2,1,0:T(8,128)} %param.15) | copy-start | bytes 24580
  27.7 66.9 %collective-permute-start = (bf16[2,4,1024,128]{3,2,1,0:T(8,128)(2,1)}, bf16[2,4,1024,128]{3,2,1,0:T(8,128)(2,1)}, u32[]{:S(2)}, u32[]{:S(2)}) collective-permute-start(bf16[2,4,1024,128]{3,2,1,0:T(8,128)(2,1)} %shard_map.84), channel_id=1, source_target_pairs={{0,24},{1,25},{2,26},{3,27},{4,28},{5,29},{6,30},{7,31},{8,0},{9,1... | collective-permute-start | bytes 6291464 | tf_op jit(solution)/shard_map/ppermute | solution.py:335
  30.2 126.3 %collective-permute-start.8 = (bf16[2176,128]{1,0:T(8,128)(2,1)S(1)}, bf16[2176,128]{1,0:T(8,128)(2,1)}, u32[]{:S(2)}, u32[]{:S(2)}) collective-permute-start(bf16[2176,128]{1,0:T(8,128)(2,1)S(1)} %copy-done.3), channel_id=1, source_target_pairs={{0,24},{1,25},{2,26},{3,27},{4,28},{5,29},{6,30},{7,31},{8,0},{9,1... | collective-permute-start | bytes 1671176 | tf_op jit(solution)/shard_map/ppermute | solution.py:335
  36.5 68.9 %collective-permute-start.1 = (bf16[2176,128]{1,0:T(8,128)(2,1)}, bf16[2176,128]{1,0:T(8,128)(2,1)S(1)}, u32[]{:S(2)}, u32[]{:S(2)}) collective-permute-start(bf16[2176,128]{1,0:T(8,128)(2,1)} %get-tuple-element.26), channel_id=1, source_target_pairs={{0,1},{1,0},{2,3},{3,2},{4,5},{5,4},{6,7},{7,6},{8,9},{9,8},{10,11... | collective-permute-start | bytes 1671176 | tf_op jit(solution)/shard_map/ppermute | solution.py:331
  36.5 71.7 %collective-permute-start.2 = (bf16[2176,128]{1,0:T(8,128)(2,1)}, bf16[2176,128]{1,0:T(8,128)(2,1)S(1)}, u32[]{:S(2)}, u32[]{:S(2)}) collective-permute-start(bf16[2176,128]{1,0:T(8,128)(2,1)} %get-tuple-element.27), channel_id=1, source_target_pairs={{0,2},{1,3},{2,0},{3,1},{4,6},{5,7},{6,4},{7,5},{8,10},{9,11},{10,... | collective-permute-start | bytes 1671176 | tf_op jit(solution)/shard_map/ppermute | solution.py:331
  38.5 71.1 %collective-permute-start.3 = (bf16[2176,128]{1,0:T(8,128)(2,1)}, bf16[2176,128]{1,0:T(8,128)(2,1)S(1)}, u32[]{:S(2)}, u32[]{:S(2)}) collective-permute-start(bf16[2176,128]{1,0:T(8,128)(2,1)} %get-tuple-element.28), channel_id=1, source_target_pairs={{0,3},{1,2},{2,1},{3,0},{4,7},{5,6},{6,5},{7,4},{8,11},{9,10},{10,... | collective-permute-start | bytes 1671176 | tf_op jit(solution)/shard_map/ppermute | solution.py:331
  93.8 11.5 %copy-start.19 = (s32[4,2]{1,0:T(4,128)}, s32[4,2]{1,0:T(4,128)S(1)}, u32[]{:S(2)}) copy-start(s32[4,2]{1,0:T(4,128)S(1)} %get-tuple-element.56.refs_0_) | copy-start | bytes 100
  94.6 63.1 %collective-permute-start.9 = (bf16[2176,128]{1,0:T(8,128)(2,1)}, bf16[2176,128]{1,0:T(8,128)(2,1)}, u32[]{:S(2)}, u32[]{:S(2)}) collective-permute-start(bf16[2176,128]{1,0:T(8,128)(2,1)} %copy-done.6), channel_id=1, source_target_pairs={{0,25},{1,24},{2,27},{3,26},{4,29},{5,28},{6,31},{7,30},{8,1},{9,0... | collective-permute-start | bytes 1671176 | tf_op jit(solution)/shard_map/ppermute | solution.py:335
  105.4 54.8 %collective-permute-start.10 = (bf16[2176,128]{1,0:T(8,128)(2,1)S(1)}, bf16[2176,128]{1,0:T(8,128)(2,1)}, u32[]{:S(2)}, u32[]{:S(2)}) collective-permute-start(bf16[2176,128]{1,0:T(8,128)(2,1)S(1)} %copy-done.5), channel_id=1, source_target_pairs={{0,26},{1,27},{2,24},{3,25},{4,30},{5,31},{6,28},{7,29},{8,2},{9,3... | collective-permute-start | bytes 1671176 | tf_op jit(solution)/shard_map/ppermute | solution.py:335
  108.2 52.8 %collective-permute-start.11 = (bf16[2176,128]{1,0:T(8,128)(2,1)S(1)}, bf16[2176,128]{1,0:T(8,128)(2,1)}, u32[]{:S(2)}, u32[]{:S(2)}) collective-permute-start(bf16[2176,128]{1,0:T(8,128)(2,1)S(1)} %get-tuple-element.35), channel_id=1, source_target_pairs={{0,27},{1,26},{2,25},{3,24},{4,31},{5,30},{6,29},{7,28},{8,3},{9,2... | collective-permute-start | bytes 1671176 | tf_op jit(solution)/shard_map/ppermute | solution.py:335
  111.2 76.5 %all-to-all-start.1 = ((bf16[8,1536,128]{2,1,0:T(8,128)(2,1)}), bf16[8,1536,128]{2,1,0:T(8,128)(2,1)}, u32[]{:S(2)}, u32[]{:S(2)}) async-start(bf16[8,1536,128]{2,1,0:T(8,128)(2,1)} %shard_map.91), calls=%async_computation.1 | async-start | bytes 6291456 | tf_op jit(solution)/shard_map/all_to_all | solution.py:389
  155.0 66.8 %collective-permute-start.4 = (bf16[128,1024]{1,0:T(8,128)(2,1)}, bf16[128,1024]{1,0:T(8,128)(2,1)S(1)}, u32[]{:S(2)}, u32[]{:S(2)}) collective-permute-start(bf16[128,1024]{1,0:T(8,128)(2,1)} %get-tuple-element.29.refs_1_), channel_id=1, source_target_pairs={{0,24},{1,25},{2,26},{3,27},{4,28},{5,29},{6,30},{7,31},{8,0},{9,1... | collective-permute-start | bytes 786440 | tf_op jit(solution)/shard_map/ppermute | solution.py:335
  156.5 65.4 %collective-permute-start.5 = (bf16[128,1024]{1,0:T(8,128)(2,1)}, bf16[128,1024]{1,0:T(8,128)(2,1)S(1)}, u32[]{:S(2)}, u32[]{:S(2)}) collective-permute-start(bf16[128,1024]{1,0:T(8,128)(2,1)} %get-tuple-element.30), channel_id=1, source_target_pairs={{0,25},{1,24},{2,27},{3,26},{4,29},{5,28},{6,31},{7,30},{8,1},{9,0... | collective-permute-start | bytes 786440 | tf_op jit(solution)/shard_map/ppermute | solution.py:335
  157.8 64.1 %collective-permute-start.6 = (bf16[128,1024]{1,0:T(8,128)(2,1)}, bf16[128,1024]{1,0:T(8,128)(2,1)S(1)}, u32[]{:S(2)}, u32[]{:S(2)}) collective-permute-start(bf16[128,1024]{1,0:T(8,128)(2,1)} %get-tuple-element.31), channel_id=1, source_target_pairs={{0,26},{1,27},{2,24},{3,25},{4,30},{5,31},{6,28},{7,29},{8,2},{9,3... | collective-permute-start | bytes 786440 | tf_op jit(solution)/shard_map/ppermute | solution.py:335
  160.2 61.7 %collective-permute-start.7 = (bf16[128,1024]{1,0:T(8,128)(2,1)}, bf16[128,1024]{1,0:T(8,128)(2,1)S(1)}, u32[]{:S(2)}, u32[]{:S(2)}) collective-permute-start(bf16[128,1024]{1,0:T(8,128)(2,1)} %get-tuple-element.32), channel_id=1, source_target_pairs={{0,27},{1,26},{2,25},{3,24},{4,31},{5,30},{6,29},{7,28},{8,3},{9,2... | collective-permute-start | bytes 786440 | tf_op jit(solution)/shard_map/ppermute | solution.py:335
  188.4 35.7 %all-to-all-start.2 = ((bf16[8,512,128]{2,1,0:T(8,128)(2,1)}), bf16[8,512,128]{2,1,0:T(8,128)(2,1)S(1)}, u32[]{:S(2)}, u32[]{:S(2)}) async-start(bf16[8,512,128]{2,1,0:T(8,128)(2,1)} %shard_map.94), calls=%async_computation.2 | async-start | bytes 2097152 | tf_op jit(solution)/shard_map/all_to_all | solution.py:389
  234.6 13.0 %collective-permute-start.12 = (bf16[128,1024]{1,0:T(8,128)(2,1)}, bf16[128,1024]{1,0:T(8,128)(2,1)S(1)}, u32[]{:S(2)}, u32[]{:S(2)}) collective-permute-start(bf16[128,1024]{1,0:T(8,128)(2,1)} %get-tuple-element.37.refs_1_), channel_id=1, source_target_pairs={{0,2},{1,3},{2,0},{3,1},{4,6},{5,7},{6,4},{7,5},{8,10},{9,11},{10,... | collective-permute-start | bytes 786440 | tf_op jit(solution)/shard_map/ppermute | solution.py:331
  237.4 13.0 %collective-permute-start.13 = (bf16[128,1024]{1,0:T(8,128)(2,1)}, bf16[128,1024]{1,0:T(8,128)(2,1)S(1)}, u32[]{:S(2)}, u32[]{:S(2)}) collective-permute-start(bf16[128,1024]{1,0:T(8,128)(2,1)} %get-tuple-element.40), channel_id=1, source_target_pairs={{0,3},{1,2},{2,1},{3,0},{4,7},{5,6},{6,5},{7,4},{8,11},{9,10},{10,... | collective-permute-start | bytes 786440 | tf_op jit(solution)/shard_map/ppermute | solution.py:331
  251.8 1.7 collective-permute-start.14
  (16 other events, 21.9 us)

commit v18 on v15

--- a/solution.py
+++ b/solution.py
@@ -338,12 +338,7 @@
     cuts = [[(0, blocks)]] * (own - 1) + [[(0, cut), (cut, blocks)]]
 
     moved = own > 1
-    chosen = retrieved[0]
-    if moved:
-        chosen = delivered(chosen, 0)
-
-    def listed(i):
-        source = chosen if i == own - 1 else retrieved[0]
+    def listed(i, source):
         mine = lax.dynamic_index_in_dim(source, at * own + i, 0, keepdims=False)
         mine = jnp.stack(
             [lax.dynamic_index_in_dim(mine, home * group + (at ^ x), 0, keepdims=False) for x in range(group)]
@@ -388,7 +383,11 @@
             latest = lax.all_to_all(piece, "seq", split_axis=0, concat_axis=0, tiled=True)
             pieces.append(latest)
             held = packed
-        picks, starts = listed(i)
+        if i == own - 1 and moved:
+            chosen = delivered(after(retrieved[0], *opened), 0)
+        else:
+            chosen, opened = retrieved[0], [latest, *packed[1:]]
+        picks, starts = listed(i, chosen)
         run = functools.partial(attend, picks=picks, heads=heads, dim=dim, scale=scale)
         acc = None
         for j in range(len(pieces) - 1):

time: 262 us -> 263 us (level)
    ppermute x6, waiting for transfers between devices: 13.7 us -> 65.6 us  [swapped(): return lax.ppermute(value, 'seq', [(p, p ^ step) for p in range(seq)])]
    ppermute x10, waiting for transfers between devices: 48 us -> 6.05 us  [delivered(): return lax.ppermute(value, ('section', 'seq'), pairs)]
    all_to_all x3, waiting for transfers between devices: 27 us -> 18.2 us  [shards(): lax.all_to_all(piece, 'seq', split_axis=0, concat_axis=0, tiled=True)]
    unnamed x48 -> x49, local copies, waits for them, and re-layouts: 9.75 us -> 8.88 us
    pallas_call x8 -> x9, Pallas kernels: 6.15 us -> 6.74 us  [after(): pl.pallas_call(lambda *refs: None, out_shape=jax.ShapeDtypeStruct(value.s...]
  transfers between devices with their start and end apart: 19 -> 19, of which waited for: 6 -> 8; matrix products, arithmetic and copies ran while one was open for 2% -> 2% of each run, Pallas kernels for 38% -> 38%
where the time goes in v18:
time: 263 us; the launch traced here: 261 us
  Pallas kernels  121 us (46%)
  waiting for transfers between devices  89.9 us (34%)
  starting transfers between devices  37.6 us (14%)
  local copies, waits for them, and re-layouts  9.75 us (4%)
  other arithmetic  2.69 us (1%)
    pallas_call x4, Pallas kernels, attend(): pl.pallas_call(functools.partial(attend_kernel, heads, dim, rows, scale,...  81.8 us
    ppermute x6, waiting for transfers between devices, swapped(): return lax.ppermute(value, 'seq', [(p, p ^ step) for p in range(seq)])  65.6 us
    all_to_all x3, waiting for transfers between devices, shards(): lax.all_to_all(piece, 'seq', split_axis=0, concat_axis=0, tiled=True)  18.2 us
    ppermute x10, starting transfers between devices, delivered(): return lax.ppermute(value, ('section', 'seq'), pairs)  18 us
    all_to_all x3, starting transfers between devices, shards(): lax.all_to_all(piece, 'seq', split_axis=0, concat_axis=0, tiled=True)  15.3 us
    pallas_call x2, Pallas kernels, pack(): pl.pallas_call(functools.partial(pack_kernel, own, group, index, spans, w...  13.1 us
    pallas_call x2, Pallas kernels, prepare(): pl.pallas_call(functools.partial(prepare_kernel, heads, dim, scale, own,...  9.01 us
    unnamed x49, local copies, waits for them, and re-layouts  8.88 us
  transfers between devices with their start and end apart: 19, of which 8 were waited for; matrix products, arithmetic and copies ran while one was open for 2% of the time, Pallas kernels for 38%

profile of v18, /device:TPU:0, one launch (start us, length us, event | category | flops | bytes accessed | tf_op | source)
XLA Modules:
  0.0 261.3 jit_solution(1656569182649405654)
XLA Ops:
  0.8 6.7 %shard_map.88 = bf16[8,2,1024,128]{3,2,1,0:T(8,128)(2,1)} custom-call(bf16[1024,1024]{1,0:T(8,128)(2,1)} %bitcast.43, bf16[1024,1024]{1,0:T(8,128)(2,1)} %bitcast.45), custom_call_target="tpu_custom_call" | custom-call | bytes 4194304 | tf_op jit(solution)/shard_map/pallas_call | solution.py:84
  7.5 6.5 %all-to-all-start = ((bf16[8,2048,128]{2,1,0:T(8,128)(2,1)}), bf16[8,2048,128]{2,1,0:T(8,128)(2,1)}, u32[]{:S(2)}, u32[]{:S(2)}) async-start(bf16[8,2048,128]{2,1,0:T(8,128)(2,1)} %bitcast.42), calls=%async_computation | async-start | bytes 8388608 | tf_op jit(solution)/shard_map/all_to_all | solution.py:383
  14.1 4.0 %shard_map.82 = (bf16[2176,128]{1,0:T(8,128)(2,1)S(1)}, bf16[2176,128]{1,0:T(8,128)(2,1)S(1)}, bf16[2176,128]{1,0:T(8,128)(2,1)S(1)}, bf16[2176,128]{1,0:T(8,128)(2,1)S(1)}) custom-call(f32[64]{0:T(128)S(1)} %divide_bitcast_fusion.gate_ref, s32[1]{0:T(128)} %bitcast.at_ref, bf16[128,8192]{1,0:T(8,128)(2,1)S(1)} %bitcast.36, bf16[128,8192]{1,0:T(8,128)(2,1)} %bitcast.47, ...), custom_call_target="tpu_custom_call" | custom-call | flops 4194304 | bytes 6291456 | tf_op jit(solution)/shard_map/pallas_call | solution.py:130
  21.8 6.8 %shard_map.84 = bf16[2,4,1024,128]{3,2,1,0:T(8,128)(2,1)} custom-call(s32[1]{0:T(128)} %shard_map.83.at_ref, bf16[1024,1024]{1,0:T(8,128)(2,1)} %bitcast.44, bf16[1024,1024]{1,0:T(8,128)(2,1)} %bitcast.46), custom_call_target="tpu_custom_call" | custom-call | bytes 3145728 | tf_op jit(solution)/shard_map/pallas_call | solution.py:42
  28.6 2.4 collective-permute-start
  31.1 5.0 %shard_map.87 = (bf16[2176,128]{1,0:T(8,128)(2,1)S(1)}, bf16[2176,128]{1,0:T(8,128)(2,1)}, bf16[2176,128]{1,0:T(8,128)(2,1)}, bf16[2176,128]{1,0:T(8,128)(2,1)}) custom-call(f32[64]{0:T(128)S(1)} %divide_bitcast_fusion.gate_ref, s32[1]{0:T(128)} %bitcast.at_ref, bf16[128,8192]{1,0:T(8,128)(2,1)S(1)} %bitcast.37, bf16[128,8192]{1,0:T(8,128)(2,1)} %bitcast.48, ...), custom_call_target="tpu_custom_call" | custom-call | flops 4194304 | bytes 6291456 | tf_op jit(solution)/shard_map/pallas_call | solution.py:130
  37.1 1.8 collective-permute-start.2
  40.7 54.1 %collective-permute-done.2.refs_2_.refs_3_.refs_4_ = bf16[2176,128]{1,0:T(8,128)(2,1)S(1)} collective-permute-done((bf16[2176,128]{1,0:T(8,128)(2,1)}, bf16[2176,128]{1,0:T(8,128)(2,1)S(1)}, u32[]{:S(2)}, u32[]{:S(2)}) %collective-permute-start.2) | collective-permute-done | bytes 557088 | tf_op jit(solution)/shard_map/ppermute | solution.py:331
  94.8 4.3 %collective-permute-start.11 = (bf16[2176,128]{1,0:T(8,128)(2,1)}, bf16[2176,128]{1,0:T(8,128)(2,1)}, u32[]{:S(2)}, u32[]{:S(2)}) collective-permute-start(bf16[2176,128]{1,0:T(8,128)(2,1)} %copy-done.4), channel_id=1, source_target_pairs={{0,26},{1,27},{2,24},{3,25},{4,30},{5,31},{6,28},{7,29},{8,2},{9,3... | collective-permute-start | bytes 1671176 | tf_op jit(solution)/shard_map/ppermute | solution.py:335
  99.0 7.7 %collective-permute-done.3.refs_3_.refs_4_.refs_5_ = bf16[2176,128]{1,0:T(8,128)(2,1)S(1)} collective-permute-done((bf16[2176,128]{1,0:T(8,128)(2,1)}, bf16[2176,128]{1,0:T(8,128)(2,1)S(1)}, u32[]{:S(2)}, u32[]{:S(2)}) %collective-permute-start.3) | collective-permute-done | bytes 557088 | tf_op jit(solution)/shard_map/ppermute | solution.py:331
  108.9 2.4 collective-permute-start.8
  112.4 6.4 %shard_map.85 = (bf16[8,2,640,128]{3,2,1,0:T(8,128)(2,1)}, bf16[8,2,384,128]{3,2,1,0:T(8,128)(2,1)}) custom-call(bf16[2,4,1024,128]{3,2,1,0:T(8,128)(2,1)} %collective-permute-done.refs_0_), custom_call_target="tpu_custom_call" | custom-call | bytes 4194304 | tf_op jit(solution)/shard_map/pallas_call | solution.py:84
  120.7 5.1 %all-to-all-start.1 = ((bf16[8,1280,128]{2,1,0:T(8,128)(2,1)}), bf16[8,1280,128]{2,1,0:T(8,128)(2,1)}, u32[]{:S(2)}, u32[]{:S(2)}) async-start(bf16[8,1280,128]{2,1,0:T(8,128)(2,1)} %shard_map.92), calls=%async_computation.1 | async-start | bytes 5242880 | tf_op jit(solution)/shard_map/all_to_all | solution.py:383
  125.8 6.0 %collective-permute-done.8 = s32[8,8,32]{2,1,0:T(8,128)S(1)} collective-permute-done((s32[8,8,32]{2,1,0:T(8,128)}, s32[8,8,32]{2,1,0:T(8,128)S(1)}, u32[]{:S(2)}, u32[]{:S(2)}) %collective-permute-start.8) | collective-permute-done | bytes 8224 | tf_op jit(solution)/shard_map/ppermute | solution.py:335
  132.9 36.1 %shard_map.89 = (bf16[128,1024]{1,0:T(8,128)(2,1)}, bf16[128,1024]{1,0:T(8,128)(2,1)}, bf16[128,1024]{1,0:T(8,128)(2,1)}, bf16[128,1024]{1,0:T(8,128)(2,1)}) custom-call(s32[4,32]{1,0:T(4,128)} %select_reduce_fusion.1.picks_ref, s32[4,2]{1,0:T(4,128)} %shard_map.86.starts_ref, bf16[2176,128]{1,0:T(8,128)(2,1)} %copy-done.1, bf16[2176,128]{1,0:T(8,128)(2,1)} %copy-done.6, ...), custom_call_target="tpu_custom_call" | custom-call | flops 51539607552 | tf_op jit(solution)/shard_map/pallas_call | solution.py:253
  173.3 4.6 %collective-permute-start.6 = (bf16[128,1024]{1,0:T(8,128)(2,1)}, bf16[128,1024]{1,0:T(8,128)(2,1)S(1)}, u32[]{:S(2)}, u32[]{:S(2)}) collective-permute-start(bf16[128,1024]{1,0:T(8,128)(2,1)} %get-tuple-element.31), channel_id=1, source_target_pairs={{0,26},{1,27},{2,24},{3,25},{4,30},{5,31},{6,28},{7,29},{8,2},{9,3... | collective-permute-start | bytes 786440 | tf_op jit(solution)/shard_map/ppermute | solution.py:335
  178.4 7.9 %all-to-all-done.1.refs_1_ = bf16[8,1280,128]{2,1,0:T(8,128)(2,1)} async-done(((bf16[8,1280,128]{2,1,0:T(8,128)(2,1)}), bf16[8,1280,128]{2,1,0:T(8,128)(2,1)}, u32[]{:S(2)}, u32[]{:S(2)}) %all-to-all-start.1) | async-done | bytes 2621472 | tf_op jit(solution)/shard_map/all_to_all | solution.py:383
  187.0 3.8 %all-to-all-start.2 = ((bf16[8,768,128]{2,1,0:T(8,128)(2,1)}), bf16[8,768,128]{2,1,0:T(8,128)(2,1)S(1)}, u32[]{:S(2)}, u32[]{:S(2)}) async-start(bf16[8,768,128]{2,1,0:T(8,128)(2,1)} %shard_map.95), calls=%async_computation.2 | async-start | bytes 3145728 | tf_op jit(solution)/shard_map/all_to_all | solution.py:383
  190.7 26.4 %shard_map.93.refs_1_.refs_3_ = f32[4,1024,128]{2,1,0:T(8,128)} custom-call(s32[4,32]{1,0:T(4,128)} %select_reduce_fusion.picks_ref, s32[4,2]{1,0:T(4,128)} %shard_map.91.starts_ref, bf16[2176,128]{1,0:T(8,128)(2,1)} %copy-done.16, bf16[2176,128]{1,0:T(8,128)(2,1)} %collective-permute-done.10.refs_1_.refs_3_, ...), custom_call_target="tpu_custom_call" | custom-call | flops 32212254720 | tf_op jit(solution)/shard_map/pallas_call | solution.py:253
  219.5 8.8 %all-to-all-done.2 = bf16[8,768,128]{2,1,0:T(8,128)(2,1)S(1)} async-done(((bf16[8,768,128]{2,1,0:T(8,128)(2,1)}), bf16[8,768,128]{2,1,0:T(8,128)(2,1)S(1)}, u32[]{:S(2)}, u32[]{:S(2)}) %all-to-all-start.2) | async-done | bytes 1572896 | tf_op jit(solution)/shard_map/all_to_all | solution.py:383
  229.5 10.3 %shard_map.96 = (bf16[128,1024]{1,0:T(8,128)(2,1)}, bf16[128,1024]{1,0:T(8,128)(2,1)}) custom-call(s32[4,32]{1,0:T(4,128)} %select_reduce_fusion.picks_ref, s32[4,2]{1,0:T(4,128)} %shard_map.94.starts_ref, bf16[2176,128]{1,0:T(8,128)(2,1)} %collective-permute-done.11.refs_2_.refs_4_.refs_0_, bf16[2176,128]{1,0:T(8,128)(2,1)} %copy-done.17, ...), custom_call_target="tpu_custom_call" | custom-call | flops 9663676416 | tf_op jit(solution)/shard_map/pallas_call | solution.py:253
  241.6 9.0 %shard_map.98 = (bf16[128,1024]{1,0:T(8,128)(2,1)}, bf16[128,1024]{1,0:T(8,128)(2,1)}) custom-call(s32[4,32]{1,0:T(4,128)} %select_reduce_fusion.picks_ref, s32[4,2]{1,0:T(4,128)} %shard_map.97.starts_ref, bf16[2176,128]{1,0:T(8,128)(2,1)} %copy-done.16, bf16[2176,128]{1,0:T(8,128)(2,1)} %collective-permute-done.10.refs_1_.refs_3_, ...), custom_call_target="tpu_custom_call" | custom-call | flops 9663676416 | tf_op jit(solution)/shard_map/pallas_call | solution.py:253
  250.6 2.5 collective-permute-done.14.refs_2_.refs_7_
  257.5 3.8 %shard_map.100 = bf16[128,8192]{1,0:T(8,128)(2,1)} custom-call(s32[1]{0:T(128)} %bitcast.at_ref, bf16[128,1024]{1,0:T(8,128)(2,1)} %copy-done.10, bf16[128,1024]{1,0:T(8,128)(2,1)} %copy-done.11, bf16[128,1024]{1,0:T(8,128)(2,1)} %copy-done.12, bf16[128,1024]{1,0:T(8,128)(2,1)} %copy-done.13, bf16[128,1024]{1,0:T(8,128)(2,1)} %get-tuple-element.38.refs_4_, ...), custom_call_target="tpu_custom_call" | custom-call | bytes 4194304 | tf_op jit(solution)/shard_map/pallas_call | solution.py:283
  (97 shorter events, 28.8 us)
Async XLA Ops:
  0.8 38.9 %copy-start.19 = (s32[1,8,8,32]{3,2,1,0:T(8,128)}, s32[1,8,8,32]{3,2,1,0:T(8,128)S(1)}, u32[]{:S(2)}) copy-start(s32[1,8,8,32]{3,2,1,0:T(8,128)S(1)} %copy.38) | copy-start | bytes 24580
  7.5 100.7 %all-to-all-start = ((bf16[8,2048,128]{2,1,0:T(8,128)(2,1)}), bf16[8,2048,128]{2,1,0:T(8,128)(2,1)}, u32[]{:S(2)}, u32[]{:S(2)}) async-start(bf16[8,2048,128]{2,1,0:T(8,128)(2,1)} %bitcast.42), calls=%async_computation | async-start | bytes 8388608 | tf_op jit(solution)/shard_map/all_to_all | solution.py:383
  28.6 10.5 %copy-start.3 = (bf16[2176,128]{1,0:T(8,128)(2,1)S(1)}, bf16[2176,128]{1,0:T(8,128)(2,1)}, u32[]{:S(2)}) copy-start(bf16[2176,128]{1,0:T(8,128)(2,1)} %copy-done.2) | copy-start | bytes 1671172
  28.6 82.7 %collective-permute-start = (bf16[2,4,1024,128]{3,2,1,0:T(8,128)(2,1)}, bf16[2,4,1024,128]{3,2,1,0:T(8,128)(2,1)}, u32[]{:S(2)}, u32[]{:S(2)}) collective-permute-start(bf16[2,4,1024,128]{3,2,1,0:T(8,128)(2,1)} %shard_map.84), channel_id=1, source_target_pairs={{0,24},{1,25},{2,26},{3,27},{4,28},{5,29},{6,30},{7,31},{8,0},{9,1... | collective-permute-start | bytes 6291464 | tf_op jit(solution)/shard_map/ppermute | solution.py:335
  36.9 2.7 %collective-permute-start.1 = (bf16[2176,128]{1,0:T(8,128)(2,1)}, bf16[2176,128]{1,0:T(8,128)(2,1)S(1)}, u32[]{:S(2)}, u32[]{:S(2)}) collective-permute-start(bf16[2176,128]{1,0:T(8,128)(2,1)} %get-tuple-element.26), channel_id=1, source_target_pairs={{0,1},{1,0},{2,3},{3,2},{4,5},{5,4},{6,7},{7,6},{8,9},{9,8},{10,11... | collective-permute-start | bytes 1671176 | tf_op jit(solution)/shard_map/ppermute | solution.py:331
  37.1 57.6 %collective-permute-start.2 = (bf16[2176,128]{1,0:T(8,128)(2,1)}, bf16[2176,128]{1,0:T(8,128)(2,1)S(1)}, u32[]{:S(2)}, u32[]{:S(2)}) collective-permute-start(bf16[2176,128]{1,0:T(8,128)(2,1)} %get-tuple-element.27), channel_id=1, source_target_pairs={{0,2},{1,3},{2,0},{3,1},{4,6},{5,7},{6,4},{7,5},{8,10},{9,11},{10,... | collective-permute-start | bytes 1671176 | tf_op jit(solution)/shard_map/ppermute | solution.py:331
  38.9 67.8 %collective-permute-start.3 = (bf16[2176,128]{1,0:T(8,128)(2,1)}, bf16[2176,128]{1,0:T(8,128)(2,1)S(1)}, u32[]{:S(2)}, u32[]{:S(2)}) collective-permute-start(bf16[2176,128]{1,0:T(8,128)(2,1)} %get-tuple-element.28), channel_id=1, source_target_pairs={{0,3},{1,2},{2,1},{3,0},{4,7},{5,6},{6,5},{7,4},{8,11},{9,10},{10,... | collective-permute-start | bytes 1671176 | tf_op jit(solution)/shard_map/ppermute | solution.py:331
  39.1 134.2 %collective-permute-start.9 = (bf16[2176,128]{1,0:T(8,128)(2,1)S(1)}, bf16[2176,128]{1,0:T(8,128)(2,1)S(1)}, u32[]{:S(2)}, u32[]{:S(2)}) collective-permute-start(bf16[2176,128]{1,0:T(8,128)(2,1)S(1)} %copy-done.3), channel_id=1, source_target_pairs={{0,24},{1,25},{2,26},{3,27},{4,28},{5,29},{6,30},{7,31},{8,0},{9,1... | collective-permute-start | bytes 1671176 | tf_op jit(solution)/shard_map/ppermute | solution.py:335
  39.6 68.5 %copy-start.6 = (bf16[2176,128]{1,0:T(8,128)(2,1)}, bf16[2176,128]{1,0:T(8,128)(2,1)S(1)}, u32[]{:S(2)}) copy-start(bf16[2176,128]{1,0:T(8,128)(2,1)S(1)} %collective-permute-done.1.refs_1_.refs_2_.refs_3_) | copy-start | bytes 1671172
  39.6 133.6 %collective-permute-start.10 = (bf16[2176,128]{1,0:T(8,128)(2,1)}, bf16[2176,128]{1,0:T(8,128)(2,1)}, u32[]{:S(2)}, u32[]{:S(2)}) collective-permute-start(bf16[2176,128]{1,0:T(8,128)(2,1)} %copy-done.5), channel_id=1, source_target_pairs={{0,25},{1,24},{2,27},{3,26},{4,29},{5,28},{6,31},{7,30},{8,1},{9,0... | collective-permute-start | bytes 1671176 | tf_op jit(solution)/shard_map/ppermute | solution.py:335
  94.8 13.4 %copy-start.7 = (bf16[2176,128]{1,0:T(8,128)(2,1)}, bf16[2176,128]{1,0:T(8,128)(2,1)S(1)}, u32[]{:S(2)}) copy-start(bf16[2176,128]{1,0:T(8,128)(2,1)S(1)} %collective-permute-done.2.refs_2_.refs_3_.refs_4_) | copy-start | bytes 1671172
  94.8 83.2 %collective-permute-start.11 = (bf16[2176,128]{1,0:T(8,128)(2,1)}, bf16[2176,128]{1,0:T(8,128)(2,1)}, u32[]{:S(2)}, u32[]{:S(2)}) collective-permute-start(bf16[2176,128]{1,0:T(8,128)(2,1)} %copy-done.4), channel_id=1, source_target_pairs={{0,26},{1,27},{2,24},{3,25},{4,30},{5,31},{6,28},{7,29},{8,2},{9,3... | collective-permute-start | bytes 1671176 | tf_op jit(solution)/shard_map/ppermute | solution.py:335
  108.9 22.9 %collective-permute-start.8 = (s32[8,8,32]{2,1,0:T(8,128)}, s32[8,8,32]{2,1,0:T(8,128)S(1)}, u32[]{:S(2)}, u32[]{:S(2)}) collective-permute-start(s32[8,8,32]{2,1,0:T(8,128)} %shard_map.90), channel_id=1, source_target_pairs={{0,24},{1,25},{2,26},{3,27},{4,28},{5,29},{6,30},{7,31},{8,0},{9,1... | collective-permute-start | bytes 24584 | tf_op jit(solution)/shard_map/ppermute | solution.py:335
  111.3 67.0 %collective-permute-start.12 = (bf16[2176,128]{1,0:T(8,128)(2,1)S(1)}, bf16[2176,128]{1,0:T(8,128)(2,1)S(1)}, u32[]{:S(2)}, u32[]{:S(2)}) collective-permute-start(bf16[2176,128]{1,0:T(8,128)(2,1)S(1)} %get-tuple-element.35), channel_id=1, source_target_pairs={{0,27},{1,26},{2,25},{3,24},{4,31},{5,30},{6,29},{7,28},{8,3},{9,2... | collective-permute-start | bytes 1671176 | tf_op jit(solution)/shard_map/ppermute | solution.py:335
  120.7 65.6 %all-to-all-start.1 = ((bf16[8,1280,128]{2,1,0:T(8,128)(2,1)}), bf16[8,1280,128]{2,1,0:T(8,128)(2,1)}, u32[]{:S(2)}, u32[]{:S(2)}) async-start(bf16[8,1280,128]{2,1,0:T(8,128)(2,1)} %shard_map.92), calls=%async_computation.1 | async-start | bytes 5242880 | tf_op jit(solution)/shard_map/all_to_all | solution.py:383
  169.0 48.1 %collective-permute-start.4 = (bf16[128,1024]{1,0:T(8,128)(2,1)}, bf16[128,1024]{1,0:T(8,128)(2,1)S(1)}, u32[]{:S(2)}, u32[]{:S(2)}) collective-permute-start(bf16[128,1024]{1,0:T(8,128)(2,1)} %get-tuple-element.29.refs_1_), channel_id=1, source_target_pairs={{0,24},{1,25},{2,26},{3,27},{4,28},{5,29},{6,30},{7,31},{8,0},{9,1... | collective-permute-start | bytes 786440 | tf_op jit(solution)/shard_map/ppermute | solution.py:335
  171.1 15.8 %copy-start.20 = (s32[4,2]{1,0:T(4,128)}, s32[4,2]{1,0:T(4,128)S(1)}, u32[]{:S(2)}) copy-start(s32[4,2]{1,0:T(4,128)S(1)} %get-tuple-element.56.refs_0_) | copy-start | bytes 100
  173.3 43.9 %collective-permute-start.5 = (bf16[128,1024]{1,0:T(8,128)(2,1)}, bf16[128,1024]{1,0:T(8,128)(2,1)S(1)}, u32[]{:S(2)}, u32[]{:S(2)}) collective-permute-start(bf16[128,1024]{1,0:T(8,128)(2,1)} %get-tuple-element.30), channel_id=1, source_target_pairs={{0,25},{1,24},{2,27},{3,26},{4,29},{5,28},{6,31},{7,30},{8,1},{9,0... | collective-permute-start | bytes 786440 | tf_op jit(solution)/shard_map/ppermute | solution.py:335
  173.3 43.9 %collective-permute-start.6 = (bf16[128,1024]{1,0:T(8,128)(2,1)}, bf16[128,1024]{1,0:T(8,128)(2,1)S(1)}, u32[]{:S(2)}, u32[]{:S(2)}) collective-permute-start(bf16[128,1024]{1,0:T(8,128)(2,1)} %get-tuple-element.31), channel_id=1, source_target_pairs={{0,26},{1,27},{2,24},{3,25},{4,30},{5,31},{6,28},{7,29},{8,2},{9,3... | collective-permute-start | bytes 786440 | tf_op jit(solution)/shard_map/ppermute | solution.py:335
  177.9 39.2 %collective-permute-start.7 = (bf16[128,1024]{1,0:T(8,128)(2,1)}, bf16[128,1024]{1,0:T(8,128)(2,1)S(1)}, u32[]{:S(2)}, u32[]{:S(2)}) collective-permute-start(bf16[128,1024]{1,0:T(8,128)(2,1)} %get-tuple-element.32), channel_id=1, source_target_pairs={{0,27},{1,26},{2,25},{3,24},{4,31},{5,30},{6,29},{7,28},{8,3},{9,2... | collective-permute-start | bytes 786440 | tf_op jit(solution)/shard_map/ppermute | solution.py:335
  187.0 41.3 %all-to-all-start.2 = ((bf16[8,768,128]{2,1,0:T(8,128)(2,1)}), bf16[8,768,128]{2,1,0:T(8,128)(2,1)S(1)}, u32[]{:S(2)}, u32[]{:S(2)}) async-start(bf16[8,768,128]{2,1,0:T(8,128)(2,1)} %shard_map.95), calls=%async_computation.2 | async-start | bytes 3145728 | tf_op jit(solution)/shard_map/all_to_all | solution.py:383
  240.4 10.2 %collective-permute-start.13 = (bf16[128,1024]{1,0:T(8,128)(2,1)}, bf16[128,1024]{1,0:T(8,128)(2,1)S(1)}, u32[]{:S(2)}, u32[]{:S(2)}) collective-permute-start(bf16[128,1024]{1,0:T(8,128)(2,1)} %get-tuple-element.37.refs_1_), channel_id=1, source_target_pairs={{0,2},{1,3},{2,0},{3,1},{4,6},{5,7},{6,4},{7,5},{8,10},{9,11},{10,... | collective-permute-start | bytes 786440 | tf_op jit(solution)/shard_map/ppermute | solution.py:331
  240.4 12.6 %collective-permute-start.14 = (bf16[128,1024]{1,0:T(8,128)(2,1)}, bf16[128,1024]{1,0:T(8,128)(2,1)S(1)}, u32[]{:S(2)}, u32[]{:S(2)}) collective-permute-start(bf16[128,1024]{1,0:T(8,128)(2,1)} %get-tuple-element.40), channel_id=1, source_target_pairs={{0,3},{1,2},{2,1},{3,0},{4,7},{5,6},{6,5},{7,4},{8,11},{9,10},{10,... | collective-permute-start | bytes 786440 | tf_op jit(solution)/shard_map/ppermute | solution.py:331
  254.4 2.4 collective-permute-start.15
  (18 other events, 45.2 us)

commit v19 on v16

--- a/solution.py
+++ b/solution.py
@@ -118,14 +118,14 @@
             delta = jnp.sum(product, axis=1, keepdims=True)
             for part, term in enumerate(split_parts(delta)):
                 stats = jnp.where(lane == 2 * part * heads + h, term, stats)
-        packed_ref[2 * heads * rows:, :] = stats.astype(jnp.bfloat16)
+        packed_ref[2 * heads * rows:, :] = stats.T[:2 * PARTS * heads].astype(jnp.bfloat16)
 
 
 def prepare(grad_out, queries, mem_out, row_total, gates, at, kv_heads, dim, scale, own, index):
     rows, width = grad_out.shape
     heads = width // dim // kv_heads
     group = kv_heads // own
-    span = 2 * heads * rows + rows
+    span = 2 * heads * (rows + PARTS)
     wide = pl.BlockSpec((rows, width), lambda i, *_: (0, 0))
     return pl.pallas_call(
         functools.partial(prepare_kernel, heads, dim, scale, own, index),
@@ -162,6 +162,7 @@
             query_ref[...] = packed[...]
 
     terms = query_ref[2 * count:, :].astype(jnp.float32)
+    terms = jnp.concatenate([terms, jnp.zeros((dim - terms.shape[0], rows), jnp.float32)], axis=0).T
     stats = terms
     for part in range(1, PARTS):
         stats = stats + pltpu.roll(terms, dim - 2 * part * heads, 1)
@@ -237,7 +238,7 @@
 def attend(packed, memory, acc, picks, starts, heads, dim, scale, last, first=0):
     tiles = len(packed)
     span = packed[0].shape[0]
-    rows = span // (2 * heads + 1)
+    rows = span // (2 * heads) - PARTS
     fresh = acc is None
     width = heads * rows
     holders = memory.shape[0]

time: 253 us -> 253 us (level)
  Pallas kernels: 121 us -> 126 us
    pallas_call x4, Pallas kernels: 82.7 us -> 86.8 us  [attend(): pl.pallas_call(functools.partial(attend_kernel, heads, dim, rows, scale,...]
  transfers between devices with their start and end apart: 18 -> 18, of which waited for: 4 -> 3; matrix products, arithmetic and copies ran while one was open for 2% -> 2% of each run, Pallas kernels for 40% -> 40%
where the time goes in v19:
time: 253 us
  Pallas kernels  126 us (50%)
  blocking collectives  53.3 us (21%)
  starting transfers between devices  33.3 us (13%)
  waiting for transfers between devices  27.9 us (11%)
  local copies, waits for them, and re-layouts  9.92 us (4%)
  other arithmetic  2.73 us (1%)
    pallas_call x4, Pallas kernels, attend(): pl.pallas_call(functools.partial(attend_kernel, heads, dim, rows, scale,...  86.8 us
    all_gather x1, blocking collectives, shards(): of_all = lax.all_gather(chosen, 'section')  53.3 us
    all_to_all x3, waiting for transfers between devices, shards(): lax.all_to_all(piece, 'seq', split_axis=0, concat_axis=0, tiled=True)  26.5 us
    all_to_all x3, starting transfers between devices, shards(): lax.all_to_all(piece, 'seq', split_axis=0, concat_axis=0, tiled=True)  16 us
    pallas_call x2, Pallas kernels, pack(): pl.pallas_call(functools.partial(pack_kernel, own, group, index, spans, w...  13.1 us
    ppermute x9, starting transfers between devices, delivered(): return lax.ppermute(value, ('section', 'seq'), pairs)  13 us
    pallas_call x2, Pallas kernels, prepare(): pl.pallas_call(functools.partial(prepare_kernel, heads, dim, scale, own,...  9.35 us
    unnamed x46, local copies, waits for them, and re-layouts  9.03 us
  transfers between devices with their start and end apart: 18, of which 3 were waited for; matrix products, arithmetic and copies ran while one was open for 2% of the time, Pallas kernels for 40%

profile of v19, /device:TPU:0, one launch (start us, length us, event | category | flops | bytes accessed | tf_op | source)
XLA Modules:
  0.0 253.2 jit_solution(8453312500685335384)
XLA Ops:
  0.0 6.7 %shard_map.88 = bf16[8,2,1024,128]{3,2,1,0:T(8,128)(2,1)} custom-call(bf16[1024,1024]{1,0:T(8,128)(2,1)} %bitcast.42, bf16[1024,1024]{1,0:T(8,128)(2,1)} %bitcast.44), custom_call_target="tpu_custom_call" | custom-call | bytes 4194304 | tf_op jit(solution)/shard_map/pallas_call | solution.py:84
  6.7 6.5 %all-to-all-start = ((bf16[8,2048,128]{2,1,0:T(8,128)(2,1)}), bf16[8,2048,128]{2,1,0:T(8,128)(2,1)}, u32[]{:S(2)}, u32[]{:S(2)}) async-start(bf16[8,2048,128]{2,1,0:T(8,128)(2,1)} %bitcast.41), calls=%async_computation | async-start | bytes 8388608 | tf_op jit(solution)/shard_map/all_to_all | solution.py:390
  13.3 4.2 %shard_map.82 = (bf16[2096,128]{1,0:T(8,128)(2,1)S(1)}, bf16[2096,128]{1,0:T(8,128)(2,1)S(1)}, bf16[2096,128]{1,0:T(8,128)(2,1)S(1)}, bf16[2096,128]{1,0:T(8,128)(2,1)S(1)}) custom-call(f32[64]{0:T(128)S(1)} %divide_bitcast_fusion.gate_ref, s32[1]{0:T(128)} %bitcast.at_ref, bf16[128,8192]{1,0:T(8,128)(2,1)S(1)} %bitcast.35, bf16[128,8192]{1,0:T(8,128)(2,1)} %bitcast.46, ...), custom_call_target="tpu_custom_call" | custom-call | flops 4194304 | bytes 6291456 | tf_op jit(solution)/shard_map/pallas_call | solution.py:130
  19.9 1.2 shard_map.83.at_ref
  21.1 6.8 %shard_map.84 = bf16[2,4,1024,128]{3,2,1,0:T(8,128)(2,1)} custom-call(s32[1]{0:T(128)} %shard_map.83.at_ref, bf16[1024,1024]{1,0:T(8,128)(2,1)} %bitcast.43, bf16[1024,1024]{1,0:T(8,128)(2,1)} %bitcast.45), custom_call_target="tpu_custom_call" | custom-call | bytes 3145728 | tf_op jit(solution)/shard_map/pallas_call | solution.py:42
  27.9 2.4 collective-permute-start
  30.9 5.2 %shard_map.87 = (bf16[2096,128]{1,0:T(8,128)(2,1)S(1)}, bf16[2096,128]{1,0:T(8,128)(2,1)}, bf16[2096,128]{1,0:T(8,128)(2,1)}, bf16[2096,128]{1,0:T(8,128)(2,1)}) custom-call(f32[64]{0:T(128)S(1)} %divide_bitcast_fusion.gate_ref, s32[1]{0:T(128)} %bitcast.at_ref, bf16[128,8192]{1,0:T(8,128)(2,1)S(1)} %bitcast.36, bf16[128,8192]{1,0:T(8,128)(2,1)} %bitcast.47, ...), custom_call_target="tpu_custom_call" | custom-call | flops 4194304 | bytes 6291456 | tf_op jit(solution)/shard_map/pallas_call | solution.py:130
  36.9 2.0 collective-permute-start.2
  39.1 53.3 %all_gather.3 = s32[4,8,8,32]{3,2,1,0:T(8,128)S(1)} all-gather(s32[1,8,8,32]{3,2,1,0:T(8,128)S(1)} %copy-done.18), channel_id=1, replica_groups=mesh['section'=4,'seq'=8] {'section'}, dimensions={0}, use_global_device_ids=true | all-gather | bytes 40960 | tf_op jit(solution)/shard_map/all_gather | solution.py:344
  96.5 6.4 %shard_map.85 = (bf16[8,2,640,128]{3,2,1,0:T(8,128)(2,1)}, bf16[8,2,384,128]{3,2,1,0:T(8,128)(2,1)}) custom-call(bf16[2,4,1024,128]{3,2,1,0:T(8,128)(2,1)} %collective-permute-done.refs_0_), custom_call_target="tpu_custom_call" | custom-call | bytes 4194304 | tf_op jit(solution)/shard_map/pallas_call | solution.py:84
  104.2 2.8 %collective-permute-start.10 = (bf16[2096,128]{1,0:T(8,128)(2,1)S(1)}, bf16[2096,128]{1,0:T(8,128)(2,1)}, u32[]{:S(2)}, u32[]{:S(2)}) collective-permute-start(bf16[2096,128]{1,0:T(8,128)(2,1)S(1)} %copy-done.5), channel_id=1, source_target_pairs={{0,26},{1,27},{2,24},{3,25},{4,30},{5,31},{6,28},{7,29},{8,2},{9,3... | collective-permute-start | bytes 1609736 | tf_op jit(solution)/shard_map/ppermute | solution.py:336
  107.0 1.4 collective-permute-start.11
  110.0 4.7 %all-to-all-start.1 = ((bf16[8,1280,128]{2,1,0:T(8,128)(2,1)}), bf16[8,1280,128]{2,1,0:T(8,128)(2,1)}, u32[]{:S(2)}, u32[]{:S(2)}) async-start(bf16[8,1280,128]{2,1,0:T(8,128)(2,1)} %shard_map.91), calls=%async_computation.1 | async-start | bytes 5242880 | tf_op jit(solution)/shard_map/all_to_all | solution.py:390
  114.7 36.6 %shard_map.89 = (bf16[128,1024]{1,0:T(8,128)(2,1)}, bf16[128,1024]{1,0:T(8,128)(2,1)}, bf16[128,1024]{1,0:T(8,128)(2,1)}, bf16[128,1024]{1,0:T(8,128)(2,1)}) custom-call(s32[4,32]{1,0:T(4,128)} %select_reduce_fusion.1.picks_ref, s32[4,2]{1,0:T(4,128)} %shard_map.86.starts_ref, bf16[2096,128]{1,0:T(8,128)(2,1)} %copy-done.3, bf16[2096,128]{1,0:T(8,128)(2,1)} %copy-done.14, ...), custom_call_target="tpu_custom_call" | custom-call | flops 51539607552 | tf_op jit(solution)/shard_map/pallas_call | solution.py:254
  152.8 1.3 collective-permute-start.5
  154.1 2.4 collective-permute-start.6
  157.4 16.7 %all-to-all-done.1.refs_1_ = bf16[8,1280,128]{2,1,0:T(8,128)(2,1)} async-done(((bf16[8,1280,128]{2,1,0:T(8,128)(2,1)}), bf16[8,1280,128]{2,1,0:T(8,128)(2,1)}, u32[]{:S(2)}, u32[]{:S(2)}) %all-to-all-start.1) | async-done | bytes 2621472 | tf_op jit(solution)/shard_map/all_to_all | solution.py:390
  174.8 4.7 %all-to-all-start.2 = ((bf16[8,768,128]{2,1,0:T(8,128)(2,1)}), bf16[8,768,128]{2,1,0:T(8,128)(2,1)S(1)}, u32[]{:S(2)}, u32[]{:S(2)}) async-start(bf16[8,768,128]{2,1,0:T(8,128)(2,1)} %shard_map.94), calls=%async_computation.2 | async-start | bytes 3145728 | tf_op jit(solution)/shard_map/all_to_all | solution.py:390
  179.5 25.6 %shard_map.92.refs_1_.refs_3_ = f32[4,1024,128]{2,1,0:T(8,128)} custom-call(s32[4,32]{1,0:T(4,128)} %select_reduce_fusion.picks_ref, s32[4,2]{1,0:T(4,128)} %shard_map.90.starts_ref, bf16[2096,128]{1,0:T(8,128)(2,1)} %collective-permute-done.8.refs_0_.refs_2_, bf16[2096,128]{1,0:T(8,128)(2,1)} %collective-permute-done.9.refs_1_.refs_3_, ...), custom_call_target="tpu_custom_call" | custom-call | flops 32212254720 | tf_op jit(solution)/shard_map/pallas_call | solution.py:254
  207.5 9.8 %all-to-all-done.2 = bf16[8,768,128]{2,1,0:T(8,128)(2,1)S(1)} async-done(((bf16[8,768,128]{2,1,0:T(8,128)(2,1)}), bf16[8,768,128]{2,1,0:T(8,128)(2,1)S(1)}, u32[]{:S(2)}, u32[]{:S(2)}) %all-to-all-start.2) | async-done | bytes 1572896 | tf_op jit(solution)/shard_map/all_to_all | solution.py:390
  218.5 11.9 %shard_map.95 = (bf16[128,1024]{1,0:T(8,128)(2,1)}, bf16[128,1024]{1,0:T(8,128)(2,1)}) custom-call(s32[4,32]{1,0:T(4,128)} %select_reduce_fusion.picks_ref, s32[4,2]{1,0:T(4,128)} %shard_map.93.starts_ref, bf16[2096,128]{1,0:T(8,128)(2,1)} %collective-permute-done.10.refs_2_.refs_4_.refs_0_, ...), custom_call_target="tpu_custom_call" | custom-call | flops 9663676416 | tf_op jit(solution)/shard_map/pallas_call | solution.py:254
  232.1 12.6 %shard_map.97 = (bf16[128,1024]{1,0:T(8,128)(2,1)}, bf16[128,1024]{1,0:T(8,128)(2,1)}) custom-call(s32[4,32]{1,0:T(4,128)} %select_reduce_fusion.picks_ref, s32[4,2]{1,0:T(4,128)} %shard_map.96.starts_ref, bf16[2096,128]{1,0:T(8,128)(2,1)} %collective-permute-done.8.refs_0_.refs_2_, bf16[2096,128]{1,0:T(8,128)(2,1)} %collective-permute-done.9.refs_1_.refs_3_, ...), custom_call_target="tpu_custom_call" | custom-call | flops 9663676416 | tf_op jit(solution)/shard_map/pallas_call | solution.py:254
  247.4 1.4 collective-permute-done.14.refs_5_
  249.4 3.8 %shard_map.99 = bf16[128,8192]{1,0:T(8,128)(2,1)} custom-call(s32[1]{0:T(128)} %bitcast.at_ref, bf16[128,1024]{1,0:T(8,128)(2,1)} %copy-done.8, bf16[128,1024]{1,0:T(8,128)(2,1)} %copy-done.9, bf16[128,1024]{1,0:T(8,128)(2,1)} %copy-done.10, bf16[128,1024]{1,0:T(8,128)(2,1)} %copy-done.11, bf16[128,1024]{1,0:T(8,128)(2,1)} %get-tuple-element.38.refs_4_, ...), custom_call_target="tpu_custom_call" | custom-call | bytes 4194304 | tf_op jit(solution)/shard_map/pallas_call | solution.py:284
  (92 shorter events, 22.5 us)
Async XLA Ops:
  6.7 6.6 %copy-start.21 = (f32[1,64]{1,0:T(1,128)S(1)}, f32[1,64]{1,0:T(1,128)}, u32[]{:S(2)}) copy-start(f32[1,64]{1,0:T(1,128)} %param.12) | copy-start | bytes 772
  6.7 6.6 %copy-start = (bf16[1,128,8192]{2,1,0:T(8,128)(2,1)S(1)}, bf16[1,128,8192]{2,1,0:T(8,128)(2,1)}, u32[]{:S(2)}) copy-start(bf16[1,128,8192]{2,1,0:T(8,128)(2,1)} %param.8) | copy-start | bytes 6291460
  6.7 101.8 %all-to-all-start = ((bf16[8,2048,128]{2,1,0:T(8,128)(2,1)}), bf16[8,2048,128]{2,1,0:T(8,128)(2,1)}, u32[]{:S(2)}, u32[]{:S(2)}) async-start(bf16[8,2048,128]{2,1,0:T(8,128)(2,1)} %bitcast.41), calls=%async_computation | async-start | bytes 8388608 | tf_op jit(solution)/shard_map/all_to_all | solution.py:390
  21.1 9.3 %copy-start.2 = (bf16[2096,128]{1,0:T(8,128)(2,1)S(1)}, bf16[2096,128]{1,0:T(8,128)(2,1)}, u32[]{:S(2)}) copy-start(bf16[2096,128]{1,0:T(8,128)(2,1)} %copy-done.1) | copy-start | bytes 1609732
  27.9 11.1 %copy-start.18 = (s32[1,8,8,32]{3,2,1,0:T(8,128)S(1)}, s32[1,8,8,32]{3,2,1,0:T(8,128)}, u32[]{:S(2)}) copy-start(s32[1,8,8,32]{3,2,1,0:T(8,128)} %param.15) | copy-start | bytes 24580
  27.9 68.1 %collective-permute-start = (bf16[2,4,1024,128]{3,2,1,0:T(8,128)(2,1)}, bf16[2,4,1024,128]{3,2,1,0:T(8,128)(2,1)}, u32[]{:S(2)}, u32[]{:S(2)}) collective-permute-start(bf16[2,4,1024,128]{3,2,1,0:T(8,128)(2,1)} %shard_map.84), channel_id=1, source_target_pairs={{0,24},{1,25},{2,26},{3,27},{4,28},{5,29},{6,30},{7,31},{8,0},{9,1... | collective-permute-start | bytes 6291464 | tf_op jit(solution)/shard_map/ppermute | solution.py:336
  30.4 122.4 %collective-permute-start.8 = (bf16[2096,128]{1,0:T(8,128)(2,1)S(1)}, bf16[2096,128]{1,0:T(8,128)(2,1)}, u32[]{:S(2)}, u32[]{:S(2)}) collective-permute-start(bf16[2096,128]{1,0:T(8,128)(2,1)S(1)} %copy-done.2), channel_id=1, source_target_pairs={{0,24},{1,25},{2,26},{3,27},{4,28},{5,29},{6,30},{7,31},{8,0},{9,1... | collective-permute-start | bytes 1609736 | tf_op jit(solution)/shard_map/ppermute | solution.py:336
  36.9 67.3 %collective-permute-start.1 = (bf16[2096,128]{1,0:T(8,128)(2,1)}, bf16[2096,128]{1,0:T(8,128)(2,1)S(1)}, u32[]{:S(2)}, u32[]{:S(2)}) collective-permute-start(bf16[2096,128]{1,0:T(8,128)(2,1)} %get-tuple-element.26), channel_id=1, source_target_pairs={{0,1},{1,0},{2,3},{3,2},{4,5},{5,4},{6,7},{7,6},{8,9},{9,8},{10,11... | collective-permute-start | bytes 1609736 | tf_op jit(solution)/shard_map/ppermute | solution.py:332
  36.9 70.1 %collective-permute-start.2 = (bf16[2096,128]{1,0:T(8,128)(2,1)}, bf16[2096,128]{1,0:T(8,128)(2,1)S(1)}, u32[]{:S(2)}, u32[]{:S(2)}) collective-permute-start(bf16[2096,128]{1,0:T(8,128)(2,1)} %get-tuple-element.27), channel_id=1, source_target_pairs={{0,2},{1,3},{2,0},{3,1},{4,6},{5,7},{6,4},{7,5},{8,10},{9,11},{10,... | collective-permute-start | bytes 1609736 | tf_op jit(solution)/shard_map/ppermute | solution.py:332
  38.9 69.5 %collective-permute-start.3 = (bf16[2096,128]{1,0:T(8,128)(2,1)}, bf16[2096,128]{1,0:T(8,128)(2,1)S(1)}, u32[]{:S(2)}, u32[]{:S(2)}) collective-permute-start(bf16[2096,128]{1,0:T(8,128)(2,1)} %get-tuple-element.28), channel_id=1, source_target_pairs={{0,3},{1,2},{2,1},{3,0},{4,7},{5,6},{6,5},{7,4},{8,11},{9,10},{10,... | collective-permute-start | bytes 1609736 | tf_op jit(solution)/shard_map/ppermute | solution.py:332
  93.6 10.6 %copy-start.19 = (s32[4,2]{1,0:T(4,128)}, s32[4,2]{1,0:T(4,128)S(1)}, u32[]{:S(2)}) copy-start(s32[4,2]{1,0:T(4,128)S(1)} %get-tuple-element.56.refs_0_) | copy-start | bytes 100
  96.0 8.1 %copy-start.5 = (bf16[2096,128]{1,0:T(8,128)(2,1)S(1)}, bf16[2096,128]{1,0:T(8,128)(2,1)}, u32[]{:S(2)}) copy-start(bf16[2096,128]{1,0:T(8,128)(2,1)} %copy-done.4) | copy-start | bytes 1609732
  96.1 58.0 %collective-permute-start.9 = (bf16[2096,128]{1,0:T(8,128)(2,1)}, bf16[2096,128]{1,0:T(8,128)(2,1)}, u32[]{:S(2)}, u32[]{:S(2)}) collective-permute-start(bf16[2096,128]{1,0:T(8,128)(2,1)} %copy-done.6), channel_id=1, source_target_pairs={{0,25},{1,24},{2,27},{3,26},{4,29},{5,28},{6,31},{7,30},{8,1},{9,0... | collective-permute-start | bytes 1609736 | tf_op jit(solution)/shard_map/ppermute | solution.py:336
  104.2 52.3 %collective-permute-start.10 = (bf16[2096,128]{1,0:T(8,128)(2,1)S(1)}, bf16[2096,128]{1,0:T(8,128)(2,1)}, u32[]{:S(2)}, u32[]{:S(2)}) collective-permute-start(bf16[2096,128]{1,0:T(8,128)(2,1)S(1)} %copy-done.5), channel_id=1, source_target_pairs={{0,26},{1,27},{2,24},{3,25},{4,30},{5,31},{6,28},{7,29},{8,2},{9,3... | collective-permute-start | bytes 1609736 | tf_op jit(solution)/shard_map/ppermute | solution.py:336
  107.0 50.3 %collective-permute-start.11 = (bf16[2096,128]{1,0:T(8,128)(2,1)S(1)}, bf16[2096,128]{1,0:T(8,128)(2,1)}, u32[]{:S(2)}, u32[]{:S(2)}) collective-permute-start(bf16[2096,128]{1,0:T(8,128)(2,1)S(1)} %get-tuple-element.35), channel_id=1, source_target_pairs={{0,27},{1,26},{2,25},{3,24},{4,31},{5,30},{6,29},{7,28},{8,3},{9,2... | collective-permute-start | bytes 1609736 | tf_op jit(solution)/shard_map/ppermute | solution.py:336
  110.0 64.1 %all-to-all-start.1 = ((bf16[8,1280,128]{2,1,0:T(8,128)(2,1)}), bf16[8,1280,128]{2,1,0:T(8,128)(2,1)}, u32[]{:S(2)}, u32[]{:S(2)}) async-start(bf16[8,1280,128]{2,1,0:T(8,128)(2,1)} %shard_map.91), calls=%async_computation.1 | async-start | bytes 5242880 | tf_op jit(solution)/shard_map/all_to_all | solution.py:390
  151.3 53.8 %collective-permute-start.4 = (bf16[128,1024]{1,0:T(8,128)(2,1)}, bf16[128,1024]{1,0:T(8,128)(2,1)S(1)}, u32[]{:S(2)}, u32[]{:S(2)}) collective-permute-start(bf16[128,1024]{1,0:T(8,128)(2,1)} %get-tuple-element.29.refs_1_), channel_id=1, source_target_pairs={{0,24},{1,25},{2,26},{3,27},{4,28},{5,29},{6,30},{7,31},{8,0},{9,1... | collective-permute-start | bytes 786440 | tf_op jit(solution)/shard_map/ppermute | solution.py:336
  152.8 52.4 %collective-permute-start.5 = (bf16[128,1024]{1,0:T(8,128)(2,1)}, bf16[128,1024]{1,0:T(8,128)(2,1)S(1)}, u32[]{:S(2)}, u32[]{:S(2)}) collective-permute-start(bf16[128,1024]{1,0:T(8,128)(2,1)} %get-tuple-element.30), channel_id=1, source_target_pairs={{0,25},{1,24},{2,27},{3,26},{4,29},{5,28},{6,31},{7,30},{8,1},{9,0... | collective-permute-start | bytes 786440 | tf_op jit(solution)/shard_map/ppermute | solution.py:336
  154.1 51.1 %collective-permute-start.6 = (bf16[128,1024]{1,0:T(8,128)(2,1)}, bf16[128,1024]{1,0:T(8,128)(2,1)S(1)}, u32[]{:S(2)}, u32[]{:S(2)}) collective-permute-start(bf16[128,1024]{1,0:T(8,128)(2,1)} %get-tuple-element.31), channel_id=1, source_target_pairs={{0,26},{1,27},{2,24},{3,25},{4,30},{5,31},{6,28},{7,29},{8,2},{9,3... | collective-permute-start | bytes 786440 | tf_op jit(solution)/shard_map/ppermute | solution.py:336
  156.5 48.7 %collective-permute-start.7 = (bf16[128,1024]{1,0:T(8,128)(2,1)}, bf16[128,1024]{1,0:T(8,128)(2,1)S(1)}, u32[]{:S(2)}, u32[]{:S(2)}) collective-permute-start(bf16[128,1024]{1,0:T(8,128)(2,1)} %get-tuple-element.32), channel_id=1, source_target_pairs={{0,27},{1,26},{2,25},{3,24},{4,31},{5,30},{6,29},{7,28},{8,3},{9,2... | collective-permute-start | bytes 786440 | tf_op jit(solution)/shard_map/ppermute | solution.py:336
  174.8 42.6 %all-to-all-start.2 = ((bf16[8,768,128]{2,1,0:T(8,128)(2,1)}), bf16[8,768,128]{2,1,0:T(8,128)(2,1)S(1)}, u32[]{:S(2)}, u32[]{:S(2)}) async-start(bf16[8,768,128]{2,1,0:T(8,128)(2,1)} %shard_map.94), calls=%async_computation.2 | async-start | bytes 3145728 | tf_op jit(solution)/shard_map/all_to_all | solution.py:390
  231.1 13.6 %collective-permute-start.12 = (bf16[128,1024]{1,0:T(8,128)(2,1)}, bf16[128,1024]{1,0:T(8,128)(2,1)S(1)}, u32[]{:S(2)}, u32[]{:S(2)}) collective-permute-start(bf16[128,1024]{1,0:T(8,128)(2,1)} %get-tuple-element.37.refs_1_), channel_id=1, source_target_pairs={{0,2},{1,3},{2,0},{3,1},{4,6},{5,7},{6,4},{7,5},{8,10},{9,11},{10,... | collective-permute-start | bytes 786440 | tf_op jit(solution)/shard_map/ppermute | solution.py:332
  231.1 13.6 %collective-permute-start.13 = (bf16[128,1024]{1,0:T(8,128)(2,1)}, bf16[128,1024]{1,0:T(8,128)(2,1)S(1)}, u32[]{:S(2)}, u32[]{:S(2)}) collective-permute-start(bf16[128,1024]{1,0:T(8,128)(2,1)} %get-tuple-element.40), channel_id=1, source_target_pairs={{0,3},{1,2},{2,1},{3,0},{4,7},{5,6},{6,5},{7,4},{8,11},{9,10},{10,... | collective-permute-start | bytes 786440 | tf_op jit(solution)/shard_map/ppermute | solution.py:332
  246.2 2.5 collective-permute-start.14
  (16 other events, 22.8 us)
